TPU v7x, 256 devices: a whole 4x4x8 slice. The times are simulated.
256 devices in a mesh: sec: 16 (over y, z_lo, core), row: 16 (over z_hi, x).
Axes of the slice: x: 4, y: 4, z: 8 (z_hi: 4, z_lo: 2; z = z_hi * 2 + z_lo), core: 2. Of those that a mesh axis runs over, the one named last changes fastest.
Arguments:
- env_in: bfloat16 [32, 16, 2, 256, 512], P('row', 'sec'), may hold values from -6 to 6
- ket_mps: bfloat16 [4, 16, 2, 512, 512], P(None, 'sec'), may hold values from -0.25 to 0.25
- bra_mps: bfloat16 [4, 16, 2, 256, 256], P(None, 'sec'), may hold values from -0.375 to 0.375
- ket_sizes: int32 [16, 2], replicated, may hold values from 64 to 512, as said below
- bra_sizes: int32 [16, 2], replicated, may hold values from 64 to 256, as said below
- entries: int32 [32, 8, 3], P('row'), may hold values from 0 to 31, as said below
- coeffs: float32 [32, 8], P('row'), may hold values from -3 to 3
Outputs:
- env_out: bfloat16 [32, 16, 2, 256, 512], P('row', 'sec')
Inputs may be any that keep to these rules, and one draw needn't show every extreme that they name: `ket_sizes`: each ket sector size is at least 64 and at most 512; one sector has exactly 512. `bra_sizes`: each bra sector size is at least 64 and at most 256; one sector has exactly 256. `entries`: every entry (wo, sp, s) of input channel wi conserves charge: c(wo) = c(wi) + n(sp) - n(s); sp and s lie in 0 to 3.
All inputs are finite; a program needn't handle non-finite values.
Results may differ from a plain program's by a relative error of at most 0.014.
Values may be sent and summed in bfloat16 or wider, within the bound.
No kernel may reach another device: no remote copies, remote signals or barrier semaphores. Data moves between devices by JAX's collectives and lax.ppermute only.
A program may use at most 128 MiB of HBM per device.

v0:
```python
import jax
import jax.numpy as jnp
from jax import lax
from jax.sharding import PartitionSpec as P

EPW = 8


def passed_along(value, axis, steps):
    count = lax.axis_size(axis)
    first, last = (max(0, -steps), min(count, count - steps))
    return lax.ppermute(value, axis, [(source, source + steps) for source in range(first, last)])


def extended(cells, sides, width):
    for axis, dim in sides:
        count = lax.axis_size(axis)
        ends = count - 1
        head = lax.slice_in_dim(cells, 0, width, axis=dim)
        tail = lax.slice_in_dim(cells, cells.shape[dim] - width, cells.shape[dim], axis=dim)
        cells = jnp.concatenate(
            [
                lax.ppermute(tail, axis, [(i, (i + 1) % count) for i in range(ends)]),
                cells,
                lax.ppermute(head, axis, [((i + 1) % count, i) for i in range(ends)]),
            ],
            axis=dim,
        )
    return cells


def channel_charge(channel):
    klass = channel % 9
    return (klass % 3 - 1, klass // 3 - 1)


def keep_block(block, rows, cols):
    keep_rows = lax.broadcasted_iota(jnp.int32, block.shape, block.ndim - 2) < rows[..., None, None]
    keep_cols = lax.broadcasted_iota(jnp.int32, block.shape, block.ndim - 1) < cols[..., None, None]
    return jnp.where(keep_rows & keep_cols, block, jnp.zeros_like(block))


def body(env_in, ket_mps, bra_mps, ket_sizes, bra_sizes, entries, coeffs):
    chans, _, sec_b, bra_w, ket_w = env_in.shape
    my_a = lax.axis_index("sec")
    first_w = lax.axis_index("row") * chans
    ket_ext = jnp.pad(ket_sizes, 2)
    bra_ext = jnp.pad(bra_sizes, 2)
    zero = jnp.zeros((), jnp.int32)

    def sizes_at(ext, shift_a, shift_b):
        return lax.dynamic_slice(ext, (my_a + shift_a + 2, shift_b + 2), (1, sec_b))

    lower_env, lower_ket = passed_along((env_in, ket_mps[1::2]), "sec", 1)
    env_two = jnp.pad(
        jnp.concatenate([lower_env, env_in], axis=1), ((0, 0), (0, 0), (1, 0), (0, 0), (0, 0))
    )
    ket_all = jnp.pad(
        jnp.concatenate([ket_mps, lower_ket], axis=0), ((0, 0), (0, 0), (1, 0), (0, 0), (0, 0))
    )
    bra_rim = extended(bra_mps, (("sec", 1),), 1)
    bra_all = jnp.pad(bra_rim, ((0, 0), (0, 0), (1, 1), (0, 0), (0, 0)))

    def entry_term(item):
        chan = item // EPW
        slot = item % EPW
        out_w = entries[chan, slot, 0]
        phys_bra = entries[chan, slot, 1]
        phys_ket = entries[chan, slot, 2]
        value = coeffs[chan, slot]
        up_a = phys_ket % 2
        up_b = phys_ket // 2
        in_a, in_b = channel_charge(first_w + chan)
        out_a, out_b = channel_charge(out_w)
        env_blk = lax.dynamic_slice(
            env_two, (chan, 1 - up_a, 1 - up_b, zero, zero), (1, 1, sec_b, bra_w, ket_w)
        )[0]
        ket_index = jnp.where(up_a == 0, phys_ket, 4 + phys_ket // 2)
        ket_blk = lax.dynamic_slice(
            ket_all, (ket_index, zero, 1 - up_b, zero, zero), (1, 1, sec_b, ket_w, ket_w)
        )[0]
        bra_blk = lax.dynamic_slice(
            bra_all, (phys_bra, 1 + out_a, 1 + out_b, zero, zero), (1, 1, sec_b, bra_w, bra_w)
        )[0]
        ket_src = sizes_at(ket_ext, -up_a, -up_b)
        env_blk = keep_block(env_blk, sizes_at(bra_ext, in_a - up_a, in_b - up_b), ket_src)
        ket_blk = keep_block(ket_blk, ket_src, sizes_at(ket_ext, zero, zero))
        bra_blk = keep_block(
            bra_blk,
            sizes_at(bra_ext, out_a - phys_bra % 2, out_b - phys_bra // 2),
            sizes_at(bra_ext, out_a, out_b),
        )
        half = jnp.einsum(
            "abik,abkl->abil", env_blk, ket_blk, preferred_element_type=jnp.float32
        ).astype(jnp.bfloat16)
        return value * jnp.einsum(
            "abij,abil->abjl", bra_blk, half, preferred_element_type=jnp.float32
        )

    count = chans * lax.axis_size("row")

    def step(item, partial_value):
        out_w = entries[item // EPW, item % EPW, 0]
        inside = (out_w >= zero) & (out_w < zero + count)

        def add_term(acc):
            where_at = (out_w, zero, zero, zero, zero)
            old = lax.dynamic_slice(acc, where_at, (1, 1, sec_b, bra_w, ket_w))
            return lax.dynamic_update_slice(acc, old + entry_term(item)[None], where_at)

        return lax.cond(inside, add_term, lambda acc: acc, partial_value)

    return lax.psum_scatter(
        lax.fori_loop(
            0, chans * EPW, step, jnp.zeros((count, 1, sec_b, bra_w, ket_w), jnp.float32)
        ).astype(jnp.bfloat16),
        "row",
        scatter_dimension=0,
        tiled=True,
    )


def solution(mesh):
    placed = (
        P("row", "sec", None, None, None),
        P(None, "sec", None, None, None),
        P(None, "sec", None, None, None),
        P(),
        P(),
        P("row", None, None),
        P("row", None),
    )
    return jax.shard_map(
        body,
        mesh=mesh,
        in_specs=placed,
        out_specs=P("row", "sec", None, None, None),
        check_vma=False,
    )
```

profile of v0, /device:TPU:12, one launch (start us, length us, event | category | flops | bytes accessed | tf_op | source)
XLA Modules:
  0.0 594.7 jit_solution(4223533753655322057)
XLA Ops:
  21.9 6.9 %collective-permute-done.2 = bf16[2,1,2,256,512]{4,3,2,1,0:T(8,128)(2,1)} collective-permute-done((bf16[2,1,2,256,512]{4,3,2,1,0:T(8,128)(2,1)}, bf16[2,1,2,256,512]{4,3,2,1,0:T(8,128)(2,1)}, u32[]{:S(2)}, u32[]{:S(2)}) %collective-permute-start.2) | collective-permute-done | bytes 1048608 | tf_op jit(solution)/shard_map/ppermute | solution.py:12
  32.3 14.2 %collective-permute-done = bf16[4,1,2,256,256]{3,4,2,1,0:T(8,128)(2,1)} collective-permute-done((bf16[4,1,2,256,256]{3,4,2,1,0:T(8,128)(2,1)S(1)}, bf16[4,1,2,256,256]{3,4,2,1,0:T(8,128)(2,1)}, u32[]{:S(2)}, u32[]{:S(2)}) %collective-permute-start) | collective-permute-done | bytes 1048608 | tf_op jit(solution)/shard_map/ppermute | solution.py:23
  46.5 4.4 fusion.51
  50.9 17.9 %collective-permute-done.3 = bf16[2,1,2,512,512]{4,3,2,1,0:T(8,128)(2,1)S(1)} collective-permute-done((bf16[2,1,2,512,512]{4,3,2,1,0:T(8,128)(2,1)}, bf16[2,1,2,512,512]{4,3,2,1,0:T(8,128)(2,1)S(1)}, u32[]{:S(2)}, u32[]{:S(2)}) %collective-permute-start.3) | collective-permute-done | bytes 2097184 | tf_op jit(solution)/shard_map/ppermute | solution.py:12
  68.8 4.4 fusion.46
  73.2 11.3 %broadcast_in_dim.4 = f32[32,1,2,256,512]{4,3,2,1,0:T(8,128)} broadcast(f32[]{:T(128)} %constant.222.clone.1), dimensions={} | broadcast | bytes 33554436 | tf_op jit(solution)/shard_map/broadcast_in_dim | solution.py:115
  84.5 275.6 %while.18 = (s32[]{:T(128)}, f32[32,1,2,256,512]{4,3,2,1,0:T(8,128)}, s32[2,8,3]{1,0,2:T(2,128)S(1)}, f32[2,8]{1,0:T(2,128)S(1)}, s32[]{:T(128)}, /*index=5*/s32...) while((s32[]{:T(128)}, ...), condition=%wide.region_3.4_spmd, body=%wide.region_0.3_spmd.sunk | while | flops 407109824 | bytes 3942862 | solution.py:114
  86.3 15.4 %conditional.2 = (f32[32,1,2,256,512]{4,3,2,1,0:T(8,128)}) conditional(s32[]{:T(128)} %convert_element_type.28, f32[32,1,2,256,512]{4,3,2,1,0:T(8,128)} %get-tuple-element.440, (s32[]{:T(128)}, f32[32,1,2,256,512]{4,3,2,1,0:T(8,128)}, s32[]{:T(128)}, f32[2,8]{1,0:T(2,128)S(1)}, s32[2,8,3]{1,0,2:T(2,128)S(1)}, /*index=5*/s32[]{:T(128)}, ...), branch_computations={%region_1.1_spmd, %region_2.2_spmd} | conditional | flops 407109792 | bytes 3942368 | solution.py:111
  97.5 4.3 fusion.4
  103.6 15.4 %conditional.2 = (f32[32,1,2,256,512]{4,3,2,1,0:T(8,128)}) conditional(s32[]{:T(128)} %convert_element_type.28, f32[32,1,2,256,512]{4,3,2,1,0:T(8,128)} %get-tuple-element.440, (s32[]{:T(128)}, f32[32,1,2,256,512]{4,3,2,1,0:T(8,128)}, s32[]{:T(128)}, f32[2,8]{1,0:T(2,128)S(1)}, s32[2,8,3]{1,0,2:T(2,128)S(1)}, /*index=5*/s32[]{:T(128)}, ...), branch_computations={%region_1.1_spmd, %region_2.2_spmd} | conditional | flops 407109792 | bytes 3942368 | solution.py:111
  120.8 15.4 %conditional.2 = (f32[32,1,2,256,512]{4,3,2,1,0:T(8,128)}) conditional(s32[]{:T(128)} %convert_element_type.28, f32[32,1,2,256,512]{4,3,2,1,0:T(8,128)} %get-tuple-element.440, (s32[]{:T(128)}, f32[32,1,2,256,512]{4,3,2,1,0:T(8,128)}, s32[]{:T(128)}, f32[2,8]{1,0:T(2,128)S(1)}, s32[2,8,3]{1,0,2:T(2,128)S(1)}, /*index=5*/s32[]{:T(128)}, ...), branch_computations={%region_1.1_spmd, %region_2.2_spmd} | conditional | flops 407109792 | bytes 3942368 | solution.py:111
  131.9 4.3 fusion.4
  138.0 15.4 %conditional.2 = (f32[32,1,2,256,512]{4,3,2,1,0:T(8,128)}) conditional(s32[]{:T(128)} %convert_element_type.28, f32[32,1,2,256,512]{4,3,2,1,0:T(8,128)} %get-tuple-element.440, (s32[]{:T(128)}, f32[32,1,2,256,512]{4,3,2,1,0:T(8,128)}, s32[]{:T(128)}, f32[2,8]{1,0:T(2,128)S(1)}, s32[2,8,3]{1,0,2:T(2,128)S(1)}, /*index=5*/s32[]{:T(128)}, ...), branch_computations={%region_1.1_spmd, %region_2.2_spmd} | conditional | flops 407109792 | bytes 3942368 | solution.py:111
  155.2 15.4 %conditional.2 = (f32[32,1,2,256,512]{4,3,2,1,0:T(8,128)}) conditional(s32[]{:T(128)} %convert_element_type.28, f32[32,1,2,256,512]{4,3,2,1,0:T(8,128)} %get-tuple-element.440, (s32[]{:T(128)}, f32[32,1,2,256,512]{4,3,2,1,0:T(8,128)}, s32[]{:T(128)}, f32[2,8]{1,0:T(2,128)S(1)}, s32[2,8,3]{1,0,2:T(2,128)S(1)}, /*index=5*/s32[]{:T(128)}, ...), branch_computations={%region_1.1_spmd, %region_2.2_spmd} | conditional | flops 407109792 | bytes 3942368 | solution.py:111
  172.5 15.4 %conditional.2 = (f32[32,1,2,256,512]{4,3,2,1,0:T(8,128)}) conditional(s32[]{:T(128)} %convert_element_type.28, f32[32,1,2,256,512]{4,3,2,1,0:T(8,128)} %get-tuple-element.440, (s32[]{:T(128)}, f32[32,1,2,256,512]{4,3,2,1,0:T(8,128)}, s32[]{:T(128)}, f32[2,8]{1,0:T(2,128)S(1)}, s32[2,8,3]{1,0,2:T(2,128)S(1)}, /*index=5*/s32[]{:T(128)}, ...), branch_computations={%region_1.1_spmd, %region_2.2_spmd} | conditional | flops 407109792 | bytes 3942368 | solution.py:111
  183.6 4.3 fusion.4
  189.7 15.4 %conditional.2 = (f32[32,1,2,256,512]{4,3,2,1,0:T(8,128)}) conditional(s32[]{:T(128)} %convert_element_type.28, f32[32,1,2,256,512]{4,3,2,1,0:T(8,128)} %get-tuple-element.440, (s32[]{:T(128)}, f32[32,1,2,256,512]{4,3,2,1,0:T(8,128)}, s32[]{:T(128)}, f32[2,8]{1,0:T(2,128)S(1)}, s32[2,8,3]{1,0,2:T(2,128)S(1)}, /*index=5*/s32[]{:T(128)}, ...), branch_computations={%region_1.1_spmd, %region_2.2_spmd} | conditional | flops 407109792 | bytes 3942368 | solution.py:111
  200.9 4.3 fusion.4
  207.0 15.4 %conditional.2 = (f32[32,1,2,256,512]{4,3,2,1,0:T(8,128)}) conditional(s32[]{:T(128)} %convert_element_type.28, f32[32,1,2,256,512]{4,3,2,1,0:T(8,128)} %get-tuple-element.440, (s32[]{:T(128)}, f32[32,1,2,256,512]{4,3,2,1,0:T(8,128)}, s32[]{:T(128)}, f32[2,8]{1,0:T(2,128)S(1)}, s32[2,8,3]{1,0,2:T(2,128)S(1)}, /*index=5*/s32[]{:T(128)}, ...), branch_computations={%region_1.1_spmd, %region_2.2_spmd} | conditional | flops 407109792 | bytes 3942368 | solution.py:111
  224.2 15.3 %conditional.2 = (f32[32,1,2,256,512]{4,3,2,1,0:T(8,128)}) conditional(s32[]{:T(128)} %convert_element_type.28, f32[32,1,2,256,512]{4,3,2,1,0:T(8,128)} %get-tuple-element.440, (s32[]{:T(128)}, f32[32,1,2,256,512]{4,3,2,1,0:T(8,128)}, s32[]{:T(128)}, f32[2,8]{1,0:T(2,128)S(1)}, s32[2,8,3]{1,0,2:T(2,128)S(1)}, /*index=5*/s32[]{:T(128)}, ...), branch_computations={%region_1.1_spmd, %region_2.2_spmd} | conditional | flops 407109792 | bytes 3942368 | solution.py:111
  241.4 15.4 %conditional.2 = (f32[32,1,2,256,512]{4,3,2,1,0:T(8,128)}) conditional(s32[]{:T(128)} %convert_element_type.28, f32[32,1,2,256,512]{4,3,2,1,0:T(8,128)} %get-tuple-element.440, (s32[]{:T(128)}, f32[32,1,2,256,512]{4,3,2,1,0:T(8,128)}, s32[]{:T(128)}, f32[2,8]{1,0:T(2,128)S(1)}, s32[2,8,3]{1,0,2:T(2,128)S(1)}, /*index=5*/s32[]{:T(128)}, ...), branch_computations={%region_1.1_spmd, %region_2.2_spmd} | conditional | flops 407109792 | bytes 3942368 | solution.py:111
  258.6 15.4 %conditional.2 = (f32[32,1,2,256,512]{4,3,2,1,0:T(8,128)}) conditional(s32[]{:T(128)} %convert_element_type.28, f32[32,1,2,256,512]{4,3,2,1,0:T(8,128)} %get-tuple-element.440, (s32[]{:T(128)}, f32[32,1,2,256,512]{4,3,2,1,0:T(8,128)}, s32[]{:T(128)}, f32[2,8]{1,0:T(2,128)S(1)}, s32[2,8,3]{1,0,2:T(2,128)S(1)}, /*index=5*/s32[]{:T(128)}, ...), branch_computations={%region_1.1_spmd, %region_2.2_spmd} | conditional | flops 407109792 | bytes 3942368 | solution.py:111
  275.8 15.4 %conditional.2 = (f32[32,1,2,256,512]{4,3,2,1,0:T(8,128)}) conditional(s32[]{:T(128)} %convert_element_type.28, f32[32,1,2,256,512]{4,3,2,1,0:T(8,128)} %get-tuple-element.440, (s32[]{:T(128)}, f32[32,1,2,256,512]{4,3,2,1,0:T(8,128)}, s32[]{:T(128)}, f32[2,8]{1,0:T(2,128)S(1)}, s32[2,8,3]{1,0,2:T(2,128)S(1)}, /*index=5*/s32[]{:T(128)}, ...), branch_computations={%region_1.1_spmd, %region_2.2_spmd} | conditional | flops 407109792 | bytes 3942368 | solution.py:111
  286.9 4.3 fusion.4
  293.0 15.4 %conditional.2 = (f32[32,1,2,256,512]{4,3,2,1,0:T(8,128)}) conditional(s32[]{:T(128)} %convert_element_type.28, f32[32,1,2,256,512]{4,3,2,1,0:T(8,128)} %get-tuple-element.440, (s32[]{:T(128)}, f32[32,1,2,256,512]{4,3,2,1,0:T(8,128)}, s32[]{:T(128)}, f32[2,8]{1,0:T(2,128)S(1)}, s32[2,8,3]{1,0,2:T(2,128)S(1)}, /*index=5*/s32[]{:T(128)}, ...), branch_computations={%region_1.1_spmd, %region_2.2_spmd} | conditional | flops 407109792 | bytes 3942368 | solution.py:111
  304.1 4.3 fusion.4
  310.3 15.4 %conditional.2 = (f32[32,1,2,256,512]{4,3,2,1,0:T(8,128)}) conditional(s32[]{:T(128)} %convert_element_type.28, f32[32,1,2,256,512]{4,3,2,1,0:T(8,128)} %get-tuple-element.440, (s32[]{:T(128)}, f32[32,1,2,256,512]{4,3,2,1,0:T(8,128)}, s32[]{:T(128)}, f32[2,8]{1,0:T(2,128)S(1)}, s32[2,8,3]{1,0,2:T(2,128)S(1)}, /*index=5*/s32[]{:T(128)}, ...), branch_computations={%region_1.1_spmd, %region_2.2_spmd} | conditional | flops 407109792 | bytes 3942368 | solution.py:111
  321.4 4.3 fusion.4
  327.5 15.4 %conditional.2 = (f32[32,1,2,256,512]{4,3,2,1,0:T(8,128)}) conditional(s32[]{:T(128)} %convert_element_type.28, f32[32,1,2,256,512]{4,3,2,1,0:T(8,128)} %get-tuple-element.440, (s32[]{:T(128)}, f32[32,1,2,256,512]{4,3,2,1,0:T(8,128)}, s32[]{:T(128)}, f32[2,8]{1,0:T(2,128)S(1)}, s32[2,8,3]{1,0,2:T(2,128)S(1)}, /*index=5*/s32[]{:T(128)}, ...), branch_computations={%region_1.1_spmd, %region_2.2_spmd} | conditional | flops 407109792 | bytes 3942368 | solution.py:111
  344.7 15.4 %conditional.2 = (f32[32,1,2,256,512]{4,3,2,1,0:T(8,128)}) conditional(s32[]{:T(128)} %convert_element_type.28, f32[32,1,2,256,512]{4,3,2,1,0:T(8,128)} %get-tuple-element.440, (s32[]{:T(128)}, f32[32,1,2,256,512]{4,3,2,1,0:T(8,128)}, s32[]{:T(128)}, f32[2,8]{1,0:T(2,128)S(1)}, s32[2,8,3]{1,0,2:T(2,128)S(1)}, /*index=5*/s32[]{:T(128)}, ...), branch_computations={%region_1.1_spmd, %region_2.2_spmd} | conditional | flops 407109792 | bytes 3942368 | solution.py:111
  360.1 17.3 %convert_element_type.23 = bf16[32,1,2,256,512]{4,3,2,1,0:T(8,128)(2,1)} convert(f32[32,1,2,256,512]{4,3,2,1,0:T(8,128)} %get-tuple-element.319) | non-fusion elementwise | flops 8388608 | bytes 50331648 | tf_op jit(solution)/shard_map/convert_element_type | solution.py:116
  377.4 210.5 %reduce-scatter.2.cloned.1.call-done = bf16[2,1,2,256,512]{4,3,2,1,0:T(8,128)(2,1)} async-done(((bf16[32,1,2,256,512]{4,3,2,1,0:T(8,128)(2,1)}), bf16[2,1,2,256,512]{4,3,2,1,0:T(8,128)(2,1)}) %reduce-scatter.2.cloned.1.call-update) | async-done | bytes 1048592 | tf_op jit(solution)/shard_map/reduce_scatter | solution.py:113
  (97 shorter events, 89.3 us)
Async XLA Ops:
  6.5 15.0 %copy-start.3 = (s32[16,2]{0,1:T(2,128)S(1)}, s32[16,2]{0,1:T(2,128)}, u32[]{:S(2)}) copy-start(s32[16,2]{0,1:T(2,128)} %param.15) | copy-start | bytes 388
  6.5 15.2 %copy-start.4 = (s32[16,2]{0,1:T(2,128)S(1)}, s32[16,2]{0,1:T(2,128)}, u32[]{:S(2)}) copy-start(s32[16,2]{0,1:T(2,128)} %param.14) | copy-start | bytes 388
  6.5 581.4 %reduce-scatter.2.cloned.1.call-start = ((), (), s32[]{:S(2)}) async-start(), calls=%async_computation.1 | async-start | bytes 17825792 | tf_op jit(solution)/shard_map/reduce_scatter | solution.py:113
  6.5 22.3 %collective-permute-start.2 = (bf16[2,1,2,256,512]{4,3,2,1,0:T(8,128)(2,1)}, bf16[2,1,2,256,512]{4,3,2,1,0:T(8,128)(2,1)}, u32[]{:S(2)}, u32[]{:S(2)}) collective-permute-start(bf16[2,1,2,256,512]{4,3,2,1,0:T(8,128)(2,1)} %param.11), channel_id=1, source_target_pairs={{0,16},{16,32},{32,48},{48,64},{64,80},{80,96},{96,112},{112,128},... | collective-permute-start | bytes 3145736 | tf_op jit(solution)/shard_map/ppermute | solution.py:12
  10.1 36.4 %collective-permute-start = (bf16[4,1,2,256,256]{3,4,2,1,0:T(8,128)(2,1)S(1)}, bf16[4,1,2,256,256]{3,4,2,1,0:T(8,128)(2,1)}, u32[]{:S(2)}, u32[]{:S(2)}) collective-permute-start(bf16[4,1,2,256,256]{3,4,2,1,0:T(8,128)(2,1)S(1)} %copy.9), channel_id=1, source_target_pairs={{0,16},{16,32},{32,48},{48,64},{64,80},{80,96},{96,112},{112,128},... | collective-permute-start | bytes 3145736 | tf_op jit(solution)/shard_map/ppermute | solution.py:23
  14.0 32.5 %collective-permute-start.1 = (bf16[4,1,2,256,256]{3,4,2,1,0:T(8,128)(2,1)S(1)}, bf16[4,1,2,256,256]{3,4,2,1,0:T(8,128)(2,1)}, u32[]{:S(2)}, u32[]{:S(2)}) collective-permute-start(bf16[4,1,2,256,256]{3,4,2,1,0:T(8,128)(2,1)S(1)} %copy.9), channel_id=1, source_target_pairs={{16,0},{32,16},{48,32},{64,48},{80,64},{96,80},{112,96},{128,112},... | collective-permute-start | bytes 3145736 | tf_op jit(solution)/shard_map/ppermute | solution.py:25
  19.6 49.2 %collective-permute-start.3 = (bf16[2,1,2,512,512]{4,3,2,1,0:T(8,128)(2,1)}, bf16[2,1,2,512,512]{4,3,2,1,0:T(8,128)(2,1)S(1)}, u32[]{:S(2)}, u32[]{:S(2)}) collective-permute-start(bf16[2,1,2,512,512]{4,3,2,1,0:T(8,128)(2,1)} %slice.3), channel_id=1, source_target_pairs={{0,16},{16,32},{32,48},{48,64},{64,80},{80,96},{96,112},{112,128},... | collective-permute-start | bytes 6291464 | tf_op jit(solution)/shard_map/ppermute | solution.py:12
  21.9 46.9 %copy-start = (bf16[4,1,2,512,512]{4,3,2,1,0:T(8,128)(2,1)S(1)}, bf16[4,1,2,512,512]{4,3,2,1,0:T(8,128)(2,1)}, u32[]{:S(2)}) copy-start(bf16[4,1,2,512,512]{4,3,2,1,0:T(8,128)(2,1)} %param.12) | copy-start | bytes 12582916
  73.2 11.3 %copy-start.1 = (s32[2,8,3]{1,0,2:T(2,128)S(1)}, s32[2,8,3]{1,0,2:T(2,128)}, u32[]{:S(2)}) copy-start(s32[2,8,3]{1,0,2:T(2,128)} %param.16) | copy-start | bytes 580
  73.2 11.3 %copy-start.2 = (f32[2,8]{1,0:T(2,128)S(1)}, f32[2,8]{1,0:T(2,128)}, u32[]{:S(2)}) copy-start(f32[2,8]{1,0:T(2,128)} %param.17) | copy-start | bytes 196
Sparse Core Ops, SparseCore 0:
  377.6 210.2 reduce-scatter.1
where the time goes:
time: 599 us; the launch traced here: 595 us
  waiting for transfers between devices  250 us (42%)
  loops' own time  175 us (29%)
  matrix products  68.2 us (11%)
  local copies, waits for them, and re-layouts  48.4 us (8%)
  other arithmetic  29.6 us (5%)
  between operations  13.5 us (2%)
  starting transfers between devices  10.4 us (2%)
    reduce_scatter x1, waiting for transfers between devices, body(): lax.psum_scatter(lax.fori_loop(0, chans * EPW, step, jnp.zeros((count, 1,...  210 us
    another operation x16, loops' own time, step(): return lax.cond(inside, add_term, lambda acc: acc, partial_value)  155 us
    dot_general x16, matrix products, entry_term(): jnp.einsum('abij,abil->abjl', bra_blk, half, preferred_element_type=jnp.f...  68.2 us
    ppermute x2, waiting for transfers between devices, passed_along(): lax.ppermute(value, axis, [(source, source + steps) for source in range(f...  24.9 us
    another operation x1, loops' own time, body(): lax.fori_loop(0, chans * EPW, step, jnp.zeros((count, 1, sec_b, bra_w, ke...  20 us
    convert_element_type x1, other arithmetic, body(): return lax.psum_scatter(lax.fori_loop(0, chans * EPW, step, jnp.zeros((co...  17.3 us
    ppermute x1, waiting for transfers between devices, extended(): lax.ppermute(tail, axis, [(i, (i + 1) % count) for i in range(ends)])  14.2 us
  transfers between devices with their start and end apart: 5, of which 4 were waited for; matrix products, arithmetic and copies ran while one was open for 2% of the time, Pallas kernels for 0%

commit v1 on v0

v1 whole, which is shorter than its diff:
```python
import functools

import jax
import jax.numpy as jnp
import numpy as np
from jax import lax
from jax.experimental import pallas as pl
from jax.experimental.pallas import tpu as pltpu
from jax.sharding import PartitionSpec as P

MW, EPW, CH = 32, 8, 2
NZ, NX = 4, 4
SECS, ROWS = 16, 16
BB, KB = 256, 512
BF, F32 = jnp.bfloat16, jnp.float32
STEPS = (0, -1, 1, 2)
VMEM_BYTES = 56 * 1024 * 1024


def charge(channel):
    klass = channel % 9
    return klass % 3 - 1, klass // 3 - 1


def live_tables():
    order, inverse, count = [], [], []
    for r in range(ROWS):
        cells = [(b, j) for b in range(2) for j in range(CH)]
        live = [(b, j) for b, j in cells if 0 <= b + charge(CH * r + j)[1] < 2]
        rest = [cell for cell in cells if cell not in live]
        line = [j * 2 + b for b, j in live + rest]
        order.append(line)
        inverse.append([line.index(c) if line.index(c) < len(live) else -1 for c in range(4)])
        count.append(len(live))
    return np.array(order, np.int32), np.array(inverse, np.int32), count


ORDER, INVERSE, COUNT = live_tables()


def row_z(r, d):
    return (r // NX + d) % NZ * NX + r % NX


def row_x(r, d):
    return r // NX * NX + (r % NX + d) % NX


def along_rows(move, owner, i):
    return [(r, move(r)) for r in range(ROWS) if COUNT[owner(r)] > i]


def pack_kernel(order, rows, cols, env, *outs):
    row_at = lax.broadcasted_iota(jnp.int32, (BB, KB), 0)
    col_at = lax.broadcasted_iota(jnp.int32, (BB, KB), 1)
    for i in range(4):
        keep = (row_at < rows[i]) & (col_at < cols[i])
        outs[i][...] = jnp.where(keep, env[order[i]], jnp.zeros((BB, KB), BF))


def terms_kernel(ints, values, inv_e, inv_o, place, *refs):
    envs, (ket, bm1, b0, bp1, bp2) = refs[:16], refs[16:21]
    outs = refs[21:37]
    env_all, bra_all, total = refs[37:]
    for n in range(16):
        env_all[n] = envs[n][...]
    for n in range(3):
        bra_all[n] = bm1[n]
        bra_all[18 + 3 + n] = bp2[n]
    for n in range(6):
        bra_all[6 + n] = b0[n]
        bra_all[12 + n] = bp1[n]

    @pl.loop(0, 32)
    def _(n):
        total[n] = jnp.zeros((BB, KB), F32)

    my_z, my_x = place[0], place[1]

    @pl.loop(0, 4 * CH * EPW)
    def _(item):
        out_w = ints[3 * item]

        @pl.when(out_w // (CH * NX) == my_z)
        def _():
            sp = ints[3 * item + 1]
            s = ints[3 * item + 2]
            value = values[item]
            k, j = item // (CH * EPW), item // EPW % CH
            ahead = (out_w % (CH * NX) // CH - my_x + NX) % NX
            slot = jnp.where(ahead == 1, 2, jnp.where(ahead == 3, 1, jnp.where(ahead == 2, 3, 0)))
            out_a, out_b = charge(out_w)
            s_a, s_b = s % 2, s // 2
            sp_a, sp_b = sp % 2, sp // 2
            for q_b in range(2):
                p_b = q_b + s_b
                e_at = inv_e[4 * k + 2 * j + q_b]
                o_at = inv_o[4 * slot + 2 * (out_w % CH) + jnp.minimum(p_b, 1)]

                @pl.when((p_b < 2) & (e_at >= 0) & (o_at >= 0))
                def _(q_b=q_b, p_b=p_b, e_at=e_at, o_at=o_at):
                    half = jnp.dot(env_all[4 * k + e_at], ket[s, q_b], preferred_element_type=F32).astype(BF)
                    b_at = 6 * (s_a + out_a + 1) + 3 * sp_a + p_b + out_b + sp_b
                    term = jnp.dot(bra_all[b_at], half, preferred_element_type=F32)
                    at = 8 * slot + 2 * o_at + s_a
                    total[at] = total[at] + value * term

    for d in range(4):
        for i in range(4):
            for up in range(2):
                outs[4 * d + i][up] = total[8 * d + 2 * i + up].astype(BF)


def body(env_in, ket_mps, bra_mps, ket_sizes, bra_sizes, entries, coeffs):
    my_a = lax.axis_index("sec")
    r = lax.axis_index("row")
    my_z, my_x = r // NX, r % NX
    ket_ext = jnp.pad(ket_sizes, 2)
    bra_ext = jnp.pad(bra_sizes, 2)
    order = lax.dynamic_index_in_dim(jnp.asarray(ORDER), r, keepdims=False)
    inverse = lax.dynamic_index_in_dim(jnp.asarray(INVERSE), r, keepdims=False)
    second = order % 2
    chan_a, chan_b = charge(CH * r + order // 2)
    block_rows = bra_ext[my_a + chan_a + 2, second + chan_b + 2]
    block_cols = ket_ext[my_a + 2, second + 2]

    smem = pl.BlockSpec(memory_space=pltpu.SMEM)
    vmem = pl.BlockSpec(memory_space=pltpu.VMEM)
    block = jax.ShapeDtypeStruct((BB, KB), BF)
    own = pl.pallas_call(
        pack_kernel,
        in_specs=[smem] * 3 + [vmem],
        out_specs=[vmem] * 4,
        out_shape=[block] * 4,
        compiler_params=pltpu.CompilerParams(vmem_limit_bytes=VMEM_BYTES),
    )(order, block_rows, block_cols, env_in.reshape(4, BB, KB))

    items = jnp.concatenate([entries.astype(F32), coeffs[..., None]], axis=-1)
    item_parts = [items] + [
        lax.ppermute(items, "row", [(n, row_z(n, -d)) for n in range(ROWS)]) for d in STEPS[1:]
    ]
    items = jnp.stack(item_parts).reshape(4 * CH * EPW, 4)
    ints = items[:, :3].astype(jnp.int32).reshape(-1)
    values = items[:, 3]

    flipped = jnp.swapaxes(bra_mps[:, 0], -1, -2)
    bra = [
        jnp.stack([flipped[n, 0], flipped[n, 1], flipped[n + 2, 1]]) for n in range(2)
    ]
    up = lambda n: [(i, i + n) for i in range(SECS - n)]
    down = lambda n: [(i + n, i) for i in range(SECS - n)]
    bra_own = jnp.concatenate(bra)

    behind, ahead, across = [], [], []
    for i in range(4):
        behind.append(lax.ppermute(own[i], "row", along_rows(lambda n: row_z(n, 1), lambda n: n, i)))
        ahead.append(lax.ppermute(own[i], "row", along_rows(lambda n: row_z(n, -1), lambda n: n, i)))
    bra_m1 = lax.ppermute(bra[0], "sec", up(1))
    bra_p1 = lax.ppermute(bra_own, "sec", down(1))
    bra_p2 = lax.ppermute(bra[1], "sec", down(2))
    for i in range(4):
        if i % 2 == 0:
            across.append(lax.ppermute(behind[i], "row", along_rows(lambda n: row_z(n, 1), lambda n: row_z(n, -1), i)))
        else:
            across.append(lax.ppermute(ahead[i], "row", along_rows(lambda n: row_z(n, -1), lambda n: row_z(n, 1), i)))

    inv_e = jnp.asarray(INVERSE)[jnp.stack([(my_z + d) % NZ * NX + my_x for d in STEPS])].reshape(-1)
    inv_o = jnp.asarray(INVERSE)[jnp.stack([my_z * NX + (my_x + d) % NX for d in STEPS])].reshape(-1)
    pair = jax.ShapeDtypeStruct((2, BB, KB), BF)
    sums = pl.pallas_call(
        terms_kernel,
        in_specs=[smem] * 5 + [vmem] * 21,
        out_specs=[vmem] * 16,
        out_shape=[pair] * 16,
        scratch_shapes=[
            pltpu.VMEM((16, BB, KB), BF),
            pltpu.VMEM((24, BB, BB), BF),
            pltpu.VMEM((32, BB, KB), F32),
        ],
        compiler_params=pltpu.CompilerParams(vmem_limit_bytes=VMEM_BYTES),
    )(ints, values, inv_e, inv_o, jnp.stack([my_z, my_x]), *own, *behind, *ahead, *across,
      ket_mps[:, 0], bra_m1, bra_own, bra_p1, bra_p2)
    mine, to_left, to_right, to_far = sums[:4], sums[4:8], sums[8:12], sums[12:]

    def added(*parts):
        return functools.reduce(jnp.add, [part.astype(F32) for part in parts])

    to_left, to_right = list(to_left), list(to_right)
    for i in range(4):
        if i % 2 == 0:
            got = lax.ppermute(to_far[i], "row", along_rows(lambda n: row_x(n, 1), lambda n: row_x(n, 2), i))
            to_right[i] = added(to_right[i], got).astype(BF)
        else:
            got = lax.ppermute(to_far[i], "row", along_rows(lambda n: row_x(n, -1), lambda n: row_x(n, 2), i))
            to_left[i] = added(to_left[i], got).astype(BF)
    here, above = [], []
    for i in range(4):
        from_left = lax.ppermute(to_right[i], "row", along_rows(lambda n: row_x(n, 1), lambda n: row_x(n, 1), i))
        from_right = lax.ppermute(to_left[i], "row", along_rows(lambda n: row_x(n, -1), lambda n: row_x(n, -1), i))
        here.append(added(mine[i][0], from_left[0], from_right[0]))
        raised = added(mine[i][1], from_left[1], from_right[1]).astype(BF)
        pairs = [(a * ROWS + n, (a + 1) * ROWS + n) for a in range(SECS - 1) for n in range(ROWS) if COUNT[n] > i]
        above.append(lax.ppermute(raised, ("sec", "row"), pairs))

    row_at = lax.broadcasted_iota(jnp.int32, (BB, KB), 0)
    col_at = lax.broadcasted_iota(jnp.int32, (BB, KB), 1)
    whole = jnp.stack([
        jnp.where((row_at < block_rows[i]) & (col_at < block_cols[i]), added(here[i], above[i]), 0.0).astype(BF)
        for i in range(4)
    ])
    out = [
        jnp.where(inverse[c] >= 0, lax.dynamic_index_in_dim(whole, jnp.maximum(inverse[c], 0), keepdims=False), jnp.zeros((BB, KB), BF))
        for c in range(4)
    ]
    return jnp.stack(out).reshape(CH, 1, 2, BB, KB)


def solution(mesh):
    placed = (
        P("row", "sec", None, None, None),
        P(None, "sec", None, None, None),
        P(None, "sec", None, None, None),
        P(),
        P(),
        P("row", None, None),
        P("row", None),
    )
    return jax.shard_map(
        body,
        mesh=mesh,
        in_specs=placed,
        out_specs=P("row", "sec", None, None, None),
        check_vma=False,
    )
```

time: 599 us -> 216 us (0.36)
  the two profiles are of different devices: /device:TPU:12 before, /device:TPU:76 now
where the time goes in v1:
time: 216 us
  starting transfers between devices  82.9 us (38%)
  waiting for transfers between devices  70 us (32%)
  Pallas kernels  24.1 us (11%)
  local copies, waits for them, and re-layouts  16.9 us (8%)
  other arithmetic  16.4 us (8%)
  between operations  5.75 us (3%)
    ppermute x4, waiting for transfers between devices, body(): lax.ppermute(own[i], 'row', along_rows(lambda n: row_z(n, -1), lambda n:...  21.9 us
    pallas_call x1, Pallas kernels, body(): pl.pallas_call(terms_kernel, in_specs=[smem] * 5 + [vmem] * 21, out_specs...  21.7 us
    ppermute x2, waiting for transfers between devices, body(): lax.ppermute(to_far[i], 'row', along_rows(lambda n: row_x(n, 1), lambda n...  16.9 us
    ppermute x1, starting transfers between devices, body(): bra_p2 = lax.ppermute(bra[1], 'sec', down(2))  15.3 us
    ppermute x4, waiting for transfers between devices, body(): lax.ppermute(to_left[i], 'row', along_rows(lambda n: row_x(n, -1), lambda...  12 us
    ppermute x4, starting transfers between devices, body(): lax.ppermute(own[i], 'row', along_rows(lambda n: row_z(n, -1), lambda n:...  10.3 us
    ppermute x2, starting transfers between devices, body(): lax.ppermute(to_far[i], 'row', along_rows(lambda n: row_x(n, 1), lambda n...  9.65 us
    ppermute x3, starting transfers between devices, body(): lax.ppermute(items, 'row', [(n, row_z(n, -d)) for n in range(ROWS)])  9.53 us
  transfers between devices with their start and end apart: 34, of which 16 were waited for; matrix products, arithmetic and copies ran while one was open for 13% of the time, Pallas kernels for 1%

profile of v1, /device:TPU:76, one launch (start us, length us, event | category | flops | bytes accessed | tf_op | source)
XLA Modules:
  0.0 216.1 jit_solution(13303285831426864222)
XLA Ops:
  1.4 5.4 %collective-permute-start.2 = (f32[2,8,4]{1,0,2:T(2,128)S(1)}, f32[2,8,4]{1,0,2:T(2,128)}, u32[]{:S(2)}, u32[]{:S(2)}) collective-permute-start(f32[2,8,4]{1,0,2:T(2,128)S(1)} %pad_maximum_fusion.5), channel_id=1, source_target_pairs={{0,8},{1,9},{2,10},{3,11},{4,12},{5,13},{6,14},{7,15},{8,0},{9,1},... | collective-permute-start | bytes 776 | tf_op jit(solution)/shard_map/ppermute | solution.py:140
  8.2 2.7 %collective-permute-start = (f32[2,8,4]{1,0,2:T(2,128)S(1)}, f32[2,8,4]{1,0,2:T(2,128)}, u32[]{:S(2)}, u32[]{:S(2)}) collective-permute-start(f32[2,8,4]{1,0,2:T(2,128)S(1)} %pad_maximum_fusion.5), channel_id=1, source_target_pairs={{0,4},{1,5},{2,6},{3,7},{4,8},{5,9},{6,10},{7,11},{8,12},{9,13},{1... | collective-permute-start | bytes 776 | tf_op jit(solution)/shard_map/ppermute | solution.py:140
  16.6 2.4 %shard_map.91 = (bf16[256,512]{1,0:T(8,128)(2,1)}, bf16[256,512]{1,0:T(8,128)(2,1)}, bf16[256,512]{1,0:T(8,128)(2,1)}, bf16[256,512]{1,0:T(8,128)(2,1)}) custom-call(s32[4]{0:T(128)} %fusion.23.order, s32[4]{0:T(128)} %gather_fusion, s32[4]{0:T(128)} %gather_fusion.1, bf16[4,256,512]{2,1,0:T(8,128)(2,1)} %bitcast.158), custom_call_target="tpu_custom_call" | custom-call | tf_op jit(solution)/shard_map/pallas_call | solution.py:130
  19.0 2.9 %collective-permute-start.8 = (bf16[256,512]{1,0:T(8,128)(2,1)}, bf16[256,512]{1,0:T(8,128)(2,1)}, u32[]{:S(2)}, u32[]{:S(2)}) collective-permute-start(bf16[256,512]{1,0:T(8,128)(2,1)} %get-tuple-element.26.refs_1_), channel_id=1, source_target_pairs={{0,12},{1,13},{2,14},{3,15},{4,0},{5,1},{6,2},{7,3},{8,4},{9,5},{1... | collective-permute-start | bytes 786440 | tf_op jit(solution)/shard_map/ppermute | solution.py:157
  26.9 3.2 %collective-permute-start.5 = (bf16[256,512]{1,0:T(8,128)(2,1)}, bf16[256,512]{1,0:T(8,128)(2,1)}, u32[]{:S(2)}, u32[]{:S(2)}) collective-permute-start(bf16[256,512]{1,0:T(8,128)(2,1)} %get-tuple-element.27.refs_2_), channel_id=1, source_target_pairs={{1,5},{2,6},{6,10},{7,11},{10,14},{11,15},{15,3},{17,21},{18,22},{... | collective-permute-start | bytes 786440 | tf_op jit(solution)/shard_map/ppermute | solution.py:156
  31.5 5.4 %collective-permute-start.10 = (bf16[256,512]{1,0:T(8,128)(2,1)}, bf16[256,512]{1,0:T(8,128)(2,1)}, u32[]{:S(2)}, u32[]{:S(2)}) collective-permute-start(bf16[256,512]{1,0:T(8,128)(2,1)} %get-tuple-element.28.refs_3_), channel_id=1, source_target_pairs={{2,14},{6,2},{11,7},{15,11},{18,30},{22,18},{27,23},{31,27},{34,46... | collective-permute-start | bytes 786440 | tf_op jit(solution)/shard_map/ppermute | solution.py:157
  36.9 1.9 collective-permute-start.6
  39.9 1.9 collective-permute-start.15
  41.8 2.4 %collective-permute-done.5.refs_6_ = bf16[256,512]{1,0:T(8,128)(2,1)} collective-permute-done((bf16[256,512]{1,0:T(8,128)(2,1)}, bf16[256,512]{1,0:T(8,128)(2,1)}, u32[]{:S(2)}, u32[]{:S(2)}) %collective-permute-start.5) | collective-permute-done | bytes 262176 | tf_op jit(solution)/shard_map/ppermute | solution.py:156
  44.2 15.3 %collective-permute-start.17 = (bf16[3,256,256]{2,1,0:T(8,128)(2,1)S(1)}, bf16[3,256,256]{2,1,0:T(8,128)(2,1)S(1)}, u32[]{:S(2)}, u32[]{:S(2)}) collective-permute-start(bf16[3,256,256]{2,1,0:T(8,128)(2,1)S(1)} %pad_maximum_fusion.3), channel_id=1, source_target_pairs={{32,0},{48,16},{64,32},{80,48},{96,64},{112,80},{128,96},{144,112}... | collective-permute-start | bytes 1179656 | tf_op jit(solution)/shard_map/ppermute | solution.py:160
  60.1 1.9 collective-permute-start.16
  63.5 1.9 collective-permute-start.9
  70.8 7.3 %collective-permute-done.7.refs_8_ = bf16[256,512]{1,0:T(8,128)(2,1)} collective-permute-done((bf16[256,512]{1,0:T(8,128)(2,1)S(1)}, bf16[256,512]{1,0:T(8,128)(2,1)}, u32[]{:S(2)}, u32[]{:S(2)}) %collective-permute-start.7) | collective-permute-done | bytes 262176 | tf_op jit(solution)/shard_map/ppermute | solution.py:157
  78.1 14.6 %collective-permute-done.9.refs_10_ = bf16[256,512]{1,0:T(8,128)(2,1)} collective-permute-done((bf16[256,512]{1,0:T(8,128)(2,1)}, bf16[256,512]{1,0:T(8,128)(2,1)}, u32[]{:S(2)}, u32[]{:S(2)}) %collective-permute-start.9) | collective-permute-done | bytes 262176 | tf_op jit(solution)/shard_map/ppermute | solution.py:157
  92.7 6.0 %collective-permute-start.13 = (bf16[256,512]{1,0:T(8,128)(2,1)}, bf16[256,512]{1,0:T(8,128)(2,1)S(1)}, u32[]{:S(2)}, u32[]{:S(2)}) collective-permute-start(bf16[256,512]{1,0:T(8,128)(2,1)} %collective-permute-done.5.refs_6_), channel_id=1, source_target_pairs={{3,7},{5,9},{6,10},{10,14},{11,15},{14,2},{15,3},{19,23},{21,25},{... | collective-permute-start | bytes 786440 | tf_op jit(solution)/shard_map/ppermute | solution.py:163
  100.7 2.5 %collective-permute-done.12.refs_13_ = bf16[256,512]{1,0:T(8,128)(2,1)} collective-permute-done((bf16[256,512]{1,0:T(8,128)(2,1)}, bf16[256,512]{1,0:T(8,128)(2,1)}, u32[]{:S(2)}, u32[]{:S(2)}) %collective-permute-start.12) | collective-permute-done | bytes 262176 | tf_op jit(solution)/shard_map/ppermute | solution.py:165
  103.2 3.9 %collective-permute-done.13.refs_14_ = bf16[256,512]{1,0:T(8,128)(2,1)S(1)} collective-permute-done((bf16[256,512]{1,0:T(8,128)(2,1)}, bf16[256,512]{1,0:T(8,128)(2,1)S(1)}, u32[]{:S(2)}, u32[]{:S(2)}) %collective-permute-start.13) | collective-permute-done | bytes 262176 | tf_op jit(solution)/shard_map/ppermute | solution.py:163
  108.2 21.7 %shard_map.92 = (bf16[2,256,512]{2,1,0:T(8,128)(2,1)}, bf16[2,256,512]{2,1,0:T(8,128)(2,1)}, bf16[2,256,512]{2,1,0:T(8,128)(2,1)}, bf16[2,256,512]{2,1,0:T(8,128...) custom-call(s32[192]{0:T(256)} %reshape.632.ints, ...), custom_call_target="tpu_custom_call" | custom-call | tf_op jit(solution)/shard_map/pallas_call | solution.py:170
  129.9 8.4 %collective-permute-start.18 = (bf16[2,256,512]{2,1,0:T(8,128)(2,1)}, bf16[2,256,512]{2,1,0:T(8,128)(2,1)S(1)}, u32[]{:S(2)}, u32[]{:S(2)}) collective-permute-start(bf16[2,256,512]{2,1,0:T(8,128)(2,1)} %get-tuple-element.31), channel_id=1, source_target_pairs={{0,1},{1,2},{2,3},{3,0},{4,5},{5,6},{6,7},{7,4},{8,9},{9,10},{10,1... | collective-permute-start | bytes 1572872 | tf_op jit(solution)/shard_map/ppermute | solution.py:191
  146.6 2.1 collective-permute-start.22
  152.4 2.3 %collective-permute-done.23 = bf16[2,256,512]{2,1,0:T(8,128)(2,1)S(1)} collective-permute-done((bf16[2,256,512]{2,1,0:T(8,128)(2,1)}, bf16[2,256,512]{2,1,0:T(8,128)(2,1)S(1)}, u32[]{:S(2)}, u32[]{:S(2)}) %collective-permute-start.23) | collective-permute-done | bytes 524320 | tf_op jit(solution)/shard_map/ppermute | solution.py:194
  157.2 16.5 %collective-permute-done.26 = bf16[2,256,512]{2,1,0:T(8,128)(2,1)S(1)} collective-permute-done((bf16[2,256,512]{2,1,0:T(8,128)(2,1)}, bf16[2,256,512]{2,1,0:T(8,128)(2,1)S(1)}, u32[]{:S(2)}, u32[]{:S(2)}) %collective-permute-start.26) | collective-permute-done | bytes 524320 | tf_op jit(solution)/shard_map/ppermute | solution.py:191
  173.7 2.0 collective-permute-start.24
  178.2 4.6 %collective-permute-start.27 = (bf16[2,256,512]{2,1,0:T(8,128)(2,1)S(1)}, bf16[2,256,512]{2,1,0:T(8,128)(2,1)S(1)}, u32[]{:S(2)}, u32[]{:S(2)}) collective-permute-start(bf16[2,256,512]{2,1,0:T(8,128)(2,1)S(1)} %add_convert_fusion.1), channel_id=1, source_target_pairs={{0,1},{1,2},{5,6},{6,7},{9,10},{10,11},{14,15},{16,17},{17,18},{21... | collective-permute-start | bytes 1572872 | tf_op jit(solution)/shard_map/ppermute | solution.py:198
  186.4 2.2 %collective-permute-done.24 = bf16[2,256,512]{2,1,0:T(8,128)(2,1)S(1)} collective-permute-done((bf16[2,256,512]{2,1,0:T(8,128)(2,1)S(1)}, bf16[2,256,512]{2,1,0:T(8,128)(2,1)S(1)}, u32[]{:S(2)}, u32[]{:S(2)}) %collective-permute-start.24) | collective-permute-done | bytes 524320 | tf_op jit(solution)/shard_map/ppermute | solution.py:199
  188.6 1.9 collective-permute-start.21
  190.6 9.2 %collective-permute-done.28 = bf16[2,256,512]{2,1,0:T(8,128)(2,1)S(1)} collective-permute-done((bf16[2,256,512]{2,1,0:T(8,128)(2,1)S(1)}, bf16[2,256,512]{2,1,0:T(8,128)(2,1)S(1)}, u32[]{:S(2)}, u32[]{:S(2)}) %collective-permute-start.28) | collective-permute-done | bytes 524320 | tf_op jit(solution)/shard_map/ppermute | solution.py:199
  199.8 1.9 collective-permute-start.25
  201.9 1.9 collective-permute-start.29
  206.0 1.9 collective-permute-start.33
  208.6 2.6 %collective-permute-done.29 = bf16[256,512]{1,0:T(8,128)(2,1)S(1)} collective-permute-done((bf16[256,512]{1,0:T(8,128)(2,1)S(1)}, bf16[256,512]{1,0:T(8,128)(2,1)S(1)}, u32[]{:S(2)}, u32[]{:S(2)}) %collective-permute-start.29) | collective-permute-done | bytes 262176 | tf_op jit(solution)/shard_map/ppermute | solution.py:203
  211.4 3.2 %collective-permute-done.33 = bf16[256,512]{1,0:T(8,128)(2,1)S(1)} collective-permute-done((bf16[256,512]{1,0:T(8,128)(2,1)S(1)}, bf16[256,512]{1,0:T(8,128)(2,1)S(1)}, u32[]{:S(2)}, u32[]{:S(2)}) %collective-permute-start.33) | collective-permute-done | bytes 262176 | tf_op jit(solution)/shard_map/ppermute | solution.py:203
  (150 shorter events, 46.5 us)
Async XLA Ops:
  1.4 25.6 %collective-permute-start.2 = (f32[2,8,4]{1,0,2:T(2,128)S(1)}, f32[2,8,4]{1,0,2:T(2,128)}, u32[]{:S(2)}, u32[]{:S(2)}) collective-permute-start(f32[2,8,4]{1,0,2:T(2,128)S(1)} %pad_maximum_fusion.5), channel_id=1, source_target_pairs={{0,8},{1,9},{2,10},{3,11},{4,12},{5,13},{6,14},{7,15},{8,0},{9,1},... | collective-permute-start | bytes 776 | tf_op jit(solution)/shard_map/ppermute | solution.py:140
  6.8 24.5 %collective-permute-start.1 = (f32[2,8,4]{1,0,2:T(2,128)S(1)}, f32[2,8,4]{1,0,2:T(2,128)}, u32[]{:S(2)}, u32[]{:S(2)}) collective-permute-start(f32[2,8,4]{1,0,2:T(2,128)S(1)} %pad_maximum_fusion.5), channel_id=1, source_target_pairs={{0,12},{1,13},{2,14},{3,15},{4,0},{5,1},{6,2},{7,3},{8,4},{9,5},{1... | collective-permute-start | bytes 776 | tf_op jit(solution)/shard_map/ppermute | solution.py:140
  8.2 23.3 %collective-permute-start = (f32[2,8,4]{1,0,2:T(2,128)S(1)}, f32[2,8,4]{1,0,2:T(2,128)}, u32[]{:S(2)}, u32[]{:S(2)}) collective-permute-start(f32[2,8,4]{1,0,2:T(2,128)S(1)} %pad_maximum_fusion.5), channel_id=1, source_target_pairs={{0,4},{1,5},{2,6},{3,7},{4,8},{5,9},{6,10},{7,11},{8,12},{9,13},{1... | collective-permute-start | bytes 776 | tf_op jit(solution)/shard_map/ppermute | solution.py:140
  19.0 17.9 %collective-permute-start.3 = (bf16[256,512]{1,0:T(8,128)(2,1)}, bf16[256,512]{1,0:T(8,128)(2,1)S(1)}, u32[]{:S(2)}, u32[]{:S(2)}) collective-permute-start(bf16[256,512]{1,0:T(8,128)(2,1)} %get-tuple-element.25.refs_0_), channel_id=1, source_target_pairs={{0,4},{1,5},{2,6},{3,7},{4,8},{5,9},{6,10},{7,11},{8,12},{9,13},{1... | collective-permute-start | bytes 786440 | tf_op jit(solution)/shard_map/ppermute | solution.py:156
  19.0 20.9 %collective-permute-start.8 = (bf16[256,512]{1,0:T(8,128)(2,1)}, bf16[256,512]{1,0:T(8,128)(2,1)}, u32[]{:S(2)}, u32[]{:S(2)}) collective-permute-start(bf16[256,512]{1,0:T(8,128)(2,1)} %get-tuple-element.26.refs_1_), channel_id=1, source_target_pairs={{0,12},{1,13},{2,14},{3,15},{4,0},{5,1},{6,2},{7,3},{8,4},{9,5},{1... | collective-permute-start | bytes 786440 | tf_op jit(solution)/shard_map/ppermute | solution.py:157
  26.9 17.2 %collective-permute-start.5 = (bf16[256,512]{1,0:T(8,128)(2,1)}, bf16[256,512]{1,0:T(8,128)(2,1)}, u32[]{:S(2)}, u32[]{:S(2)}) collective-permute-start(bf16[256,512]{1,0:T(8,128)(2,1)} %get-tuple-element.27.refs_2_), channel_id=1, source_target_pairs={{1,5},{2,6},{6,10},{7,11},{10,14},{11,15},{15,3},{17,21},{18,22},{... | collective-permute-start | bytes 786440 | tf_op jit(solution)/shard_map/ppermute | solution.py:156
  31.3 30.7 %collective-permute-start.4 = (bf16[256,512]{1,0:T(8,128)(2,1)}, bf16[256,512]{1,0:T(8,128)(2,1)S(1)}, u32[]{:S(2)}, u32[]{:S(2)}) collective-permute-start(bf16[256,512]{1,0:T(8,128)(2,1)} %get-tuple-element.26.refs_1_), channel_id=1, source_target_pairs={{0,4},{1,5},{2,6},{3,7},{4,8},{5,9},{6,10},{7,11},{8,12},{9,13},{1... | collective-permute-start | bytes 786440 | tf_op jit(solution)/shard_map/ppermute | solution.py:156
  31.5 28.6 %collective-permute-start.10 = (bf16[256,512]{1,0:T(8,128)(2,1)}, bf16[256,512]{1,0:T(8,128)(2,1)}, u32[]{:S(2)}, u32[]{:S(2)}) collective-permute-start(bf16[256,512]{1,0:T(8,128)(2,1)} %get-tuple-element.28.refs_3_), channel_id=1, source_target_pairs={{2,14},{6,2},{11,7},{15,11},{18,30},{22,18},{27,23},{31,27},{34,46... | collective-permute-start | bytes 786440 | tf_op jit(solution)/shard_map/ppermute | solution.py:157
  36.9 25.9 %collective-permute-start.6 = (bf16[256,512]{1,0:T(8,128)(2,1)}, bf16[256,512]{1,0:T(8,128)(2,1)S(1)}, u32[]{:S(2)}, u32[]{:S(2)}) collective-permute-start(bf16[256,512]{1,0:T(8,128)(2,1)} %get-tuple-element.28.refs_3_), channel_id=1, source_target_pairs={{2,6},{6,10},{11,15},{15,3},{18,22},{22,26},{27,31},{31,19},{34,38... | collective-permute-start | bytes 786440 | tf_op jit(solution)/shard_map/ppermute | solution.py:156
  39.9 52.8 %collective-permute-start.15 = (bf16[3,256,256]{2,1,0:T(8,128)(2,1)S(1)}, bf16[3,256,256]{2,1,0:T(8,128)(2,1)S(1)}, u32[]{:S(2)}, u32[]{:S(2)}) collective-permute-start(bf16[3,256,256]{2,1,0:T(8,128)(2,1)S(1)} %pad_maximum_fusion.2), channel_id=1, source_target_pairs={{0,16},{16,32},{32,48},{48,64},{64,80},{80,96},{96,112},{112,128},... | collective-permute-start | bytes 1179656 | tf_op jit(solution)/shard_map/ppermute | solution.py:158
  44.2 54.5 %collective-permute-start.17 = (bf16[3,256,256]{2,1,0:T(8,128)(2,1)S(1)}, bf16[3,256,256]{2,1,0:T(8,128)(2,1)S(1)}, u32[]{:S(2)}, u32[]{:S(2)}) collective-permute-start(bf16[3,256,256]{2,1,0:T(8,128)(2,1)S(1)} %pad_maximum_fusion.3), channel_id=1, source_target_pairs={{32,0},{48,16},{64,32},{80,48},{96,64},{112,80},{128,96},{144,112}... | collective-permute-start | bytes 1179656 | tf_op jit(solution)/shard_map/ppermute | solution.py:160
  60.1 47.0 %collective-permute-start.16 = (bf16[6,256,256]{2,1,0:T(8,128)(2,1)S(1)}, bf16[6,256,256]{2,1,0:T(8,128)(2,1)S(1)}, u32[]{:S(2)}, u32[]{:S(2)}) collective-permute-start(bf16[6,256,256]{2,1,0:T(8,128)(2,1)S(1)} %constant_dynamic-update-slice_fusion.refs_18_), channel_id=1, source_target_pairs={{16,0},{32,16},{48,32},{64,48},{80,64},{96,80},{112,96},{128,112},... | collective-permute-start | bytes 2359304 | tf_op jit(solution)/shard_map/ppermute | solution.py:159
  62.1 16.0 %collective-permute-start.7 = (bf16[256,512]{1,0:T(8,128)(2,1)S(1)}, bf16[256,512]{1,0:T(8,128)(2,1)}, u32[]{:S(2)}, u32[]{:S(2)}) collective-permute-start(bf16[256,512]{1,0:T(8,128)(2,1)S(1)} %copy-done.9), channel_id=1, source_target_pairs={{0,12},{1,13},{2,14},{3,15},{4,0},{5,1},{6,2},{7,3},{8,4},{9,5},{1... | collective-permute-start | bytes 786440 | tf_op jit(solution)/shard_map/ppermute | solution.py:157
  63.5 29.2 %collective-permute-start.9 = (bf16[256,512]{1,0:T(8,128)(2,1)}, bf16[256,512]{1,0:T(8,128)(2,1)}, u32[]{:S(2)}, u32[]{:S(2)}) collective-permute-start(bf16[256,512]{1,0:T(8,128)(2,1)} %get-tuple-element.27.refs_2_), channel_id=1, source_target_pairs={{1,13},{2,14},{6,2},{7,3},{10,6},{11,7},{15,11},{17,29},{18,30},{2... | collective-permute-start | bytes 786440 | tf_op jit(solution)/shard_map/ppermute | solution.py:157
  78.1 22.6 %collective-permute-start.11 = (bf16[256,512]{1,0:T(8,128)(2,1)}, bf16[256,512]{1,0:T(8,128)(2,1)S(1)}, u32[]{:S(2)}, u32[]{:S(2)}) collective-permute-start(bf16[256,512]{1,0:T(8,128)(2,1)} %copy-done.10), channel_id=1, source_target_pairs={{0,4},{1,5},{2,6},{3,7},{4,8},{5,9},{6,10},{7,11},{8,12},{9,13},{1... | collective-permute-start | bytes 786440 | tf_op jit(solution)/shard_map/ppermute | solution.py:163
  92.7 10.6 %collective-permute-start.12 = (bf16[256,512]{1,0:T(8,128)(2,1)}, bf16[256,512]{1,0:T(8,128)(2,1)}, u32[]{:S(2)}, u32[]{:S(2)}) collective-permute-start(bf16[256,512]{1,0:T(8,128)(2,1)} %collective-permute-done.8.refs_9_), channel_id=1, source_target_pairs={{0,12},{1,13},{2,14},{3,15},{4,0},{5,1},{6,2},{7,3},{8,4},{9,5},{1... | collective-permute-start | bytes 786440 | tf_op jit(solution)/shard_map/ppermute | solution.py:165
  92.7 14.4 %collective-permute-start.13 = (bf16[256,512]{1,0:T(8,128)(2,1)}, bf16[256,512]{1,0:T(8,128)(2,1)S(1)}, u32[]{:S(2)}, u32[]{:S(2)}) collective-permute-start(bf16[256,512]{1,0:T(8,128)(2,1)} %collective-permute-done.5.refs_6_), channel_id=1, source_target_pairs={{3,7},{5,9},{6,10},{10,14},{11,15},{14,2},{15,3},{19,23},{21,25},{... | collective-permute-start | bytes 786440 | tf_op jit(solution)/shard_map/ppermute | solution.py:163
  129.9 20.5 %collective-permute-start.18 = (bf16[2,256,512]{2,1,0:T(8,128)(2,1)}, bf16[2,256,512]{2,1,0:T(8,128)(2,1)S(1)}, u32[]{:S(2)}, u32[]{:S(2)}) collective-permute-start(bf16[2,256,512]{2,1,0:T(8,128)(2,1)} %get-tuple-element.31), channel_id=1, source_target_pairs={{0,1},{1,2},{2,3},{3,0},{4,5},{5,6},{6,7},{7,4},{8,9},{9,10},{10,1... | collective-permute-start | bytes 1572872 | tf_op jit(solution)/shard_map/ppermute | solution.py:191
  139.6 15.1 %collective-permute-start.23 = (bf16[2,256,512]{2,1,0:T(8,128)(2,1)}, bf16[2,256,512]{2,1,0:T(8,128)(2,1)S(1)}, u32[]{:S(2)}, u32[]{:S(2)}) collective-permute-start(bf16[2,256,512]{2,1,0:T(8,128)(2,1)} %get-tuple-element.36), channel_id=1, source_target_pairs={{0,3},{1,0},{2,1},{3,2},{4,7},{5,4},{6,5},{7,6},{8,11},{9,8},{10,9... | collective-permute-start | bytes 1572872 | tf_op jit(solution)/shard_map/ppermute | solution.py:194
  146.6 30.4 %collective-permute-start.20 = (bf16[2,256,512]{2,1,0:T(8,128)(2,1)}, bf16[2,256,512]{2,1,0:T(8,128)(2,1)S(1)}, u32[]{:S(2)}, u32[]{:S(2)}) collective-permute-start(bf16[2,256,512]{2,1,0:T(8,128)(2,1)} %get-tuple-element.32), channel_id=1, source_target_pairs={{0,3},{1,0},{2,1},{3,2},{4,7},{5,4},{6,5},{7,6},{8,11},{9,8},{10,9... | collective-permute-start | bytes 1572872 | tf_op jit(solution)/shard_map/ppermute | solution.py:199
  146.6 36.3 %collective-permute-start.22 = (bf16[2,256,512]{2,1,0:T(8,128)(2,1)}, bf16[2,256,512]{2,1,0:T(8,128)(2,1)S(1)}, u32[]{:S(2)}, u32[]{:S(2)}) collective-permute-start(bf16[2,256,512]{2,1,0:T(8,128)(2,1)} %get-tuple-element.34), channel_id=1, source_target_pairs={{0,1},{1,2},{2,3},{3,0},{4,5},{5,6},{6,7},{7,4},{8,9},{9,10},{10,1... | collective-permute-start | bytes 1572872 | tf_op jit(solution)/shard_map/ppermute | solution.py:198
  148.7 25.0 %collective-permute-start.26 = (bf16[2,256,512]{2,1,0:T(8,128)(2,1)}, bf16[2,256,512]{2,1,0:T(8,128)(2,1)S(1)}, u32[]{:S(2)}, u32[]{:S(2)}) collective-permute-start(bf16[2,256,512]{2,1,0:T(8,128)(2,1)} %get-tuple-element.39), channel_id=1, source_target_pairs={{0,1},{3,0},{4,5},{5,6},{8,9},{9,10},{13,14},{16,17},{19,16},{20,2... | collective-permute-start | bytes 1572872 | tf_op jit(solution)/shard_map/ppermute | solution.py:191
  150.4 27.8 %collective-permute-start.31 = (bf16[2,256,512]{2,1,0:T(8,128)(2,1)}, bf16[2,256,512]{2,1,0:T(8,128)(2,1)S(1)}, u32[]{:S(2)}, u32[]{:S(2)}) collective-permute-start(bf16[2,256,512]{2,1,0:T(8,128)(2,1)} %get-tuple-element.44), channel_id=1, source_target_pairs={{0,3},{4,7},{9,8},{13,12},{16,19},{20,23},{25,24},{29,28},{32,35},... | collective-permute-start | bytes 1572872 | tf_op jit(solution)/shard_map/ppermute | solution.py:194
  154.7 30.3 %collective-permute-start.19 = (bf16[2,256,512]{2,1,0:T(8,128)(2,1)S(1)}, bf16[2,256,512]{2,1,0:T(8,128)(2,1)S(1)}, u32[]{:S(2)}, u32[]{:S(2)}) collective-permute-start(bf16[2,256,512]{2,1,0:T(8,128)(2,1)S(1)} %add_convert_fusion.3), channel_id=1, source_target_pairs={{0,1},{1,2},{2,3},{3,0},{4,5},{5,6},{6,7},{7,4},{8,9},{9,10},{10,1... | collective-permute-start | bytes 1572872 | tf_op jit(solution)/shard_map/ppermute | solution.py:198
  173.7 14.9 %collective-permute-start.24 = (bf16[2,256,512]{2,1,0:T(8,128)(2,1)S(1)}, bf16[2,256,512]{2,1,0:T(8,128)(2,1)S(1)}, u32[]{:S(2)}, u32[]{:S(2)}) collective-permute-start(bf16[2,256,512]{2,1,0:T(8,128)(2,1)S(1)} %add_convert_fusion.2), channel_id=1, source_target_pairs={{0,3},{1,0},{2,1},{3,2},{4,7},{5,4},{6,5},{7,6},{8,11},{9,8},{10,9... | collective-permute-start | bytes 1572872 | tf_op jit(solution)/shard_map/ppermute | solution.py:199
  176.9 22.9 %collective-permute-start.28 = (bf16[2,256,512]{2,1,0:T(8,128)(2,1)S(1)}, bf16[2,256,512]{2,1,0:T(8,128)(2,1)S(1)}, u32[]{:S(2)}, u32[]{:S(2)}) collective-permute-start(bf16[2,256,512]{2,1,0:T(8,128)(2,1)S(1)} %copy-done.23), channel_id=1, source_target_pairs={{2,1},{3,2},{4,7},{7,6},{8,11},{11,10},{12,15},{18,17},{19,18},{20... | collective-permute-start | bytes 1572872 | tf_op jit(solution)/shard_map/ppermute | solution.py:199
  178.2 23.5 %collective-permute-start.27 = (bf16[2,256,512]{2,1,0:T(8,128)(2,1)S(1)}, bf16[2,256,512]{2,1,0:T(8,128)(2,1)S(1)}, u32[]{:S(2)}, u32[]{:S(2)}) collective-permute-start(bf16[2,256,512]{2,1,0:T(8,128)(2,1)S(1)} %add_convert_fusion.1), channel_id=1, source_target_pairs={{0,1},{1,2},{5,6},{6,7},{9,10},{10,11},{14,15},{16,17},{17,18},{21... | collective-permute-start | bytes 1572872 | tf_op jit(solution)/shard_map/ppermute | solution.py:198
  183.0 22.3 %collective-permute-start.30 = (bf16[2,256,512]{2,1,0:T(8,128)(2,1)S(1)}, bf16[2,256,512]{2,1,0:T(8,128)(2,1)S(1)}, u32[]{:S(2)}, u32[]{:S(2)}) collective-permute-start(bf16[2,256,512]{2,1,0:T(8,128)(2,1)S(1)} %copy-done.22), channel_id=1, source_target_pairs={{1,2},{5,6},{10,11},{14,15},{17,18},{21,22},{26,27},{30,31},{33,34... | collective-permute-start | bytes 1572872 | tf_op jit(solution)/shard_map/ppermute | solution.py:198
  184.9 20.9 %collective-permute-start.32 = (bf16[2,256,512]{2,1,0:T(8,128)(2,1)S(1)}, bf16[2,256,512]{2,1,0:T(8,128)(2,1)S(1)}, u32[]{:S(2)}, u32[]{:S(2)}) collective-permute-start(bf16[2,256,512]{2,1,0:T(8,128)(2,1)S(1)} %add_convert_fusion), channel_id=1, source_target_pairs={{3,2},{7,6},{8,11},{12,15},{19,18},{23,22},{24,27},{28,31},{35,34}... | collective-permute-start | bytes 1572872 | tf_op jit(solution)/shard_map/ppermute | solution.py:199
  188.6 19.3 %collective-permute-start.21 = (bf16[256,512]{1,0:T(8,128)(2,1)S(1)}, bf16[256,512]{1,0:T(8,128)(2,1)S(1)}, u32[]{:S(2)}, u32[]{:S(2)}) collective-permute-start(bf16[256,512]{1,0:T(8,128)(2,1)S(1)} %fusion.8), channel_id=1, source_target_pairs={{0,16},{1,17},{2,18},{3,19},{4,20},{5,21},{6,22},{7,23},{8,24},{9,... | collective-permute-start | bytes 786440 | tf_op jit(solution)/shard_map/ppermute | solution.py:203
  201.9 9.3 %collective-permute-start.29 = (bf16[256,512]{1,0:T(8,128)(2,1)S(1)}, bf16[256,512]{1,0:T(8,128)(2,1)S(1)}, u32[]{:S(2)}, u32[]{:S(2)}) collective-permute-start(bf16[256,512]{1,0:T(8,128)(2,1)S(1)} %fusion.10), channel_id=1, source_target_pairs={{1,17},{2,18},{6,22},{7,23},{10,26},{11,27},{15,31},{17,33},{18,34... | collective-permute-start | bytes 786440 | tf_op jit(solution)/shard_map/ppermute | solution.py:203
  206.0 8.6 %collective-permute-start.33 = (bf16[256,512]{1,0:T(8,128)(2,1)S(1)}, bf16[256,512]{1,0:T(8,128)(2,1)S(1)}, u32[]{:S(2)}, u32[]{:S(2)}) collective-permute-start(bf16[256,512]{1,0:T(8,128)(2,1)S(1)} %fusion.11), channel_id=1, source_target_pairs={{2,18},{6,22},{11,27},{15,31},{18,34},{22,38},{27,43},{31,47},{34,... | collective-permute-start | bytes 786440 | tf_op jit(solution)/shard_map/ppermute | solution.py:203
  (26 other events, 753.1 us)

commit v2 on v1

v2 whole, which is shorter than its diff:
```python
import functools

import jax
import jax.numpy as jnp
from jax import lax
from jax.experimental import pallas as pl
from jax.experimental.pallas import tpu as pltpu
from jax.sharding import PartitionSpec as P

EPW, CH = 8, 2
NZ, NX = 4, 4
SECS, ROWS = 16, 16
BB, KB = 256, 512
QUARTER = BB // NX
BF, F32 = jnp.bfloat16, jnp.float32
STEPS = (0, -1, 1, 2)
VMEM_BYTES = 56 * 1024 * 1024
CELLS = [(b, j) for b in range(2) for j in range(CH)]


def charge(channel):
    klass = channel % 9
    return klass % 3 - 1, klass // 3 - 1


def live_at(r, b, j):
    to_b = b + charge(CH * r + j)[1]
    return jnp.where((to_b >= 0) & (to_b < 2), 1, 0)


COUNT = [sum(0 <= b + charge(CH * r + j)[1] < 2 for b, j in CELLS) for r in range(ROWS)]


def row_z(r, d):
    return (r // NX + d) % NZ * NX + r % NX


def row_x(r, d):
    return r // NX * NX + (r % NX + d) % NX


def moved(value, move, owner, i):
    return lax.ppermute(value, "row", [(r, move(r)) for r in range(ROWS) if COUNT[owner(r)] > i])


def after(value, *others):
    return lax.optimization_barrier((value, *others))[0]


def packed_cells(r, a, ket_sizes, bra_sizes):
    places = [(jnp.int32(0), jnp.int32(0), jnp.int32(0)) for _ in range(4)]
    count = jnp.int32(0)
    for b, j in CELLS:
        out_a, out_b = charge(CH * r + j)
        live = live_at(r, b, j)
        at_a, at_b = a + out_a, jnp.clip(b + out_b, 0, 1)
        rows = jnp.where((at_a >= 0) & (at_a < SECS), bra_sizes[2 * jnp.clip(at_a, 0, SECS - 1) + at_b], 0)
        cols = ket_sizes[2 * a + b]
        for i in range(4):
            hit = (live == 1) & (count == i)
            places[i] = tuple(jnp.where(hit, new, old) for new, old in zip((2 * j + b, rows, cols), places[i]))
        count = count + live
    return places


def keep(rows, cols):
    row_at = lax.broadcasted_iota(jnp.int32, (BB, KB), 0)
    col_at = lax.broadcasted_iota(jnp.int32, (BB, KB), 1)
    return (row_at < rows) & (col_at < cols)


def pack_kernel(place, ket_sizes, bra_sizes, env, *outs):
    for i, (cell, rows, cols) in enumerate(packed_cells(place[0], place[1], ket_sizes, bra_sizes)):
        value = jnp.where(keep(rows, cols), env[cell], jnp.zeros((BB, KB), BF))
        if i < 2:
            outs[0][i] = value
        else:
            outs[i - 1][...] = value


def unpack_kernel(place, ket_sizes, bra_sizes, *refs):
    here, above, out = refs[:4], refs[4:8], refs[8]
    out[...] = jnp.zeros_like(out)
    for i, (cell, rows, cols) in enumerate(packed_cells(place[0], place[1], ket_sizes, bra_sizes)):
        value = here[i][...] + above[i][...].astype(F32)

        @pl.when(rows > 0)
        def _(value=value, cell=cell, rows=rows, cols=cols):
            out[cell] = jnp.where(keep(rows, cols), value, 0.0).astype(BF)


def terms_kernel(place, ints, values, own01, own2, own3, behind01, behind2, behind3, ahead01, ahead2, ahead3,
                 across0, across1, across2, across3, ket, bra_own, bra_rim, *refs):
    outs = refs[:16]
    env_all, bra_all, total = refs[16:]
    for k, (first, third, fourth) in enumerate(((own01, own2, own3), (behind01, behind2, behind3), (ahead01, ahead2, ahead3))):
        env_all[4 * k] = first[0]
        env_all[4 * k + 1] = first[1]
        env_all[4 * k + 2] = third[...]
        env_all[4 * k + 3] = fourth[...]
    for n, ref in enumerate((across0, across1, across2, across3)):
        env_all[12 + n] = ref[...]
    for n in range(6):
        bra_all[6 + n] = bra_own[n]
    for x in range(NX):
        lines = pl.ds(QUARTER * x, QUARTER)
        for n in range(3):
            bra_all[n, lines] = bra_rim[x, n]
            bra_all[21 + n, lines] = bra_rim[x, 9 + n]
        for n in range(6):
            bra_all[12 + n, lines] = bra_rim[x, 3 + n]

    @pl.loop(0, 32)
    def _(n):
        total[n] = jnp.zeros((BB, KB), F32)

    r = place[0]
    my_z, my_x = r // NX, r % NX

    @pl.loop(0, 4 * CH * EPW)
    def _(item):
        out_w = ints[4 * item]

        @pl.when(out_w // (CH * NX) == my_z)
        def _():
            sp = ints[4 * item + 1]
            s = ints[4 * item + 2]
            value = values[4 * item + 3]
            k, j = item // (CH * EPW), item // EPW % CH
            from_z = (my_z + jnp.where(k == 1, 3, jnp.where(k == 2, 1, jnp.where(k == 3, 2, 0)))) % NZ
            from_r = from_z * NX + my_x
            out_r, out_j = out_w // CH, out_w % CH
            forward = (out_r % NX - my_x + NX) % NX
            slot = jnp.where(forward == 1, 2, jnp.where(forward == 3, 1, jnp.where(forward == 2, 3, 0)))
            out_a, out_b = charge(out_w)
            s_a, s_b = s % 2, s // 2
            sp_a, sp_b = sp % 2, sp // 2

            def position(row, b, jj):
                low = live_at(row, 0, 0)
                inside = low + live_at(row, 0, 1) + jj * live_at(row, 1, 0)
                return jnp.where(b == 0, jj * low, inside)

            for q_b in range(2):
                p_b = q_b + s_b
                live = (p_b < 2) & (live_at(from_r, q_b, j) == 1) & (live_at(out_r, p_b, out_j) == 1)

                @pl.when(live)
                def _(q_b=q_b, p_b=p_b):
                    e_at = 4 * k + position(from_r, q_b, j)
                    half = jnp.dot(env_all[e_at], ket[s, q_b], preferred_element_type=F32).astype(BF)
                    b_at = 6 * (s_a + out_a + 1) + 3 * sp_a + p_b + out_b + sp_b
                    term = jnp.dot(bra_all[b_at], half, preferred_element_type=F32)
                    at = 8 * slot + 2 * position(out_r, p_b, out_j) + s_a
                    total[at] = total[at] + value * term

    for d in range(4):
        for i in range(4):
            for up in range(2):
                outs[4 * d + i][up] = total[8 * d + 2 * i + up].astype(BF)


def body(env_in, ket_mps, bra_mps, ket_sizes, bra_sizes, entries, coeffs):
    my_a = lax.axis_index("sec")
    r = lax.axis_index("row")
    my_x = r % NX
    place = jnp.stack([r, my_a])
    ket_flat, bra_flat = ket_sizes.reshape(-1), bra_sizes.reshape(-1)

    smem = pl.BlockSpec(memory_space=pltpu.SMEM)
    vmem = pl.BlockSpec(memory_space=pltpu.VMEM)
    block = jax.ShapeDtypeStruct((BB, KB), BF)
    pair = jax.ShapeDtypeStruct((2, BB, KB), BF)
    params = pltpu.CompilerParams(vmem_limit_bytes=VMEM_BYTES)
    own01, own2, own3 = pl.pallas_call(
        pack_kernel,
        in_specs=[smem] * 3 + [vmem],
        out_specs=[vmem] * 3,
        out_shape=[pair, block, block],
        compiler_params=params,
    )(place, ket_flat, bra_flat, env_in.reshape(4, BB, KB))

    same = lambda n: n
    z_up, z_down = (lambda n: row_z(n, 1)), (lambda n: row_z(n, -1))
    x_up, x_down, x_far = (lambda n: row_x(n, 1)), (lambda n: row_x(n, -1)), (lambda n: row_x(n, 2))

    behind01 = moved(own01, z_up, same, 0)
    ahead01 = moved(own01, z_down, same, 0)

    flipped = jnp.swapaxes(bra_mps[:, 0], -1, -2)
    six = lambda f: jnp.stack([f[0, 0], f[0, 1], f[2, 1], f[1, 0], f[1, 1], f[3, 1]])
    bra_own = six(flipped)
    strip = six(lax.dynamic_slice_in_dim(flipped, QUARTER * my_x, QUARTER, axis=2))
    up = lambda n: [(i, i + n) for i in range(SECS - n)]
    down = lambda n: [(i + n, i) for i in range(SECS - n)]
    rim = jnp.concatenate([
        lax.ppermute(strip[:3], "sec", up(1)),
        lax.ppermute(strip, "sec", down(1)),
        lax.ppermute(strip[3:], "sec", down(2)),
    ])
    bra_rim = lax.all_gather(rim, "row", axis_index_groups=[[NX * z + x for x in range(NX)] for z in range(NZ)])

    behind2 = moved(own2, z_up, same, 2)
    ahead3 = moved(own3, z_down, same, 3)
    ahead2 = moved(after(own2, ahead01), z_down, same, 2)
    behind3 = moved(after(own3, behind01), z_up, same, 3)
    across0 = moved(behind01[0], z_up, z_down, 0)
    across1 = moved(ahead01[1], z_down, z_up, 1)
    across2 = moved(behind2, z_up, z_down, 2)
    across3 = moved(ahead3, z_down, z_up, 3)

    items = jnp.concatenate([entries.reshape(-1, 3).astype(F32), coeffs.reshape(-1, 1)], axis=-1).reshape(-1)
    items = after(items, behind01, ahead01)
    values = jnp.concatenate(
        [items] + [lax.ppermute(items, "row", [(n, row_z(n, -d)) for n in range(ROWS)]) for d in STEPS[1:]]
    )
    ints = values.astype(jnp.int32)

    sums = pl.pallas_call(
        terms_kernel,
        in_specs=[smem] * 3 + [vmem] * 16,
        out_specs=[vmem] * 16,
        out_shape=[pair] * 16,
        scratch_shapes=[
            pltpu.VMEM((16, BB, KB), BF),
            pltpu.VMEM((24, BB, BB), BF),
            pltpu.VMEM((32, BB, KB), F32),
        ],
        compiler_params=params,
    )(place, ints, values, own01, own2, own3, behind01, behind2, behind3, ahead01, ahead2, ahead3,
      across0, across1, across2, across3, ket_mps[:, 0], bra_own, bra_rim)
    mine, left, right, far = sums[:4], sums[4:8], sums[8:12], sums[12:]

    def added(*parts):
        return functools.reduce(jnp.add, [part.astype(F32) for part in parts])

    far_up = {0: moved(far[0], x_up, x_far, 0)}
    far_down = {1: moved(far[1], x_down, x_far, 1)}
    from_left, from_right = {}, {}
    from_left[1] = moved(right[1], x_up, x_up, 1)
    from_right[0] = moved(left[0], x_down, x_down, 0)
    far_up[2] = moved(after(far[2], far_up[0]), x_up, x_far, 2)
    far_down[3] = moved(after(far[3], far_down[1]), x_down, x_far, 3)
    from_left[0] = moved(added(after(right[0], from_left[1]), far_up[0]).astype(BF), x_up, x_up, 0)
    from_right[1] = moved(added(after(left[1], from_right[0]), far_down[1]).astype(BF), x_down, x_down, 1)
    from_left[3] = moved(after(right[3], far_up[2]), x_up, x_up, 3)
    from_right[2] = moved(after(left[2], far_down[3]), x_down, x_down, 2)
    from_left[2] = moved(added(after(right[2], from_left[0]), far_up[2]).astype(BF), x_up, x_up, 2)
    from_right[3] = moved(added(after(left[3], from_right[1]), far_down[3]).astype(BF), x_down, x_down, 3)

    here, above = [], []
    for i in range(4):
        raised = added(mine[i][1], from_left[i][1], from_right[i][1]).astype(BF)
        pairs = [(a * ROWS + n, (a + 1) * ROWS + n) for a in range(SECS - 1) for n in range(ROWS) if COUNT[n] > i]
        above.append(lax.ppermute(raised, ("sec", "row"), pairs))
        here.append(added(mine[i][0], from_left[i][0], from_right[i][0]))

    out = pl.pallas_call(
        unpack_kernel,
        in_specs=[smem] * 3 + [vmem] * 8,
        out_specs=vmem,
        out_shape=jax.ShapeDtypeStruct((4, BB, KB), BF),
        compiler_params=params,
    )(place, ket_flat, bra_flat, *here, *above)
    return out.reshape(CH, 1, 2, BB, KB)


def solution(mesh):
    placed = (
        P("row", "sec", None, None, None),
        P(None, "sec", None, None, None),
        P(None, "sec", None, None, None),
        P(),
        P(),
        P("row", None, None),
        P("row", None),
    )
    return jax.shard_map(
        body,
        mesh=mesh,
        in_specs=placed,
        out_specs=P("row", "sec", None, None, None),
        check_vma=False,
    )
```

time: 216 us -> 228 us (1.056)
  the two profiles are of different devices: /device:TPU:76 before, /device:TPU:116 now
where the time goes in v2:
time: 228 us; the launch traced here: 226 us
  waiting for transfers between devices  106 us (46%)
  starting transfers between devices  66 us (29%)
  Pallas kernels  24.9 us (11%)
  between operations  14.1 us (6%)
  other arithmetic  9.89 us (4%)
  local copies, waits for them, and re-layouts  5.47 us (2%)
    ppermute x22, waiting for transfers between devices, moved(): lax.ppermute(value, 'row', [(r, move(r)) for r in range(ROWS) if COUNT[ow...  90.6 us
    ppermute x22, starting transfers between devices, moved(): lax.ppermute(value, 'row', [(r, move(r)) for r in range(ROWS) if COUNT[ow...  41.3 us
    pallas_call x1, Pallas kernels, body(): pl.pallas_call(terms_kernel, in_specs=[smem] * 3 + [vmem] * 16, out_specs...  19.1 us
    ppermute x3, starting transfers between devices, body(): lax.ppermute(items, 'row', [(n, row_z(n, -d)) for n in range(ROWS)])  10.2 us
    ppermute x4, starting transfers between devices, body(): above.append(lax.ppermute(raised, ('sec', 'row'), pairs))  7.63 us
    ppermute x4, waiting for transfers between devices, body(): above.append(lax.ppermute(raised, ('sec', 'row'), pairs))  5.71 us
    ppermute x3, waiting for transfers between devices, body(): lax.ppermute(items, 'row', [(n, row_z(n, -d)) for n in range(ROWS)])  5.46 us
  transfers between devices with their start and end apart: 33, of which 16 were waited for; matrix products, arithmetic and copies ran while one was open for 5% of the time, Pallas kernels for 1%

profile of v2, /device:TPU:116, one launch (start us, length us, event | category | flops | bytes accessed | tf_op | source)
XLA Modules:
  0.0 226.1 jit_solution(11704211328335352822)
XLA Ops:
  8.2 2.0 collective-permute-start.15
  10.3 2.9 %collective-permute-start.14 = (bf16[6,64,256]{2,1,0:T(8,128)(2,1)S(1)}, bf16[6,64,256]{2,1,0:T(8,128)(2,1)S(1)}, u32[]{:S(2)}, u32[]{:S(2)}) collective-permute-start(bf16[6,64,256]{2,1,0:T(8,128)(2,1)S(1)} %constant_dynamic-update-slice_fusion), channel_id=1, source_target_pairs={{16,0},{32,16},{48,32},{64,48},{80,64},{96,80},{112,96},{128,112},... | collective-permute-start | bytes 589832 | tf_op jit(solution)/shard_map/ppermute | solution.py:198
  13.2 1.9 collective-permute-start.13
  15.6 3.5 %collective-permute-done.13 = bf16[3,64,256]{2,1,0:T(8,128)(2,1)S(1)} collective-permute-done((bf16[3,64,256]{2,1,0:T(8,128)(2,1)S(1)}, bf16[3,64,256]{2,1,0:T(8,128)(2,1)S(1)}, u32[]{:S(2)}, u32[]{:S(2)}) %collective-permute-start.13) | collective-permute-done | bytes 98336 | tf_op jit(solution)/shard_map/ppermute | solution.py:197
  22.1 2.5 %shard_map.73 = (bf16[2,256,512]{2,1,0:T(8,128)(2,1)}, bf16[256,512]{1,0:T(8,128)(2,1)}, bf16[256,512]{1,0:T(8,128)(2,1)}) custom-call(s32[2]{0:T(128)} %pad_add_fusion.place, s32[32]{0:T(128)} %reshape.67.ket_sizes, s32[32]{0:T(128)} %reshape.68.bra_sizes, bf16[4,256,512]{2,1,0:T(8,128)(2,1)} %bitcast.99), custom_call_target="tpu_custom_call" | custom-call | tf_op jit(solution)/shard_map/pallas_call | solution.py:175
  24.6 4.1 %collective-permute-start = (bf16[2,256,512]{2,1,0:T(8,128)(2,1)}, bf16[2,256,512]{2,1,0:T(8,128)(2,1)S(1)}, u32[]{:S(2)}, u32[]{:S(2)}) collective-permute-start(bf16[2,256,512]{2,1,0:T(8,128)(2,1)} %get-tuple-element.35.own01), channel_id=1, source_target_pairs={{0,4},{1,5},{2,6},{3,7},{4,8},{5,9},{6,10},{7,11},{8,12},{9,13},{1... | collective-permute-start | bytes 1572872 | tf_op jit(solution)/shard_map/ppermute | solution.py:43
  28.7 4.3 %collective-permute-start.5 = (bf16[256,512]{1,0:T(8,128)(2,1)}, bf16[256,512]{1,0:T(8,128)(2,1)}, u32[]{:S(2)}, u32[]{:S(2)}) collective-permute-start(bf16[256,512]{1,0:T(8,128)(2,1)} %get-tuple-element.40.own2), channel_id=1, source_target_pairs={{1,5},{2,6},{6,10},{7,11},{10,14},{11,15},{15,3},{17,21},{18,22},{... | collective-permute-start | bytes 786440 | tf_op jit(solution)/shard_map/ppermute | solution.py:43
  33.0 3.9 %collective-permute-start.8 = (bf16[256,512]{1,0:T(8,128)(2,1)}, bf16[256,512]{1,0:T(8,128)(2,1)}, u32[]{:S(2)}, u32[]{:S(2)}) collective-permute-start(bf16[256,512]{1,0:T(8,128)(2,1)} %get-tuple-element.39.own3), channel_id=1, source_target_pairs={{2,14},{6,2},{11,7},{15,11},{18,30},{22,18},{27,23},{31,27},{34,46... | collective-permute-start | bytes 786440 | tf_op jit(solution)/shard_map/ppermute | solution.py:43
  37.8 25.7 %collective-permute-done.5.behind2 = bf16[256,512]{1,0:T(8,128)(2,1)} collective-permute-done((bf16[256,512]{1,0:T(8,128)(2,1)}, bf16[256,512]{1,0:T(8,128)(2,1)}, u32[]{:S(2)}, u32[]{:S(2)}) %collective-permute-start.5) | collective-permute-done | bytes 262176 | tf_op jit(solution)/shard_map/ppermute | solution.py:43
  63.5 5.5 %collective-permute-start.11 = (bf16[256,512]{1,0:T(8,128)(2,1)}, bf16[256,512]{1,0:T(8,128)(2,1)S(1)}, u32[]{:S(2)}, u32[]{:S(2)}) collective-permute-start(bf16[256,512]{1,0:T(8,128)(2,1)} %collective-permute-done.5.behind2), channel_id=1, source_target_pairs={{3,7},{5,9},{6,10},{10,14},{11,15},{14,2},{15,3},{19,23},{21,25},{... | collective-permute-start | bytes 786440 | tf_op jit(solution)/shard_map/ppermute | solution.py:43
  69.7 6.1 %collective-permute-start.4 = (f32[64]{0:T(128)S(1)}, f32[64]{0:T(128)S(1)}, u32[]{:S(2)}, u32[]{:S(2)}) collective-permute-start(f32[64]{0:T(128)S(1)} %reshape.70), channel_id=1, source_target_pairs={{0,8},{1,9},{2,10},{3,11},{4,12},{5,13},{6,14},{7,15},{8,0},{9,1},... | collective-permute-start | bytes 776 | tf_op jit(solution)/shard_map/ppermute | solution.py:215
  75.8 4.1 %collective-permute-start.2 = (f32[64]{0:T(128)S(1)}, f32[64]{0:T(128)S(1)}, u32[]{:S(2)}, u32[]{:S(2)}) collective-permute-start(f32[64]{0:T(128)S(1)} %reshape.70), channel_id=1, source_target_pairs={{0,4},{1,5},{2,6},{3,7},{4,8},{5,9},{6,10},{7,11},{8,12},{9,13},{1... | collective-permute-start | bytes 776 | tf_op jit(solution)/shard_map/ppermute | solution.py:215
  80.0 3.5 %collective-permute-done.11.across2 = bf16[256,512]{1,0:T(8,128)(2,1)S(1)} collective-permute-done((bf16[256,512]{1,0:T(8,128)(2,1)}, bf16[256,512]{1,0:T(8,128)(2,1)S(1)}, u32[]{:S(2)}, u32[]{:S(2)}) %collective-permute-start.11) | collective-permute-done | bytes 262176 | tf_op jit(solution)/shard_map/ppermute | solution.py:43
  83.5 5.5 %collective-permute-done.4 = f32[64]{0:T(128)S(1)} collective-permute-done((f32[64]{0:T(128)S(1)}, f32[64]{0:T(128)S(1)}, u32[]{:S(2)}, u32[]{:S(2)}) %collective-permute-start.4) | collective-permute-done | bytes 288 | tf_op jit(solution)/shard_map/ppermute | solution.py:215
  88.9 1.9 collective-permute-start.7
  90.9 4.2 %collective-permute-start.9 = (bf16[256,512]{1,0:T(8,128)(2,1)S(1)}, bf16[256,512]{1,0:T(8,128)(2,1)S(1)}, u32[]{:S(2)}, u32[]{:S(2)}) collective-permute-start(bf16[256,512]{1,0:T(8,128)(2,1)S(1)} %slice_bitcast_fusion.1), channel_id=1, source_target_pairs={{0,4},{1,5},{2,6},{3,7},{4,8},{5,9},{6,10},{7,11},{8,12},{9,13},{1... | collective-permute-start | bytes 786440 | tf_op jit(solution)/shard_map/ppermute | solution.py:43
  95.1 1.9 collective-permute-start.6
  97.8 3.0 %collective-permute-done.7.ahead2 = bf16[256,512]{1,0:T(8,128)(2,1)S(1)} collective-permute-done((bf16[256,512]{1,0:T(8,128)(2,1)S(1)}, bf16[256,512]{1,0:T(8,128)(2,1)S(1)}, u32[]{:S(2)}, u32[]{:S(2)}) %collective-permute-start.7) | collective-permute-done | bytes 262176 | tf_op jit(solution)/shard_map/ppermute | solution.py:43
  102.6 3.4 %collective-permute-done.6.behind3 = bf16[256,512]{1,0:T(8,128)(2,1)} collective-permute-done((bf16[256,512]{1,0:T(8,128)(2,1)}, bf16[256,512]{1,0:T(8,128)(2,1)}, u32[]{:S(2)}, u32[]{:S(2)}) %collective-permute-start.6) | collective-permute-done | bytes 262176 | tf_op jit(solution)/shard_map/ppermute | solution.py:43
  106.0 19.1 %shard_map.74 = (bf16[2,256,512]{2,1,0:T(8,128)(2,1)}, bf16[2,256,512]{2,1,0:T(8,128)(2,1)}, bf16[2,256,512]{2,1,0:T(8,128)(2,1)}, bf16[2,256,512]{2,1,0:T(8,128...) custom-call(s32[2]{0:T(128)} %pad_add_fusion.place, ...), custom_call_target="tpu_custom_call" | custom-call | tf_op jit(solution)/shard_map/pallas_call | solution.py:219
  125.3 2.0 collective-permute-start.19
  127.3 1.9 collective-permute-start.20
  129.3 11.0 %collective-permute-done.16 = bf16[2,256,512]{2,1,0:T(8,128)(2,1)S(1)} collective-permute-done((bf16[2,256,512]{2,1,0:T(8,128)(2,1)}, bf16[2,256,512]{2,1,0:T(8,128)(2,1)S(1)}, u32[]{:S(2)}, u32[]{:S(2)}) %collective-permute-start.16) | collective-permute-done | bytes 524320 | tf_op jit(solution)/shard_map/ppermute | solution.py:43
  140.3 8.7 %collective-permute-done.17 = bf16[2,256,512]{2,1,0:T(8,128)(2,1)S(1)} collective-permute-done((bf16[2,256,512]{2,1,0:T(8,128)(2,1)}, bf16[2,256,512]{2,1,0:T(8,128)(2,1)S(1)}, u32[]{:S(2)}, u32[]{:S(2)}) %collective-permute-start.17) | collective-permute-done | bytes 524320 | tf_op jit(solution)/shard_map/ppermute | solution.py:43
  153.6 2.7 %collective-permute-start.21 = (bf16[2,256,512]{2,1,0:T(8,128)(2,1)S(1)}, bf16[2,256,512]{2,1,0:T(8,128)(2,1)S(1)}, u32[]{:S(2)}, u32[]{:S(2)}) collective-permute-start(bf16[2,256,512]{2,1,0:T(8,128)(2,1)S(1)} %add_convert_fusion.2), channel_id=1, source_target_pairs={{0,3},{1,0},{2,1},{3,2},{4,7},{5,4},{6,5},{7,6},{8,11},{9,8},{10,9... | collective-permute-start | bytes 1572872 | tf_op jit(solution)/shard_map/ppermute | solution.py:43
  156.3 9.8 %collective-permute-done.22 = bf16[2,256,512]{2,1,0:T(8,128)(2,1)S(1)} collective-permute-done((bf16[2,256,512]{2,1,0:T(8,128)(2,1)}, bf16[2,256,512]{2,1,0:T(8,128)(2,1)S(1)}, u32[]{:S(2)}, u32[]{:S(2)}) %collective-permute-start.22) | collective-permute-done | bytes 524320 | tf_op jit(solution)/shard_map/ppermute | solution.py:43
  167.4 9.9 %collective-permute-done.18 = bf16[2,256,512]{2,1,0:T(8,128)(2,1)S(1)} collective-permute-done((bf16[2,256,512]{2,1,0:T(8,128)(2,1)S(1)}, bf16[2,256,512]{2,1,0:T(8,128)(2,1)S(1)}, u32[]{:S(2)}, u32[]{:S(2)}) %collective-permute-start.18) | collective-permute-done | bytes 524320 | tf_op jit(solution)/shard_map/ppermute | solution.py:43
  178.5 1.9 collective-permute-start.23
  187.1 9.2 %collective-permute-done.23 = bf16[2,256,512]{2,1,0:T(8,128)(2,1)S(1)} collective-permute-done((bf16[2,256,512]{2,1,0:T(8,128)(2,1)S(1)}, bf16[2,256,512]{2,1,0:T(8,128)(2,1)S(1)}, u32[]{:S(2)}, u32[]{:S(2)}) %collective-permute-start.23) | collective-permute-done | bytes 524320 | tf_op jit(solution)/shard_map/ppermute | solution.py:43
  203.0 3.5 %collective-permute-done.27 = bf16[2,256,512]{2,1,0:T(8,128)(2,1)S(1)} collective-permute-done((bf16[2,256,512]{2,1,0:T(8,128)(2,1)S(1)}, bf16[2,256,512]{2,1,0:T(8,128)(2,1)S(1)}, u32[]{:S(2)}, u32[]{:S(2)}) %collective-permute-start.27) | collective-permute-done | bytes 524320 | tf_op jit(solution)/shard_map/ppermute | solution.py:43
  209.5 5.7 %collective-permute-done.31.refs_7_ = bf16[256,512]{1,0:T(8,128)(2,1)S(1)} collective-permute-done((bf16[256,512]{1,0:T(8,128)(2,1)S(1)}, bf16[256,512]{1,0:T(8,128)(2,1)S(1)}, u32[]{:S(2)}, u32[]{:S(2)}) %collective-permute-start.31) | collective-permute-done | bytes 262176 | tf_op jit(solution)/shard_map/ppermute | solution.py:255
  215.9 3.3 %shard_map.75 = bf16[4,256,512]{2,1,0:T(8,128)(2,1)} custom-call(s32[2]{0:T(128)} %pad_add_fusion.place, s32[32]{0:T(128)} %reshape.67.ket_sizes, s32[32]{0:T(128)} %reshape.68.bra_sizes, f32[256,512]{1,0:T(8,128)} %get-tuple-element.74.refs_0_, f32[256,512]{1,0:T(8,128)} %get-tuple-element.72.refs_1_, f32[256,512]{1,0:T(8,128)} %get-tuple-element.70.refs_2_, ...), custom_call_target="tpu_custom_call" | custom-call | tf_op jit(solution)/shard_map/pallas_call | solution.py:258
  (127 shorter events, 33.3 us)
Async XLA Ops:
  6.5 99.4 %all-gather.3.cloned.1.call-start = ((), (), s32[]{:S(2)}) async-start(), calls=%async_computation | async-start | bytes 1966080 | tf_op jit(solution)/shard_map/all_gather | solution.py:201
  8.2 7.4 %collective-permute-start.15 = (bf16[3,64,256]{2,1,0:T(8,128)(2,1)S(1)}, bf16[3,64,256]{2,1,0:T(8,128)(2,1)S(1)}, u32[]{:S(2)}, u32[]{:S(2)}) collective-permute-start(bf16[3,64,256]{2,1,0:T(8,128)(2,1)S(1)} %pad_maximum_fusion.2), channel_id=1, source_target_pairs={{32,0},{48,16},{64,32},{80,48},{96,64},{112,80},{128,96},{144,112}... | collective-permute-start | bytes 294920 | tf_op jit(solution)/shard_map/ppermute | solution.py:199
  10.3 8.8 %collective-permute-start.14 = (bf16[6,64,256]{2,1,0:T(8,128)(2,1)S(1)}, bf16[6,64,256]{2,1,0:T(8,128)(2,1)S(1)}, u32[]{:S(2)}, u32[]{:S(2)}) collective-permute-start(bf16[6,64,256]{2,1,0:T(8,128)(2,1)S(1)} %constant_dynamic-update-slice_fusion), channel_id=1, source_target_pairs={{16,0},{32,16},{48,32},{64,48},{80,64},{96,80},{112,96},{128,112},... | collective-permute-start | bytes 589832 | tf_op jit(solution)/shard_map/ppermute | solution.py:198
  24.6 45.1 %collective-permute-start.1 = (bf16[2,256,512]{2,1,0:T(8,128)(2,1)}, bf16[2,256,512]{2,1,0:T(8,128)(2,1)S(1)}, u32[]{:S(2)}, u32[]{:S(2)}) collective-permute-start(bf16[2,256,512]{2,1,0:T(8,128)(2,1)} %get-tuple-element.35.own01), channel_id=1, source_target_pairs={{0,12},{1,13},{2,14},{3,15},{4,0},{5,1},{6,2},{7,3},{8,4},{9,5},{1... | collective-permute-start | bytes 1572872 | tf_op jit(solution)/shard_map/ppermute | solution.py:43
  24.6 45.2 %collective-permute-start = (bf16[2,256,512]{2,1,0:T(8,128)(2,1)}, bf16[2,256,512]{2,1,0:T(8,128)(2,1)S(1)}, u32[]{:S(2)}, u32[]{:S(2)}) collective-permute-start(bf16[2,256,512]{2,1,0:T(8,128)(2,1)} %get-tuple-element.35.own01), channel_id=1, source_target_pairs={{0,4},{1,5},{2,6},{3,7},{4,8},{5,9},{6,10},{7,11},{8,12},{9,13},{1... | collective-permute-start | bytes 1572872 | tf_op jit(solution)/shard_map/ppermute | solution.py:43
  28.7 34.8 %collective-permute-start.5 = (bf16[256,512]{1,0:T(8,128)(2,1)}, bf16[256,512]{1,0:T(8,128)(2,1)}, u32[]{:S(2)}, u32[]{:S(2)}) collective-permute-start(bf16[256,512]{1,0:T(8,128)(2,1)} %get-tuple-element.40.own2), channel_id=1, source_target_pairs={{1,5},{2,6},{6,10},{7,11},{10,14},{11,15},{15,3},{17,21},{18,22},{... | collective-permute-start | bytes 786440 | tf_op jit(solution)/shard_map/ppermute | solution.py:43
  33.0 36.0 %collective-permute-start.8 = (bf16[256,512]{1,0:T(8,128)(2,1)}, bf16[256,512]{1,0:T(8,128)(2,1)}, u32[]{:S(2)}, u32[]{:S(2)}) collective-permute-start(bf16[256,512]{1,0:T(8,128)(2,1)} %get-tuple-element.39.own3), channel_id=1, source_target_pairs={{2,14},{6,2},{11,7},{15,11},{18,30},{22,18},{27,23},{31,27},{34,46... | collective-permute-start | bytes 786440 | tf_op jit(solution)/shard_map/ppermute | solution.py:43
  63.5 20.0 %collective-permute-start.11 = (bf16[256,512]{1,0:T(8,128)(2,1)}, bf16[256,512]{1,0:T(8,128)(2,1)S(1)}, u32[]{:S(2)}, u32[]{:S(2)}) collective-permute-start(bf16[256,512]{1,0:T(8,128)(2,1)} %collective-permute-done.5.behind2), channel_id=1, source_target_pairs={{3,7},{5,9},{6,10},{10,14},{11,15},{14,2},{15,3},{19,23},{21,25},{... | collective-permute-start | bytes 786440 | tf_op jit(solution)/shard_map/ppermute | solution.py:43
  69.0 28.8 %collective-permute-start.12 = (bf16[256,512]{1,0:T(8,128)(2,1)}, bf16[256,512]{1,0:T(8,128)(2,1)S(1)}, u32[]{:S(2)}, u32[]{:S(2)}) collective-permute-start(bf16[256,512]{1,0:T(8,128)(2,1)} %collective-permute-done.8.ahead3), channel_id=1, source_target_pairs={{2,14},{7,3},{11,7},{14,10},{18,30},{23,19},{27,23},{30,26},{34,46... | collective-permute-start | bytes 786440 | tf_op jit(solution)/shard_map/ppermute | solution.py:43
  69.7 19.2 %collective-permute-start.4 = (f32[64]{0:T(128)S(1)}, f32[64]{0:T(128)S(1)}, u32[]{:S(2)}, u32[]{:S(2)}) collective-permute-start(f32[64]{0:T(128)S(1)} %reshape.70), channel_id=1, source_target_pairs={{0,8},{1,9},{2,10},{3,11},{4,12},{5,13},{6,14},{7,15},{8,0},{9,1},... | collective-permute-start | bytes 776 | tf_op jit(solution)/shard_map/ppermute | solution.py:215
  75.8 15.0 %collective-permute-start.3 = (f32[64]{0:T(128)S(1)}, f32[64]{0:T(128)S(1)}, u32[]{:S(2)}, u32[]{:S(2)}) collective-permute-start(f32[64]{0:T(128)S(1)} %reshape.70), channel_id=1, source_target_pairs={{0,12},{1,13},{2,14},{3,15},{4,0},{5,1},{6,2},{7,3},{8,4},{9,5},{1... | collective-permute-start | bytes 776 | tf_op jit(solution)/shard_map/ppermute | solution.py:215
  75.8 19.3 %collective-permute-start.2 = (f32[64]{0:T(128)S(1)}, f32[64]{0:T(128)S(1)}, u32[]{:S(2)}, u32[]{:S(2)}) collective-permute-start(f32[64]{0:T(128)S(1)} %reshape.70), channel_id=1, source_target_pairs={{0,4},{1,5},{2,6},{3,7},{4,8},{5,9},{6,10},{7,11},{8,12},{9,13},{1... | collective-permute-start | bytes 776 | tf_op jit(solution)/shard_map/ppermute | solution.py:215
  83.5 14.3 %collective-permute-start.10 = (bf16[256,512]{1,0:T(8,128)(2,1)S(1)}, bf16[256,512]{1,0:T(8,128)(2,1)S(1)}, u32[]{:S(2)}, u32[]{:S(2)}) collective-permute-start(bf16[256,512]{1,0:T(8,128)(2,1)S(1)} %slice_bitcast_fusion), channel_id=1, source_target_pairs={{0,12},{1,13},{2,14},{3,15},{4,0},{5,1},{6,2},{7,3},{8,4},{9,5},{1... | collective-permute-start | bytes 786440 | tf_op jit(solution)/shard_map/ppermute | solution.py:43
  88.9 11.9 %collective-permute-start.7 = (bf16[256,512]{1,0:T(8,128)(2,1)S(1)}, bf16[256,512]{1,0:T(8,128)(2,1)S(1)}, u32[]{:S(2)}, u32[]{:S(2)}) collective-permute-start(bf16[256,512]{1,0:T(8,128)(2,1)S(1)} %copy-done.9), channel_id=1, source_target_pairs={{1,13},{2,14},{6,2},{7,3},{10,6},{11,7},{15,11},{17,29},{18,30},{2... | collective-permute-start | bytes 786440 | tf_op jit(solution)/shard_map/ppermute | solution.py:43
  90.9 11.0 %collective-permute-start.9 = (bf16[256,512]{1,0:T(8,128)(2,1)S(1)}, bf16[256,512]{1,0:T(8,128)(2,1)S(1)}, u32[]{:S(2)}, u32[]{:S(2)}) collective-permute-start(bf16[256,512]{1,0:T(8,128)(2,1)S(1)} %slice_bitcast_fusion.1), channel_id=1, source_target_pairs={{0,4},{1,5},{2,6},{3,7},{4,8},{5,9},{6,10},{7,11},{8,12},{9,13},{1... | collective-permute-start | bytes 786440 | tf_op jit(solution)/shard_map/ppermute | solution.py:43
  95.1 10.9 %collective-permute-start.6 = (bf16[256,512]{1,0:T(8,128)(2,1)}, bf16[256,512]{1,0:T(8,128)(2,1)}, u32[]{:S(2)}, u32[]{:S(2)}) collective-permute-start(bf16[256,512]{1,0:T(8,128)(2,1)} %get-tuple-element.39.own3), channel_id=1, source_target_pairs={{2,6},{6,10},{11,15},{15,3},{18,22},{22,26},{27,31},{31,19},{34,38... | collective-permute-start | bytes 786440 | tf_op jit(solution)/shard_map/ppermute | solution.py:43
  125.1 15.1 %collective-permute-start.16 = (bf16[2,256,512]{2,1,0:T(8,128)(2,1)}, bf16[2,256,512]{2,1,0:T(8,128)(2,1)S(1)}, u32[]{:S(2)}, u32[]{:S(2)}) collective-permute-start(bf16[2,256,512]{2,1,0:T(8,128)(2,1)} %get-tuple-element.43), channel_id=1, source_target_pairs={{0,1},{1,2},{2,3},{3,0},{4,5},{5,6},{6,7},{7,4},{8,9},{9,10},{10,1... | collective-permute-start | bytes 1572872 | tf_op jit(solution)/shard_map/ppermute | solution.py:43
  125.2 23.8 %collective-permute-start.17 = (bf16[2,256,512]{2,1,0:T(8,128)(2,1)}, bf16[2,256,512]{2,1,0:T(8,128)(2,1)S(1)}, u32[]{:S(2)}, u32[]{:S(2)}) collective-permute-start(bf16[2,256,512]{2,1,0:T(8,128)(2,1)} %get-tuple-element.45), channel_id=1, source_target_pairs={{0,1},{1,2},{2,3},{3,0},{4,5},{5,6},{6,7},{7,4},{8,9},{9,10},{10,1... | collective-permute-start | bytes 1572872 | tf_op jit(solution)/shard_map/ppermute | solution.py:43
  125.3 26.4 %collective-permute-start.19 = (bf16[2,256,512]{2,1,0:T(8,128)(2,1)}, bf16[2,256,512]{2,1,0:T(8,128)(2,1)S(1)}, u32[]{:S(2)}, u32[]{:S(2)}) collective-permute-start(bf16[2,256,512]{2,1,0:T(8,128)(2,1)} %get-tuple-element.46), channel_id=1, source_target_pairs={{0,3},{1,0},{2,1},{3,2},{4,7},{5,4},{6,5},{7,6},{8,11},{9,8},{10,9... | collective-permute-start | bytes 1572872 | tf_op jit(solution)/shard_map/ppermute | solution.py:43
  127.3 24.4 %collective-permute-start.20 = (bf16[2,256,512]{2,1,0:T(8,128)(2,1)}, bf16[2,256,512]{2,1,0:T(8,128)(2,1)S(1)}, u32[]{:S(2)}, u32[]{:S(2)}) collective-permute-start(bf16[2,256,512]{2,1,0:T(8,128)(2,1)} %get-tuple-element.50), channel_id=1, source_target_pairs={{0,3},{1,0},{2,1},{3,2},{4,7},{5,4},{6,5},{7,6},{8,11},{9,8},{10,9... | collective-permute-start | bytes 1572872 | tf_op jit(solution)/shard_map/ppermute | solution.py:43
  149.0 17.1 %collective-permute-start.22 = (bf16[2,256,512]{2,1,0:T(8,128)(2,1)}, bf16[2,256,512]{2,1,0:T(8,128)(2,1)S(1)}, u32[]{:S(2)}, u32[]{:S(2)}) collective-permute-start(bf16[2,256,512]{2,1,0:T(8,128)(2,1)} %get-tuple-element.55), channel_id=1, source_target_pairs={{0,1},{3,0},{4,5},{5,6},{8,9},{9,10},{13,14},{16,17},{19,16},{20,2... | collective-permute-start | bytes 1572872 | tf_op jit(solution)/shard_map/ppermute | solution.py:43
  151.6 25.7 %collective-permute-start.18 = (bf16[2,256,512]{2,1,0:T(8,128)(2,1)S(1)}, bf16[2,256,512]{2,1,0:T(8,128)(2,1)S(1)}, u32[]{:S(2)}, u32[]{:S(2)}) collective-permute-start(bf16[2,256,512]{2,1,0:T(8,128)(2,1)S(1)} %add_convert_fusion.3), channel_id=1, source_target_pairs={{0,1},{1,2},{2,3},{3,0},{4,5},{5,6},{6,7},{7,4},{8,9},{9,10},{10,1... | collective-permute-start | bytes 1572872 | tf_op jit(solution)/shard_map/ppermute | solution.py:43
  151.7 31.7 %collective-permute-start.24 = (bf16[2,256,512]{2,1,0:T(8,128)(2,1)}, bf16[2,256,512]{2,1,0:T(8,128)(2,1)S(1)}, u32[]{:S(2)}, u32[]{:S(2)}) collective-permute-start(bf16[2,256,512]{2,1,0:T(8,128)(2,1)} %get-tuple-element.58), channel_id=1, source_target_pairs={{0,3},{4,7},{9,8},{13,12},{16,19},{20,23},{25,24},{29,28},{32,35},... | collective-permute-start | bytes 1572872 | tf_op jit(solution)/shard_map/ppermute | solution.py:43
  153.6 31.1 %collective-permute-start.21 = (bf16[2,256,512]{2,1,0:T(8,128)(2,1)S(1)}, bf16[2,256,512]{2,1,0:T(8,128)(2,1)S(1)}, u32[]{:S(2)}, u32[]{:S(2)}) collective-permute-start(bf16[2,256,512]{2,1,0:T(8,128)(2,1)S(1)} %add_convert_fusion.2), channel_id=1, source_target_pairs={{0,3},{1,0},{2,1},{3,2},{4,7},{5,4},{6,5},{7,6},{8,11},{9,8},{10,9... | collective-permute-start | bytes 1572872 | tf_op jit(solution)/shard_map/ppermute | solution.py:43
  166.1 37.0 %collective-permute-start.26 = (bf16[2,256,512]{2,1,0:T(8,128)(2,1)}, bf16[2,256,512]{2,1,0:T(8,128)(2,1)S(1)}, u32[]{:S(2)}, u32[]{:S(2)}) collective-permute-start(bf16[2,256,512]{2,1,0:T(8,128)(2,1)} %get-tuple-element.62), channel_id=1, source_target_pairs={{1,2},{5,6},{10,11},{14,15},{17,18},{21,22},{26,27},{30,31},{33,34... | collective-permute-start | bytes 1572872 | tf_op jit(solution)/shard_map/ppermute | solution.py:43
  178.5 17.9 %collective-permute-start.23 = (bf16[2,256,512]{2,1,0:T(8,128)(2,1)S(1)}, bf16[2,256,512]{2,1,0:T(8,128)(2,1)S(1)}, u32[]{:S(2)}, u32[]{:S(2)}) collective-permute-start(bf16[2,256,512]{2,1,0:T(8,128)(2,1)S(1)} %add_convert_fusion.1), channel_id=1, source_target_pairs={{0,1},{1,2},{5,6},{6,7},{9,10},{10,11},{14,15},{16,17},{17,18},{21... | collective-permute-start | bytes 1572872 | tf_op jit(solution)/shard_map/ppermute | solution.py:43
  181.4 28.0 %collective-permute-start.28 = (bf16[256,512]{1,0:T(8,128)(2,1)S(1)}, bf16[256,512]{1,0:T(8,128)(2,1)S(1)}, u32[]{:S(2)}, u32[]{:S(2)}) collective-permute-start(bf16[256,512]{1,0:T(8,128)(2,1)S(1)} %get-tuple-element.73), channel_id=1, source_target_pairs={{0,16},{1,17},{2,18},{3,19},{4,20},{5,21},{6,22},{7,23},{8,24},{9,... | collective-permute-start | bytes 786440 | tf_op jit(solution)/shard_map/ppermute | solution.py:255
  183.4 16.8 %collective-permute-start.25 = (bf16[2,256,512]{2,1,0:T(8,128)(2,1)S(1)}, bf16[2,256,512]{2,1,0:T(8,128)(2,1)S(1)}, u32[]{:S(2)}, u32[]{:S(2)}) collective-permute-start(bf16[2,256,512]{2,1,0:T(8,128)(2,1)S(1)} %copy-done.22), channel_id=1, source_target_pairs={{2,1},{3,2},{4,7},{7,6},{8,11},{11,10},{12,15},{18,17},{19,18},{20... | collective-permute-start | bytes 1572872 | tf_op jit(solution)/shard_map/ppermute | solution.py:43
  184.8 21.7 %collective-permute-start.27 = (bf16[2,256,512]{2,1,0:T(8,128)(2,1)S(1)}, bf16[2,256,512]{2,1,0:T(8,128)(2,1)S(1)}, u32[]{:S(2)}, u32[]{:S(2)}) collective-permute-start(bf16[2,256,512]{2,1,0:T(8,128)(2,1)S(1)} %add_convert_fusion), channel_id=1, source_target_pairs={{3,2},{7,6},{8,11},{12,15},{19,18},{23,22},{24,27},{28,31},{35,34}... | collective-permute-start | bytes 1572872 | tf_op jit(solution)/shard_map/ppermute | solution.py:43
  196.3 13.1 %collective-permute-start.29 = (bf16[256,512]{1,0:T(8,128)(2,1)S(1)}, bf16[256,512]{1,0:T(8,128)(2,1)S(1)}, u32[]{:S(2)}, u32[]{:S(2)}) collective-permute-start(bf16[256,512]{1,0:T(8,128)(2,1)S(1)} %get-tuple-element.71), channel_id=1, source_target_pairs={{0,16},{1,17},{2,18},{3,19},{4,20},{5,21},{6,22},{7,23},{8,24},{9,... | collective-permute-start | bytes 786440 | tf_op jit(solution)/shard_map/ppermute | solution.py:255
  201.1 8.4 %collective-permute-start.30 = (bf16[256,512]{1,0:T(8,128)(2,1)S(1)}, bf16[256,512]{1,0:T(8,128)(2,1)S(1)}, u32[]{:S(2)}, u32[]{:S(2)}) collective-permute-start(bf16[256,512]{1,0:T(8,128)(2,1)S(1)} %get-tuple-element.69), channel_id=1, source_target_pairs={{1,17},{2,18},{6,22},{7,23},{10,26},{11,27},{15,31},{17,33},{18,34... | collective-permute-start | bytes 786440 | tf_op jit(solution)/shard_map/ppermute | solution.py:255
  207.5 7.7 %collective-permute-start.31 = (bf16[256,512]{1,0:T(8,128)(2,1)S(1)}, bf16[256,512]{1,0:T(8,128)(2,1)S(1)}, u32[]{:S(2)}, u32[]{:S(2)}) collective-permute-start(bf16[256,512]{1,0:T(8,128)(2,1)S(1)} %get-tuple-element.67), channel_id=1, source_target_pairs={{2,18},{6,22},{11,27},{15,31},{18,34},{22,38},{27,43},{31,47},{34,... | collective-permute-start | bytes 786440 | tf_op jit(solution)/shard_map/ppermute | solution.py:255
  (25 other events, 603.5 us)
Sparse Core Ops, SparseCore 0:
  20.1 30.5 all-gather.2

commit v3 on v2

v3 whole, which is shorter than its diff:
```python
import functools

import jax
import jax.numpy as jnp
from jax import lax
from jax.experimental import pallas as pl
from jax.experimental.pallas import tpu as pltpu
from jax.sharding import PartitionSpec as P

EPW, CH = 8, 2
NZ, NX = 4, 4
SECS, ROWS = 16, 16
BB, KB = 256, 512
QUARTER = BB // NX
BF, F32 = jnp.bfloat16, jnp.float32
STEPS = (0, -1, 1, 2)
VMEM_BYTES = 56 * 1024 * 1024
HEAD = 16
BRA_CELLS = ((0, 0), (0, 1), (2, 1), (1, 0), (1, 1), (3, 1))
CELLS = [(b, j) for b in range(2) for j in range(CH)]


def charge(channel):
    klass = channel % 9
    return klass % 3 - 1, klass // 3 - 1


def live_at(r, b, j):
    to_b = b + charge(CH * r + j)[1]
    return jnp.where((to_b >= 0) & (to_b < 2), 1, 0)


COUNT = [sum(0 <= b + charge(CH * r + j)[1] < 2 for b, j in CELLS) for r in range(ROWS)]


def row_z(r, d):
    return (r // NX + d) % NZ * NX + r % NX


def row_x(r, d):
    return r // NX * NX + (r % NX + d) % NX


def packed_cells(r, a, ket_sizes, bra_sizes):
    places = [(jnp.int32(0), jnp.int32(0), jnp.int32(0)) for _ in range(4)]
    count = jnp.int32(0)
    for b, j in CELLS:
        out_a, out_b = charge(CH * r + j)
        live = live_at(r, b, j)
        at_a, at_b = a + out_a, jnp.clip(b + out_b, 0, 1)
        rows = jnp.where((at_a >= 0) & (at_a < SECS), bra_sizes[2 * jnp.clip(at_a, 0, SECS - 1) + at_b], 0)
        cols = ket_sizes[2 * a + b]
        for i in range(4):
            hit = (live == 1) & (count == i)
            places[i] = tuple(jnp.where(hit, new, old) for new, old in zip((2 * j + b, rows, cols), places[i]))
        count = count + live
    return places, count


def live_count(r):
    return sum(live_at(r, b, j) for b, j in CELLS)


def keep(rows, cols):
    row_at = lax.broadcasted_iota(jnp.int32, (BB, KB), 0)
    col_at = lax.broadcasted_iota(jnp.int32, (BB, KB), 1)
    return (row_at < rows) & (col_at < cols)


def prepare_kernel(place, ket_sizes, bra_sizes, entries, coeffs, env, bra, pair, third, moving, strip, strip_low, strip_high):
    r, a = place[0], place[1]
    lane = lax.broadcasted_iota(jnp.int32, (HEAD, KB), 1)
    slot, field = lane // 8, lane % 8
    targets = (pair.at[0], pair.at[1], third, moving)
    places, count = packed_cells(r, a, ket_sizes, bra_sizes)
    for i, (cell, rows, cols) in enumerate(places):
        j, b = cell // 2, cell % 2
        head = jnp.zeros((HEAD, KB), F32)
        for n in range(EPW):
            at = EPW * j + n
            part = jnp.where(field < 3, 0.0, coeffs[at])
            for f in range(3):
                part = jnp.where(field == f, entries[3 * at + f].astype(F32), part)
            part = jnp.where(field == 7, (b + 1).astype(F32), part)
            head = jnp.where(slot == n, part, head)
        first = head.astype(BF).astype(F32)
        second = (head - first).astype(BF).astype(F32)
        last = head - first - second
        head = jnp.where(field == 4, second, jnp.where(field == 5, last, first))
        head = jnp.where(i < count, head, 0.0)
        targets[i][:HEAD] = head.astype(BF)
        targets[i][HEAD:] = jnp.where(keep(rows, cols), env[cell], jnp.zeros((BB, KB), BF))

    lines = pl.ds(pl.multiple_of(r % NX * QUARTER, QUARTER), QUARTER)
    for n, (sp, to_b) in enumerate(BRA_CELLS):
        value = bra[sp, to_b, lines]
        strip[n] = value
        if n < 3:
            strip_low[n] = value
        else:
            strip_high[n - 3] = value


def unpack_kernel(place, ket_sizes, bra_sizes, *refs):
    here, above, out = refs[:4], refs[4:8], refs[8]
    out[...] = jnp.zeros_like(out)
    for i, (cell, rows, cols) in enumerate(packed_cells(place[0], place[1], ket_sizes, bra_sizes)[0]):

        @pl.when(rows > 0)
        def _(i=i, cell=cell, rows=rows, cols=cols):
            value = here[i][...] + above[i][...].astype(F32)
            out[cell] = jnp.where(keep(rows, cols), value, 0.0).astype(BF)


def terms_kernel(place, ket_sizes, ints, values, own01, own2, behind01, behind2, ahead01, ahead2,
                 across0, across1, across2a, across2b, ket, bra_own, bra_rim, *refs):
    outs = refs[:16]
    env_all, bra_all, total = refs[16:]
    for k, (two, third) in enumerate(((own01, own2), (behind01, behind2), (ahead01, ahead2))):
        env_all[3 * k] = two[0, HEAD:]
        env_all[3 * k + 1] = two[1, HEAD:]
        env_all[3 * k + 2] = third[HEAD:]
    env_all[9] = across0[HEAD:]
    env_all[10] = across1[HEAD:]
    env_all[11, : BB // 2] = across2a[HEAD:]
    env_all[11, BB // 2 :] = across2b[...]
    for n, (sp, to_b) in enumerate(BRA_CELLS):
        bra_all[6 + n] = bra_own[sp, to_b]
    for x in range(NX):
        lines = pl.ds(QUARTER * x, QUARTER)
        for n in range(3):
            bra_all[n, lines] = bra_rim[x, n]
            bra_all[21 + n, lines] = bra_rim[x, 9 + n]
        for n in range(6):
            bra_all[12 + n, lines] = bra_rim[x, 3 + n]

    r, a = place[0], place[1]
    my_z, my_x = r // NX, r % NX
    for d in range(4):
        for i in range(4):

            @pl.when(i < live_count(row_x(r, STEPS[d])))
            def _(at=8 * d + 2 * i):
                total[at] = jnp.zeros((BB, KB), F32)
                total[at + 1] = jnp.zeros((BB, KB), F32)

    @pl.loop(0, 12 * EPW)
    def _(item):
        base = 64 * (item // EPW) + 8 * (item % EPW)
        out_w, s, code = ints[base], ints[base + 2], ints[base + 7]
        p_b, s_a = code - 1 + s // 2, s % 2
        out_r, out_j = out_w // CH, out_w % CH

        @pl.when((code > 0) & (out_w // (CH * NX) == my_z) & (p_b < 2) & (a + s_a < SECS))
        def _():
            q_b = code - 1

            @pl.when(live_at(out_r, p_b, out_j) == 1)
            def _():
                sp = ints[base + 1]
                value = values[base + 3] + values[base + 4] + values[base + 5]
                forward = (out_r % NX - my_x + NX) % NX
                slot = jnp.where(forward == 1, 2, jnp.where(forward == 3, 1, jnp.where(forward == 2, 3, 0)))
                out_a, out_b = charge(out_w)
                low = live_at(out_r, 0, 0)
                inside = low + live_at(out_r, 0, 1) + out_j * live_at(out_r, 1, 0)
                position = jnp.where(p_b == 0, out_j * low, inside)
                b_at = 6 * (s_a + out_a + 1) + 3 * (sp % 2) + p_b + out_b + sp // 2
                at = 8 * slot + 2 * position + s_a
                e_at = item // EPW
                to_size = ket_sizes[2 * (a + s_a) + p_b]
                from_size = ket_sizes[2 * a + q_b]
                for n in range(2):
                    cols = pl.ds(n * (KB // 2), KB // 2)

                    def run(depth, cols=cols):
                        half = jnp.dot(env_all[e_at, :, :depth], ket[s, q_b, :depth, cols], preferred_element_type=F32)
                        term = lax.dot_general(
                            bra_all[b_at], half.astype(BF), (((0,), (0,)), ((), ())), preferred_element_type=F32
                        )
                        total[at, :, cols] = total[at, :, cols] + value * term

                    wide = to_size > n * (KB // 2)
                    pl.when(wide & (from_size > KB // 2))(functools.partial(run, KB))
                    pl.when(wide & (from_size <= KB // 2))(functools.partial(run, KB // 2))

    for d in (3, 2, 1, 0):
        for i in range(4):

            @pl.when(i < live_count(row_x(r, STEPS[d])))
            def _(d=d, i=i):
                for up in range(2):
                    outs[4 * d + i][up] = total[8 * d + 2 * i + up].astype(BF)


def body(env_in, ket_mps, bra_mps, ket_sizes, bra_sizes, entries, coeffs):
    my_a = lax.axis_index("sec")
    r = lax.axis_index("row")
    place = jnp.stack([r, my_a])
    ket_flat, bra_flat = ket_sizes.reshape(-1), bra_sizes.reshape(-1)

    smem = pl.BlockSpec(memory_space=pltpu.SMEM)
    vmem = pl.BlockSpec(memory_space=pltpu.VMEM)
    shape = jax.ShapeDtypeStruct
    pair = shape((2, BB, KB), BF)
    params = pltpu.CompilerParams(vmem_limit_bytes=VMEM_BYTES)
    own01, own2, moving, strip, strip_low, strip_high = pl.pallas_call(
        prepare_kernel,
        in_specs=[smem] * 5 + [vmem] * 2,
        out_specs=[vmem] * 6,
        out_shape=[
            shape((2, HEAD + BB, KB), BF),
            shape((HEAD + BB, KB), BF),
            shape((HEAD + BB, KB), BF),
            shape((6, QUARTER, BB), BF),
            shape((3, QUARTER, BB), BF),
            shape((3, QUARTER, BB), BF),
        ],
        compiler_params=params,
    )(place, ket_flat, bra_flat, entries.reshape(-1), coeffs.reshape(-1), env_in.reshape(4, BB, KB), bra_mps[:, 0])

    same = lambda n: n
    z_up, z_down = (lambda n: row_z(n, 1)), (lambda n: row_z(n, -1))
    x_up, x_down, x_far = (lambda n: row_x(n, 1)), (lambda n: row_x(n, -1)), (lambda n: row_x(n, 2))

    def sent(value, move, owner, rows):
        return lax.ppermute(value, "row", [(n, move(n)) for n in range(ROWS) if owner(n) in rows])

    everyone = set(range(ROWS))
    full = [n for n in range(ROWS) if COUNT[n] == 4]
    takers, lent = set(), []
    for n in full:
        taker = next(m for m in (row_x(n, 1), row_x(n, -1)) if COUNT[m] == 2 and m not in takers)
        takers.add(taker)
        lent.append((n, taker))
    three = {n for n in range(ROWS) if COUNT[n] > 2} | takers
    behind01 = sent(own01, z_up, same, everyone)
    ahead01 = sent(own01, z_down, same, everyone)
    own2 = own2 + lax.ppermute(moving, "row", lent)
    behind2 = sent(own2, z_up, same, three)
    ahead2 = sent(own2, z_down, same, three)
    across0 = sent(behind01[0], z_up, z_down, everyone)
    across1 = sent(ahead01[1], z_down, z_up, everyone)
    across2a = sent(behind2[: HEAD + BB // 2], z_up, z_down, three)
    across2b = sent(ahead2[HEAD + BB // 2 :], z_down, z_up, three)

    up = lambda n: [(i, i + n) for i in range(SECS - n)]
    down = lambda n: [(i + n, i) for i in range(SECS - n)]
    rim = jnp.concatenate([
        lax.ppermute(strip_low, "sec", up(1)),
        lax.ppermute(strip, "sec", down(1)),
        lax.ppermute(strip_high, "sec", down(2)),
    ])
    bra_rim = lax.all_gather(rim, "row", axis_index_groups=[[NX * z + x for x in range(NX)] for z in range(NZ)])

    heads = [own01[0], own01[1], own2, behind01[0], behind01[1], behind2, ahead01[0], ahead01[1], ahead2,
             across0, across1, across2a]
    values = jnp.concatenate([head[0, :64] for head in heads]).astype(F32)

    sums = pl.pallas_call(
        terms_kernel,
        in_specs=[smem] * 4 + [vmem] * 13,
        out_specs=[vmem] * 16,
        out_shape=[pair] * 16,
        scratch_shapes=[
            pltpu.VMEM((12, BB, KB), BF),
            pltpu.VMEM((24, BB, BB), BF),
            pltpu.VMEM((32, BB, KB), F32),
        ],
        compiler_params=params,
    )(place, ket_flat, values.astype(jnp.int32), values, own01, own2, behind01, behind2, ahead01, ahead2,
      across0, across1, across2a, across2b, ket_mps[:, 0], bra_mps[:, 0], bra_rim)
    mine, left, right, far = sums[:4], sums[4:8], sums[8:12], sums[12:]

    def added(*parts):
        return functools.reduce(jnp.add, [part.astype(F32) for part in parts])

    def moved(value, move, owner, i):
        return sent(value, move, owner, {n for n in range(ROWS) if COUNT[n] > i})

    far_up = {i: moved(far[i], x_up, x_far, i) for i in (0, 2)}
    far_down = {i: moved(far[i], x_down, x_far, i) for i in (1, 3)}
    from_left = {i: moved(right[i], x_up, x_up, i) for i in (1, 3)}
    from_right = {i: moved(left[i], x_down, x_down, i) for i in (0, 2)}
    for i in (0, 2):
        from_left[i] = moved(added(right[i], far_up[i]).astype(BF), x_up, x_up, i)
    for i in (1, 3):
        from_right[i] = moved(added(left[i], far_down[i]).astype(BF), x_down, x_down, i)

    here, above = [], []
    for i in range(4):
        raised = added(mine[i][1], from_left[i][1], from_right[i][1]).astype(BF)
        pairs = [(a * ROWS + n, (a + 1) * ROWS + n) for a in range(SECS - 1) for n in range(ROWS) if COUNT[n] > i]
        above.append(lax.ppermute(raised, ("sec", "row"), pairs))
        here.append(added(mine[i][0], from_left[i][0], from_right[i][0]))

    out = pl.pallas_call(
        unpack_kernel,
        in_specs=[smem] * 3 + [vmem] * 8,
        out_specs=vmem,
        out_shape=shape((4, BB, KB), BF),
        compiler_params=params,
    )(place, ket_flat, bra_flat, *here, *above)
    return out.reshape(CH, 1, 2, BB, KB)


def solution(mesh):
    placed = (
        P("row", "sec", None, None, None),
        P(None, "sec", None, None, None),
        P(None, "sec", None, None, None),
        P(),
        P(),
        P("row", None, None),
        P("row", None),
    )
    return jax.shard_map(
        body,
        mesh=mesh,
        in_specs=placed,
        out_specs=P("row", "sec", None, None, None),
        check_vma=False,
    )
```

time: 228 us -> 218 us (0.956)
  the two profiles are of different devices: /device:TPU:116 before, /device:TPU:92 now
where the time goes in v3:
time: 218 us; the launch traced here: 220 us
  waiting for transfers between devices  93.1 us (43%)
  starting transfers between devices  59.4 us (27%)
  Pallas kernels  34.9 us (16%)
  between operations  13.9 us (6%)
  other arithmetic  10.9 us (5%)
  local copies, waits for them, and re-layouts  8.12 us (4%)
    ppermute x20, waiting for transfers between devices, sent(): lax.ppermute(value, 'row', [(n, move(n)) for n in range(ROWS) if owner(n)...  82.3 us
    ppermute x20, starting transfers between devices, sent(): lax.ppermute(value, 'row', [(n, move(n)) for n in range(ROWS) if owner(n)...  40 us
    pallas_call x1, Pallas kernels, body(): pl.pallas_call(terms_kernel, in_specs=[smem] * 4 + [vmem] * 13, out_specs...  28.6 us
    ppermute x4, starting transfers between devices, body(): above.append(lax.ppermute(raised, ('sec', 'row'), pairs))  7.64 us
    ppermute x4, waiting for transfers between devices, body(): above.append(lax.ppermute(raised, ('sec', 'row'), pairs))  6.62 us
  transfers between devices with their start and end apart: 29, of which 11 were waited for; matrix products, arithmetic and copies ran while one was open for 5% of the time, Pallas kernels for 0%

profile of v3, /device:TPU:92, one launch (start us, length us, event | category | flops | bytes accessed | tf_op | source)
XLA Modules:
  0.0 220.3 jit_solution(9020225001190007613)
XLA Ops:
  6.5 1.3 reshape.65.coeffs
  12.7 3.0 %shard_map.73 = (bf16[2,272,512]{2,1,0:T(8,128)(2,1)}, bf16[272,512]{1,0:T(8,128)(2,1)}, bf16[272,512]{1,0:T(8,128)(2,1)}, bf16[6,64,256]{2,1,0:T(8,128)(2,1)}, ...) custom-call(s32[2]{0:T(128)} %pad_add_fusion.place, s32[32]{0:T(128)} %reshape.62.ket_sizes, ...), custom_call_target="tpu_custom_call" | custom-call | tf_op jit(solution)/shard_map/pallas_call | solution.py:207
  15.7 1.9 collective-permute-start.9
  17.6 4.0 %collective-permute-start.11 = (bf16[3,64,256]{2,1,0:T(8,128)(2,1)}, bf16[3,64,256]{2,1,0:T(8,128)(2,1)S(1)}, u32[]{:S(2)}, u32[]{:S(2)}) collective-permute-start(bf16[3,64,256]{2,1,0:T(8,128)(2,1)} %get-tuple-element.32), channel_id=1, source_target_pairs={{32,0},{48,16},{64,32},{80,48},{96,64},{112,80},{128,96},{144,112}... | collective-permute-start | bytes 294920 | tf_op jit(solution)/shard_map/ppermute | solution.py:252
  21.7 3.4 %collective-permute-start.10 = (bf16[6,64,256]{2,1,0:T(8,128)(2,1)}, bf16[6,64,256]{2,1,0:T(8,128)(2,1)S(1)}, u32[]{:S(2)}, u32[]{:S(2)}) collective-permute-start(bf16[6,64,256]{2,1,0:T(8,128)(2,1)} %get-tuple-element.31), channel_id=1, source_target_pairs={{16,0},{32,16},{48,32},{64,48},{80,64},{96,80},{112,96},{128,112},... | collective-permute-start | bytes 589832 | tf_op jit(solution)/shard_map/ppermute | solution.py:251
  25.0 2.5 %collective-permute-start = (bf16[272,512]{1,0:T(8,128)(2,1)}, bf16[272,512]{1,0:T(8,128)(2,1)S(1)}, u32[]{:S(2)}, u32[]{:S(2)}) collective-permute-start(bf16[272,512]{1,0:T(8,128)(2,1)} %get-tuple-element.29), channel_id=1, source_target_pairs={{2,3},{6,5},{11,8},{15,12},{18,19},{22,21},{27,24},{31,28},{34,35}... | collective-permute-start | bytes 835592 | tf_op jit(solution)/shard_map/ppermute | solution.py:239
  29.0 4.1 %collective-permute-done = bf16[272,512]{1,0:T(8,128)(2,1)S(1)} collective-permute-done((bf16[272,512]{1,0:T(8,128)(2,1)}, bf16[272,512]{1,0:T(8,128)(2,1)S(1)}, u32[]{:S(2)}, u32[]{:S(2)}) %collective-permute-start) | collective-permute-done | bytes 278560 | tf_op jit(solution)/shard_map/ppermute | solution.py:239
  34.1 4.8 %collective-permute-start.4 = (bf16[272,512]{1,0:T(8,128)(2,1)S(1)}, bf16[272,512]{1,0:T(8,128)(2,1)S(1)}, u32[]{:S(2)}, u32[]{:S(2)}) collective-permute-start(bf16[272,512]{1,0:T(8,128)(2,1)S(1)} %add.83.own2), channel_id=1, source_target_pairs={{1,13},{2,14},{3,15},{5,1},{6,2},{7,3},{8,4},{10,6},{11,7},{12,8},... | collective-permute-start | bytes 835592 | tf_op jit(solution)/shard_map/ppermute | solution.py:227
  39.0 3.1 %collective-permute-start.2 = (bf16[272,512]{1,0:T(8,128)(2,1)S(1)}, bf16[272,512]{1,0:T(8,128)(2,1)S(1)}, u32[]{:S(2)}, u32[]{:S(2)}) collective-permute-start(bf16[272,512]{1,0:T(8,128)(2,1)S(1)} %add.83.own2), channel_id=1, source_target_pairs={{1,5},{2,6},{3,7},{5,9},{6,10},{7,11},{8,12},{10,14},{11,15},{12,0... | collective-permute-start | bytes 835592 | tf_op jit(solution)/shard_map/ppermute | solution.py:227
  43.0 24.2 %collective-permute-done.4.ahead2 = bf16[272,512]{1,0:T(8,128)(2,1)S(1)} collective-permute-done((bf16[272,512]{1,0:T(8,128)(2,1)S(1)}, bf16[272,512]{1,0:T(8,128)(2,1)S(1)}, u32[]{:S(2)}, u32[]{:S(2)}) %collective-permute-start.4) | collective-permute-done | bytes 278560 | tf_op jit(solution)/shard_map/ppermute | solution.py:227
  67.2 1.5 collective-permute-start.8
  70.1 4.7 %collective-permute-start.6 = (bf16[272,512]{1,0:T(8,128)(2,1)S(1)}, bf16[272,512]{1,0:T(8,128)(2,1)S(1)}, u32[]{:S(2)}, u32[]{:S(2)}) collective-permute-start(bf16[272,512]{1,0:T(8,128)(2,1)S(1)} %get-tuple-element.57), channel_id=1, source_target_pairs={{0,12},{1,13},{2,14},{3,15},{4,0},{5,1},{6,2},{7,3},{8,4},{9,5},{1... | collective-permute-start | bytes 835592 | tf_op jit(solution)/shard_map/ppermute | solution.py:227
  75.7 10.6 %collective-permute-done.6.across1 = bf16[272,512]{1,0:T(8,128)(2,1)S(1)} collective-permute-done((bf16[272,512]{1,0:T(8,128)(2,1)S(1)}, bf16[272,512]{1,0:T(8,128)(2,1)S(1)}, u32[]{:S(2)}, u32[]{:S(2)}) %collective-permute-start.6) | collective-permute-done | bytes 278560 | tf_op jit(solution)/shard_map/ppermute | solution.py:227
  86.2 5.0 %collective-permute-done.5.across0 = bf16[272,512]{1,0:T(8,128)(2,1)S(1)} collective-permute-done((bf16[272,512]{1,0:T(8,128)(2,1)S(1)}, bf16[272,512]{1,0:T(8,128)(2,1)S(1)}, u32[]{:S(2)}, u32[]{:S(2)}) %collective-permute-start.5) | collective-permute-done | bytes 278560 | tf_op jit(solution)/shard_map/ppermute | solution.py:227
  92.7 28.6 %shard_map.74 = (bf16[2,256,512]{2,1,0:T(8,128)(2,1)}, bf16[2,256,512]{2,1,0:T(8,128)(2,1)}, bf16[2,256,512]{2,1,0:T(8,128)(2,1)}, bf16[2,256,512]{2,1,0:T(8,128...) custom-call(s32[2]{0:T(128)} %pad_add_fusion.place, ...), custom_call_target="tpu_custom_call" | custom-call | tf_op jit(solution)/shard_map/pallas_call | solution.py:260
  121.3 6.0 %collective-permute-start.12 = (bf16[2,256,512]{2,1,0:T(8,128)(2,1)}, bf16[2,256,512]{2,1,0:T(8,128)(2,1)S(1)}, u32[]{:S(2)}, u32[]{:S(2)}) collective-permute-start(bf16[2,256,512]{2,1,0:T(8,128)(2,1)} %get-tuple-element.35), channel_id=1, source_target_pairs={{0,1},{1,2},{2,3},{3,0},{4,5},{5,6},{6,7},{7,4},{8,9},{9,10},{10,1... | collective-permute-start | bytes 1572872 | tf_op jit(solution)/shard_map/ppermute | solution.py:227
  127.3 2.1 collective-permute-start.15
  130.7 9.3 %collective-permute-done.12 = bf16[2,256,512]{2,1,0:T(8,128)(2,1)S(1)} collective-permute-done((bf16[2,256,512]{2,1,0:T(8,128)(2,1)}, bf16[2,256,512]{2,1,0:T(8,128)(2,1)S(1)}, u32[]{:S(2)}, u32[]{:S(2)}) %collective-permute-start.12) | collective-permute-done | bytes 524320 | tf_op jit(solution)/shard_map/ppermute | solution.py:227
  140.0 1.5 collective-permute-start.20
  144.6 13.3 %collective-permute-done.18 = bf16[2,256,512]{2,1,0:T(8,128)(2,1)S(1)} collective-permute-done((bf16[2,256,512]{2,1,0:T(8,128)(2,1)}, bf16[2,256,512]{2,1,0:T(8,128)(2,1)S(1)}, u32[]{:S(2)}, u32[]{:S(2)}) %collective-permute-start.18) | collective-permute-done | bytes 524320 | tf_op jit(solution)/shard_map/ppermute | solution.py:227
  159.1 2.1 collective-permute-start.17
  162.7 8.2 %collective-permute-done.13 = bf16[2,256,512]{2,1,0:T(8,128)(2,1)S(1)} collective-permute-done((bf16[2,256,512]{2,1,0:T(8,128)(2,1)S(1)}, bf16[2,256,512]{2,1,0:T(8,128)(2,1)S(1)}, u32[]{:S(2)}, u32[]{:S(2)}) %collective-permute-start.13) | collective-permute-done | bytes 524320 | tf_op jit(solution)/shard_map/ppermute | solution.py:227
  170.9 7.2 %collective-permute-start.19 = (bf16[2,256,512]{2,1,0:T(8,128)(2,1)S(1)}, bf16[2,256,512]{2,1,0:T(8,128)(2,1)S(1)}, u32[]{:S(2)}, u32[]{:S(2)}) collective-permute-start(bf16[2,256,512]{2,1,0:T(8,128)(2,1)S(1)} %add_convert_fusion.1), channel_id=1, source_target_pairs={{0,1},{1,2},{5,6},{6,7},{9,10},{10,11},{14,15},{16,17},{17,18},{21... | collective-permute-start | bytes 1572872 | tf_op jit(solution)/shard_map/ppermute | solution.py:227
  180.5 7.7 %collective-permute-done.17 = bf16[2,256,512]{2,1,0:T(8,128)(2,1)S(1)} collective-permute-done((bf16[2,256,512]{2,1,0:T(8,128)(2,1)S(1)}, bf16[2,256,512]{2,1,0:T(8,128)(2,1)S(1)}, u32[]{:S(2)}, u32[]{:S(2)}) %collective-permute-start.17) | collective-permute-done | bytes 524320 | tf_op jit(solution)/shard_map/ppermute | solution.py:227
  188.2 1.9 collective-permute-start.24
  191.2 1.9 collective-permute-start.25
  193.1 3.9 %collective-permute-done.19 = bf16[2,256,512]{2,1,0:T(8,128)(2,1)S(1)} collective-permute-done((bf16[2,256,512]{2,1,0:T(8,128)(2,1)S(1)}, bf16[2,256,512]{2,1,0:T(8,128)(2,1)S(1)}, u32[]{:S(2)}, u32[]{:S(2)}) %collective-permute-start.19) | collective-permute-done | bytes 524320 | tf_op jit(solution)/shard_map/ppermute | solution.py:227
  198.0 1.9 collective-permute-start.26
  200.9 1.9 collective-permute-start.27
  202.9 3.7 %collective-permute-done.26.refs_6_ = bf16[256,512]{1,0:T(8,128)(2,1)S(1)} collective-permute-done((bf16[256,512]{1,0:T(8,128)(2,1)S(1)}, bf16[256,512]{1,0:T(8,128)(2,1)S(1)}, u32[]{:S(2)}, u32[]{:S(2)}) %collective-permute-start.26) | collective-permute-done | bytes 262176 | tf_op jit(solution)/shard_map/ppermute | solution.py:294
  206.5 3.0 %collective-permute-done.27.refs_7_ = bf16[256,512]{1,0:T(8,128)(2,1)S(1)} collective-permute-done((bf16[256,512]{1,0:T(8,128)(2,1)S(1)}, bf16[256,512]{1,0:T(8,128)(2,1)S(1)}, u32[]{:S(2)}, u32[]{:S(2)}) %collective-permute-start.27) | collective-permute-done | bytes 262176 | tf_op jit(solution)/shard_map/ppermute | solution.py:294
  210.2 3.2 %shard_map.75 = bf16[4,256,512]{2,1,0:T(8,128)(2,1)} custom-call(s32[2]{0:T(128)} %pad_add_fusion.place, s32[32]{0:T(128)} %reshape.62.ket_sizes, s32[32]{0:T(128)} %reshape.63.bra_sizes, f32[256,512]{1,0:T(8,128)} %get-tuple-element.56.refs_0_, f32[256,512]{1,0:T(8,128)} %get-tuple-element.54.refs_1_, f32[256,512]{1,0:T(8,128)} %get-tuple-element.52.refs_2_, ...), custom_call_target="tpu_custom_call" | custom-call | tf_op jit(solution)/shard_map/pallas_call | solution.py:297
  (102 shorter events, 24.8 us)
Async XLA Ops:
  6.5 85.5 %all-gather.3.cloned.1.call-start = ((), (), s32[]{:S(2)}) async-start(), calls=%async_computation | async-start | bytes 1966080 | tf_op jit(solution)/shard_map/all_gather | solution.py:254
  15.7 18.4 %collective-permute-start.9 = (bf16[3,64,256]{2,1,0:T(8,128)(2,1)}, bf16[3,64,256]{2,1,0:T(8,128)(2,1)S(1)}, u32[]{:S(2)}, u32[]{:S(2)}) collective-permute-start(bf16[3,64,256]{2,1,0:T(8,128)(2,1)} %get-tuple-element.30), channel_id=1, source_target_pairs={{0,16},{16,32},{32,48},{48,64},{64,80},{80,96},{96,112},{112,128},... | collective-permute-start | bytes 294920 | tf_op jit(solution)/shard_map/ppermute | solution.py:250
  17.6 21.3 %collective-permute-start.11 = (bf16[3,64,256]{2,1,0:T(8,128)(2,1)}, bf16[3,64,256]{2,1,0:T(8,128)(2,1)S(1)}, u32[]{:S(2)}, u32[]{:S(2)}) collective-permute-start(bf16[3,64,256]{2,1,0:T(8,128)(2,1)} %get-tuple-element.32), channel_id=1, source_target_pairs={{32,0},{48,16},{64,32},{80,48},{96,64},{112,80},{128,96},{144,112}... | collective-permute-start | bytes 294920 | tf_op jit(solution)/shard_map/ppermute | solution.py:252
  21.7 20.4 %collective-permute-start.10 = (bf16[6,64,256]{2,1,0:T(8,128)(2,1)}, bf16[6,64,256]{2,1,0:T(8,128)(2,1)S(1)}, u32[]{:S(2)}, u32[]{:S(2)}) collective-permute-start(bf16[6,64,256]{2,1,0:T(8,128)(2,1)} %get-tuple-element.31), channel_id=1, source_target_pairs={{16,0},{32,16},{48,32},{64,48},{80,64},{96,80},{112,96},{128,112},... | collective-permute-start | bytes 589832 | tf_op jit(solution)/shard_map/ppermute | solution.py:251
  25.0 8.0 %collective-permute-start = (bf16[272,512]{1,0:T(8,128)(2,1)}, bf16[272,512]{1,0:T(8,128)(2,1)S(1)}, u32[]{:S(2)}, u32[]{:S(2)}) collective-permute-start(bf16[272,512]{1,0:T(8,128)(2,1)} %get-tuple-element.29), channel_id=1, source_target_pairs={{2,3},{6,5},{11,8},{15,12},{18,19},{22,21},{27,24},{31,28},{34,35}... | collective-permute-start | bytes 835592 | tf_op jit(solution)/shard_map/ppermute | solution.py:239
  27.5 42.5 %collective-permute-start.3 = (bf16[2,272,512]{2,1,0:T(8,128)(2,1)}, bf16[2,272,512]{2,1,0:T(8,128)(2,1)S(1)}, u32[]{:S(2)}, u32[]{:S(2)}) collective-permute-start(bf16[2,272,512]{2,1,0:T(8,128)(2,1)} %get-tuple-element.27.own01), channel_id=1, source_target_pairs={{0,12},{1,13},{2,14},{3,15},{4,0},{5,1},{6,2},{7,3},{8,4},{9,5},{1... | collective-permute-start | bytes 1671176 | tf_op jit(solution)/shard_map/ppermute | solution.py:227
  33.1 41.7 %collective-permute-start.1 = (bf16[2,272,512]{2,1,0:T(8,128)(2,1)}, bf16[2,272,512]{2,1,0:T(8,128)(2,1)S(1)}, u32[]{:S(2)}, u32[]{:S(2)}) collective-permute-start(bf16[2,272,512]{2,1,0:T(8,128)(2,1)} %get-tuple-element.27.own01), channel_id=1, source_target_pairs={{0,4},{1,5},{2,6},{3,7},{4,8},{5,9},{6,10},{7,11},{8,12},{9,13},{1... | collective-permute-start | bytes 1671176 | tf_op jit(solution)/shard_map/ppermute | solution.py:227
  34.1 57.9 %copy-start.2 = (bf16[272,512]{1,0:T(8,128)(2,1)}, bf16[272,512]{1,0:T(8,128)(2,1)S(1)}, u32[]{:S(2)}) copy-start(bf16[272,512]{1,0:T(8,128)(2,1)S(1)} %add.83.own2) | copy-start | bytes 835588
  34.1 33.0 %collective-permute-start.4 = (bf16[272,512]{1,0:T(8,128)(2,1)S(1)}, bf16[272,512]{1,0:T(8,128)(2,1)S(1)}, u32[]{:S(2)}, u32[]{:S(2)}) collective-permute-start(bf16[272,512]{1,0:T(8,128)(2,1)S(1)} %add.83.own2), channel_id=1, source_target_pairs={{1,13},{2,14},{3,15},{5,1},{6,2},{7,3},{8,4},{10,6},{11,7},{12,8},... | collective-permute-start | bytes 835592 | tf_op jit(solution)/shard_map/ppermute | solution.py:227
  39.0 29.7 %collective-permute-start.2 = (bf16[272,512]{1,0:T(8,128)(2,1)S(1)}, bf16[272,512]{1,0:T(8,128)(2,1)S(1)}, u32[]{:S(2)}, u32[]{:S(2)}) collective-permute-start(bf16[272,512]{1,0:T(8,128)(2,1)S(1)} %add.83.own2), channel_id=1, source_target_pairs={{1,5},{2,6},{3,7},{5,9},{6,10},{7,11},{8,12},{10,14},{11,15},{12,0... | collective-permute-start | bytes 835592 | tf_op jit(solution)/shard_map/ppermute | solution.py:227
  67.2 24.8 %collective-permute-start.8 = (bf16[128,512]{1,0:T(8,128)(2,1)S(1)}, bf16[128,512]{1,0:T(8,128)(2,1)S(1)}, u32[]{:S(2)}, u32[]{:S(2)}) collective-permute-start(bf16[128,512]{1,0:T(8,128)(2,1)S(1)} %slice.195), channel_id=1, source_target_pairs={{1,13},{2,14},{3,15},{4,0},{6,2},{7,3},{8,4},{11,7},{13,9},{14,10}... | collective-permute-start | bytes 393224 | tf_op jit(solution)/shard_map/ppermute | solution.py:227
  68.7 6.9 %collective-permute-start.7 = (bf16[144,512]{1,0:T(8,128)(2,1)S(1)}, bf16[144,512]{1,0:T(8,128)(2,1)S(1)}, u32[]{:S(2)}, u32[]{:S(2)}) collective-permute-start(bf16[144,512]{1,0:T(8,128)(2,1)S(1)} %slice.193), channel_id=1, source_target_pairs={{0,4},{3,7},{5,9},{6,10},{7,11},{9,13},{10,14},{11,15},{12,0},{14,... | collective-permute-start | bytes 442376 | tf_op jit(solution)/shard_map/ppermute | solution.py:227
  70.1 16.1 %collective-permute-start.6 = (bf16[272,512]{1,0:T(8,128)(2,1)S(1)}, bf16[272,512]{1,0:T(8,128)(2,1)S(1)}, u32[]{:S(2)}, u32[]{:S(2)}) collective-permute-start(bf16[272,512]{1,0:T(8,128)(2,1)S(1)} %get-tuple-element.57), channel_id=1, source_target_pairs={{0,12},{1,13},{2,14},{3,15},{4,0},{5,1},{6,2},{7,3},{8,4},{9,5},{1... | collective-permute-start | bytes 835592 | tf_op jit(solution)/shard_map/ppermute | solution.py:227
  74.9 16.4 %collective-permute-start.5 = (bf16[272,512]{1,0:T(8,128)(2,1)S(1)}, bf16[272,512]{1,0:T(8,128)(2,1)S(1)}, u32[]{:S(2)}, u32[]{:S(2)}) collective-permute-start(bf16[272,512]{1,0:T(8,128)(2,1)S(1)} %get-tuple-element.60), channel_id=1, source_target_pairs={{0,4},{1,5},{2,6},{3,7},{4,8},{5,9},{6,10},{7,11},{8,12},{9,13},{1... | collective-permute-start | bytes 835592 | tf_op jit(solution)/shard_map/ppermute | solution.py:227
  121.3 56.9 %copy-start.9 = (bf16[2,256,512]{2,1,0:T(8,128)(2,1)S(1)}, bf16[2,256,512]{2,1,0:T(8,128)(2,1)}, u32[]{:S(2)}) copy-start(bf16[2,256,512]{2,1,0:T(8,128)(2,1)} %get-tuple-element.33) | copy-start | bytes 1572868
  121.3 18.7 %collective-permute-start.12 = (bf16[2,256,512]{2,1,0:T(8,128)(2,1)}, bf16[2,256,512]{2,1,0:T(8,128)(2,1)S(1)}, u32[]{:S(2)}, u32[]{:S(2)}) collective-permute-start(bf16[2,256,512]{2,1,0:T(8,128)(2,1)} %get-tuple-element.35), channel_id=1, source_target_pairs={{0,1},{1,2},{2,3},{3,0},{4,5},{5,6},{6,7},{7,4},{8,9},{9,10},{10,1... | collective-permute-start | bytes 1572872 | tf_op jit(solution)/shard_map/ppermute | solution.py:227
  127.3 15.4 %collective-permute-start.16 = (bf16[2,256,512]{2,1,0:T(8,128)(2,1)}, bf16[2,256,512]{2,1,0:T(8,128)(2,1)S(1)}, u32[]{:S(2)}, u32[]{:S(2)}) collective-permute-start(bf16[2,256,512]{2,1,0:T(8,128)(2,1)} %get-tuple-element.40), channel_id=1, source_target_pairs={{0,3},{1,0},{2,1},{3,2},{4,7},{5,4},{6,5},{7,6},{8,11},{9,8},{10,9... | collective-permute-start | bytes 1572872 | tf_op jit(solution)/shard_map/ppermute | solution.py:227
  127.3 34.1 %collective-permute-start.14 = (bf16[2,256,512]{2,1,0:T(8,128)(2,1)}, bf16[2,256,512]{2,1,0:T(8,128)(2,1)S(1)}, u32[]{:S(2)}, u32[]{:S(2)}) collective-permute-start(bf16[2,256,512]{2,1,0:T(8,128)(2,1)} %get-tuple-element.36), channel_id=1, source_target_pairs={{0,3},{1,0},{2,1},{3,2},{4,7},{5,4},{6,5},{7,6},{8,11},{9,8},{10,9... | collective-permute-start | bytes 1572872 | tf_op jit(solution)/shard_map/ppermute | solution.py:227
  127.3 51.9 %collective-permute-start.15 = (bf16[2,256,512]{2,1,0:T(8,128)(2,1)}, bf16[2,256,512]{2,1,0:T(8,128)(2,1)S(1)}, u32[]{:S(2)}, u32[]{:S(2)}) collective-permute-start(bf16[2,256,512]{2,1,0:T(8,128)(2,1)} %get-tuple-element.38), channel_id=1, source_target_pairs={{0,1},{1,2},{2,3},{3,0},{4,5},{5,6},{6,7},{7,4},{8,9},{9,10},{10,1... | collective-permute-start | bytes 1572872 | tf_op jit(solution)/shard_map/ppermute | solution.py:227
  129.4 28.6 %collective-permute-start.18 = (bf16[2,256,512]{2,1,0:T(8,128)(2,1)}, bf16[2,256,512]{2,1,0:T(8,128)(2,1)S(1)}, u32[]{:S(2)}, u32[]{:S(2)}) collective-permute-start(bf16[2,256,512]{2,1,0:T(8,128)(2,1)} %get-tuple-element.43), channel_id=1, source_target_pairs={{0,1},{3,0},{4,5},{5,6},{8,9},{9,10},{13,14},{16,17},{19,16},{20,2... | collective-permute-start | bytes 1572872 | tf_op jit(solution)/shard_map/ppermute | solution.py:227
  140.0 51.1 %collective-permute-start.20 = (bf16[2,256,512]{2,1,0:T(8,128)(2,1)}, bf16[2,256,512]{2,1,0:T(8,128)(2,1)S(1)}, u32[]{:S(2)}, u32[]{:S(2)}) collective-permute-start(bf16[2,256,512]{2,1,0:T(8,128)(2,1)} %get-tuple-element.44), channel_id=1, source_target_pairs={{2,1},{3,2},{4,7},{7,6},{8,11},{11,10},{12,15},{18,17},{19,18},{20... | collective-permute-start | bytes 1572872 | tf_op jit(solution)/shard_map/ppermute | solution.py:227
  142.7 16.4 %collective-permute-start.22 = (bf16[2,256,512]{2,1,0:T(8,128)(2,1)}, bf16[2,256,512]{2,1,0:T(8,128)(2,1)S(1)}, u32[]{:S(2)}, u32[]{:S(2)}) collective-permute-start(bf16[2,256,512]{2,1,0:T(8,128)(2,1)} %get-tuple-element.48), channel_id=1, source_target_pairs={{0,3},{4,7},{9,8},{13,12},{16,19},{20,23},{25,24},{29,28},{32,35},... | collective-permute-start | bytes 1572872 | tf_op jit(solution)/shard_map/ppermute | solution.py:227
  144.6 52.3 %copy-start.7 = (bf16[2,256,512]{2,1,0:T(8,128)(2,1)S(1)}, bf16[2,256,512]{2,1,0:T(8,128)(2,1)}, u32[]{:S(2)}) copy-start(bf16[2,256,512]{2,1,0:T(8,128)(2,1)} %get-tuple-element.41) | copy-start | bytes 1572868
  157.9 13.0 %collective-permute-start.13 = (bf16[2,256,512]{2,1,0:T(8,128)(2,1)S(1)}, bf16[2,256,512]{2,1,0:T(8,128)(2,1)S(1)}, u32[]{:S(2)}, u32[]{:S(2)}) collective-permute-start(bf16[2,256,512]{2,1,0:T(8,128)(2,1)S(1)} %add_convert_fusion.3), channel_id=1, source_target_pairs={{0,1},{1,2},{2,3},{3,0},{4,5},{5,6},{6,7},{7,4},{8,9},{9,10},{10,1... | collective-permute-start | bytes 1572872 | tf_op jit(solution)/shard_map/ppermute | solution.py:227
  159.1 29.1 %collective-permute-start.17 = (bf16[2,256,512]{2,1,0:T(8,128)(2,1)S(1)}, bf16[2,256,512]{2,1,0:T(8,128)(2,1)S(1)}, u32[]{:S(2)}, u32[]{:S(2)}) collective-permute-start(bf16[2,256,512]{2,1,0:T(8,128)(2,1)S(1)} %add_convert_fusion.2), channel_id=1, source_target_pairs={{0,3},{1,0},{2,1},{3,2},{4,7},{5,4},{6,5},{7,6},{8,11},{9,8},{10,9... | collective-permute-start | bytes 1572872 | tf_op jit(solution)/shard_map/ppermute | solution.py:227
  161.4 38.5 %collective-permute-start.21 = (bf16[2,256,512]{2,1,0:T(8,128)(2,1)S(1)}, bf16[2,256,512]{2,1,0:T(8,128)(2,1)S(1)}, u32[]{:S(2)}, u32[]{:S(2)}) collective-permute-start(bf16[2,256,512]{2,1,0:T(8,128)(2,1)S(1)} %copy-done.18), channel_id=1, source_target_pairs={{1,2},{5,6},{10,11},{14,15},{17,18},{21,22},{26,27},{30,31},{33,34... | collective-permute-start | bytes 1572872 | tf_op jit(solution)/shard_map/ppermute | solution.py:227
  170.9 26.0 %collective-permute-start.19 = (bf16[2,256,512]{2,1,0:T(8,128)(2,1)S(1)}, bf16[2,256,512]{2,1,0:T(8,128)(2,1)S(1)}, u32[]{:S(2)}, u32[]{:S(2)}) collective-permute-start(bf16[2,256,512]{2,1,0:T(8,128)(2,1)S(1)} %add_convert_fusion.1), channel_id=1, source_target_pairs={{0,1},{1,2},{5,6},{6,7},{9,10},{10,11},{14,15},{16,17},{17,18},{21... | collective-permute-start | bytes 1572872 | tf_op jit(solution)/shard_map/ppermute | solution.py:227
  179.2 20.7 %collective-permute-start.23 = (bf16[2,256,512]{2,1,0:T(8,128)(2,1)S(1)}, bf16[2,256,512]{2,1,0:T(8,128)(2,1)S(1)}, u32[]{:S(2)}, u32[]{:S(2)}) collective-permute-start(bf16[2,256,512]{2,1,0:T(8,128)(2,1)S(1)} %add_convert_fusion), channel_id=1, source_target_pairs={{3,2},{7,6},{8,11},{12,15},{19,18},{23,22},{24,27},{28,31},{35,34}... | collective-permute-start | bytes 1572872 | tf_op jit(solution)/shard_map/ppermute | solution.py:227
  188.2 14.6 %collective-permute-start.24 = (bf16[256,512]{1,0:T(8,128)(2,1)S(1)}, bf16[256,512]{1,0:T(8,128)(2,1)S(1)}, u32[]{:S(2)}, u32[]{:S(2)}) collective-permute-start(bf16[256,512]{1,0:T(8,128)(2,1)S(1)} %get-tuple-element.55), channel_id=1, source_target_pairs={{0,16},{1,17},{2,18},{3,19},{4,20},{5,21},{6,22},{7,23},{8,24},{9,... | collective-permute-start | bytes 786440 | tf_op jit(solution)/shard_map/ppermute | solution.py:294
  191.2 11.7 %collective-permute-start.25 = (bf16[256,512]{1,0:T(8,128)(2,1)S(1)}, bf16[256,512]{1,0:T(8,128)(2,1)S(1)}, u32[]{:S(2)}, u32[]{:S(2)}) collective-permute-start(bf16[256,512]{1,0:T(8,128)(2,1)S(1)} %get-tuple-element.53), channel_id=1, source_target_pairs={{0,16},{1,17},{2,18},{3,19},{4,20},{5,21},{6,22},{7,23},{8,24},{9,... | collective-permute-start | bytes 786440 | tf_op jit(solution)/shard_map/ppermute | solution.py:294
  198.0 8.6 %collective-permute-start.26 = (bf16[256,512]{1,0:T(8,128)(2,1)S(1)}, bf16[256,512]{1,0:T(8,128)(2,1)S(1)}, u32[]{:S(2)}, u32[]{:S(2)}) collective-permute-start(bf16[256,512]{1,0:T(8,128)(2,1)S(1)} %get-tuple-element.51), channel_id=1, source_target_pairs={{1,17},{2,18},{6,22},{7,23},{10,26},{11,27},{15,31},{17,33},{18,34... | collective-permute-start | bytes 786440 | tf_op jit(solution)/shard_map/ppermute | solution.py:294
  200.9 8.6 %collective-permute-start.27 = (bf16[256,512]{1,0:T(8,128)(2,1)S(1)}, bf16[256,512]{1,0:T(8,128)(2,1)S(1)}, u32[]{:S(2)}, u32[]{:S(2)}) collective-permute-start(bf16[256,512]{1,0:T(8,128)(2,1)S(1)} %get-tuple-element.49), channel_id=1, source_target_pairs={{2,18},{6,22},{11,27},{15,31},{18,34},{22,38},{27,43},{31,47},{34,... | collective-permute-start | bytes 786440 | tf_op jit(solution)/shard_map/ppermute | solution.py:294
  (16 other events, 295.7 us)
Sparse Core Ops, SparseCore 0:
  43.1 30.9 all-gather.2

commit v4 on v3

v4 whole, which is shorter than its diff:
```python
import functools

import jax
import jax.numpy as jnp
from jax import lax
from jax.experimental import pallas as pl
from jax.experimental.pallas import tpu as pltpu
from jax.sharding import PartitionSpec as P

EPW, CH = 8, 2
NZ, NX = 4, 4
SECS, ROWS = 16, 16
BB, KB = 256, 512
QUARTER = BB // NX
BF, F32 = jnp.bfloat16, jnp.float32
STEPS = (0, -1, 1, 2)
VMEM_BYTES = 56 * 1024 * 1024
HEAD = 16
BRA_CELLS = ((0, 0), (0, 1), (2, 1), (1, 0), (1, 1), (3, 1))
CELLS = [(b, j) for b in range(2) for j in range(CH)]


def charge(channel):
    klass = channel % 9
    return klass % 3 - 1, klass // 3 - 1


def live_at(r, b, j):
    to_b = b + charge(CH * r + j)[1]
    return jnp.where((to_b >= 0) & (to_b < 2), 1, 0)


COUNT = [sum(0 <= b + charge(CH * r + j)[1] < 2 for b, j in CELLS) for r in range(ROWS)]


def row_z(r, d):
    return (r // NX + d) % NZ * NX + r % NX


def row_x(r, d):
    return r // NX * NX + (r % NX + d) % NX


def packed_cells(r, a, ket_sizes, bra_sizes):
    places = [(jnp.int32(0), jnp.int32(0), jnp.int32(0)) for _ in range(4)]
    count = jnp.int32(0)
    for b, j in CELLS:
        out_a, out_b = charge(CH * r + j)
        live = live_at(r, b, j)
        at_a, at_b = a + out_a, jnp.clip(b + out_b, 0, 1)
        rows = jnp.where((at_a >= 0) & (at_a < SECS), bra_sizes[at_b, jnp.clip(at_a, 0, SECS - 1)], 0)
        cols = ket_sizes[b, a]
        for i in range(4):
            hit = (live == 1) & (count == i)
            places[i] = tuple(jnp.where(hit, new, old) for new, old in zip((2 * j + b, rows, cols), places[i]))
        count = count + live
    return places, count


def live_count(r):
    return sum(live_at(r, b, j) for b, j in CELLS)


def keep(rows, cols):
    row_at = lax.broadcasted_iota(jnp.int32, (BB, KB), 0)
    col_at = lax.broadcasted_iota(jnp.int32, (BB, KB), 1)
    return (row_at < rows) & (col_at < cols)


def prepare_kernel(place, ket_sizes, bra_sizes, entries, coeffs, env, first_out, second_out, third_out, moving):
    r, a = place[0], place[1]
    lane = lax.broadcasted_iota(jnp.int32, (HEAD, KB), 1)
    slot, field = lane // 8, lane % 8
    places, count = packed_cells(r, a, ket_sizes, bra_sizes)
    for i, (cell, rows, cols) in enumerate(places):
        target = (first_out, second_out, third_out, moving)[i]
        j, b = cell // 2, cell % 2
        head = jnp.zeros((HEAD, KB), F32)
        for n in range(EPW):
            part = jnp.where(field < 3, 0.0, coeffs[j, n])
            for f in range(3):
                part = jnp.where(field == f, entries[f, j, n].astype(F32), part)
            part = jnp.where(field == 7, (b + 1).astype(F32), part)
            head = jnp.where(slot == n, part, head)
        first = head.astype(BF).astype(F32)
        second = (head - first).astype(BF).astype(F32)
        last = head - first - second
        head = jnp.where(field == 4, second, jnp.where(field == 5, last, first))
        head = jnp.where(i < count, head, 0.0)
        target[:HEAD] = head.astype(BF)
        target[HEAD:] = jnp.where(keep(rows, cols), env[cell], jnp.zeros((BB, KB), BF))


def bra_kernel(place, bra, flipped, strip, strip_low, strip_high):
    r = place[0]
    lines = pl.ds(pl.multiple_of(r % NX * QUARTER, QUARTER), QUARTER)
    for n, (sp, to_b) in enumerate(BRA_CELLS):
        flipped[n] = bra[sp, to_b].T
        value = flipped[n, lines]
        strip[n] = value
        if n < 3:
            strip_low[n] = value
        else:
            strip_high[n - 3] = value


def unpack_kernel(place, ket_sizes, bra_sizes, *refs):
    here, above, out = refs[:4], refs[4:6], refs[6]
    out[...] = jnp.zeros_like(out)
    for i, (cell, rows, cols) in enumerate(packed_cells(place[0], place[1], ket_sizes, bra_sizes)[0]):

        @pl.when(rows > 0)
        def _(i=i, cell=cell, rows=rows, cols=cols):
            value = here[i][...] + above[i // 2][i % 2].astype(F32)
            out[cell] = jnp.where(keep(rows, cols), value, 0.0).astype(BF)


def terms_kernel(place, ket_sizes, ints, values, *refs):
    envs, across2b, ket_in, bra_own, rim0, rim1, rim2 = refs[:12], *refs[12:18]
    outs = refs[18:34]
    env_all, ket, bra_all, total, rounded, env_sem, ket_sem, bra_sem, out_sem = refs[34:]
    x = place[0] % NX
    copies = []
    for n in range(12):
        rows = BB if n < 11 else BB // 2
        copies.append(pltpu.make_async_copy(envs[n].at[pl.ds(HEAD, rows)], env_all.at[n, pl.ds(0, rows)], env_sem.at[n]))
    copies.append(pltpu.make_async_copy(across2b, env_all.at[11, pl.ds(BB // 2, BB // 2)], env_sem.at[12]))
    copies += [pltpu.make_async_copy(ket_in.at[s], ket.at[s], ket_sem.at[s]) for s in range(4)]
    copies.append(pltpu.make_async_copy(bra_own, bra_all.at[pl.ds(6, 6)], bra_sem.at[0]))
    y = NX - 1 - x
    for n, (ref, at, owner) in enumerate(((rim0, 0, x), (rim1, 0, x + 1 - 2 * (x % 2)), (rim2, 0, y), (rim2, 12, y + 1 - 2 * (y % 2)))):
        lines = pl.ds(pl.multiple_of(QUARTER * owner, QUARTER), QUARTER)
        for m, (first, count, to) in enumerate(((0, 3, 0), (3, 6, 12), (9, 3, 21))):
            copies.append(pltpu.make_async_copy(
                ref.at[pl.ds(at + first, count)], bra_all.at[pl.ds(to, count), lines], bra_sem.at[1 + 3 * n + m]
            ))
    for copy in copies:
        copy.start()

    r, a = place[0], place[1]
    my_z, my_x = r // NX, r % NX
    for d in range(4):
        for i in range(4):

            @pl.when(i < live_count(row_x(r, STEPS[d])))
            def _(at=8 * d + 2 * i):
                total[at] = jnp.zeros((BB, KB), F32)
                total[at + 1] = jnp.zeros((BB, KB), F32)

    for copy in copies:
        copy.wait()

    @pl.loop(0, 12 * EPW)
    def _(item):
        base = 64 * (item // EPW) + 8 * (item % EPW)
        out_w, s, code = ints[base], ints[base + 2], ints[base + 7]
        p_b, s_a = code - 1 + s // 2, s % 2
        out_r, out_j = out_w // CH, out_w % CH

        @pl.when((code > 0) & (out_w // (CH * NX) == my_z) & (p_b < 2) & (a + s_a < SECS))
        def _():
            q_b = code - 1

            @pl.when(live_at(out_r, p_b, out_j) == 1)
            def _():
                sp = ints[base + 1]
                value = values[base + 3] + values[base + 4] + values[base + 5]
                forward = (out_r % NX - my_x + NX) % NX
                slot = jnp.where(forward == 1, 2, jnp.where(forward == 3, 1, jnp.where(forward == 2, 3, 0)))
                out_a, out_b = charge(out_w)
                low = live_at(out_r, 0, 0)
                inside = low + live_at(out_r, 0, 1) + out_j * live_at(out_r, 1, 0)
                position = jnp.where(p_b == 0, out_j * low, inside)
                b_at = 6 * (s_a + out_a + 1) + 3 * (sp % 2) + p_b + out_b + sp // 2
                at = 8 * slot + 2 * position + s_a
                e_at = item // EPW
                to_size = ket_sizes[p_b, a + s_a]
                from_size = ket_sizes[q_b, a]
                for n in range(2):
                    cols = pl.ds(n * (KB // 2), KB // 2)

                    def run(depth, cols=cols):
                        half = jnp.dot(env_all[e_at, :, :depth], ket[s, q_b, :depth, cols], preferred_element_type=F32)
                        term = jnp.dot(bra_all[b_at], half.astype(BF), preferred_element_type=F32)
                        total[at, :, cols] = total[at, :, cols] + value * term

                    wide = to_size > n * (KB // 2)
                    pl.when(wide & (from_size > KB // 2))(functools.partial(run, KB))
                    pl.when(wide & (from_size <= KB // 2))(functools.partial(run, KB // 2))

    def stored(d, i):
        return pltpu.make_async_copy(rounded.at[4 * d + i], outs[4 * d + i], out_sem.at[4 * d + i])

    for d in (3, 2, 1, 0):
        for i in range(4):

            @pl.when(i < live_count(row_x(r, STEPS[d])))
            def _(d=d, i=i):
                for up in range(2):
                    rounded[4 * d + i, up] = total[8 * d + 2 * i + up].astype(BF)
                stored(d, i).start()

    for d in (3, 2, 1, 0):
        for i in range(4):

            @pl.when(i < live_count(row_x(r, STEPS[d])))
            def _(d=d, i=i):
                stored(d, i).wait()


def body(env_in, ket_mps, bra_mps, ket_sizes, bra_sizes, entries, coeffs):
    my_a = lax.axis_index("sec")
    r = lax.axis_index("row")
    place = jnp.stack([r, my_a])
    ket_flat, bra_flat = ket_sizes.T, bra_sizes.T

    smem = pl.BlockSpec(memory_space=pltpu.SMEM)
    vmem = pl.BlockSpec(memory_space=pltpu.VMEM)
    shape = jax.ShapeDtypeStruct
    pair = shape((2, BB, KB), BF)
    params = pltpu.CompilerParams(vmem_limit_bytes=VMEM_BYTES)
    payload = shape((HEAD + BB, KB), BF)
    own0, own1, own2, moving = pl.pallas_call(
        prepare_kernel,
        in_specs=[smem] * 5 + [vmem],
        out_specs=[vmem] * 4,
        out_shape=[payload] * 4,
        compiler_params=params,
    )(place, ket_flat, bra_flat, entries.transpose(2, 0, 1), coeffs, env_in.reshape(4, BB, KB))

    same = lambda n: n
    z_up, z_down = (lambda n: row_z(n, 1)), (lambda n: row_z(n, -1))
    x_up, x_down, x_far = (lambda n: row_x(n, 1)), (lambda n: row_x(n, -1)), (lambda n: row_x(n, 2))

    def sent(value, move, owner, rows):
        return lax.ppermute(value, "row", [(n, move(n)) for n in range(ROWS) if owner(n) in rows])

    everyone = set(range(ROWS))
    full = [n for n in range(ROWS) if COUNT[n] == 4]
    takers, lent = set(), []
    for n in full:
        taker = next(m for m in (row_x(n, 1), row_x(n, -1)) if COUNT[m] == 2 and m not in takers)
        takers.add(taker)
        lent.append((n, taker))
    three = {n for n in range(ROWS) if COUNT[n] > 2} | takers
    behind0 = sent(own0, z_up, same, everyone)
    ahead1 = sent(own1, z_down, same, everyone)
    own2 = own2 + lax.ppermute(moving, "row", lent)
    behind1 = sent(own1, z_up, same, everyone)
    ahead0 = sent(own0, z_down, same, everyone)
    behind2 = sent(own2, z_up, same, three)
    ahead2 = sent(own2, z_down, same, three)
    across0 = sent(behind0, z_up, z_down, everyone)
    across1 = sent(ahead1, z_down, z_up, everyone)
    across2a = sent(behind2[: HEAD + BB // 2], z_up, z_down, three)
    across2b = sent(ahead2[HEAD + BB // 2 :], z_down, z_up, three)

    bra_in = lax.optimization_barrier((bra_mps, behind0, ahead1))[0]
    bra_own, strip, strip_low, strip_high = pl.pallas_call(
        bra_kernel,
        in_specs=[smem, vmem],
        out_specs=[vmem] * 4,
        out_shape=[
            shape((6, BB, BB), BF),
            shape((6, QUARTER, BB), BF),
            shape((3, QUARTER, BB), BF),
            shape((3, QUARTER, BB), BF),
        ],
        compiler_params=params,
    )(place, bra_in[:, 0])
    up = lambda n: [(i, i + n) for i in range(SECS - n)]
    down = lambda n: [(i + n, i) for i in range(SECS - n)]
    rim0 = jnp.concatenate([
        lax.ppermute(strip_low, "sec", up(1)),
        lax.ppermute(strip, "sec", down(1)),
        lax.ppermute(strip_high, "sec", down(2)),
    ])
    rim1 = lax.ppermute(rim0, "row", [(n, n ^ 1) for n in range(ROWS)])
    rim2 = lax.ppermute(jnp.concatenate([rim0, rim1]), "row", [(n, n ^ 3) for n in range(ROWS)])

    envs = [own0, own1, own2, behind0, behind1, behind2, ahead0, ahead1, ahead2, across0, across1, across2a]
    values = jnp.concatenate([part[0, :64] for part in envs]).astype(F32)

    hbm = pl.BlockSpec(memory_space=pl.ANY)
    sums = pl.pallas_call(
        terms_kernel,
        in_specs=[smem] * 4 + [hbm] * 18,
        out_specs=[hbm] * 16,
        out_shape=[pair] * 16,
        scratch_shapes=[
            pltpu.VMEM((12, BB, KB), BF),
            pltpu.VMEM((4, 2, KB, KB), BF),
            pltpu.VMEM((24, BB, BB), BF),
            pltpu.VMEM((32, BB, KB), F32),
            pltpu.VMEM((16, 2, BB, KB), BF),
            pltpu.SemaphoreType.DMA((13,)),
            pltpu.SemaphoreType.DMA((4,)),
            pltpu.SemaphoreType.DMA((13,)),
            pltpu.SemaphoreType.DMA((16,)),
        ],
        compiler_params=params,
    )(place, ket_flat, values.astype(jnp.int32), values, *envs, across2b, ket_mps[:, 0], bra_own, rim0, rim1, rim2)
    mine, left, right, far = sums[:4], sums[4:8], sums[8:12], sums[12:]

    def added(*parts):
        return functools.reduce(jnp.add, [part.astype(F32) for part in parts])

    def moved(value, move, owner, i):
        return sent(value, move, owner, {n for n in range(ROWS) if COUNT[n] > i})

    far_up = {i: moved(far[i], x_up, x_far, i) for i in (0, 2)}
    far_down = {i: moved(far[i], x_down, x_far, i) for i in (1, 3)}
    from_left = {i: moved(right[i], x_up, x_up, i) for i in (1, 3)}
    from_right = {i: moved(left[i], x_down, x_down, i) for i in (0, 2)}
    for i in (0, 2):
        from_left[i] = moved(added(right[i], far_up[i]).astype(BF), x_up, x_up, i)
    for i in (1, 3):
        from_right[i] = moved(added(left[i], far_down[i]).astype(BF), x_down, x_down, i)

    here = [added(mine[i][0], from_left[i][0], from_right[i][0]) for i in range(4)]
    raised = [added(mine[i][1], from_left[i][1], from_right[i][1]).astype(BF) for i in range(4)]
    above = []
    for i in (0, 2):
        pairs = [(a * ROWS + n, (a + 1) * ROWS + n) for a in range(SECS - 1) for n in range(ROWS) if COUNT[n] > i]
        above.append(lax.ppermute(jnp.stack(raised[i : i + 2]), ("sec", "row"), pairs))

    out = pl.pallas_call(
        unpack_kernel,
        in_specs=[smem] * 3 + [vmem] * 6,
        out_specs=vmem,
        out_shape=shape((4, BB, KB), BF),
        compiler_params=params,
    )(place, ket_flat, bra_flat, *here, *above)
    return out.reshape(CH, 1, 2, BB, KB)


def solution(mesh):
    placed = (
        P("row", "sec", None, None, None),
        P(None, "sec", None, None, None),
        P(None, "sec", None, None, None),
        P(),
        P(),
        P("row", None, None),
        P("row", None),
    )
    return jax.shard_map(
        body,
        mesh=mesh,
        in_specs=placed,
        out_specs=P("row", "sec", None, None, None),
        check_vma=False,
    )
```

time: 218 us -> 198 us (0.908); the launches traced: 220 us -> 196 us
  waiting for transfers between devices: 93.1 us -> 77.1 us
  between operations: 13.9 us -> 0.59 us
  Pallas kernels: 34.9 us -> 39.6 us
  starting transfers between devices: 59.4 us -> 63 us
  local copies, waits for them, and re-layouts: 8.12 us -> 5.32 us
    ppermute x20 -> x22, waiting for transfers between devices: 82.3 us -> 50.8 us  [sent(): lax.ppermute(value, 'row', [(n, move(n)) for n in range(ROWS) if owner(n)...]
    ppermute x4, waiting for transfers between devices: 6.62 us -> 17.7 us  [the longest x2 9.45 us: body(): lax.ppermute(jnp.stack(raised[i:i + 2]), ('sec', 'row'), pairs)]
    ppermute x1, waiting for transfers between devices: 0.01 us -> 8.56 us  [body(): lax.ppermute(strip, 'sec', down(1))]
    pallas_call x3 -> x4, Pallas kernels: 34.9 us -> 39.6 us  [the longest x1 31.2 us: body(): pl.pallas_call(terms_kernel, in_specs=[smem] * 4 + [hbm] * 18, out_specs=...]
    ppermute x1, waiting for transfers between devices: 4.08 us -> 0.01 us  [body(): own2 = own2 + lax.ppermute(moving, 'row', lent)]
    ppermute x4, starting transfers between devices: 7.64 us -> 11 us  [the longest x1 7.05 us: body(): rim1 = lax.ppermute(rim0, 'row', [(n, n ^ 1) for n in range(ROWS)])]
    reshape x4 -> x0, local copies, waits for them, and re-layouts: 3.2 us -> none  [the longest x1 1.33 us: body(): coeffs.reshape(-1)]
    ppermute x20 -> x22, starting transfers between devices: 40 us -> 39.5 us  [sent(): lax.ppermute(value, 'row', [(n, move(n)) for n in range(ROWS) if owner(n)...]
  transfers between devices with their start and end apart: 29 -> 30, of which waited for: 11 -> 11; matrix products, arithmetic and copies ran while one was open for 5% -> 6% of each run, Pallas kernels for 0% -> 1%
where the time goes in v4:
time: 198 us; the launch traced here: 196 us
  waiting for transfers between devices  77.1 us (39%)
  starting transfers between devices  63 us (32%)
  Pallas kernels  39.6 us (20%)
  other arithmetic  10.3 us (5%)
  local copies, waits for them, and re-layouts  5.32 us (3%)
    ppermute x22, waiting for transfers between devices, sent(): lax.ppermute(value, 'row', [(n, move(n)) for n in range(ROWS) if owner(n)...  50.8 us
    ppermute x22, starting transfers between devices, sent(): lax.ppermute(value, 'row', [(n, move(n)) for n in range(ROWS) if owner(n)...  39.5 us
    pallas_call x1, Pallas kernels, body(): pl.pallas_call(terms_kernel, in_specs=[smem] * 4 + [hbm] * 18, out_specs=...  31.2 us
    ppermute x2, waiting for transfers between devices, body(): lax.ppermute(jnp.stack(raised[i:i + 2]), ('sec', 'row'), pairs)  9.45 us
    ppermute x1, waiting for transfers between devices, body(): lax.ppermute(strip, 'sec', down(1))  8.56 us
    ppermute x1, waiting for transfers between devices, body(): lax.ppermute(jnp.concatenate([rim0, rim1]), 'row', [(n, n ^ 3) for n in r...  8.22 us
    ppermute x1, starting transfers between devices, body(): rim1 = lax.ppermute(rim0, 'row', [(n, n ^ 1) for n in range(ROWS)])  7.05 us
    ppermute x1, starting transfers between devices, body(): lax.ppermute(strip_high, 'sec', down(2))  4.82 us
  transfers between devices with their start and end apart: 30, of which 11 were waited for; matrix products, arithmetic and copies ran while one was open for 6% of the time, Pallas kernels for 1%

profile of v4, /device:TPU:92, one launch (start us, length us, event | category | flops | bytes accessed | tf_op | source)
XLA Modules:
  0.0 195.9 jit_solution(7514384915651809939)
XLA Ops:
  0.7 2.6 %shard_map.73 = (bf16[272,512]{1,0:T(8,128)(2,1)}, bf16[272,512]{1,0:T(8,128)(2,1)}, bf16[272,512]{1,0:T(8,128)(2,1)}, bf16[272,512]{1,0:T(8,128)(2,1)}) custom-call(s32[2]{0:T(128)} %pad_add_fusion.place, s32[2,16]{1,0:T(2,128)} %bitcast.46, s32[2,16]{1,0:T(2,128)} %bitcast.49, s32[3,2,8]{2,1,0:T(2,128)} %bitcast.51, f32[2,8]{1,0:T(2,128)} %coeffs.1, ...), custom_call_target="tpu_custom_call" | custom-call | tf_op jit(solution)/shard_map/pallas_call | solution.py:223
  3.2 2.4 %collective-permute-start = (bf16[272,512]{1,0:T(8,128)(2,1)}, bf16[272,512]{1,0:T(8,128)(2,1)S(1)}, u32[]{:S(2)}, u32[]{:S(2)}) collective-permute-start(bf16[272,512]{1,0:T(8,128)(2,1)} %get-tuple-element.33), channel_id=1, source_target_pairs={{2,3},{6,5},{11,8},{15,12},{18,19},{22,21},{27,24},{31,28},{34,35}... | collective-permute-start | bytes 835592 | tf_op jit(solution)/shard_map/ppermute | solution.py:248
  6.1 3.8 %collective-permute-start.1 = (bf16[272,512]{1,0:T(8,128)(2,1)}, bf16[272,512]{1,0:T(8,128)(2,1)S(1)}, u32[]{:S(2)}, u32[]{:S(2)}) collective-permute-start(bf16[272,512]{1,0:T(8,128)(2,1)} %get-tuple-element.30.refs_0_), channel_id=1, source_target_pairs={{0,4},{1,5},{2,6},{3,7},{4,8},{5,9},{6,10},{7,11},{8,12},{9,13},{1... | collective-permute-start | bytes 835592 | tf_op jit(solution)/shard_map/ppermute | solution.py:236
  9.9 4.1 %collective-permute-start.2 = (bf16[272,512]{1,0:T(8,128)(2,1)}, bf16[272,512]{1,0:T(8,128)(2,1)S(1)}, u32[]{:S(2)}, u32[]{:S(2)}) collective-permute-start(bf16[272,512]{1,0:T(8,128)(2,1)} %get-tuple-element.31.refs_1_), channel_id=1, source_target_pairs={{0,4},{1,5},{2,6},{3,7},{4,8},{5,9},{6,10},{7,11},{8,12},{9,13},{1... | collective-permute-start | bytes 835592 | tf_op jit(solution)/shard_map/ppermute | solution.py:236
  15.8 2.0 %collective-permute-start.6 = (bf16[272,512]{1,0:T(8,128)(2,1)S(1)}, bf16[272,512]{1,0:T(8,128)(2,1)S(1)}, u32[]{:S(2)}, u32[]{:S(2)}) collective-permute-start(bf16[272,512]{1,0:T(8,128)(2,1)S(1)} %add.83.refs_2_), channel_id=1, source_target_pairs={{1,13},{2,14},{3,15},{5,1},{6,2},{7,3},{8,4},{10,6},{11,7},{12,8},... | collective-permute-start | bytes 835592 | tf_op jit(solution)/shard_map/ppermute | solution.py:236
  18.4 6.0 %collective-permute-start.3 = (bf16[272,512]{1,0:T(8,128)(2,1)S(1)}, bf16[272,512]{1,0:T(8,128)(2,1)S(1)}, u32[]{:S(2)}, u32[]{:S(2)}) collective-permute-start(bf16[272,512]{1,0:T(8,128)(2,1)S(1)} %add.83.refs_2_), channel_id=1, source_target_pairs={{1,5},{2,6},{3,7},{5,9},{6,10},{7,11},{8,12},{10,14},{11,15},{12,0... | collective-permute-start | bytes 835592 | tf_op jit(solution)/shard_map/ppermute | solution.py:236
  24.4 11.4 %collective-permute-done.5.refs_7_ = bf16[272,512]{1,0:T(8,128)(2,1)S(1)} collective-permute-done((bf16[272,512]{1,0:T(8,128)(2,1)}, bf16[272,512]{1,0:T(8,128)(2,1)S(1)}, u32[]{:S(2)}, u32[]{:S(2)}) %collective-permute-start.5) | collective-permute-done | bytes 278560 | tf_op jit(solution)/shard_map/ppermute | solution.py:236
  35.7 2.6 %shard_map.74 = (bf16[6,256,256]{2,1,0:T(8,128)(2,1)}, bf16[6,64,256]{2,1,0:T(8,128)(2,1)}, bf16[3,64,256]{2,1,0:T(8,128)(2,1)}, bf16[3,64,256]{2,1,0:T(8,128)(2,1)}) custom-call(s32[2]{0:T(128)} %pad_add_fusion.place, bf16[4,2,256,256]{3,2,1,0:T(8,128)(2,1)} %bitcast.45), custom_call_target="tpu_custom_call" | custom-call | tf_op jit(solution)/shard_map/pallas_call | solution.py:259
  38.3 1.9 collective-permute-start.11
  40.3 4.8 %collective-permute-start.13 = (bf16[3,64,256]{2,1,0:T(8,128)(2,1)}, bf16[3,64,256]{2,1,0:T(8,128)(2,1)S(1)}, u32[]{:S(2)}, u32[]{:S(2)}) collective-permute-start(bf16[3,64,256]{2,1,0:T(8,128)(2,1)} %get-tuple-element.38), channel_id=1, source_target_pairs={{32,0},{48,16},{64,32},{80,48},{96,64},{112,80},{128,96},{144,112}... | collective-permute-start | bytes 294920 | tf_op jit(solution)/shard_map/ppermute | solution.py:276
  45.1 3.4 %collective-permute-start.12 = (bf16[6,64,256]{2,1,0:T(8,128)(2,1)}, bf16[6,64,256]{2,1,0:T(8,128)(2,1)S(1)}, u32[]{:S(2)}, u32[]{:S(2)}) collective-permute-start(bf16[6,64,256]{2,1,0:T(8,128)(2,1)} %get-tuple-element.37), channel_id=1, source_target_pairs={{16,0},{32,16},{48,32},{64,48},{80,64},{96,80},{112,96},{128,112},... | collective-permute-start | bytes 589832 | tf_op jit(solution)/shard_map/ppermute | solution.py:275
  48.5 2.3 %collective-permute-start.7 = (bf16[272,512]{1,0:T(8,128)(2,1)S(1)}, bf16[272,512]{1,0:T(8,128)(2,1)S(1)}, u32[]{:S(2)}, u32[]{:S(2)}) collective-permute-start(bf16[272,512]{1,0:T(8,128)(2,1)S(1)} %collective-permute-done.1.refs_3_), channel_id=1, source_target_pairs={{0,4},{1,5},{2,6},{3,7},{4,8},{5,9},{6,10},{7,11},{8,12},{9,13},{1... | collective-permute-start | bytes 835592 | tf_op jit(solution)/shard_map/ppermute | solution.py:236
  50.8 8.6 %collective-permute-done.12 = bf16[6,64,256]{2,1,0:T(8,128)(2,1)S(1)} collective-permute-done((bf16[6,64,256]{2,1,0:T(8,128)(2,1)}, bf16[6,64,256]{2,1,0:T(8,128)(2,1)S(1)}, u32[]{:S(2)}, u32[]{:S(2)}) %collective-permute-start.12) | collective-permute-done | bytes 196640 | tf_op jit(solution)/shard_map/ppermute | solution.py:275
  59.5 7.0 %collective-permute-start.14 = (bf16[12,64,256]{2,1,0:T(8,128)(2,1)S(1)}, bf16[12,64,256]{2,1,0:T(8,128)(2,1)S(1)}, u32[]{:S(2)}, u32[]{:S(2)}) collective-permute-start(bf16[12,64,256]{2,1,0:T(8,128)(2,1)S(1)} %constant_dynamic-update-slice_fusion.refs_15_), channel_id=1, source_target_pairs={{0,1},{1,0},{2,3},{3,2},{4,5},{5,4},{6,7},{7,6},{8,9},{9,8},{10,11... | collective-permute-start | bytes 1179656 | tf_op jit(solution)/shard_map/ppermute | solution.py:278
  67.2 7.5 %collective-permute-start.10 = (bf16[128,512]{1,0:T(8,128)(2,1)}, bf16[128,512]{1,0:T(8,128)(2,1)}, u32[]{:S(2)}, u32[]{:S(2)}) collective-permute-start(bf16[128,512]{1,0:T(8,128)(2,1)} %slice.163), channel_id=1, source_target_pairs={{1,13},{2,14},{3,15},{4,0},{6,2},{7,3},{8,4},{11,7},{13,9},{14,10}... | collective-permute-start | bytes 393224 | tf_op jit(solution)/shard_map/ppermute | solution.py:236
  74.7 1.3 collective-permute-start.9
  80.0 8.2 %collective-permute-done.15.refs_17_ = bf16[24,64,256]{2,1,0:T(8,128)(2,1)S(1)} collective-permute-done((bf16[24,64,256]{2,1,0:T(8,128)(2,1)S(1)}, bf16[24,64,256]{2,1,0:T(8,128)(2,1)S(1)}, u32[]{:S(2)}, u32[]{:S(2)}) %collective-permute-start.15) | collective-permute-done | bytes 786464 | tf_op jit(solution)/shard_map/ppermute | solution.py:279
  89.1 31.2 %shard_map.75 = (bf16[2,256,512]{2,1,0:T(8,128)(2,1)}, bf16[2,256,512]{2,1,0:T(8,128)(2,1)}, bf16[2,256,512]{2,1,0:T(8,128)(2,1)}, bf16[2,256,512]{2,1,0:T(8,128...) custom-call(s32[2]{0:T(128)} %pad_add_fusion.place, ...), custom_call_target="tpu_custom_call" | custom-call | tf_op jit(solution)/shard_map/pallas_call | solution.py:285
  120.5 2.0 %collective-permute-start.20 = (bf16[2,256,512]{2,1,0:T(8,128)(2,1)}, bf16[2,256,512]{2,1,0:T(8,128)(2,1)S(1)}, u32[]{:S(2)}, u32[]{:S(2)}) collective-permute-start(bf16[2,256,512]{2,1,0:T(8,128)(2,1)} %get-tuple-element.46), channel_id=1, source_target_pairs={{0,3},{1,0},{2,1},{3,2},{4,7},{5,4},{6,5},{7,6},{8,11},{9,8},{10,9... | collective-permute-start | bytes 1572872 | tf_op jit(solution)/shard_map/ppermute | solution.py:236
  122.5 2.0 %collective-permute-start.19 = (bf16[2,256,512]{2,1,0:T(8,128)(2,1)}, bf16[2,256,512]{2,1,0:T(8,128)(2,1)S(1)}, u32[]{:S(2)}, u32[]{:S(2)}) collective-permute-start(bf16[2,256,512]{2,1,0:T(8,128)(2,1)} %get-tuple-element.44), channel_id=1, source_target_pairs={{0,1},{1,2},{2,3},{3,0},{4,5},{5,6},{6,7},{7,4},{8,9},{9,10},{10,1... | collective-permute-start | bytes 1572872 | tf_op jit(solution)/shard_map/ppermute | solution.py:236
  125.8 9.7 %collective-permute-done.16 = bf16[2,256,512]{2,1,0:T(8,128)(2,1)S(1)} collective-permute-done((bf16[2,256,512]{2,1,0:T(8,128)(2,1)}, bf16[2,256,512]{2,1,0:T(8,128)(2,1)S(1)}, u32[]{:S(2)}, u32[]{:S(2)}) %collective-permute-start.16) | collective-permute-done | bytes 524320 | tf_op jit(solution)/shard_map/ppermute | solution.py:236
  138.7 19.0 %collective-permute-done.22 = bf16[2,256,512]{2,1,0:T(8,128)(2,1)S(1)} collective-permute-done((bf16[2,256,512]{2,1,0:T(8,128)(2,1)}, bf16[2,256,512]{2,1,0:T(8,128)(2,1)S(1)}, u32[]{:S(2)}, u32[]{:S(2)}) %collective-permute-start.22) | collective-permute-done | bytes 524320 | tf_op jit(solution)/shard_map/ppermute | solution.py:236
  159.0 1.3 collective-permute-start.24
  160.5 1.4 collective-permute-start.25
  162.0 3.4 %collective-permute-done.17 = bf16[2,256,512]{2,1,0:T(8,128)(2,1)S(1)} collective-permute-done((bf16[2,256,512]{2,1,0:T(8,128)(2,1)S(1)}, bf16[2,256,512]{2,1,0:T(8,128)(2,1)S(1)}, u32[]{:S(2)}, u32[]{:S(2)}) %collective-permute-start.17) | collective-permute-done | bytes 524320 | tf_op jit(solution)/shard_map/ppermute | solution.py:236
  165.4 1.9 collective-permute-start.23
  168.3 1.3 collective-permute-start.27
  170.7 1.9 collective-permute-start.28
  172.6 4.7 %collective-permute-done.23 = bf16[2,256,512]{2,1,0:T(8,128)(2,1)S(1)} collective-permute-done((bf16[2,256,512]{2,1,0:T(8,128)(2,1)S(1)}, bf16[2,256,512]{2,1,0:T(8,128)(2,1)S(1)}, u32[]{:S(2)}, u32[]{:S(2)}) %collective-permute-start.23) | collective-permute-done | bytes 524320 | tf_op jit(solution)/shard_map/ppermute | solution.py:236
  180.4 1.9 collective-permute-start.29
  182.4 9.4 %collective-permute-done.29.refs_5_ = bf16[2,256,512]{2,1,0:T(8,128)(2,1)S(1)} collective-permute-done((bf16[2,256,512]{2,1,0:T(8,128)(2,1)S(1)}, bf16[2,256,512]{2,1,0:T(8,128)(2,1)S(1)}, u32[]{:S(2)}, u32[]{:S(2)}) %collective-permute-start.29) | collective-permute-done | bytes 524320 | tf_op jit(solution)/shard_map/ppermute | solution.py:325
  192.6 3.2 %shard_map.76 = bf16[4,256,512]{2,1,0:T(8,128)(2,1)} custom-call(s32[2]{0:T(128)} %pad_add_fusion.place, s32[2,16]{1,0:T(2,128)} %bitcast.48, s32[2,16]{1,0:T(2,128)} %bitcast.50, f32[256,512]{1,0:T(8,128)} %get-tuple-element.60.refs_0_, f32[256,512]{1,0:T(8,128)} %get-tuple-element.62.refs_1_, f32[256,512]{1,0:T(8,128)} %get-tuple-element.56.refs_2_, ...), custom_call_target="tpu_custom_call" | custom-call | tf_op jit(solution)/shard_map/pallas_call | solution.py:327
  (107 shorter events, 20.9 us)
Async XLA Ops:
  3.2 11.5 %collective-permute-start = (bf16[272,512]{1,0:T(8,128)(2,1)}, bf16[272,512]{1,0:T(8,128)(2,1)S(1)}, u32[]{:S(2)}, u32[]{:S(2)}) collective-permute-start(bf16[272,512]{1,0:T(8,128)(2,1)} %get-tuple-element.33), channel_id=1, source_target_pairs={{2,3},{6,5},{11,8},{15,12},{18,19},{22,21},{27,24},{31,28},{34,35}... | collective-permute-start | bytes 835592 | tf_op jit(solution)/shard_map/ppermute | solution.py:248
  5.7 34.6 %collective-permute-start.4 = (bf16[272,512]{1,0:T(8,128)(2,1)}, bf16[272,512]{1,0:T(8,128)(2,1)S(1)}, u32[]{:S(2)}, u32[]{:S(2)}) collective-permute-start(bf16[272,512]{1,0:T(8,128)(2,1)} %get-tuple-element.30.refs_0_), channel_id=1, source_target_pairs={{0,12},{1,13},{2,14},{3,15},{4,0},{5,1},{6,2},{7,3},{8,4},{9,5},{1... | collective-permute-start | bytes 835592 | tf_op jit(solution)/shard_map/ppermute | solution.py:236
  6.1 12.3 %collective-permute-start.1 = (bf16[272,512]{1,0:T(8,128)(2,1)}, bf16[272,512]{1,0:T(8,128)(2,1)S(1)}, u32[]{:S(2)}, u32[]{:S(2)}) collective-permute-start(bf16[272,512]{1,0:T(8,128)(2,1)} %get-tuple-element.30.refs_0_), channel_id=1, source_target_pairs={{0,4},{1,5},{2,6},{3,7},{4,8},{5,9},{6,10},{7,11},{8,12},{9,13},{1... | collective-permute-start | bytes 835592 | tf_op jit(solution)/shard_map/ppermute | solution.py:236
  9.9 25.8 %collective-permute-start.5 = (bf16[272,512]{1,0:T(8,128)(2,1)}, bf16[272,512]{1,0:T(8,128)(2,1)S(1)}, u32[]{:S(2)}, u32[]{:S(2)}) collective-permute-start(bf16[272,512]{1,0:T(8,128)(2,1)} %get-tuple-element.31.refs_1_), channel_id=1, source_target_pairs={{0,12},{1,13},{2,14},{3,15},{4,0},{5,1},{6,2},{7,3},{8,4},{9,5},{1... | collective-permute-start | bytes 835592 | tf_op jit(solution)/shard_map/ppermute | solution.py:236
  9.9 35.2 %collective-permute-start.2 = (bf16[272,512]{1,0:T(8,128)(2,1)}, bf16[272,512]{1,0:T(8,128)(2,1)S(1)}, u32[]{:S(2)}, u32[]{:S(2)}) collective-permute-start(bf16[272,512]{1,0:T(8,128)(2,1)} %get-tuple-element.31.refs_1_), channel_id=1, source_target_pairs={{0,4},{1,5},{2,6},{3,7},{4,8},{5,9},{6,10},{7,11},{8,12},{9,13},{1... | collective-permute-start | bytes 835592 | tf_op jit(solution)/shard_map/ppermute | solution.py:236
  15.8 72.4 %copy-start.1 = (bf16[272,512]{1,0:T(8,128)(2,1)}, bf16[272,512]{1,0:T(8,128)(2,1)S(1)}, u32[]{:S(2)}) copy-start(bf16[272,512]{1,0:T(8,128)(2,1)S(1)} %add.83.refs_2_) | copy-start | bytes 835588
  15.8 50.7 %collective-permute-start.6 = (bf16[272,512]{1,0:T(8,128)(2,1)S(1)}, bf16[272,512]{1,0:T(8,128)(2,1)S(1)}, u32[]{:S(2)}, u32[]{:S(2)}) collective-permute-start(bf16[272,512]{1,0:T(8,128)(2,1)S(1)} %add.83.refs_2_), channel_id=1, source_target_pairs={{1,13},{2,14},{3,15},{5,1},{6,2},{7,3},{8,4},{10,6},{11,7},{12,8},... | collective-permute-start | bytes 835592 | tf_op jit(solution)/shard_map/ppermute | solution.py:236
  18.3 57.9 %copy-start.14 = (bf16[272,512]{1,0:T(8,128)(2,1)}, bf16[272,512]{1,0:T(8,128)(2,1)S(1)}, u32[]{:S(2)}) copy-start(bf16[272,512]{1,0:T(8,128)(2,1)S(1)} %collective-permute-done.1.refs_3_) | copy-start | bytes 835588
  18.4 56.3 %collective-permute-start.3 = (bf16[272,512]{1,0:T(8,128)(2,1)S(1)}, bf16[272,512]{1,0:T(8,128)(2,1)S(1)}, u32[]{:S(2)}, u32[]{:S(2)}) collective-permute-start(bf16[272,512]{1,0:T(8,128)(2,1)S(1)} %add.83.refs_2_), channel_id=1, source_target_pairs={{1,5},{2,6},{3,7},{5,9},{6,10},{7,11},{8,12},{10,14},{11,15},{12,0... | collective-permute-start | bytes 835592 | tf_op jit(solution)/shard_map/ppermute | solution.py:236
  38.3 10.2 %collective-permute-start.11 = (bf16[3,64,256]{2,1,0:T(8,128)(2,1)}, bf16[3,64,256]{2,1,0:T(8,128)(2,1)S(1)}, u32[]{:S(2)}, u32[]{:S(2)}) collective-permute-start(bf16[3,64,256]{2,1,0:T(8,128)(2,1)} %get-tuple-element.36), channel_id=1, source_target_pairs={{0,16},{16,32},{32,48},{48,64},{64,80},{80,96},{96,112},{112,128},... | collective-permute-start | bytes 294920 | tf_op jit(solution)/shard_map/ppermute | solution.py:274
  40.3 19.2 %collective-permute-start.13 = (bf16[3,64,256]{2,1,0:T(8,128)(2,1)}, bf16[3,64,256]{2,1,0:T(8,128)(2,1)S(1)}, u32[]{:S(2)}, u32[]{:S(2)}) collective-permute-start(bf16[3,64,256]{2,1,0:T(8,128)(2,1)} %get-tuple-element.38), channel_id=1, source_target_pairs={{32,0},{48,16},{64,32},{80,48},{96,64},{112,80},{128,96},{144,112}... | collective-permute-start | bytes 294920 | tf_op jit(solution)/shard_map/ppermute | solution.py:276
  45.1 14.3 %collective-permute-start.12 = (bf16[6,64,256]{2,1,0:T(8,128)(2,1)}, bf16[6,64,256]{2,1,0:T(8,128)(2,1)S(1)}, u32[]{:S(2)}, u32[]{:S(2)}) collective-permute-start(bf16[6,64,256]{2,1,0:T(8,128)(2,1)} %get-tuple-element.37), channel_id=1, source_target_pairs={{16,0},{32,16},{48,32},{64,48},{80,64},{96,80},{112,96},{128,112},... | collective-permute-start | bytes 589832 | tf_op jit(solution)/shard_map/ppermute | solution.py:275
  48.5 27.7 %collective-permute-start.7 = (bf16[272,512]{1,0:T(8,128)(2,1)S(1)}, bf16[272,512]{1,0:T(8,128)(2,1)S(1)}, u32[]{:S(2)}, u32[]{:S(2)}) collective-permute-start(bf16[272,512]{1,0:T(8,128)(2,1)S(1)} %collective-permute-done.1.refs_3_), channel_id=1, source_target_pairs={{0,4},{1,5},{2,6},{3,7},{4,8},{5,9},{6,10},{7,11},{8,12},{9,13},{1... | collective-permute-start | bytes 835592 | tf_op jit(solution)/shard_map/ppermute | solution.py:236
  59.4 16.9 %collective-permute-start.8 = (bf16[272,512]{1,0:T(8,128)(2,1)S(1)}, bf16[272,512]{1,0:T(8,128)(2,1)S(1)}, u32[]{:S(2)}, u32[]{:S(2)}) collective-permute-start(bf16[272,512]{1,0:T(8,128)(2,1)S(1)} %collective-permute-done.5.refs_7_), channel_id=1, source_target_pairs={{0,12},{1,13},{2,14},{3,15},{4,0},{5,1},{6,2},{7,3},{8,4},{9,5},{1... | collective-permute-start | bytes 835592 | tf_op jit(solution)/shard_map/ppermute | solution.py:236
  59.5 16.6 %collective-permute-start.14 = (bf16[12,64,256]{2,1,0:T(8,128)(2,1)S(1)}, bf16[12,64,256]{2,1,0:T(8,128)(2,1)S(1)}, u32[]{:S(2)}, u32[]{:S(2)}) collective-permute-start(bf16[12,64,256]{2,1,0:T(8,128)(2,1)S(1)} %constant_dynamic-update-slice_fusion.refs_15_), channel_id=1, source_target_pairs={{0,1},{1,0},{2,3},{3,2},{4,5},{5,4},{6,7},{7,6},{8,9},{9,8},{10,11... | collective-permute-start | bytes 1179656 | tf_op jit(solution)/shard_map/ppermute | solution.py:278
  67.2 12.8 %collective-permute-start.10 = (bf16[128,512]{1,0:T(8,128)(2,1)}, bf16[128,512]{1,0:T(8,128)(2,1)}, u32[]{:S(2)}, u32[]{:S(2)}) collective-permute-start(bf16[128,512]{1,0:T(8,128)(2,1)} %slice.163), channel_id=1, source_target_pairs={{1,13},{2,14},{3,15},{4,0},{6,2},{7,3},{8,4},{11,7},{13,9},{14,10}... | collective-permute-start | bytes 393224 | tf_op jit(solution)/shard_map/ppermute | solution.py:236
  74.7 4.0 %collective-permute-start.9 = (bf16[144,512]{1,0:T(8,128)(2,1)S(1)}, bf16[144,512]{1,0:T(8,128)(2,1)S(1)}, u32[]{:S(2)}, u32[]{:S(2)}) collective-permute-start(bf16[144,512]{1,0:T(8,128)(2,1)S(1)} %slice.161), channel_id=1, source_target_pairs={{0,4},{3,7},{5,9},{6,10},{7,11},{9,13},{10,14},{11,15},{12,0},{14,... | collective-permute-start | bytes 442376 | tf_op jit(solution)/shard_map/ppermute | solution.py:236
  76.1 12.1 %collective-permute-start.15 = (bf16[24,64,256]{2,1,0:T(8,128)(2,1)S(1)}, bf16[24,64,256]{2,1,0:T(8,128)(2,1)S(1)}, u32[]{:S(2)}, u32[]{:S(2)}) collective-permute-start(bf16[24,64,256]{2,1,0:T(8,128)(2,1)S(1)} %pad_maximum_fusion), channel_id=1, source_target_pairs={{0,3},{1,2},{2,1},{3,0},{4,7},{5,6},{6,5},{7,4},{8,11},{9,10},{10,... | collective-permute-start | bytes 2359304 | tf_op jit(solution)/shard_map/ppermute | solution.py:279
  120.4 15.1 %collective-permute-start.16 = (bf16[2,256,512]{2,1,0:T(8,128)(2,1)}, bf16[2,256,512]{2,1,0:T(8,128)(2,1)S(1)}, u32[]{:S(2)}, u32[]{:S(2)}) collective-permute-start(bf16[2,256,512]{2,1,0:T(8,128)(2,1)} %get-tuple-element.41), channel_id=1, source_target_pairs={{0,1},{1,2},{2,3},{3,0},{4,5},{5,6},{6,7},{7,4},{8,9},{9,10},{10,1... | collective-permute-start | bytes 1572872 | tf_op jit(solution)/shard_map/ppermute | solution.py:236
  120.5 17.0 %collective-permute-start.20 = (bf16[2,256,512]{2,1,0:T(8,128)(2,1)}, bf16[2,256,512]{2,1,0:T(8,128)(2,1)S(1)}, u32[]{:S(2)}, u32[]{:S(2)}) collective-permute-start(bf16[2,256,512]{2,1,0:T(8,128)(2,1)} %get-tuple-element.46), channel_id=1, source_target_pairs={{0,3},{1,0},{2,1},{3,2},{4,7},{5,4},{6,5},{7,6},{8,11},{9,8},{10,9... | collective-permute-start | bytes 1572872 | tf_op jit(solution)/shard_map/ppermute | solution.py:236
  122.5 38.0 %collective-permute-start.18 = (bf16[2,256,512]{2,1,0:T(8,128)(2,1)}, bf16[2,256,512]{2,1,0:T(8,128)(2,1)S(1)}, u32[]{:S(2)}, u32[]{:S(2)}) collective-permute-start(bf16[2,256,512]{2,1,0:T(8,128)(2,1)} %get-tuple-element.42), channel_id=1, source_target_pairs={{0,3},{1,0},{2,1},{3,2},{4,7},{5,4},{6,5},{7,6},{8,11},{9,8},{10,9... | collective-permute-start | bytes 1572872 | tf_op jit(solution)/shard_map/ppermute | solution.py:236
  122.5 45.8 %collective-permute-start.19 = (bf16[2,256,512]{2,1,0:T(8,128)(2,1)}, bf16[2,256,512]{2,1,0:T(8,128)(2,1)S(1)}, u32[]{:S(2)}, u32[]{:S(2)}) collective-permute-start(bf16[2,256,512]{2,1,0:T(8,128)(2,1)} %get-tuple-element.44), channel_id=1, source_target_pairs={{0,1},{1,2},{2,3},{3,0},{4,5},{5,6},{6,7},{7,4},{8,9},{9,10},{10,1... | collective-permute-start | bytes 1572872 | tf_op jit(solution)/shard_map/ppermute | solution.py:236
  124.5 33.3 %collective-permute-start.22 = (bf16[2,256,512]{2,1,0:T(8,128)(2,1)}, bf16[2,256,512]{2,1,0:T(8,128)(2,1)S(1)}, u32[]{:S(2)}, u32[]{:S(2)}) collective-permute-start(bf16[2,256,512]{2,1,0:T(8,128)(2,1)} %get-tuple-element.49), channel_id=1, source_target_pairs={{0,1},{3,0},{4,5},{5,6},{8,9},{9,10},{13,14},{16,17},{19,16},{20,2... | collective-permute-start | bytes 1572872 | tf_op jit(solution)/shard_map/ppermute | solution.py:236
  135.5 23.5 %collective-permute-start.26 = (bf16[2,256,512]{2,1,0:T(8,128)(2,1)}, bf16[2,256,512]{2,1,0:T(8,128)(2,1)S(1)}, u32[]{:S(2)}, u32[]{:S(2)}) collective-permute-start(bf16[2,256,512]{2,1,0:T(8,128)(2,1)} %get-tuple-element.54), channel_id=1, source_target_pairs={{0,3},{4,7},{9,8},{13,12},{16,19},{20,23},{25,24},{29,28},{32,35},... | collective-permute-start | bytes 1572872 | tf_op jit(solution)/shard_map/ppermute | solution.py:236
  137.5 27.9 %collective-permute-start.17 = (bf16[2,256,512]{2,1,0:T(8,128)(2,1)S(1)}, bf16[2,256,512]{2,1,0:T(8,128)(2,1)S(1)}, u32[]{:S(2)}, u32[]{:S(2)}) collective-permute-start(bf16[2,256,512]{2,1,0:T(8,128)(2,1)S(1)} %add_convert_fusion.3), channel_id=1, source_target_pairs={{0,1},{1,2},{2,3},{3,0},{4,5},{5,6},{6,7},{7,4},{8,9},{9,10},{10,1... | collective-permute-start | bytes 1572872 | tf_op jit(solution)/shard_map/ppermute | solution.py:236
  157.8 11.8 %collective-permute-start.21 = (bf16[2,256,512]{2,1,0:T(8,128)(2,1)S(1)}, bf16[2,256,512]{2,1,0:T(8,128)(2,1)S(1)}, u32[]{:S(2)}, u32[]{:S(2)}) collective-permute-start(bf16[2,256,512]{2,1,0:T(8,128)(2,1)S(1)} %add_convert_fusion.2), channel_id=1, source_target_pairs={{0,3},{1,0},{2,1},{3,2},{4,7},{5,4},{6,5},{7,6},{8,11},{9,8},{10,9... | collective-permute-start | bytes 1572872 | tf_op jit(solution)/shard_map/ppermute | solution.py:236
  159.0 13.6 %collective-permute-start.24 = (bf16[2,256,512]{2,1,0:T(8,128)(2,1)S(1)}, bf16[2,256,512]{2,1,0:T(8,128)(2,1)S(1)}, u32[]{:S(2)}, u32[]{:S(2)}) collective-permute-start(bf16[2,256,512]{2,1,0:T(8,128)(2,1)S(1)} %copy-done.21), channel_id=1, source_target_pairs={{2,1},{3,2},{4,7},{7,6},{8,11},{11,10},{12,15},{18,17},{19,18},{20... | collective-permute-start | bytes 1572872 | tf_op jit(solution)/shard_map/ppermute | solution.py:236
  160.5 17.8 %collective-permute-start.25 = (bf16[2,256,512]{2,1,0:T(8,128)(2,1)S(1)}, bf16[2,256,512]{2,1,0:T(8,128)(2,1)S(1)}, u32[]{:S(2)}, u32[]{:S(2)}) collective-permute-start(bf16[2,256,512]{2,1,0:T(8,128)(2,1)S(1)} %copy-done.20), channel_id=1, source_target_pairs={{1,2},{5,6},{10,11},{14,15},{17,18},{21,22},{26,27},{30,31},{33,34... | collective-permute-start | bytes 1572872 | tf_op jit(solution)/shard_map/ppermute | solution.py:236
  165.4 12.0 %collective-permute-start.23 = (bf16[2,256,512]{2,1,0:T(8,128)(2,1)S(1)}, bf16[2,256,512]{2,1,0:T(8,128)(2,1)S(1)}, u32[]{:S(2)}, u32[]{:S(2)}) collective-permute-start(bf16[2,256,512]{2,1,0:T(8,128)(2,1)S(1)} %add_convert_fusion.1), channel_id=1, source_target_pairs={{0,1},{1,2},{5,6},{6,7},{9,10},{10,11},{14,15},{16,17},{17,18},{21... | collective-permute-start | bytes 1572872 | tf_op jit(solution)/shard_map/ppermute | solution.py:236
  168.3 11.1 %collective-permute-start.27 = (bf16[2,256,512]{2,1,0:T(8,128)(2,1)S(1)}, bf16[2,256,512]{2,1,0:T(8,128)(2,1)S(1)}, u32[]{:S(2)}, u32[]{:S(2)}) collective-permute-start(bf16[2,256,512]{2,1,0:T(8,128)(2,1)S(1)} %add_convert_fusion), channel_id=1, source_target_pairs={{3,2},{7,6},{8,11},{12,15},{19,18},{23,22},{24,27},{28,31},{35,34}... | collective-permute-start | bytes 1572872 | tf_op jit(solution)/shard_map/ppermute | solution.py:236
  170.7 11.7 %collective-permute-start.28 = (bf16[2,256,512]{2,1,0:T(8,128)(2,1)S(1)}, bf16[2,256,512]{2,1,0:T(8,128)(2,1)S(1)}, u32[]{:S(2)}, u32[]{:S(2)}) collective-permute-start(bf16[2,256,512]{2,1,0:T(8,128)(2,1)S(1)} %pad_maximum_fusion.1), channel_id=1, source_target_pairs={{0,16},{1,17},{2,18},{3,19},{4,20},{5,21},{6,22},{7,23},{8,24},{9,... | collective-permute-start | bytes 1572872 | tf_op jit(solution)/shard_map/ppermute | solution.py:325
  180.4 11.4 %collective-permute-start.29 = (bf16[2,256,512]{2,1,0:T(8,128)(2,1)S(1)}, bf16[2,256,512]{2,1,0:T(8,128)(2,1)S(1)}, u32[]{:S(2)}, u32[]{:S(2)}) collective-permute-start(bf16[2,256,512]{2,1,0:T(8,128)(2,1)S(1)} %pad_maximum_fusion.2), channel_id=1, source_target_pairs={{1,17},{2,18},{6,22},{7,23},{10,26},{11,27},{15,31},{17,33},{18,34... | collective-permute-start | bytes 1572872 | tf_op jit(solution)/shard_map/ppermute | solution.py:325
  (20 other events, 419.0 us)

commit v5 on v4

--- a/solution.py
+++ b/solution.py
@@ -12,12 +12,17 @@
 SECS, ROWS = 16, 16
 BB, KB = 256, 512
 QUARTER = BB // NX
+TOGETHER = 2
 BF, F32 = jnp.bfloat16, jnp.float32
 STEPS = (0, -1, 1, 2)
 VMEM_BYTES = 56 * 1024 * 1024
 HEAD = 16
 BRA_CELLS = ((0, 0), (0, 1), (2, 1), (1, 0), (1, 1), (3, 1))
 CELLS = [(b, j) for b in range(2) for j in range(CH)]
+
+
+def after(value, *others):
+    return lax.optimization_barrier((value, *others))[0] if others else value
 
 
 def charge(channel):
@@ -115,17 +120,17 @@
             out[cell] = jnp.where(keep(rows, cols), value, 0.0).astype(BF)
 
 
-def terms_kernel(place, ket_sizes, ints, values, *refs):
+def terms_kernel(place, ints, values, *refs):
     envs, across2b, ket_in, bra_own, rim0, rim1, rim2 = refs[:12], *refs[12:18]
     outs = refs[18:34]
-    env_all, ket, bra_all, total, rounded, env_sem, ket_sem, bra_sem, out_sem = refs[34:]
+    env_all, ket, bra_all, total, rounded, todo, scale, env_sem, ket_sem, bra_sem, out_sem = refs[34:]
     x = place[0] % NX
     copies = []
     for n in range(12):
         rows = BB if n < 11 else BB // 2
         copies.append(pltpu.make_async_copy(envs[n].at[pl.ds(HEAD, rows)], env_all.at[n, pl.ds(0, rows)], env_sem.at[n]))
     copies.append(pltpu.make_async_copy(across2b, env_all.at[11, pl.ds(BB // 2, BB // 2)], env_sem.at[12]))
-    copies += [pltpu.make_async_copy(ket_in.at[s], ket.at[s], ket_sem.at[s]) for s in range(4)]
+    copies += [pltpu.make_async_copy(ket_in.at[s], ket.at[pl.ds(2 * s, 2)], ket_sem.at[s]) for s in range(4)]
     copies.append(pltpu.make_async_copy(bra_own, bra_all.at[pl.ds(6, 6)], bra_sem.at[0]))
     y = NX - 1 - x
     for n, (ref, at, owner) in enumerate(((rim0, 0, x), (rim1, 0, x + 1 - 2 * (x % 2)), (rim2, 0, y), (rim2, 12, y + 1 - 2 * (y % 2)))):
@@ -147,46 +152,53 @@
                 total[at] = jnp.zeros((BB, KB), F32)
                 total[at + 1] = jnp.zeros((BB, KB), F32)
 
+    def listed(item, count):
+        base = 64 * (item // EPW) + 8 * (item % EPW)
+        out_w, sp, s, code = ints[base], ints[base + 1], ints[base + 2], ints[base + 7]
+        q_b = code - 1
+        p_b, s_a = q_b + s // 2, s % 2
+        out_r, out_j = out_w // CH, out_w % CH
+        forward = (out_r % NX - my_x + NX) % NX
+        slot = jnp.where(forward == 1, 2, jnp.where(forward == 3, 1, jnp.where(forward == 2, 3, 0)))
+        out_a, out_b = charge(out_w)
+        low = live_at(out_r, 0, 0)
+        inside = low + live_at(out_r, 0, 1) + out_j * live_at(out_r, 1, 0)
+        position = jnp.where(p_b == 0, out_j * low, inside)
+        live = (code > 0) & (out_w // (CH * NX) == my_z) & (p_b < 2) & (a + s_a < SECS)
+        live = live & (live_at(out_r, p_b, out_j) == 1)
+
+        @pl.when(live)
+        def _():
+            todo[4 * count] = item // EPW
+            todo[4 * count + 1] = 2 * s + q_b
+            todo[4 * count + 2] = 6 * (s_a + out_a + 1) + 3 * (sp % 2) + p_b + out_b + sp // 2
+            todo[4 * count + 3] = 8 * slot + 2 * position + s_a
+            scale[count] = values[base + 3] + values[base + 4] + values[base + 5]
+
+        return count + jnp.where(live, 1, 0)
+
+    count = lax.fori_loop(0, 12 * EPW, listed, jnp.int32(0))
+    for n in range(TOGETHER - 1):
+        for field in range(3):
+            todo[4 * (count + n) + field] = 0
+        todo[4 * (count + n) + 3] = 32
+        scale[count + n] = 0.0
+
     for copy in copies:
         copy.wait()
 
-    @pl.loop(0, 12 * EPW)
-    def _(item):
-        base = 64 * (item // EPW) + 8 * (item % EPW)
-        out_w, s, code = ints[base], ints[base + 2], ints[base + 7]
-        p_b, s_a = code - 1 + s // 2, s % 2
-        out_r, out_j = out_w // CH, out_w % CH
-
-        @pl.when((code > 0) & (out_w // (CH * NX) == my_z) & (p_b < 2) & (a + s_a < SECS))
-        def _():
-            q_b = code - 1
-
-            @pl.when(live_at(out_r, p_b, out_j) == 1)
-            def _():
-                sp = ints[base + 1]
-                value = values[base + 3] + values[base + 4] + values[base + 5]
-                forward = (out_r % NX - my_x + NX) % NX
-                slot = jnp.where(forward == 1, 2, jnp.where(forward == 3, 1, jnp.where(forward == 2, 3, 0)))
-                out_a, out_b = charge(out_w)
-                low = live_at(out_r, 0, 0)
-                inside = low + live_at(out_r, 0, 1) + out_j * live_at(out_r, 1, 0)
-                position = jnp.where(p_b == 0, out_j * low, inside)
-                b_at = 6 * (s_a + out_a + 1) + 3 * (sp % 2) + p_b + out_b + sp // 2
-                at = 8 * slot + 2 * position + s_a
-                e_at = item // EPW
-                to_size = ket_sizes[p_b, a + s_a]
-                from_size = ket_sizes[q_b, a]
-                for n in range(2):
-                    cols = pl.ds(n * (KB // 2), KB // 2)
-
-                    def run(depth, cols=cols):
-                        half = jnp.dot(env_all[e_at, :, :depth], ket[s, q_b, :depth, cols], preferred_element_type=F32)
-                        term = jnp.dot(bra_all[b_at], half.astype(BF), preferred_element_type=F32)
-                        total[at, :, cols] = total[at, :, cols] + value * term
-
-                    wide = to_size > n * (KB // 2)
-                    pl.when(wide & (from_size > KB // 2))(functools.partial(run, KB))
-                    pl.when(wide & (from_size <= KB // 2))(functools.partial(run, KB // 2))
+    @pl.loop(0, (count + TOGETHER - 1) // TOGETHER)
+    def _(step):
+        places = [step * TOGETHER + n for n in range(TOGETHER)]
+        halves = [
+            jnp.dot(env_all[todo[4 * n]], ket[todo[4 * n + 1]], preferred_element_type=F32).astype(BF) for n in places
+        ]
+        terms = [
+            jnp.dot(bra_all[todo[4 * n + 2]], half, preferred_element_type=F32) for n, half in zip(places, halves)
+        ]
+        for n, term in zip(places, terms):
+            at = todo[4 * n + 3]
+            total[at] = total[at] + scale[n] * term
 
     def stored(d, i):
         return pltpu.make_async_copy(rounded.at[4 * d + i], outs[4 * d + i], out_sem.at[4 * d + i])
@@ -246,8 +258,8 @@
     behind0 = sent(own0, z_up, same, everyone)
     ahead1 = sent(own1, z_down, same, everyone)
     own2 = own2 + lax.ppermute(moving, "row", lent)
-    behind1 = sent(own1, z_up, same, everyone)
-    ahead0 = sent(own0, z_down, same, everyone)
+    behind1 = sent(after(own1, behind0, ahead1), z_up, same, everyone)
+    ahead0 = sent(after(own0, behind0, ahead1), z_down, same, everyone)
     behind2 = sent(own2, z_up, same, three)
     ahead2 = sent(own2, z_down, same, three)
     across0 = sent(behind0, z_up, z_down, everyone)
@@ -284,22 +296,24 @@
     hbm = pl.BlockSpec(memory_space=pl.ANY)
     sums = pl.pallas_call(
         terms_kernel,
-        in_specs=[smem] * 4 + [hbm] * 18,
+        in_specs=[smem] * 3 + [hbm] * 18,
         out_specs=[hbm] * 16,
         out_shape=[pair] * 16,
         scratch_shapes=[
             pltpu.VMEM((12, BB, KB), BF),
-            pltpu.VMEM((4, 2, KB, KB), BF),
+            pltpu.VMEM((8, KB, KB), BF),
             pltpu.VMEM((24, BB, BB), BF),
-            pltpu.VMEM((32, BB, KB), F32),
+            pltpu.VMEM((33, BB, KB), F32),
             pltpu.VMEM((16, 2, BB, KB), BF),
+            pltpu.SMEM((4 * (12 * EPW + TOGETHER),), jnp.int32),
+            pltpu.SMEM((12 * EPW + TOGETHER,), F32),
             pltpu.SemaphoreType.DMA((13,)),
             pltpu.SemaphoreType.DMA((4,)),
             pltpu.SemaphoreType.DMA((13,)),
             pltpu.SemaphoreType.DMA((16,)),
         ],
         compiler_params=params,
-    )(place, ket_flat, values.astype(jnp.int32), values, *envs, across2b, ket_mps[:, 0], bra_own, rim0, rim1, rim2)
+    )(place, values.astype(jnp.int32), values, *envs, across2b, ket_mps[:, 0], bra_own, rim0, rim1, rim2)
     mine, left, right, far = sums[:4], sums[4:8], sums[8:12], sums[12:]
 
     def added(*parts):
@@ -308,21 +322,21 @@
     def moved(value, move, owner, i):
         return sent(value, move, owner, {n for n in range(ROWS) if COUNT[n] > i})
 
-    far_up = {i: moved(far[i], x_up, x_far, i) for i in (0, 2)}
-    far_down = {i: moved(far[i], x_down, x_far, i) for i in (1, 3)}
-    from_left = {i: moved(right[i], x_up, x_up, i) for i in (1, 3)}
-    from_right = {i: moved(left[i], x_down, x_down, i) for i in (0, 2)}
-    for i in (0, 2):
-        from_left[i] = moved(added(right[i], far_up[i]).astype(BF), x_up, x_up, i)
-    for i in (1, 3):
-        from_right[i] = moved(added(left[i], far_down[i]).astype(BF), x_down, x_down, i)
-
-    here = [added(mine[i][0], from_left[i][0], from_right[i][0]) for i in range(4)]
-    raised = [added(mine[i][1], from_left[i][1], from_right[i][1]).astype(BF) for i in range(4)]
+    far_up, far_down, from_left, from_right = {}, {}, {}, {}
+    gate = ()
     above = []
     for i in (0, 2):
+        far_up[i] = moved(after(far[i], *gate), x_up, x_far, i)
+        far_down[i + 1] = moved(after(far[i + 1], *gate), x_down, x_far, i + 1)
+        from_left[i + 1] = moved(after(right[i + 1], *gate), x_up, x_up, i + 1)
+        from_right[i] = moved(after(left[i], *gate), x_down, x_down, i)
+        from_left[i] = moved(added(right[i], far_up[i]).astype(BF), x_up, x_up, i)
+        from_right[i + 1] = moved(added(left[i + 1], far_down[i + 1]).astype(BF), x_down, x_down, i + 1)
+        gate = (far_up[i], far_down[i + 1])
+        raised = [added(mine[n][1], from_left[n][1], from_right[n][1]).astype(BF) for n in (i, i + 1)]
         pairs = [(a * ROWS + n, (a + 1) * ROWS + n) for a in range(SECS - 1) for n in range(ROWS) if COUNT[n] > i]
-        above.append(lax.ppermute(jnp.stack(raised[i : i + 2]), ("sec", "row"), pairs))
+        above.append(lax.ppermute(jnp.stack(raised), ("sec", "row"), pairs))
+    here = [added(mine[n][0], from_left[n][0], from_right[n][0]) for n in range(4)]
 
     out = pl.pallas_call(
         unpack_kernel,

time: 198 us -> 208 us (1.051)
  the two profiles are of different devices: /device:TPU:92 before, /device:TPU:36 now
where the time goes in v5:
time: 208 us
  starting transfers between devices  84.1 us (40%)
  waiting for transfers between devices  78.6 us (38%)
  Pallas kernels  29 us (14%)
  other arithmetic  10.3 us (5%)
  local copies, waits for them, and re-layouts  5.32 us (3%)
    ppermute x22, starting transfers between devices, sent(): lax.ppermute(value, 'row', [(n, move(n)) for n in range(ROWS) if owner(n)...  64.8 us
    ppermute x22, waiting for transfers between devices, sent(): lax.ppermute(value, 'row', [(n, move(n)) for n in range(ROWS) if owner(n)...  46.5 us
    pallas_call x1, Pallas kernels, body(): pl.pallas_call(terms_kernel, in_specs=[smem] * 3 + [hbm] * 18, out_specs=...  20.7 us
    ppermute x1, waiting for transfers between devices, body(): lax.ppermute(strip_high, 'sec', down(2))  9 us
    ppermute x2, waiting for transfers between devices, body(): above.append(lax.ppermute(jnp.stack(raised), ('sec', 'row'), pairs))  8.55 us
    ppermute x1, waiting for transfers between devices, body(): lax.ppermute(jnp.concatenate([rim0, rim1]), 'row', [(n, n ^ 3) for n in r...  8.3 us
    ppermute x1, waiting for transfers between devices, body(): lax.ppermute(strip_low, 'sec', up(1))  5.01 us
    ppermute x1, starting transfers between devices, body(): rim1 = lax.ppermute(rim0, 'row', [(n, n ^ 1) for n in range(ROWS)])  4.77 us
  transfers between devices with their start and end apart: 30, of which 15 were waited for; matrix products, arithmetic and copies ran while one was open for 5% of the time, Pallas kernels for 1%

profile of v5, /device:TPU:36, one launch (start us, length us, event | category | flops | bytes accessed | tf_op | source)
XLA Modules:
  0.0 207.9 jit_solution(5481072003428234417)
XLA Ops:
  0.7 2.6 %shard_map.73 = (bf16[272,512]{1,0:T(8,128)(2,1)}, bf16[272,512]{1,0:T(8,128)(2,1)}, bf16[272,512]{1,0:T(8,128)(2,1)}, bf16[272,512]{1,0:T(8,128)(2,1)}) custom-call(s32[2]{0:T(128)} %pad_add_fusion.place, s32[2,16]{1,0:T(2,128)} %bitcast.46, s32[2,16]{1,0:T(2,128)} %bitcast.48, s32[3,2,8]{2,1,0:T(2,128)} %bitcast.50, f32[2,8]{1,0:T(2,128)} %coeffs.1, ...), custom_call_target="tpu_custom_call" | custom-call | tf_op jit(solution)/shard_map/pallas_call | solution.py:235
  3.2 3.1 %collective-permute-start = (bf16[272,512]{1,0:T(8,128)(2,1)}, bf16[272,512]{1,0:T(8,128)(2,1)S(1)}, u32[]{:S(2)}, u32[]{:S(2)}) collective-permute-start(bf16[272,512]{1,0:T(8,128)(2,1)} %get-tuple-element.39), channel_id=1, source_target_pairs={{2,3},{6,5},{11,8},{15,12},{18,19},{22,21},{27,24},{31,28},{34,35}... | collective-permute-start | bytes 835592 | tf_op jit(solution)/shard_map/ppermute | solution.py:260
  6.3 2.7 %collective-permute-start.1 = (bf16[272,512]{1,0:T(8,128)(2,1)}, bf16[272,512]{1,0:T(8,128)(2,1)S(1)}, u32[]{:S(2)}, u32[]{:S(2)}) collective-permute-start(bf16[272,512]{1,0:T(8,128)(2,1)} %get-tuple-element.41.refs_0_), channel_id=1, source_target_pairs={{0,4},{1,5},{2,6},{3,7},{4,8},{5,9},{6,10},{7,11},{8,12},{9,13},{1... | collective-permute-start | bytes 835592 | tf_op jit(solution)/shard_map/ppermute | solution.py:248
  13.6 2.4 %collective-permute-start.6 = (bf16[272,512]{1,0:T(8,128)(2,1)S(1)}, bf16[272,512]{1,0:T(8,128)(2,1)S(1)}, u32[]{:S(2)}, u32[]{:S(2)}) collective-permute-start(bf16[272,512]{1,0:T(8,128)(2,1)S(1)} %add.83.refs_2_), channel_id=1, source_target_pairs={{1,13},{2,14},{3,15},{5,1},{6,2},{7,3},{8,4},{10,6},{11,7},{12,8},... | collective-permute-start | bytes 835592 | tf_op jit(solution)/shard_map/ppermute | solution.py:248
  16.0 4.4 %collective-permute-start.4 = (bf16[272,512]{1,0:T(8,128)(2,1)S(1)}, bf16[272,512]{1,0:T(8,128)(2,1)S(1)}, u32[]{:S(2)}, u32[]{:S(2)}) collective-permute-start(bf16[272,512]{1,0:T(8,128)(2,1)S(1)} %add.83.refs_2_), channel_id=1, source_target_pairs={{1,5},{2,6},{3,7},{5,9},{6,10},{7,11},{8,12},{10,14},{11,15},{12,0... | collective-permute-start | bytes 835592 | tf_op jit(solution)/shard_map/ppermute | solution.py:248
  20.4 2.4 %collective-permute-done.1.refs_3_ = bf16[272,512]{1,0:T(8,128)(2,1)S(1)} collective-permute-done((bf16[272,512]{1,0:T(8,128)(2,1)}, bf16[272,512]{1,0:T(8,128)(2,1)S(1)}, u32[]{:S(2)}, u32[]{:S(2)}) %collective-permute-start.1) | collective-permute-done | bytes 278560 | tf_op jit(solution)/shard_map/ppermute | solution.py:248
  22.8 1.9 collective-permute-done.2.refs_7_
  24.7 2.7 %collective-permute-start.3 = (bf16[272,512]{1,0:T(8,128)(2,1)}, bf16[272,512]{1,0:T(8,128)(2,1)S(1)}, u32[]{:S(2)}, u32[]{:S(2)}) collective-permute-start(bf16[272,512]{1,0:T(8,128)(2,1)} %get-tuple-element.40.refs_1_), channel_id=1, source_target_pairs={{0,4},{1,5},{2,6},{3,7},{4,8},{5,9},{6,10},{7,11},{8,12},{9,13},{1... | collective-permute-start | bytes 835592 | tf_op jit(solution)/shard_map/ppermute | solution.py:248
  27.4 2.5 %shard_map.74 = (bf16[6,256,256]{2,1,0:T(8,128)(2,1)}, bf16[6,64,256]{2,1,0:T(8,128)(2,1)}, bf16[3,64,256]{2,1,0:T(8,128)(2,1)}, bf16[3,64,256]{2,1,0:T(8,128)(2,1)}) custom-call(s32[2]{0:T(128)} %pad_add_fusion.place, bf16[4,2,256,256]{3,2,1,0:T(8,128)(2,1)} %bitcast.45), custom_call_target="tpu_custom_call" | custom-call | tf_op jit(solution)/shard_map/pallas_call | solution.py:271
  31.8 3.6 %collective-permute-start.12 = (bf16[6,64,256]{2,1,0:T(8,128)(2,1)}, bf16[6,64,256]{2,1,0:T(8,128)(2,1)S(1)}, u32[]{:S(2)}, u32[]{:S(2)}) collective-permute-start(bf16[6,64,256]{2,1,0:T(8,128)(2,1)} %get-tuple-element.45), channel_id=1, source_target_pairs={{16,0},{32,16},{48,32},{64,48},{80,64},{96,80},{112,96},{128,112},... | collective-permute-start | bytes 589832 | tf_op jit(solution)/shard_map/ppermute | solution.py:287
  35.5 5.0 %collective-permute-done.11 = bf16[3,64,256]{2,1,0:T(8,128)(2,1)S(1)} collective-permute-done((bf16[3,64,256]{2,1,0:T(8,128)(2,1)}, bf16[3,64,256]{2,1,0:T(8,128)(2,1)S(1)}, u32[]{:S(2)}, u32[]{:S(2)}) %collective-permute-start.11) | collective-permute-done | bytes 98336 | tf_op jit(solution)/shard_map/ppermute | solution.py:286
  40.5 5.3 %collective-permute-start.5 = (bf16[272,512]{1,0:T(8,128)(2,1)}, bf16[272,512]{1,0:T(8,128)(2,1)S(1)}, u32[]{:S(2)}, u32[]{:S(2)}) collective-permute-start(bf16[272,512]{1,0:T(8,128)(2,1)} %get-tuple-element.41.refs_0_), channel_id=1, source_target_pairs={{0,12},{1,13},{2,14},{3,15},{4,0},{5,1},{6,2},{7,3},{8,4},{9,5},{1... | collective-permute-start | bytes 835592 | tf_op jit(solution)/shard_map/ppermute | solution.py:248
  47.7 9.0 %collective-permute-done.13 = bf16[3,64,256]{2,1,0:T(8,128)(2,1)S(1)} collective-permute-done((bf16[3,64,256]{2,1,0:T(8,128)(2,1)}, bf16[3,64,256]{2,1,0:T(8,128)(2,1)S(1)}, u32[]{:S(2)}, u32[]{:S(2)}) %collective-permute-start.13) | collective-permute-done | bytes 98336 | tf_op jit(solution)/shard_map/ppermute | solution.py:288
  56.8 4.1 %collective-permute-start.8 = (bf16[272,512]{1,0:T(8,128)(2,1)S(1)}, bf16[272,512]{1,0:T(8,128)(2,1)S(1)}, u32[]{:S(2)}, u32[]{:S(2)}) collective-permute-start(bf16[272,512]{1,0:T(8,128)(2,1)S(1)} %collective-permute-done.2.refs_7_), channel_id=1, source_target_pairs={{0,12},{1,13},{2,14},{3,15},{4,0},{5,1},{6,2},{7,3},{8,4},{9,5},{1... | collective-permute-start | bytes 835592 | tf_op jit(solution)/shard_map/ppermute | solution.py:248
  60.9 4.8 %collective-permute-start.14 = (bf16[12,64,256]{2,1,0:T(8,128)(2,1)S(1)}, bf16[12,64,256]{2,1,0:T(8,128)(2,1)S(1)}, u32[]{:S(2)}, u32[]{:S(2)}) collective-permute-start(bf16[12,64,256]{2,1,0:T(8,128)(2,1)S(1)} %constant_dynamic-update-slice_fusion.refs_15_), channel_id=1, source_target_pairs={{0,1},{1,0},{2,3},{3,2},{4,5},{5,4},{6,7},{7,6},{8,9},{9,8},{10,11... | collective-permute-start | bytes 1179656 | tf_op jit(solution)/shard_map/ppermute | solution.py:290
  66.4 6.4 %collective-permute-done.7.refs_9_ = bf16[272,512]{1,0:T(8,128)(2,1)S(1)} collective-permute-done((bf16[272,512]{1,0:T(8,128)(2,1)S(1)}, bf16[272,512]{1,0:T(8,128)(2,1)S(1)}, u32[]{:S(2)}, u32[]{:S(2)}) %collective-permute-start.7) | collective-permute-done | bytes 278560 | tf_op jit(solution)/shard_map/ppermute | solution.py:248
  72.8 3.6 %collective-permute-start.10 = (bf16[128,512]{1,0:T(8,128)(2,1)}, bf16[128,512]{1,0:T(8,128)(2,1)}, u32[]{:S(2)}, u32[]{:S(2)}) collective-permute-start(bf16[128,512]{1,0:T(8,128)(2,1)} %slice.163), channel_id=1, source_target_pairs={{1,13},{2,14},{3,15},{4,0},{6,2},{7,3},{8,4},{11,7},{13,9},{14,10}... | collective-permute-start | bytes 393224 | tf_op jit(solution)/shard_map/ppermute | solution.py:248
  79.4 8.1 %collective-permute-done.9.refs_11_ = bf16[144,512]{1,0:T(8,128)(2,1)S(1)} collective-permute-done((bf16[144,512]{1,0:T(8,128)(2,1)S(1)}, bf16[144,512]{1,0:T(8,128)(2,1)S(1)}, u32[]{:S(2)}, u32[]{:S(2)}) %collective-permute-start.9) | collective-permute-done | bytes 147488 | tf_op jit(solution)/shard_map/ppermute | solution.py:248
  88.9 8.3 %collective-permute-done.15.refs_17_ = bf16[24,64,256]{2,1,0:T(8,128)(2,1)S(1)} collective-permute-done((bf16[24,64,256]{2,1,0:T(8,128)(2,1)S(1)}, bf16[24,64,256]{2,1,0:T(8,128)(2,1)S(1)}, u32[]{:S(2)}, u32[]{:S(2)}) %collective-permute-start.15) | collective-permute-done | bytes 786464 | tf_op jit(solution)/shard_map/ppermute | solution.py:291
  98.1 20.7 %shard_map.75 = (bf16[2,256,512]{2,1,0:T(8,128)(2,1)}, bf16[2,256,512]{2,1,0:T(8,128)(2,1)}, bf16[2,256,512]{2,1,0:T(8,128)(2,1)}, bf16[2,256,512]{2,1,0:T(8,128...) custom-call(s32[2]{0:T(128)} %pad_add_fusion.place, ...), custom_call_target="tpu_custom_call" | custom-call | tf_op jit(solution)/shard_map/pallas_call | solution.py:297
  118.9 8.2 %collective-permute-start.16 = (bf16[2,256,512]{2,1,0:T(8,128)(2,1)}, bf16[2,256,512]{2,1,0:T(8,128)(2,1)S(1)}, u32[]{:S(2)}, u32[]{:S(2)}) collective-permute-start(bf16[2,256,512]{2,1,0:T(8,128)(2,1)} %get-tuple-element.49), channel_id=1, source_target_pairs={{0,1},{1,2},{2,3},{3,0},{4,5},{5,6},{6,7},{7,4},{8,9},{9,10},{10,1... | collective-permute-start | bytes 1572872 | tf_op jit(solution)/shard_map/ppermute | solution.py:248
  127.1 2.1 collective-permute-start.19
  129.2 10.6 %collective-permute-done.16 = bf16[2,256,512]{2,1,0:T(8,128)(2,1)S(1)} collective-permute-done((bf16[2,256,512]{2,1,0:T(8,128)(2,1)}, bf16[2,256,512]{2,1,0:T(8,128)(2,1)S(1)}, u32[]{:S(2)}, u32[]{:S(2)}) %collective-permute-start.16) | collective-permute-done | bytes 524320 | tf_op jit(solution)/shard_map/ppermute | solution.py:248
  139.8 2.4 %collective-permute-done.20 = bf16[2,256,512]{2,1,0:T(8,128)(2,1)S(1)} collective-permute-done((bf16[2,256,512]{2,1,0:T(8,128)(2,1)}, bf16[2,256,512]{2,1,0:T(8,128)(2,1)S(1)}, u32[]{:S(2)}, u32[]{:S(2)}) %collective-permute-start.20) | collective-permute-done | bytes 524320 | tf_op jit(solution)/shard_map/ppermute | solution.py:248
  144.1 2.5 %collective-permute-start.17 = (bf16[2,256,512]{2,1,0:T(8,128)(2,1)S(1)}, bf16[2,256,512]{2,1,0:T(8,128)(2,1)S(1)}, u32[]{:S(2)}, u32[]{:S(2)}) collective-permute-start(bf16[2,256,512]{2,1,0:T(8,128)(2,1)S(1)} %add_convert_fusion.3), channel_id=1, source_target_pairs={{0,1},{1,2},{2,3},{3,0},{4,5},{5,6},{6,7},{7,4},{8,9},{9,10},{10,1... | collective-permute-start | bytes 1572872 | tf_op jit(solution)/shard_map/ppermute | solution.py:248
  148.5 10.6 %collective-permute-start.21 = (bf16[2,256,512]{2,1,0:T(8,128)(2,1)S(1)}, bf16[2,256,512]{2,1,0:T(8,128)(2,1)S(1)}, u32[]{:S(2)}, u32[]{:S(2)}) collective-permute-start(bf16[2,256,512]{2,1,0:T(8,128)(2,1)S(1)} %add_convert_fusion.2), channel_id=1, source_target_pairs={{0,3},{1,0},{2,1},{3,2},{4,7},{5,4},{6,5},{7,6},{8,11},{9,8},{10,9... | collective-permute-start | bytes 1572872 | tf_op jit(solution)/shard_map/ppermute | solution.py:248
  160.4 8.0 %collective-permute-start.24 = (bf16[2,256,512]{2,1,0:T(8,128)(2,1)S(1)}, bf16[2,256,512]{2,1,0:T(8,128)(2,1)S(1)}, u32[]{:S(2)}, u32[]{:S(2)}) collective-permute-start(bf16[2,256,512]{2,1,0:T(8,128)(2,1)S(1)} %copy-done.21), channel_id=1, source_target_pairs={{2,1},{3,2},{4,7},{7,6},{8,11},{11,10},{12,15},{18,17},{19,18},{20... | collective-permute-start | bytes 1572872 | tf_op jit(solution)/shard_map/ppermute | solution.py:248
  176.2 1.9 collective-permute-start.28
  178.1 8.2 %collective-permute-done.24 = bf16[2,256,512]{2,1,0:T(8,128)(2,1)S(1)} collective-permute-done((bf16[2,256,512]{2,1,0:T(8,128)(2,1)S(1)}, bf16[2,256,512]{2,1,0:T(8,128)(2,1)S(1)}, u32[]{:S(2)}, u32[]{:S(2)}) %collective-permute-start.24) | collective-permute-done | bytes 524320 | tf_op jit(solution)/shard_map/ppermute | solution.py:248
  186.4 4.3 %collective-permute-done.23 = bf16[2,256,512]{2,1,0:T(8,128)(2,1)S(1)} collective-permute-done((bf16[2,256,512]{2,1,0:T(8,128)(2,1)S(1)}, bf16[2,256,512]{2,1,0:T(8,128)(2,1)S(1)}, u32[]{:S(2)}, u32[]{:S(2)}) %collective-permute-start.23) | collective-permute-done | bytes 524320 | tf_op jit(solution)/shard_map/ppermute | solution.py:248
  195.3 8.6 %collective-permute-done.29.refs_5_ = bf16[2,256,512]{2,1,0:T(8,128)(2,1)S(1)} collective-permute-done((bf16[2,256,512]{2,1,0:T(8,128)(2,1)S(1)}, bf16[2,256,512]{2,1,0:T(8,128)(2,1)S(1)}, u32[]{:S(2)}, u32[]{:S(2)}) %collective-permute-start.29) | collective-permute-done | bytes 524320 | tf_op jit(solution)/shard_map/ppermute | solution.py:338
  204.7 3.2 %shard_map.76 = bf16[4,256,512]{2,1,0:T(8,128)(2,1)} custom-call(s32[2]{0:T(128)} %pad_add_fusion.place, s32[2,16]{1,0:T(2,128)} %bitcast.47, s32[2,16]{1,0:T(2,128)} %bitcast.49, f32[256,512]{1,0:T(8,128)} %get-tuple-element.72.refs_0_, f32[256,512]{1,0:T(8,128)} %get-tuple-element.74.refs_1_, f32[256,512]{1,0:T(8,128)} %get-tuple-element.68.refs_2_, ...), custom_call_target="tpu_custom_call" | custom-call | tf_op jit(solution)/shard_map/pallas_call | solution.py:341
  (107 shorter events, 33.1 us)
Async XLA Ops:
  3.2 9.3 %collective-permute-start = (bf16[272,512]{1,0:T(8,128)(2,1)}, bf16[272,512]{1,0:T(8,128)(2,1)S(1)}, u32[]{:S(2)}, u32[]{:S(2)}) collective-permute-start(bf16[272,512]{1,0:T(8,128)(2,1)} %get-tuple-element.39), channel_id=1, source_target_pairs={{2,3},{6,5},{11,8},{15,12},{18,19},{22,21},{27,24},{31,28},{34,35}... | collective-permute-start | bytes 835592 | tf_op jit(solution)/shard_map/ppermute | solution.py:260
  6.3 16.4 %collective-permute-start.1 = (bf16[272,512]{1,0:T(8,128)(2,1)}, bf16[272,512]{1,0:T(8,128)(2,1)S(1)}, u32[]{:S(2)}, u32[]{:S(2)}) collective-permute-start(bf16[272,512]{1,0:T(8,128)(2,1)} %get-tuple-element.41.refs_0_), channel_id=1, source_target_pairs={{0,4},{1,5},{2,6},{3,7},{4,8},{5,9},{6,10},{7,11},{8,12},{9,13},{1... | collective-permute-start | bytes 835592 | tf_op jit(solution)/shard_map/ppermute | solution.py:248
  9.0 15.7 %collective-permute-start.2 = (bf16[272,512]{1,0:T(8,128)(2,1)}, bf16[272,512]{1,0:T(8,128)(2,1)S(1)}, u32[]{:S(2)}, u32[]{:S(2)}) collective-permute-start(bf16[272,512]{1,0:T(8,128)(2,1)} %get-tuple-element.40.refs_1_), channel_id=1, source_target_pairs={{0,12},{1,13},{2,14},{3,15},{4,0},{5,1},{6,2},{7,3},{8,4},{9,5},{1... | collective-permute-start | bytes 835592 | tf_op jit(solution)/shard_map/ppermute | solution.py:248
  13.6 83.6 %copy-start.1 = (bf16[272,512]{1,0:T(8,128)(2,1)}, bf16[272,512]{1,0:T(8,128)(2,1)S(1)}, u32[]{:S(2)}) copy-start(bf16[272,512]{1,0:T(8,128)(2,1)S(1)} %add.83.refs_2_) | copy-start | bytes 835588
  13.6 43.2 %collective-permute-start.6 = (bf16[272,512]{1,0:T(8,128)(2,1)S(1)}, bf16[272,512]{1,0:T(8,128)(2,1)S(1)}, u32[]{:S(2)}, u32[]{:S(2)}) collective-permute-start(bf16[272,512]{1,0:T(8,128)(2,1)S(1)} %add.83.refs_2_), channel_id=1, source_target_pairs={{1,13},{2,14},{3,15},{5,1},{6,2},{7,3},{8,4},{10,6},{11,7},{12,8},... | collective-permute-start | bytes 835592 | tf_op jit(solution)/shard_map/ppermute | solution.py:248
  16.0 45.0 %collective-permute-start.4 = (bf16[272,512]{1,0:T(8,128)(2,1)S(1)}, bf16[272,512]{1,0:T(8,128)(2,1)S(1)}, u32[]{:S(2)}, u32[]{:S(2)}) collective-permute-start(bf16[272,512]{1,0:T(8,128)(2,1)S(1)} %add.83.refs_2_), channel_id=1, source_target_pairs={{1,5},{2,6},{3,7},{5,9},{6,10},{7,11},{8,12},{10,14},{11,15},{12,0... | collective-permute-start | bytes 835592 | tf_op jit(solution)/shard_map/ppermute | solution.py:248
  22.8 74.4 %copy-start.13 = (bf16[272,512]{1,0:T(8,128)(2,1)}, bf16[272,512]{1,0:T(8,128)(2,1)S(1)}, u32[]{:S(2)}) copy-start(bf16[272,512]{1,0:T(8,128)(2,1)S(1)} %collective-permute-done.1.refs_3_) | copy-start | bytes 835588
  24.7 51.7 %collective-permute-start.3 = (bf16[272,512]{1,0:T(8,128)(2,1)}, bf16[272,512]{1,0:T(8,128)(2,1)S(1)}, u32[]{:S(2)}, u32[]{:S(2)}) collective-permute-start(bf16[272,512]{1,0:T(8,128)(2,1)} %get-tuple-element.40.refs_1_), channel_id=1, source_target_pairs={{0,4},{1,5},{2,6},{3,7},{4,8},{5,9},{6,10},{7,11},{8,12},{9,13},{1... | collective-permute-start | bytes 835592 | tf_op jit(solution)/shard_map/ppermute | solution.py:248
  29.9 10.6 %collective-permute-start.11 = (bf16[3,64,256]{2,1,0:T(8,128)(2,1)}, bf16[3,64,256]{2,1,0:T(8,128)(2,1)S(1)}, u32[]{:S(2)}, u32[]{:S(2)}) collective-permute-start(bf16[3,64,256]{2,1,0:T(8,128)(2,1)} %get-tuple-element.44), channel_id=1, source_target_pairs={{0,16},{16,32},{32,48},{48,64},{64,80},{80,96},{96,112},{112,128},... | collective-permute-start | bytes 294920 | tf_op jit(solution)/shard_map/ppermute | solution.py:286
  31.8 13.9 %collective-permute-start.12 = (bf16[6,64,256]{2,1,0:T(8,128)(2,1)}, bf16[6,64,256]{2,1,0:T(8,128)(2,1)S(1)}, u32[]{:S(2)}, u32[]{:S(2)}) collective-permute-start(bf16[6,64,256]{2,1,0:T(8,128)(2,1)} %get-tuple-element.45), channel_id=1, source_target_pairs={{16,0},{32,16},{48,32},{64,48},{80,64},{96,80},{112,96},{128,112},... | collective-permute-start | bytes 589832 | tf_op jit(solution)/shard_map/ppermute | solution.py:287
  40.5 37.5 %collective-permute-start.5 = (bf16[272,512]{1,0:T(8,128)(2,1)}, bf16[272,512]{1,0:T(8,128)(2,1)S(1)}, u32[]{:S(2)}, u32[]{:S(2)}) collective-permute-start(bf16[272,512]{1,0:T(8,128)(2,1)} %get-tuple-element.41.refs_0_), channel_id=1, source_target_pairs={{0,12},{1,13},{2,14},{3,15},{4,0},{5,1},{6,2},{7,3},{8,4},{9,5},{1... | collective-permute-start | bytes 835592 | tf_op jit(solution)/shard_map/ppermute | solution.py:248
  45.7 10.9 %collective-permute-start.13 = (bf16[3,64,256]{2,1,0:T(8,128)(2,1)}, bf16[3,64,256]{2,1,0:T(8,128)(2,1)S(1)}, u32[]{:S(2)}, u32[]{:S(2)}) collective-permute-start(bf16[3,64,256]{2,1,0:T(8,128)(2,1)} %get-tuple-element.46), channel_id=1, source_target_pairs={{32,0},{48,16},{64,32},{80,48},{96,64},{112,80},{128,96},{144,112}... | collective-permute-start | bytes 294920 | tf_op jit(solution)/shard_map/ppermute | solution.py:288
  56.7 16.1 %collective-permute-start.7 = (bf16[272,512]{1,0:T(8,128)(2,1)S(1)}, bf16[272,512]{1,0:T(8,128)(2,1)S(1)}, u32[]{:S(2)}, u32[]{:S(2)}) collective-permute-start(bf16[272,512]{1,0:T(8,128)(2,1)S(1)} %collective-permute-done.1.refs_3_), channel_id=1, source_target_pairs={{0,4},{1,5},{2,6},{3,7},{4,8},{5,9},{6,10},{7,11},{8,12},{9,13},{1... | collective-permute-start | bytes 835592 | tf_op jit(solution)/shard_map/ppermute | solution.py:248
  56.8 21.2 %collective-permute-start.8 = (bf16[272,512]{1,0:T(8,128)(2,1)S(1)}, bf16[272,512]{1,0:T(8,128)(2,1)S(1)}, u32[]{:S(2)}, u32[]{:S(2)}) collective-permute-start(bf16[272,512]{1,0:T(8,128)(2,1)S(1)} %collective-permute-done.2.refs_7_), channel_id=1, source_target_pairs={{0,12},{1,13},{2,14},{3,15},{4,0},{5,1},{6,2},{7,3},{8,4},{9,5},{1... | collective-permute-start | bytes 835592 | tf_op jit(solution)/shard_map/ppermute | solution.py:248
  60.9 16.7 %collective-permute-start.14 = (bf16[12,64,256]{2,1,0:T(8,128)(2,1)S(1)}, bf16[12,64,256]{2,1,0:T(8,128)(2,1)S(1)}, u32[]{:S(2)}, u32[]{:S(2)}) collective-permute-start(bf16[12,64,256]{2,1,0:T(8,128)(2,1)S(1)} %constant_dynamic-update-slice_fusion.refs_15_), channel_id=1, source_target_pairs={{0,1},{1,0},{2,3},{3,2},{4,5},{5,4},{6,7},{7,6},{8,9},{9,8},{10,11... | collective-permute-start | bytes 1179656 | tf_op jit(solution)/shard_map/ppermute | solution.py:290
  72.8 16.1 %collective-permute-start.10 = (bf16[128,512]{1,0:T(8,128)(2,1)}, bf16[128,512]{1,0:T(8,128)(2,1)}, u32[]{:S(2)}, u32[]{:S(2)}) collective-permute-start(bf16[128,512]{1,0:T(8,128)(2,1)} %slice.163), channel_id=1, source_target_pairs={{1,13},{2,14},{3,15},{4,0},{6,2},{7,3},{8,4},{11,7},{13,9},{14,10}... | collective-permute-start | bytes 393224 | tf_op jit(solution)/shard_map/ppermute | solution.py:248
  76.4 11.2 %collective-permute-start.9 = (bf16[144,512]{1,0:T(8,128)(2,1)S(1)}, bf16[144,512]{1,0:T(8,128)(2,1)S(1)}, u32[]{:S(2)}, u32[]{:S(2)}) collective-permute-start(bf16[144,512]{1,0:T(8,128)(2,1)S(1)} %slice.161), channel_id=1, source_target_pairs={{0,4},{3,7},{5,9},{6,10},{7,11},{9,13},{10,14},{11,15},{12,0},{14,... | collective-permute-start | bytes 442376 | tf_op jit(solution)/shard_map/ppermute | solution.py:248
  77.8 19.4 %collective-permute-start.15 = (bf16[24,64,256]{2,1,0:T(8,128)(2,1)S(1)}, bf16[24,64,256]{2,1,0:T(8,128)(2,1)S(1)}, u32[]{:S(2)}, u32[]{:S(2)}) collective-permute-start(bf16[24,64,256]{2,1,0:T(8,128)(2,1)S(1)} %pad_maximum_fusion), channel_id=1, source_target_pairs={{0,3},{1,2},{2,1},{3,0},{4,7},{5,6},{6,5},{7,4},{8,11},{9,10},{10,... | collective-permute-start | bytes 2359304 | tf_op jit(solution)/shard_map/ppermute | solution.py:291
  118.9 20.9 %collective-permute-start.16 = (bf16[2,256,512]{2,1,0:T(8,128)(2,1)}, bf16[2,256,512]{2,1,0:T(8,128)(2,1)S(1)}, u32[]{:S(2)}, u32[]{:S(2)}) collective-permute-start(bf16[2,256,512]{2,1,0:T(8,128)(2,1)} %get-tuple-element.49), channel_id=1, source_target_pairs={{0,1},{1,2},{2,3},{3,0},{4,5},{5,6},{6,7},{7,4},{8,9},{9,10},{10,1... | collective-permute-start | bytes 1572872 | tf_op jit(solution)/shard_map/ppermute | solution.py:248
  127.1 15.1 %collective-permute-start.20 = (bf16[2,256,512]{2,1,0:T(8,128)(2,1)}, bf16[2,256,512]{2,1,0:T(8,128)(2,1)S(1)}, u32[]{:S(2)}, u32[]{:S(2)}) collective-permute-start(bf16[2,256,512]{2,1,0:T(8,128)(2,1)} %get-tuple-element.54), channel_id=1, source_target_pairs={{0,3},{1,0},{2,1},{3,2},{4,7},{5,4},{6,5},{7,6},{8,11},{9,8},{10,9... | collective-permute-start | bytes 1572872 | tf_op jit(solution)/shard_map/ppermute | solution.py:248
  127.1 41.5 %collective-permute-start.18 = (bf16[2,256,512]{2,1,0:T(8,128)(2,1)}, bf16[2,256,512]{2,1,0:T(8,128)(2,1)S(1)}, u32[]{:S(2)}, u32[]{:S(2)}) collective-permute-start(bf16[2,256,512]{2,1,0:T(8,128)(2,1)} %get-tuple-element.50), channel_id=1, source_target_pairs={{0,3},{1,0},{2,1},{3,2},{4,7},{5,4},{6,5},{7,6},{8,11},{9,8},{10,9... | collective-permute-start | bytes 1572872 | tf_op jit(solution)/shard_map/ppermute | solution.py:248
  127.1 45.3 %collective-permute-start.19 = (bf16[2,256,512]{2,1,0:T(8,128)(2,1)}, bf16[2,256,512]{2,1,0:T(8,128)(2,1)S(1)}, u32[]{:S(2)}, u32[]{:S(2)}) collective-permute-start(bf16[2,256,512]{2,1,0:T(8,128)(2,1)} %get-tuple-element.52), channel_id=1, source_target_pairs={{0,1},{1,2},{2,3},{3,0},{4,5},{5,6},{6,7},{7,4},{8,9},{9,10},{10,1... | collective-permute-start | bytes 1572872 | tf_op jit(solution)/shard_map/ppermute | solution.py:248
  142.2 6.3 %collective-permute-start.22 = (bf16[2,256,512]{2,1,0:T(8,128)(2,1)}, bf16[2,256,512]{2,1,0:T(8,128)(2,1)S(1)}, u32[]{:S(2)}, u32[]{:S(2)}) collective-permute-start(bf16[2,256,512]{2,1,0:T(8,128)(2,1)} %get-tuple-element.58), channel_id=1, source_target_pairs={{0,1},{3,0},{4,5},{5,6},{8,9},{9,10},{13,14},{16,17},{19,16},{20,2... | collective-permute-start | bytes 1572872 | tf_op jit(solution)/shard_map/ppermute | solution.py:248
  144.1 25.9 %collective-permute-start.17 = (bf16[2,256,512]{2,1,0:T(8,128)(2,1)S(1)}, bf16[2,256,512]{2,1,0:T(8,128)(2,1)S(1)}, u32[]{:S(2)}, u32[]{:S(2)}) collective-permute-start(bf16[2,256,512]{2,1,0:T(8,128)(2,1)S(1)} %add_convert_fusion.3), channel_id=1, source_target_pairs={{0,1},{1,2},{2,3},{3,0},{4,5},{5,6},{6,7},{7,4},{8,9},{9,10},{10,1... | collective-permute-start | bytes 1572872 | tf_op jit(solution)/shard_map/ppermute | solution.py:248
  146.7 13.7 %collective-permute-start.26 = (bf16[2,256,512]{2,1,0:T(8,128)(2,1)}, bf16[2,256,512]{2,1,0:T(8,128)(2,1)S(1)}, u32[]{:S(2)}, u32[]{:S(2)}) collective-permute-start(bf16[2,256,512]{2,1,0:T(8,128)(2,1)} %get-tuple-element.66), channel_id=1, source_target_pairs={{0,3},{4,7},{9,8},{13,12},{16,19},{20,23},{25,24},{29,28},{32,35},... | collective-permute-start | bytes 1572872 | tf_op jit(solution)/shard_map/ppermute | solution.py:248
  148.5 26.6 %collective-permute-start.21 = (bf16[2,256,512]{2,1,0:T(8,128)(2,1)S(1)}, bf16[2,256,512]{2,1,0:T(8,128)(2,1)S(1)}, u32[]{:S(2)}, u32[]{:S(2)}) collective-permute-start(bf16[2,256,512]{2,1,0:T(8,128)(2,1)S(1)} %add_convert_fusion.2), channel_id=1, source_target_pairs={{0,3},{1,0},{2,1},{3,2},{4,7},{5,4},{6,5},{7,6},{8,11},{9,8},{10,9... | collective-permute-start | bytes 1572872 | tf_op jit(solution)/shard_map/ppermute | solution.py:248
  160.4 26.0 %collective-permute-start.24 = (bf16[2,256,512]{2,1,0:T(8,128)(2,1)S(1)}, bf16[2,256,512]{2,1,0:T(8,128)(2,1)S(1)}, u32[]{:S(2)}, u32[]{:S(2)}) collective-permute-start(bf16[2,256,512]{2,1,0:T(8,128)(2,1)S(1)} %copy-done.21), channel_id=1, source_target_pairs={{2,1},{3,2},{4,7},{7,6},{8,11},{11,10},{12,15},{18,17},{19,18},{20... | collective-permute-start | bytes 1572872 | tf_op jit(solution)/shard_map/ppermute | solution.py:248
  168.6 23.0 %collective-permute-start.25 = (bf16[2,256,512]{2,1,0:T(8,128)(2,1)S(1)}, bf16[2,256,512]{2,1,0:T(8,128)(2,1)S(1)}, u32[]{:S(2)}, u32[]{:S(2)}) collective-permute-start(bf16[2,256,512]{2,1,0:T(8,128)(2,1)S(1)} %copy-done.20), channel_id=1, source_target_pairs={{1,2},{5,6},{10,11},{14,15},{17,18},{21,22},{26,27},{30,31},{33,34... | collective-permute-start | bytes 1572872 | tf_op jit(solution)/shard_map/ppermute | solution.py:248
  170.1 20.6 %collective-permute-start.23 = (bf16[2,256,512]{2,1,0:T(8,128)(2,1)S(1)}, bf16[2,256,512]{2,1,0:T(8,128)(2,1)S(1)}, u32[]{:S(2)}, u32[]{:S(2)}) collective-permute-start(bf16[2,256,512]{2,1,0:T(8,128)(2,1)S(1)} %add_convert_fusion.1), channel_id=1, source_target_pairs={{0,1},{1,2},{5,6},{6,7},{9,10},{10,11},{14,15},{16,17},{17,18},{21... | collective-permute-start | bytes 1572872 | tf_op jit(solution)/shard_map/ppermute | solution.py:248
  172.4 19.9 %collective-permute-start.27 = (bf16[2,256,512]{2,1,0:T(8,128)(2,1)S(1)}, bf16[2,256,512]{2,1,0:T(8,128)(2,1)S(1)}, u32[]{:S(2)}, u32[]{:S(2)}) collective-permute-start(bf16[2,256,512]{2,1,0:T(8,128)(2,1)S(1)} %add_convert_fusion), channel_id=1, source_target_pairs={{3,2},{7,6},{8,11},{12,15},{19,18},{23,22},{24,27},{28,31},{35,34}... | collective-permute-start | bytes 1572872 | tf_op jit(solution)/shard_map/ppermute | solution.py:248
  176.2 19.1 %collective-permute-start.28 = (bf16[2,256,512]{2,1,0:T(8,128)(2,1)S(1)}, bf16[2,256,512]{2,1,0:T(8,128)(2,1)S(1)}, u32[]{:S(2)}, u32[]{:S(2)}) collective-permute-start(bf16[2,256,512]{2,1,0:T(8,128)(2,1)S(1)} %pad_maximum_fusion.1), channel_id=1, source_target_pairs={{0,16},{1,17},{2,18},{3,19},{4,20},{5,21},{6,22},{7,23},{8,24},{9,... | collective-permute-start | bytes 1572872 | tf_op jit(solution)/shard_map/ppermute | solution.py:338
  193.4 10.5 %collective-permute-start.29 = (bf16[2,256,512]{2,1,0:T(8,128)(2,1)S(1)}, bf16[2,256,512]{2,1,0:T(8,128)(2,1)S(1)}, u32[]{:S(2)}, u32[]{:S(2)}) collective-permute-start(bf16[2,256,512]{2,1,0:T(8,128)(2,1)S(1)} %pad_maximum_fusion.2), channel_id=1, source_target_pairs={{1,17},{2,18},{6,22},{7,23},{10,26},{11,27},{15,31},{17,33},{18,34... | collective-permute-start | bytes 1572872 | tf_op jit(solution)/shard_map/ppermute | solution.py:338
  (20 other events, 489.3 us)

commit v6 on v5

--- a/solution.py
+++ b/solution.py
@@ -123,7 +123,7 @@
 def terms_kernel(place, ints, values, *refs):
     envs, across2b, ket_in, bra_own, rim0, rim1, rim2 = refs[:12], *refs[12:18]
     outs = refs[18:34]
-    env_all, ket, bra_all, total, rounded, todo, scale, env_sem, ket_sem, bra_sem, out_sem = refs[34:]
+    env_all, ket, bra_all, total, rounded, todo, scale, size, env_sem, ket_sem, bra_sem, out_sem = refs[34:]
     x = place[0] % NX
     copies = []
     for n in range(12):
@@ -152,32 +152,36 @@
                 total[at] = jnp.zeros((BB, KB), F32)
                 total[at + 1] = jnp.zeros((BB, KB), F32)
 
-    def listed(item, count):
+    size[0] = 0
+
+    @pl.loop(0, 12 * EPW)
+    def _(item):
         base = 64 * (item // EPW) + 8 * (item % EPW)
-        out_w, sp, s, code = ints[base], ints[base + 1], ints[base + 2], ints[base + 7]
+        out_w, s, code = ints[base], ints[base + 2], ints[base + 7]
         q_b = code - 1
         p_b, s_a = q_b + s // 2, s % 2
-        out_r, out_j = out_w // CH, out_w % CH
-        forward = (out_r % NX - my_x + NX) % NX
-        slot = jnp.where(forward == 1, 2, jnp.where(forward == 3, 1, jnp.where(forward == 2, 3, 0)))
-        out_a, out_b = charge(out_w)
-        low = live_at(out_r, 0, 0)
-        inside = low + live_at(out_r, 0, 1) + out_j * live_at(out_r, 1, 0)
-        position = jnp.where(p_b == 0, out_j * low, inside)
-        live = (code > 0) & (out_w // (CH * NX) == my_z) & (p_b < 2) & (a + s_a < SECS)
-        live = live & (live_at(out_r, p_b, out_j) == 1)
-
-        @pl.when(live)
+
+        @pl.when((code > 0) & (out_w // (CH * NX) == my_z) & (p_b < 2) & (a + s_a < SECS))
         def _():
-            todo[4 * count] = item // EPW
-            todo[4 * count + 1] = 2 * s + q_b
-            todo[4 * count + 2] = 6 * (s_a + out_a + 1) + 3 * (sp % 2) + p_b + out_b + sp // 2
-            todo[4 * count + 3] = 8 * slot + 2 * position + s_a
-            scale[count] = values[base + 3] + values[base + 4] + values[base + 5]
-
-        return count + jnp.where(live, 1, 0)
-
-    count = lax.fori_loop(0, 12 * EPW, listed, jnp.int32(0))
+            out_r, out_j = out_w // CH, out_w % CH
+
+            @pl.when(live_at(out_r, p_b, out_j) == 1)
+            def _():
+                sp, at = ints[base + 1], size[0]
+                forward = (out_r % NX - my_x + NX) % NX
+                slot = jnp.where(forward == 1, 2, jnp.where(forward == 3, 1, jnp.where(forward == 2, 3, 0)))
+                out_a, out_b = charge(out_w)
+                low = live_at(out_r, 0, 0)
+                inside = low + live_at(out_r, 0, 1) + out_j * live_at(out_r, 1, 0)
+                position = jnp.where(p_b == 0, out_j * low, inside)
+                todo[4 * at] = item // EPW
+                todo[4 * at + 1] = 2 * s + q_b
+                todo[4 * at + 2] = 6 * (s_a + out_a + 1) + 3 * (sp % 2) + p_b + out_b + sp // 2
+                todo[4 * at + 3] = 8 * slot + 2 * position + s_a
+                scale[at] = values[base + 3] + values[base + 4] + values[base + 5]
+                size[0] = at + 1
+
+    count = size[0]
     for n in range(TOGETHER - 1):
         for field in range(3):
             todo[4 * (count + n) + field] = 0
@@ -257,7 +261,8 @@
     three = {n for n in range(ROWS) if COUNT[n] > 2} | takers
     behind0 = sent(own0, z_up, same, everyone)
     ahead1 = sent(own1, z_down, same, everyone)
-    own2 = own2 + lax.ppermute(moving, "row", lent)
+    borrowed = lax.ppermute(moving, "row", lent)
+    own2 = own2 + borrowed
     behind1 = sent(after(own1, behind0, ahead1), z_up, same, everyone)
     ahead0 = sent(after(own0, behind0, ahead1), z_down, same, everyone)
     behind2 = sent(own2, z_up, same, three)
@@ -267,7 +272,7 @@
     across2a = sent(behind2[: HEAD + BB // 2], z_up, z_down, three)
     across2b = sent(ahead2[HEAD + BB // 2 :], z_down, z_up, three)
 
-    bra_in = lax.optimization_barrier((bra_mps, behind0, ahead1))[0]
+    bra_in = after(bra_mps, borrowed)
     bra_own, strip, strip_low, strip_high = pl.pallas_call(
         bra_kernel,
         in_specs=[smem, vmem],
@@ -307,6 +312,7 @@
             pltpu.VMEM((16, 2, BB, KB), BF),
             pltpu.SMEM((4 * (12 * EPW + TOGETHER),), jnp.int32),
             pltpu.SMEM((12 * EPW + TOGETHER,), F32),
+            pltpu.SMEM((1,), jnp.int32),
             pltpu.SemaphoreType.DMA((13,)),
             pltpu.SemaphoreType.DMA((4,)),
             pltpu.SemaphoreType.DMA((13,)),

time: 208 us -> 203 us (0.976); the launches traced: 208 us -> 200 us
  Pallas kernels: 29 us -> 24.3 us
  starting transfers between devices: 84.1 us -> 80.7 us
    pallas_call x1, Pallas kernels: 20.7 us -> 16.1 us  [body(): pl.pallas_call(terms_kernel, in_specs=[smem] * 3 + [hbm] * 18, out_specs=...]
    ppermute x22, starting transfers between devices: 64.8 us -> 61.5 us  [sent(): lax.ppermute(value, 'row', [(n, move(n)) for n in range(ROWS) if owner(n)...]
  transfers between devices with their start and end apart: 30 -> 30, of which waited for: 15 -> 15; matrix products, arithmetic and copies ran while one was open for 5% -> 6% of each run, Pallas kernels for 1% -> 1%
where the time goes in v6:
time: 203 us; the launch traced here: 200 us
  starting transfers between devices  80.7 us (40%)
  waiting for transfers between devices  78.7 us (39%)
  Pallas kernels  24.3 us (12%)
  other arithmetic  10.3 us (5%)
  local copies, waits for them, and re-layouts  5.32 us (3%)
    ppermute x22, starting transfers between devices, sent(): lax.ppermute(value, 'row', [(n, move(n)) for n in range(ROWS) if owner(n)...  61.5 us
    ppermute x22, waiting for transfers between devices, sent(): lax.ppermute(value, 'row', [(n, move(n)) for n in range(ROWS) if owner(n)...  46.5 us
    pallas_call x1, Pallas kernels, body(): pl.pallas_call(terms_kernel, in_specs=[smem] * 3 + [hbm] * 18, out_specs=...  16.1 us
    ppermute x1, waiting for transfers between devices, body(): lax.ppermute(strip_high, 'sec', down(2))  9 us
    ppermute x2, waiting for transfers between devices, body(): above.append(lax.ppermute(jnp.stack(raised), ('sec', 'row'), pairs))  8.55 us
    ppermute x1, waiting for transfers between devices, body(): lax.ppermute(jnp.concatenate([rim0, rim1]), 'row', [(n, n ^ 3) for n in r...  8.3 us
    ppermute x1, waiting for transfers between devices, body(): lax.ppermute(strip_low, 'sec', up(1))  5.01 us
    ppermute x1, starting transfers between devices, body(): rim1 = lax.ppermute(rim0, 'row', [(n, n ^ 1) for n in range(ROWS)])  4.77 us
  transfers between devices with their start and end apart: 30, of which 15 were waited for; matrix products, arithmetic and copies ran while one was open for 6% of the time, Pallas kernels for 1%

profile of v6, /device:TPU:36, one launch (start us, length us, event | category | flops | bytes accessed | tf_op | source)
XLA Modules:
  0.0 199.9 jit_solution(12176658134700402910)
XLA Ops:
  0.7 2.6 %shard_map.73 = (bf16[272,512]{1,0:T(8,128)(2,1)}, bf16[272,512]{1,0:T(8,128)(2,1)}, bf16[272,512]{1,0:T(8,128)(2,1)}, bf16[272,512]{1,0:T(8,128)(2,1)}) custom-call(s32[2]{0:T(128)} %pad_add_fusion.place, s32[2,16]{1,0:T(2,128)} %bitcast.46, s32[2,16]{1,0:T(2,128)} %bitcast.48, s32[3,2,8]{2,1,0:T(2,128)} %bitcast.50, f32[2,8]{1,0:T(2,128)} %coeffs.1, ...), custom_call_target="tpu_custom_call" | custom-call | tf_op jit(solution)/shard_map/pallas_call | solution.py:239
  3.2 3.1 %collective-permute-start = (bf16[272,512]{1,0:T(8,128)(2,1)}, bf16[272,512]{1,0:T(8,128)(2,1)S(1)}, u32[]{:S(2)}, u32[]{:S(2)}) collective-permute-start(bf16[272,512]{1,0:T(8,128)(2,1)} %get-tuple-element.39), channel_id=1, source_target_pairs={{2,3},{6,5},{11,8},{15,12},{18,19},{22,21},{27,24},{31,28},{34,35}... | collective-permute-start | bytes 835592 | tf_op jit(solution)/shard_map/ppermute | solution.py:264
  6.3 2.7 %collective-permute-start.1 = (bf16[272,512]{1,0:T(8,128)(2,1)}, bf16[272,512]{1,0:T(8,128)(2,1)S(1)}, u32[]{:S(2)}, u32[]{:S(2)}) collective-permute-start(bf16[272,512]{1,0:T(8,128)(2,1)} %get-tuple-element.41.refs_0_), channel_id=1, source_target_pairs={{0,4},{1,5},{2,6},{3,7},{4,8},{5,9},{6,10},{7,11},{8,12},{9,13},{1... | collective-permute-start | bytes 835592 | tf_op jit(solution)/shard_map/ppermute | solution.py:252
  13.6 2.4 %collective-permute-start.6 = (bf16[272,512]{1,0:T(8,128)(2,1)S(1)}, bf16[272,512]{1,0:T(8,128)(2,1)S(1)}, u32[]{:S(2)}, u32[]{:S(2)}) collective-permute-start(bf16[272,512]{1,0:T(8,128)(2,1)S(1)} %add.83.refs_2_), channel_id=1, source_target_pairs={{1,13},{2,14},{3,15},{5,1},{6,2},{7,3},{8,4},{10,6},{11,7},{12,8},... | collective-permute-start | bytes 835592 | tf_op jit(solution)/shard_map/ppermute | solution.py:252
  16.0 4.4 %collective-permute-start.4 = (bf16[272,512]{1,0:T(8,128)(2,1)S(1)}, bf16[272,512]{1,0:T(8,128)(2,1)S(1)}, u32[]{:S(2)}, u32[]{:S(2)}) collective-permute-start(bf16[272,512]{1,0:T(8,128)(2,1)S(1)} %add.83.refs_2_), channel_id=1, source_target_pairs={{1,5},{2,6},{3,7},{5,9},{6,10},{7,11},{8,12},{10,14},{11,15},{12,0... | collective-permute-start | bytes 835592 | tf_op jit(solution)/shard_map/ppermute | solution.py:252
  20.4 2.4 %collective-permute-done.1.refs_3_ = bf16[272,512]{1,0:T(8,128)(2,1)S(1)} collective-permute-done((bf16[272,512]{1,0:T(8,128)(2,1)}, bf16[272,512]{1,0:T(8,128)(2,1)S(1)}, u32[]{:S(2)}, u32[]{:S(2)}) %collective-permute-start.1) | collective-permute-done | bytes 278560 | tf_op jit(solution)/shard_map/ppermute | solution.py:252
  22.8 1.9 collective-permute-done.2.refs_7_
  24.7 2.7 %collective-permute-start.3 = (bf16[272,512]{1,0:T(8,128)(2,1)}, bf16[272,512]{1,0:T(8,128)(2,1)S(1)}, u32[]{:S(2)}, u32[]{:S(2)}) collective-permute-start(bf16[272,512]{1,0:T(8,128)(2,1)} %get-tuple-element.40.refs_1_), channel_id=1, source_target_pairs={{0,4},{1,5},{2,6},{3,7},{4,8},{5,9},{6,10},{7,11},{8,12},{9,13},{1... | collective-permute-start | bytes 835592 | tf_op jit(solution)/shard_map/ppermute | solution.py:252
  27.4 2.5 %shard_map.74 = (bf16[6,256,256]{2,1,0:T(8,128)(2,1)}, bf16[6,64,256]{2,1,0:T(8,128)(2,1)}, bf16[3,64,256]{2,1,0:T(8,128)(2,1)}, bf16[3,64,256]{2,1,0:T(8,128)(2,1)}) custom-call(s32[2]{0:T(128)} %pad_add_fusion.place, bf16[4,2,256,256]{3,2,1,0:T(8,128)(2,1)} %bitcast.45), custom_call_target="tpu_custom_call" | custom-call | tf_op jit(solution)/shard_map/pallas_call | solution.py:276
  31.8 3.6 %collective-permute-start.12 = (bf16[6,64,256]{2,1,0:T(8,128)(2,1)}, bf16[6,64,256]{2,1,0:T(8,128)(2,1)S(1)}, u32[]{:S(2)}, u32[]{:S(2)}) collective-permute-start(bf16[6,64,256]{2,1,0:T(8,128)(2,1)} %get-tuple-element.45), channel_id=1, source_target_pairs={{16,0},{32,16},{48,32},{64,48},{80,64},{96,80},{112,96},{128,112},... | collective-permute-start | bytes 589832 | tf_op jit(solution)/shard_map/ppermute | solution.py:292
  35.5 5.0 %collective-permute-done.11 = bf16[3,64,256]{2,1,0:T(8,128)(2,1)S(1)} collective-permute-done((bf16[3,64,256]{2,1,0:T(8,128)(2,1)}, bf16[3,64,256]{2,1,0:T(8,128)(2,1)S(1)}, u32[]{:S(2)}, u32[]{:S(2)}) %collective-permute-start.11) | collective-permute-done | bytes 98336 | tf_op jit(solution)/shard_map/ppermute | solution.py:291
  40.5 5.3 %collective-permute-start.5 = (bf16[272,512]{1,0:T(8,128)(2,1)}, bf16[272,512]{1,0:T(8,128)(2,1)S(1)}, u32[]{:S(2)}, u32[]{:S(2)}) collective-permute-start(bf16[272,512]{1,0:T(8,128)(2,1)} %get-tuple-element.41.refs_0_), channel_id=1, source_target_pairs={{0,12},{1,13},{2,14},{3,15},{4,0},{5,1},{6,2},{7,3},{8,4},{9,5},{1... | collective-permute-start | bytes 835592 | tf_op jit(solution)/shard_map/ppermute | solution.py:252
  47.7 9.0 %collective-permute-done.13 = bf16[3,64,256]{2,1,0:T(8,128)(2,1)S(1)} collective-permute-done((bf16[3,64,256]{2,1,0:T(8,128)(2,1)}, bf16[3,64,256]{2,1,0:T(8,128)(2,1)S(1)}, u32[]{:S(2)}, u32[]{:S(2)}) %collective-permute-start.13) | collective-permute-done | bytes 98336 | tf_op jit(solution)/shard_map/ppermute | solution.py:293
  56.8 4.1 %collective-permute-start.8 = (bf16[272,512]{1,0:T(8,128)(2,1)S(1)}, bf16[272,512]{1,0:T(8,128)(2,1)S(1)}, u32[]{:S(2)}, u32[]{:S(2)}) collective-permute-start(bf16[272,512]{1,0:T(8,128)(2,1)S(1)} %collective-permute-done.2.refs_7_), channel_id=1, source_target_pairs={{0,12},{1,13},{2,14},{3,15},{4,0},{5,1},{6,2},{7,3},{8,4},{9,5},{1... | collective-permute-start | bytes 835592 | tf_op jit(solution)/shard_map/ppermute | solution.py:252
  60.9 4.8 %collective-permute-start.14 = (bf16[12,64,256]{2,1,0:T(8,128)(2,1)S(1)}, bf16[12,64,256]{2,1,0:T(8,128)(2,1)S(1)}, u32[]{:S(2)}, u32[]{:S(2)}) collective-permute-start(bf16[12,64,256]{2,1,0:T(8,128)(2,1)S(1)} %constant_dynamic-update-slice_fusion.refs_15_), channel_id=1, source_target_pairs={{0,1},{1,0},{2,3},{3,2},{4,5},{5,4},{6,7},{7,6},{8,9},{9,8},{10,11... | collective-permute-start | bytes 1179656 | tf_op jit(solution)/shard_map/ppermute | solution.py:295
  66.4 6.4 %collective-permute-done.7.refs_9_ = bf16[272,512]{1,0:T(8,128)(2,1)S(1)} collective-permute-done((bf16[272,512]{1,0:T(8,128)(2,1)S(1)}, bf16[272,512]{1,0:T(8,128)(2,1)S(1)}, u32[]{:S(2)}, u32[]{:S(2)}) %collective-permute-start.7) | collective-permute-done | bytes 278560 | tf_op jit(solution)/shard_map/ppermute | solution.py:252
  72.8 3.6 %collective-permute-start.10 = (bf16[128,512]{1,0:T(8,128)(2,1)}, bf16[128,512]{1,0:T(8,128)(2,1)}, u32[]{:S(2)}, u32[]{:S(2)}) collective-permute-start(bf16[128,512]{1,0:T(8,128)(2,1)} %slice.163), channel_id=1, source_target_pairs={{1,13},{2,14},{3,15},{4,0},{6,2},{7,3},{8,4},{11,7},{13,9},{14,10}... | collective-permute-start | bytes 393224 | tf_op jit(solution)/shard_map/ppermute | solution.py:252
  79.4 8.1 %collective-permute-done.9.refs_11_ = bf16[144,512]{1,0:T(8,128)(2,1)S(1)} collective-permute-done((bf16[144,512]{1,0:T(8,128)(2,1)S(1)}, bf16[144,512]{1,0:T(8,128)(2,1)S(1)}, u32[]{:S(2)}, u32[]{:S(2)}) %collective-permute-start.9) | collective-permute-done | bytes 147488 | tf_op jit(solution)/shard_map/ppermute | solution.py:252
  88.9 8.3 %collective-permute-done.15.refs_17_ = bf16[24,64,256]{2,1,0:T(8,128)(2,1)S(1)} collective-permute-done((bf16[24,64,256]{2,1,0:T(8,128)(2,1)S(1)}, bf16[24,64,256]{2,1,0:T(8,128)(2,1)S(1)}, u32[]{:S(2)}, u32[]{:S(2)}) %collective-permute-start.15) | collective-permute-done | bytes 786464 | tf_op jit(solution)/shard_map/ppermute | solution.py:296
  98.1 16.1 %shard_map.75 = (bf16[2,256,512]{2,1,0:T(8,128)(2,1)}, bf16[2,256,512]{2,1,0:T(8,128)(2,1)}, bf16[2,256,512]{2,1,0:T(8,128)(2,1)}, bf16[2,256,512]{2,1,0:T(8,128...) custom-call(s32[2]{0:T(128)} %pad_add_fusion.place, ...), custom_call_target="tpu_custom_call" | custom-call | tf_op jit(solution)/shard_map/pallas_call | solution.py:302
  114.2 3.1 %collective-permute-start.16 = (bf16[2,256,512]{2,1,0:T(8,128)(2,1)}, bf16[2,256,512]{2,1,0:T(8,128)(2,1)S(1)}, u32[]{:S(2)}, u32[]{:S(2)}) collective-permute-start(bf16[2,256,512]{2,1,0:T(8,128)(2,1)} %get-tuple-element.49), channel_id=1, source_target_pairs={{0,1},{1,2},{2,3},{3,0},{4,5},{5,6},{6,7},{7,4},{8,9},{9,10},{10,1... | collective-permute-start | bytes 1572872 | tf_op jit(solution)/shard_map/ppermute | solution.py:252
  119.3 10.6 %collective-permute-done.16 = bf16[2,256,512]{2,1,0:T(8,128)(2,1)S(1)} collective-permute-done((bf16[2,256,512]{2,1,0:T(8,128)(2,1)}, bf16[2,256,512]{2,1,0:T(8,128)(2,1)S(1)}, u32[]{:S(2)}, u32[]{:S(2)}) %collective-permute-start.16) | collective-permute-done | bytes 524320 | tf_op jit(solution)/shard_map/ppermute | solution.py:252
  129.9 2.4 %collective-permute-done.20 = bf16[2,256,512]{2,1,0:T(8,128)(2,1)S(1)} collective-permute-done((bf16[2,256,512]{2,1,0:T(8,128)(2,1)}, bf16[2,256,512]{2,1,0:T(8,128)(2,1)S(1)}, u32[]{:S(2)}, u32[]{:S(2)}) %collective-permute-start.20) | collective-permute-done | bytes 524320 | tf_op jit(solution)/shard_map/ppermute | solution.py:252
  134.3 4.4 %collective-permute-start.17 = (bf16[2,256,512]{2,1,0:T(8,128)(2,1)S(1)}, bf16[2,256,512]{2,1,0:T(8,128)(2,1)S(1)}, u32[]{:S(2)}, u32[]{:S(2)}) collective-permute-start(bf16[2,256,512]{2,1,0:T(8,128)(2,1)S(1)} %add_convert_fusion.3), channel_id=1, source_target_pairs={{0,1},{1,2},{2,3},{3,0},{4,5},{5,6},{6,7},{7,4},{8,9},{9,10},{10,1... | collective-permute-start | bytes 1572872 | tf_op jit(solution)/shard_map/ppermute | solution.py:252
  140.5 13.5 %collective-permute-start.21 = (bf16[2,256,512]{2,1,0:T(8,128)(2,1)S(1)}, bf16[2,256,512]{2,1,0:T(8,128)(2,1)S(1)}, u32[]{:S(2)}, u32[]{:S(2)}) collective-permute-start(bf16[2,256,512]{2,1,0:T(8,128)(2,1)S(1)} %add_convert_fusion.2), channel_id=1, source_target_pairs={{0,3},{1,0},{2,1},{3,2},{4,7},{5,4},{6,5},{7,6},{8,11},{9,8},{10,9... | collective-permute-start | bytes 1572872 | tf_op jit(solution)/shard_map/ppermute | solution.py:252
  155.2 5.1 %collective-permute-start.24 = (bf16[2,256,512]{2,1,0:T(8,128)(2,1)S(1)}, bf16[2,256,512]{2,1,0:T(8,128)(2,1)S(1)}, u32[]{:S(2)}, u32[]{:S(2)}) collective-permute-start(bf16[2,256,512]{2,1,0:T(8,128)(2,1)S(1)} %copy-done.21), channel_id=1, source_target_pairs={{2,1},{3,2},{4,7},{7,6},{8,11},{11,10},{12,15},{18,17},{19,18},{20... | collective-permute-start | bytes 1572872 | tf_op jit(solution)/shard_map/ppermute | solution.py:252
  168.1 1.9 collective-permute-start.28
  170.1 8.2 %collective-permute-done.24 = bf16[2,256,512]{2,1,0:T(8,128)(2,1)S(1)} collective-permute-done((bf16[2,256,512]{2,1,0:T(8,128)(2,1)S(1)}, bf16[2,256,512]{2,1,0:T(8,128)(2,1)S(1)}, u32[]{:S(2)}, u32[]{:S(2)}) %collective-permute-start.24) | collective-permute-done | bytes 524320 | tf_op jit(solution)/shard_map/ppermute | solution.py:252
  178.3 4.3 %collective-permute-done.23 = bf16[2,256,512]{2,1,0:T(8,128)(2,1)S(1)} collective-permute-done((bf16[2,256,512]{2,1,0:T(8,128)(2,1)S(1)}, bf16[2,256,512]{2,1,0:T(8,128)(2,1)S(1)}, u32[]{:S(2)}, u32[]{:S(2)}) %collective-permute-start.23) | collective-permute-done | bytes 524320 | tf_op jit(solution)/shard_map/ppermute | solution.py:252
  185.4 1.9 collective-permute-start.29
  187.3 8.6 %collective-permute-done.29.refs_5_ = bf16[2,256,512]{2,1,0:T(8,128)(2,1)S(1)} collective-permute-done((bf16[2,256,512]{2,1,0:T(8,128)(2,1)S(1)}, bf16[2,256,512]{2,1,0:T(8,128)(2,1)S(1)}, u32[]{:S(2)}, u32[]{:S(2)}) %collective-permute-start.29) | collective-permute-done | bytes 524320 | tf_op jit(solution)/shard_map/ppermute | solution.py:344
  196.7 3.2 %shard_map.76 = bf16[4,256,512]{2,1,0:T(8,128)(2,1)} custom-call(s32[2]{0:T(128)} %pad_add_fusion.place, s32[2,16]{1,0:T(2,128)} %bitcast.47, s32[2,16]{1,0:T(2,128)} %bitcast.49, f32[256,512]{1,0:T(8,128)} %get-tuple-element.72.refs_0_, f32[256,512]{1,0:T(8,128)} %get-tuple-element.74.refs_1_, f32[256,512]{1,0:T(8,128)} %get-tuple-element.68.refs_2_, ...), custom_call_target="tpu_custom_call" | custom-call | tf_op jit(solution)/shard_map/pallas_call | solution.py:347
  (107 shorter events, 33.3 us)
Async XLA Ops:
  3.2 9.3 %collective-permute-start = (bf16[272,512]{1,0:T(8,128)(2,1)}, bf16[272,512]{1,0:T(8,128)(2,1)S(1)}, u32[]{:S(2)}, u32[]{:S(2)}) collective-permute-start(bf16[272,512]{1,0:T(8,128)(2,1)} %get-tuple-element.39), channel_id=1, source_target_pairs={{2,3},{6,5},{11,8},{15,12},{18,19},{22,21},{27,24},{31,28},{34,35}... | collective-permute-start | bytes 835592 | tf_op jit(solution)/shard_map/ppermute | solution.py:264
  6.3 16.4 %collective-permute-start.1 = (bf16[272,512]{1,0:T(8,128)(2,1)}, bf16[272,512]{1,0:T(8,128)(2,1)S(1)}, u32[]{:S(2)}, u32[]{:S(2)}) collective-permute-start(bf16[272,512]{1,0:T(8,128)(2,1)} %get-tuple-element.41.refs_0_), channel_id=1, source_target_pairs={{0,4},{1,5},{2,6},{3,7},{4,8},{5,9},{6,10},{7,11},{8,12},{9,13},{1... | collective-permute-start | bytes 835592 | tf_op jit(solution)/shard_map/ppermute | solution.py:252
  9.0 15.7 %collective-permute-start.2 = (bf16[272,512]{1,0:T(8,128)(2,1)}, bf16[272,512]{1,0:T(8,128)(2,1)S(1)}, u32[]{:S(2)}, u32[]{:S(2)}) collective-permute-start(bf16[272,512]{1,0:T(8,128)(2,1)} %get-tuple-element.40.refs_1_), channel_id=1, source_target_pairs={{0,12},{1,13},{2,14},{3,15},{4,0},{5,1},{6,2},{7,3},{8,4},{9,5},{1... | collective-permute-start | bytes 835592 | tf_op jit(solution)/shard_map/ppermute | solution.py:252
  13.6 83.6 %copy-start.1 = (bf16[272,512]{1,0:T(8,128)(2,1)}, bf16[272,512]{1,0:T(8,128)(2,1)S(1)}, u32[]{:S(2)}) copy-start(bf16[272,512]{1,0:T(8,128)(2,1)S(1)} %add.83.refs_2_) | copy-start | bytes 835588
  13.6 43.2 %collective-permute-start.6 = (bf16[272,512]{1,0:T(8,128)(2,1)S(1)}, bf16[272,512]{1,0:T(8,128)(2,1)S(1)}, u32[]{:S(2)}, u32[]{:S(2)}) collective-permute-start(bf16[272,512]{1,0:T(8,128)(2,1)S(1)} %add.83.refs_2_), channel_id=1, source_target_pairs={{1,13},{2,14},{3,15},{5,1},{6,2},{7,3},{8,4},{10,6},{11,7},{12,8},... | collective-permute-start | bytes 835592 | tf_op jit(solution)/shard_map/ppermute | solution.py:252
  16.0 45.0 %collective-permute-start.4 = (bf16[272,512]{1,0:T(8,128)(2,1)S(1)}, bf16[272,512]{1,0:T(8,128)(2,1)S(1)}, u32[]{:S(2)}, u32[]{:S(2)}) collective-permute-start(bf16[272,512]{1,0:T(8,128)(2,1)S(1)} %add.83.refs_2_), channel_id=1, source_target_pairs={{1,5},{2,6},{3,7},{5,9},{6,10},{7,11},{8,12},{10,14},{11,15},{12,0... | collective-permute-start | bytes 835592 | tf_op jit(solution)/shard_map/ppermute | solution.py:252
  22.8 74.4 %copy-start.13 = (bf16[272,512]{1,0:T(8,128)(2,1)}, bf16[272,512]{1,0:T(8,128)(2,1)S(1)}, u32[]{:S(2)}) copy-start(bf16[272,512]{1,0:T(8,128)(2,1)S(1)} %collective-permute-done.1.refs_3_) | copy-start | bytes 835588
  24.7 51.7 %collective-permute-start.3 = (bf16[272,512]{1,0:T(8,128)(2,1)}, bf16[272,512]{1,0:T(8,128)(2,1)S(1)}, u32[]{:S(2)}, u32[]{:S(2)}) collective-permute-start(bf16[272,512]{1,0:T(8,128)(2,1)} %get-tuple-element.40.refs_1_), channel_id=1, source_target_pairs={{0,4},{1,5},{2,6},{3,7},{4,8},{5,9},{6,10},{7,11},{8,12},{9,13},{1... | collective-permute-start | bytes 835592 | tf_op jit(solution)/shard_map/ppermute | solution.py:252
  29.9 10.6 %collective-permute-start.11 = (bf16[3,64,256]{2,1,0:T(8,128)(2,1)}, bf16[3,64,256]{2,1,0:T(8,128)(2,1)S(1)}, u32[]{:S(2)}, u32[]{:S(2)}) collective-permute-start(bf16[3,64,256]{2,1,0:T(8,128)(2,1)} %get-tuple-element.44), channel_id=1, source_target_pairs={{0,16},{16,32},{32,48},{48,64},{64,80},{80,96},{96,112},{112,128},... | collective-permute-start | bytes 294920 | tf_op jit(solution)/shard_map/ppermute | solution.py:291
  31.8 13.9 %collective-permute-start.12 = (bf16[6,64,256]{2,1,0:T(8,128)(2,1)}, bf16[6,64,256]{2,1,0:T(8,128)(2,1)S(1)}, u32[]{:S(2)}, u32[]{:S(2)}) collective-permute-start(bf16[6,64,256]{2,1,0:T(8,128)(2,1)} %get-tuple-element.45), channel_id=1, source_target_pairs={{16,0},{32,16},{48,32},{64,48},{80,64},{96,80},{112,96},{128,112},... | collective-permute-start | bytes 589832 | tf_op jit(solution)/shard_map/ppermute | solution.py:292
  40.5 37.5 %collective-permute-start.5 = (bf16[272,512]{1,0:T(8,128)(2,1)}, bf16[272,512]{1,0:T(8,128)(2,1)S(1)}, u32[]{:S(2)}, u32[]{:S(2)}) collective-permute-start(bf16[272,512]{1,0:T(8,128)(2,1)} %get-tuple-element.41.refs_0_), channel_id=1, source_target_pairs={{0,12},{1,13},{2,14},{3,15},{4,0},{5,1},{6,2},{7,3},{8,4},{9,5},{1... | collective-permute-start | bytes 835592 | tf_op jit(solution)/shard_map/ppermute | solution.py:252
  45.7 10.9 %collective-permute-start.13 = (bf16[3,64,256]{2,1,0:T(8,128)(2,1)}, bf16[3,64,256]{2,1,0:T(8,128)(2,1)S(1)}, u32[]{:S(2)}, u32[]{:S(2)}) collective-permute-start(bf16[3,64,256]{2,1,0:T(8,128)(2,1)} %get-tuple-element.46), channel_id=1, source_target_pairs={{32,0},{48,16},{64,32},{80,48},{96,64},{112,80},{128,96},{144,112}... | collective-permute-start | bytes 294920 | tf_op jit(solution)/shard_map/ppermute | solution.py:293
  56.7 16.1 %collective-permute-start.7 = (bf16[272,512]{1,0:T(8,128)(2,1)S(1)}, bf16[272,512]{1,0:T(8,128)(2,1)S(1)}, u32[]{:S(2)}, u32[]{:S(2)}) collective-permute-start(bf16[272,512]{1,0:T(8,128)(2,1)S(1)} %collective-permute-done.1.refs_3_), channel_id=1, source_target_pairs={{0,4},{1,5},{2,6},{3,7},{4,8},{5,9},{6,10},{7,11},{8,12},{9,13},{1... | collective-permute-start | bytes 835592 | tf_op jit(solution)/shard_map/ppermute | solution.py:252
  56.8 21.2 %collective-permute-start.8 = (bf16[272,512]{1,0:T(8,128)(2,1)S(1)}, bf16[272,512]{1,0:T(8,128)(2,1)S(1)}, u32[]{:S(2)}, u32[]{:S(2)}) collective-permute-start(bf16[272,512]{1,0:T(8,128)(2,1)S(1)} %collective-permute-done.2.refs_7_), channel_id=1, source_target_pairs={{0,12},{1,13},{2,14},{3,15},{4,0},{5,1},{6,2},{7,3},{8,4},{9,5},{1... | collective-permute-start | bytes 835592 | tf_op jit(solution)/shard_map/ppermute | solution.py:252
  60.9 16.7 %collective-permute-start.14 = (bf16[12,64,256]{2,1,0:T(8,128)(2,1)S(1)}, bf16[12,64,256]{2,1,0:T(8,128)(2,1)S(1)}, u32[]{:S(2)}, u32[]{:S(2)}) collective-permute-start(bf16[12,64,256]{2,1,0:T(8,128)(2,1)S(1)} %constant_dynamic-update-slice_fusion.refs_15_), channel_id=1, source_target_pairs={{0,1},{1,0},{2,3},{3,2},{4,5},{5,4},{6,7},{7,6},{8,9},{9,8},{10,11... | collective-permute-start | bytes 1179656 | tf_op jit(solution)/shard_map/ppermute | solution.py:295
  72.8 16.1 %collective-permute-start.10 = (bf16[128,512]{1,0:T(8,128)(2,1)}, bf16[128,512]{1,0:T(8,128)(2,1)}, u32[]{:S(2)}, u32[]{:S(2)}) collective-permute-start(bf16[128,512]{1,0:T(8,128)(2,1)} %slice.163), channel_id=1, source_target_pairs={{1,13},{2,14},{3,15},{4,0},{6,2},{7,3},{8,4},{11,7},{13,9},{14,10}... | collective-permute-start | bytes 393224 | tf_op jit(solution)/shard_map/ppermute | solution.py:252
  76.4 11.2 %collective-permute-start.9 = (bf16[144,512]{1,0:T(8,128)(2,1)S(1)}, bf16[144,512]{1,0:T(8,128)(2,1)S(1)}, u32[]{:S(2)}, u32[]{:S(2)}) collective-permute-start(bf16[144,512]{1,0:T(8,128)(2,1)S(1)} %slice.161), channel_id=1, source_target_pairs={{0,4},{3,7},{5,9},{6,10},{7,11},{9,13},{10,14},{11,15},{12,0},{14,... | collective-permute-start | bytes 442376 | tf_op jit(solution)/shard_map/ppermute | solution.py:252
  77.8 19.4 %collective-permute-start.15 = (bf16[24,64,256]{2,1,0:T(8,128)(2,1)S(1)}, bf16[24,64,256]{2,1,0:T(8,128)(2,1)S(1)}, u32[]{:S(2)}, u32[]{:S(2)}) collective-permute-start(bf16[24,64,256]{2,1,0:T(8,128)(2,1)S(1)} %pad_maximum_fusion), channel_id=1, source_target_pairs={{0,3},{1,2},{2,1},{3,0},{4,7},{5,6},{6,5},{7,4},{8,11},{9,10},{10,... | collective-permute-start | bytes 2359304 | tf_op jit(solution)/shard_map/ppermute | solution.py:296
  114.2 15.8 %collective-permute-start.16 = (bf16[2,256,512]{2,1,0:T(8,128)(2,1)}, bf16[2,256,512]{2,1,0:T(8,128)(2,1)S(1)}, u32[]{:S(2)}, u32[]{:S(2)}) collective-permute-start(bf16[2,256,512]{2,1,0:T(8,128)(2,1)} %get-tuple-element.49), channel_id=1, source_target_pairs={{0,1},{1,2},{2,3},{3,0},{4,5},{5,6},{6,7},{7,4},{8,9},{9,10},{10,1... | collective-permute-start | bytes 1572872 | tf_op jit(solution)/shard_map/ppermute | solution.py:252
  117.2 15.1 %collective-permute-start.20 = (bf16[2,256,512]{2,1,0:T(8,128)(2,1)}, bf16[2,256,512]{2,1,0:T(8,128)(2,1)S(1)}, u32[]{:S(2)}, u32[]{:S(2)}) collective-permute-start(bf16[2,256,512]{2,1,0:T(8,128)(2,1)} %get-tuple-element.54), channel_id=1, source_target_pairs={{0,3},{1,0},{2,1},{3,2},{4,7},{5,4},{6,5},{7,6},{8,11},{9,8},{10,9... | collective-permute-start | bytes 1572872 | tf_op jit(solution)/shard_map/ppermute | solution.py:252
  117.3 43.3 %collective-permute-start.18 = (bf16[2,256,512]{2,1,0:T(8,128)(2,1)}, bf16[2,256,512]{2,1,0:T(8,128)(2,1)S(1)}, u32[]{:S(2)}, u32[]{:S(2)}) collective-permute-start(bf16[2,256,512]{2,1,0:T(8,128)(2,1)} %get-tuple-element.50), channel_id=1, source_target_pairs={{0,3},{1,0},{2,1},{3,2},{4,7},{5,4},{6,5},{7,6},{8,11},{9,8},{10,9... | collective-permute-start | bytes 1572872 | tf_op jit(solution)/shard_map/ppermute | solution.py:252
  118.7 45.6 %collective-permute-start.19 = (bf16[2,256,512]{2,1,0:T(8,128)(2,1)}, bf16[2,256,512]{2,1,0:T(8,128)(2,1)S(1)}, u32[]{:S(2)}, u32[]{:S(2)}) collective-permute-start(bf16[2,256,512]{2,1,0:T(8,128)(2,1)} %get-tuple-element.52), channel_id=1, source_target_pairs={{0,1},{1,2},{2,3},{3,0},{4,5},{5,6},{6,7},{7,4},{8,9},{9,10},{10,1... | collective-permute-start | bytes 1572872 | tf_op jit(solution)/shard_map/ppermute | solution.py:252
  132.3 8.2 %collective-permute-start.22 = (bf16[2,256,512]{2,1,0:T(8,128)(2,1)}, bf16[2,256,512]{2,1,0:T(8,128)(2,1)S(1)}, u32[]{:S(2)}, u32[]{:S(2)}) collective-permute-start(bf16[2,256,512]{2,1,0:T(8,128)(2,1)} %get-tuple-element.58), channel_id=1, source_target_pairs={{0,1},{3,0},{4,5},{5,6},{8,9},{9,10},{13,14},{16,17},{19,16},{20,2... | collective-permute-start | bytes 1572872 | tf_op jit(solution)/shard_map/ppermute | solution.py:252
  134.3 27.8 %collective-permute-start.17 = (bf16[2,256,512]{2,1,0:T(8,128)(2,1)S(1)}, bf16[2,256,512]{2,1,0:T(8,128)(2,1)S(1)}, u32[]{:S(2)}, u32[]{:S(2)}) collective-permute-start(bf16[2,256,512]{2,1,0:T(8,128)(2,1)S(1)} %add_convert_fusion.3), channel_id=1, source_target_pairs={{0,1},{1,2},{2,3},{3,0},{4,5},{5,6},{6,7},{7,4},{8,9},{9,10},{10,1... | collective-permute-start | bytes 1572872 | tf_op jit(solution)/shard_map/ppermute | solution.py:252
  138.6 16.6 %collective-permute-start.26 = (bf16[2,256,512]{2,1,0:T(8,128)(2,1)}, bf16[2,256,512]{2,1,0:T(8,128)(2,1)S(1)}, u32[]{:S(2)}, u32[]{:S(2)}) collective-permute-start(bf16[2,256,512]{2,1,0:T(8,128)(2,1)} %get-tuple-element.66), channel_id=1, source_target_pairs={{0,3},{4,7},{9,8},{13,12},{16,19},{20,23},{25,24},{29,28},{32,35},... | collective-permute-start | bytes 1572872 | tf_op jit(solution)/shard_map/ppermute | solution.py:252
  140.5 26.6 %collective-permute-start.21 = (bf16[2,256,512]{2,1,0:T(8,128)(2,1)S(1)}, bf16[2,256,512]{2,1,0:T(8,128)(2,1)S(1)}, u32[]{:S(2)}, u32[]{:S(2)}) collective-permute-start(bf16[2,256,512]{2,1,0:T(8,128)(2,1)S(1)} %add_convert_fusion.2), channel_id=1, source_target_pairs={{0,3},{1,0},{2,1},{3,2},{4,7},{5,4},{6,5},{7,6},{8,11},{9,8},{10,9... | collective-permute-start | bytes 1572872 | tf_op jit(solution)/shard_map/ppermute | solution.py:252
  155.2 23.1 %collective-permute-start.24 = (bf16[2,256,512]{2,1,0:T(8,128)(2,1)S(1)}, bf16[2,256,512]{2,1,0:T(8,128)(2,1)S(1)}, u32[]{:S(2)}, u32[]{:S(2)}) collective-permute-start(bf16[2,256,512]{2,1,0:T(8,128)(2,1)S(1)} %copy-done.21), channel_id=1, source_target_pairs={{2,1},{3,2},{4,7},{7,6},{8,11},{11,10},{12,15},{18,17},{19,18},{20... | collective-permute-start | bytes 1572872 | tf_op jit(solution)/shard_map/ppermute | solution.py:252
  160.6 23.1 %collective-permute-start.25 = (bf16[2,256,512]{2,1,0:T(8,128)(2,1)S(1)}, bf16[2,256,512]{2,1,0:T(8,128)(2,1)S(1)}, u32[]{:S(2)}, u32[]{:S(2)}) collective-permute-start(bf16[2,256,512]{2,1,0:T(8,128)(2,1)S(1)} %copy-done.20), channel_id=1, source_target_pairs={{1,2},{5,6},{10,11},{14,15},{17,18},{21,22},{26,27},{30,31},{33,34... | collective-permute-start | bytes 1572872 | tf_op jit(solution)/shard_map/ppermute | solution.py:252
  162.0 20.6 %collective-permute-start.23 = (bf16[2,256,512]{2,1,0:T(8,128)(2,1)S(1)}, bf16[2,256,512]{2,1,0:T(8,128)(2,1)S(1)}, u32[]{:S(2)}, u32[]{:S(2)}) collective-permute-start(bf16[2,256,512]{2,1,0:T(8,128)(2,1)S(1)} %add_convert_fusion.1), channel_id=1, source_target_pairs={{0,1},{1,2},{5,6},{6,7},{9,10},{10,11},{14,15},{16,17},{17,18},{21... | collective-permute-start | bytes 1572872 | tf_op jit(solution)/shard_map/ppermute | solution.py:252
  164.4 20.0 %collective-permute-start.27 = (bf16[2,256,512]{2,1,0:T(8,128)(2,1)S(1)}, bf16[2,256,512]{2,1,0:T(8,128)(2,1)S(1)}, u32[]{:S(2)}, u32[]{:S(2)}) collective-permute-start(bf16[2,256,512]{2,1,0:T(8,128)(2,1)S(1)} %add_convert_fusion), channel_id=1, source_target_pairs={{3,2},{7,6},{8,11},{12,15},{19,18},{23,22},{24,27},{28,31},{35,34}... | collective-permute-start | bytes 1572872 | tf_op jit(solution)/shard_map/ppermute | solution.py:252
  168.1 19.2 %collective-permute-start.28 = (bf16[2,256,512]{2,1,0:T(8,128)(2,1)S(1)}, bf16[2,256,512]{2,1,0:T(8,128)(2,1)S(1)}, u32[]{:S(2)}, u32[]{:S(2)}) collective-permute-start(bf16[2,256,512]{2,1,0:T(8,128)(2,1)S(1)} %pad_maximum_fusion.1), channel_id=1, source_target_pairs={{0,16},{1,17},{2,18},{3,19},{4,20},{5,21},{6,22},{7,23},{8,24},{9,... | collective-permute-start | bytes 1572872 | tf_op jit(solution)/shard_map/ppermute | solution.py:344
  185.4 10.5 %collective-permute-start.29 = (bf16[2,256,512]{2,1,0:T(8,128)(2,1)S(1)}, bf16[2,256,512]{2,1,0:T(8,128)(2,1)S(1)}, u32[]{:S(2)}, u32[]{:S(2)}) collective-permute-start(bf16[2,256,512]{2,1,0:T(8,128)(2,1)S(1)} %pad_maximum_fusion.2), channel_id=1, source_target_pairs={{1,17},{2,18},{6,22},{7,23},{10,26},{11,27},{15,31},{17,33},{18,34... | collective-permute-start | bytes 1572872 | tf_op jit(solution)/shard_map/ppermute | solution.py:344
  (20 other events, 477.8 us)

commit v7 on v6

v7 whole, which is shorter than its diff:
```python
import functools

import jax
import jax.numpy as jnp
from jax import lax
from jax.experimental import pallas as pl
from jax.experimental.pallas import tpu as pltpu
from jax.sharding import PartitionSpec as P

EPW, CH = 8, 2
NZ, NX = 4, 4
SECS, ROWS = 16, 16
BB, KB = 256, 512
QUARTER = BB // NX
TOGETHER = 2
BF, F32 = jnp.bfloat16, jnp.float32
STEPS = (0, -1, 1, 2)
VMEM_BYTES = 56 * 1024 * 1024
HEAD = 16
BRA_CELLS = ((0, 0), (0, 1), (2, 1), (1, 0), (1, 1), (3, 1))
CELLS = [(b, j) for b in range(2) for j in range(CH)]


def after(value, *others):
    return lax.optimization_barrier((value, *others))[0] if others else value


def charge(channel):
    klass = channel % 9
    return klass % 3 - 1, klass // 3 - 1


def live_at(r, b, j):
    to_b = b + charge(CH * r + j)[1]
    return jnp.where((to_b >= 0) & (to_b < 2), 1, 0)


COUNT = [[sum(0 <= b + charge(CH * r + j)[1] < 2 for j in range(CH)) for r in range(ROWS)] for b in range(2)]


def row_z(r, d):
    return (r // NX + d) % NZ * NX + r % NX


def row_x(r, d):
    return r // NX * NX + (r % NX + d) % NX


def packed_cells(r, a, ket_sizes, bra_sizes):
    places = []
    for b in range(2):
        first, second = live_at(r, b, 0), live_at(r, b, 1)
        for j, live in ((1 - first, first + second > 0), (jnp.int32(1), first + second > 1)):
            out_a, out_b = charge(CH * r + j)
            at_a, at_b = a + out_a, jnp.clip(b + out_b, 0, 1)
            rows = jnp.where(live & (at_a >= 0) & (at_a < SECS), bra_sizes[at_b, jnp.clip(at_a, 0, SECS - 1)], 0)
            places.append((2 * j + b, rows, ket_sizes[b, a], live))
    return places


def live_count(r, b):
    return live_at(r, b, 0) + live_at(r, b, 1)


def keep(rows, cols):
    row_at = lax.broadcasted_iota(jnp.int32, (BB, KB), 0)
    col_at = lax.broadcasted_iota(jnp.int32, (BB, KB), 1)
    return (row_at < rows) & (col_at < cols)


def prepare_kernel(place, ket_sizes, bra_sizes, entries, coeffs, env, *outs):
    r, a = place[0], place[1]
    lane = lax.broadcasted_iota(jnp.int32, (HEAD, KB), 1)
    slot, field = lane // 8, lane % 8
    for i, (cell, rows, cols, live) in enumerate(packed_cells(r, a, ket_sizes, bra_sizes)):
        target = outs[i]
        j, b = cell // 2, cell % 2
        head = jnp.zeros((HEAD, KB), F32)
        for n in range(EPW):
            part = jnp.where(field < 3, 0.0, coeffs[j, n])
            for f in range(3):
                part = jnp.where(field == f, entries[f, j, n].astype(F32), part)
            part = jnp.where(field == 7, (b + 1).astype(F32), part)
            head = jnp.where(slot == n, part, head)
        first = head.astype(BF).astype(F32)
        second = (head - first).astype(BF).astype(F32)
        last = head - first - second
        head = jnp.where(field == 4, second, jnp.where(field == 5, last, first))
        head = jnp.where(live, head, 0.0)
        target[:HEAD] = head.astype(BF)
        target[HEAD:] = jnp.where(keep(rows, cols), env[cell], jnp.zeros((BB, KB), BF))


def bra_kernel(place, bra, flipped, strip, strip_low, strip_high):
    r = place[0]
    lines = pl.ds(pl.multiple_of(r % NX * QUARTER, QUARTER), QUARTER)
    for n, (sp, to_b) in enumerate(BRA_CELLS):
        flipped[n] = bra[sp, to_b].T
        value = flipped[n, lines]
        strip[n] = value
        if n < 3:
            strip_low[n] = value
        else:
            strip_high[n - 3] = value


def unpack_kernel(place, ket_sizes, bra_sizes, *refs):
    here, above, out = refs[:4], refs[4:6], refs[6]
    out[...] = jnp.zeros_like(out)
    for i, (cell, rows, cols, _) in enumerate(packed_cells(place[0], place[1], ket_sizes, bra_sizes)):

        @pl.when(rows > 0)
        def _(i=i, cell=cell, rows=rows, cols=cols):
            value = here[i][...] + above[i // 2][i % 2].astype(F32)
            out[cell] = jnp.where(keep(rows, cols), value, 0.0).astype(BF)


def terms_kernel(to_b, place, ints, values, *refs):
    envs = refs[: 8 * (to_b + 1)]
    ket_in, bra_own, rim0, rim1, rim2 = refs[len(envs) : len(envs) + 5]
    outs = refs[len(envs) + 5 : len(envs) + 13]
    env_all, ket, bra_all, total, rounded, todo, scale, size, env_sem, ket_sem, bra_sem, out_sem = refs[len(envs) + 13 :]
    x = place[0] % NX
    copies = [
        pltpu.make_async_copy(ref.at[pl.ds(HEAD, BB)], env_all.at[n], env_sem.at[n]) for n, ref in enumerate(envs)
    ]
    for from_b in range(to_b + 1):
        for n in range(2):
            at = 2 * from_b + n
            copies.append(pltpu.make_async_copy(ket_in.at[2 * (to_b - from_b) + n, from_b], ket.at[at], ket_sem.at[at]))
    copies.append(pltpu.make_async_copy(bra_own, bra_all.at[pl.ds(6, 6)], bra_sem.at[0]))
    y = NX - 1 - x
    for n, (ref, at, owner) in enumerate(((rim0, 0, x), (rim1, 0, x + 1 - 2 * (x % 2)), (rim2, 0, y), (rim2, 12, y + 1 - 2 * (y % 2)))):
        lines = pl.ds(pl.multiple_of(QUARTER * owner, QUARTER), QUARTER)
        for m, (first, count, to) in enumerate(((0, 3, 0), (3, 6, 12), (9, 3, 21))):
            copies.append(pltpu.make_async_copy(
                ref.at[pl.ds(at + first, count)], bra_all.at[pl.ds(to, count), lines], bra_sem.at[1 + 3 * n + m]
            ))
    for copy in copies:
        copy.start()

    r, a = place[0], place[1]
    my_z, my_x = r // NX, r % NX
    for d in range(4):
        for i in range(2):

            @pl.when(i < live_count(row_x(r, STEPS[d]), to_b))
            def _(at=4 * d + 2 * i):
                total[at] = jnp.zeros((BB, KB), F32)
                total[at + 1] = jnp.zeros((BB, KB), F32)

    size[0] = 0

    @pl.loop(0, len(envs) * EPW)
    def _(item):
        base = 64 * (item // EPW) + 8 * (item % EPW)
        out_w, s, code = ints[base], ints[base + 2], ints[base + 7]
        q_b = code - 1
        s_a = s % 2

        @pl.when((code > 0) & (out_w // (CH * NX) == my_z) & (q_b + s // 2 == to_b) & (a + s_a < SECS))
        def _():
            out_r, out_j = out_w // CH, out_w % CH

            @pl.when(live_at(out_r, to_b, out_j) == 1)
            def _():
                sp, at = ints[base + 1], size[0]
                forward = (out_r % NX - my_x + NX) % NX
                slot = jnp.where(forward == 1, 2, jnp.where(forward == 3, 1, jnp.where(forward == 2, 3, 0)))
                out_a, out_b = charge(out_w)
                todo[4 * at] = item // EPW
                todo[4 * at + 1] = 2 * q_b + s_a
                todo[4 * at + 2] = 6 * (s_a + out_a + 1) + 3 * (sp % 2) + to_b + out_b + sp // 2
                todo[4 * at + 3] = 4 * slot + 2 * out_j * live_at(out_r, to_b, 0) + s_a
                scale[at] = values[base + 3] + values[base + 4] + values[base + 5]
                size[0] = at + 1

    count = size[0]
    for n in range(TOGETHER - 1):
        for field in range(3):
            todo[4 * (count + n) + field] = 0
        todo[4 * (count + n) + 3] = 16
        scale[count + n] = 0.0

    for copy in copies:
        copy.wait()

    @pl.loop(0, (count + TOGETHER - 1) // TOGETHER)
    def _(step):
        places = [step * TOGETHER + n for n in range(TOGETHER)]
        halves = [
            jnp.dot(env_all[todo[4 * n]], ket[todo[4 * n + 1]], preferred_element_type=F32).astype(BF) for n in places
        ]
        terms = [
            jnp.dot(bra_all[todo[4 * n + 2]], half, preferred_element_type=F32) for n, half in zip(places, halves)
        ]
        for n, term in zip(places, terms):
            at = todo[4 * n + 3]
            total[at] = total[at] + scale[n] * term

    def stored(d, i):
        return pltpu.make_async_copy(rounded.at[2 * d + i], outs[2 * d + i], out_sem.at[2 * d + i])

    for d in (3, 2, 1, 0):
        for i in range(2):

            @pl.when(i < live_count(row_x(r, STEPS[d]), to_b))
            def _(d=d, i=i):
                for up in range(2):
                    rounded[2 * d + i, up] = total[4 * d + 2 * i + up].astype(BF)
                stored(d, i).start()

    for d in (3, 2, 1, 0):
        for i in range(2):

            @pl.when(i < live_count(row_x(r, STEPS[d]), to_b))
            def _(d=d, i=i):
                stored(d, i).wait()


def body(env_in, ket_mps, bra_mps, ket_sizes, bra_sizes, entries, coeffs):
    my_a = lax.axis_index("sec")
    r = lax.axis_index("row")
    place = jnp.stack([r, my_a])
    ket_flat, bra_flat = ket_sizes.T, bra_sizes.T

    smem = pl.BlockSpec(memory_space=pltpu.SMEM)
    vmem = pl.BlockSpec(memory_space=pltpu.VMEM)
    shape = jax.ShapeDtypeStruct
    pair = shape((2, BB, KB), BF)
    params = pltpu.CompilerParams(vmem_limit_bytes=VMEM_BYTES)
    payload = shape((HEAD + BB, KB), BF)
    packed = pl.pallas_call(
        prepare_kernel,
        in_specs=[smem] * 5 + [vmem],
        out_specs=[vmem] * 4,
        out_shape=[payload] * 4,
        compiler_params=params,
    )(place, ket_flat, bra_flat, entries.transpose(2, 0, 1), coeffs, env_in.reshape(4, BB, KB))

    same = lambda n: n
    z_up, z_down = (lambda n: row_z(n, 1)), (lambda n: row_z(n, -1))
    x_up, x_down, x_far = (lambda n: row_x(n, 1)), (lambda n: row_x(n, -1)), (lambda n: row_x(n, 2))

    def sent(value, move, owner, b, i):
        return lax.ppermute(value, "row", [(n, move(n)) for n in range(ROWS) if COUNT[b][owner(n)] > i])

    def gathered(b, *gates):
        gate, late = gates if gates else ((), ())
        own0, own1 = packed[2 * b : 2 * b + 2]
        behind0 = sent(after(own0, *gate), z_up, same, b, 0)
        ahead1 = sent(after(own1, *gate), z_down, same, b, 1)
        behind1 = sent(after(own1, *late), z_up, same, b, 1)
        ahead0 = sent(after(own0, *late), z_down, same, b, 0)
        across0 = sent(behind0, z_up, z_down, b, 0)
        across1 = sent(ahead1, z_down, z_up, b, 1)
        return [own0, own1, behind0, behind1, ahead0, ahead1, across0, across1]

    low = gathered(0)

    bra_own, strip, strip_low, strip_high = pl.pallas_call(
        bra_kernel,
        in_specs=[smem, vmem],
        out_specs=[vmem] * 4,
        out_shape=[
            shape((6, BB, BB), BF),
            shape((6, QUARTER, BB), BF),
            shape((3, QUARTER, BB), BF),
            shape((3, QUARTER, BB), BF),
        ],
        compiler_params=params,
    )(place, after(bra_mps, packed[0])[:, 0])
    up = lambda n: [(i, i + n) for i in range(SECS - n)]
    down = lambda n: [(i + n, i) for i in range(SECS - n)]
    rim0 = jnp.concatenate([
        lax.ppermute(strip_low, "sec", up(1)),
        lax.ppermute(strip, "sec", down(1)),
        lax.ppermute(strip_high, "sec", down(2)),
    ])
    rim1 = lax.ppermute(rim0, "row", [(n, n ^ 1) for n in range(ROWS)])
    rim2 = lax.ppermute(jnp.concatenate([rim0, rim1]), "row", [(n, n ^ 3) for n in range(ROWS)])

    hbm = pl.BlockSpec(memory_space=pl.ANY)

    def terms(b, envs):
        values = jnp.concatenate([part[0, :64] for part in envs]).astype(F32)
        return pl.pallas_call(
            functools.partial(terms_kernel, b),
            in_specs=[smem] * 3 + [hbm] * (len(envs) + 5),
            out_specs=[hbm] * 8,
            out_shape=[pair] * 8,
            scratch_shapes=[
                pltpu.VMEM((len(envs), BB, KB), BF),
                pltpu.VMEM((4, KB, KB), BF),
                pltpu.VMEM((24, BB, BB), BF),
                pltpu.VMEM((17, BB, KB), F32),
                pltpu.VMEM((8, 2, BB, KB), BF),
                pltpu.SMEM((4 * (len(envs) * EPW + TOGETHER),), jnp.int32),
                pltpu.SMEM((len(envs) * EPW + TOGETHER,), F32),
                pltpu.SMEM((1,), jnp.int32),
                pltpu.SemaphoreType.DMA((len(envs),)),
                pltpu.SemaphoreType.DMA((4,)),
                pltpu.SemaphoreType.DMA((13,)),
                pltpu.SemaphoreType.DMA((8,)),
            ],
            compiler_params=params,
        )(place, values.astype(jnp.int32), values, *envs, ket_mps[:, 0], bra_own, rim0, rim1, rim2)

    def added(*parts):
        return functools.reduce(jnp.add, [part.astype(F32) for part in parts])

    def reduced(b, sums):
        mine, left, right, far = (sums[2 * d : 2 * d + 2] for d in range(4))
        far_up = sent(far[0], x_up, x_far, b, 0)
        far_down = sent(far[1], x_down, x_far, b, 1)
        from_left = [None, sent(right[1], x_up, x_up, b, 1)]
        from_right = [sent(left[0], x_down, x_down, b, 0), None]
        from_left[0] = sent(added(right[0], far_up).astype(BF), x_up, x_up, b, 0)
        from_right[1] = sent(added(left[1], far_down).astype(BF), x_down, x_down, b, 1)
        raised = [added(mine[n][1], from_left[n][1], from_right[n][1]).astype(BF) for n in range(2)]
        pairs = [(a * ROWS + n, (a + 1) * ROWS + n) for a in range(SECS - 1) for n in range(ROWS) if COUNT[b][n]]
        above = lax.ppermute(jnp.stack(raised), ("sec", "row"), pairs)
        here = [added(mine[n][0], from_left[n][0], from_right[n][0]) for n in range(2)]
        return here, above, from_left + from_right

    sums0 = terms(0, low)
    high = gathered(1, [low[3], low[4]], sums0[6:])
    here0, above0, arrived = reduced(0, sums0)
    low[0] = after(low[0], *arrived)
    here1, above1, _ = reduced(1, terms(1, low + high))
    here, above = here0 + here1, [above0, above1]

    out = pl.pallas_call(
        unpack_kernel,
        in_specs=[smem] * 3 + [vmem] * 6,
        out_specs=vmem,
        out_shape=shape((4, BB, KB), BF),
        compiler_params=params,
    )(place, ket_flat, bra_flat, *here, *above)
    return out.reshape(CH, 1, 2, BB, KB)


def solution(mesh):
    placed = (
        P("row", "sec", None, None, None),
        P(None, "sec", None, None, None),
        P(None, "sec", None, None, None),
        P(),
        P(),
        P("row", None, None),
        P("row", None),
    )
    return jax.shard_map(
        body,
        mesh=mesh,
        in_specs=placed,
        out_specs=P("row", "sec", None, None, None),
        check_vma=False,
    )
```

time: 203 us -> 208 us (1.025)
  the two profiles are of different devices: /device:TPU:36 before, /device:TPU:12 now
where the time goes in v7:
time: 208 us; the launch traced here: 207 us
  starting transfers between devices  89.8 us (43%)
  waiting for transfers between devices  70.8 us (34%)
  Pallas kernels  29.2 us (14%)
  other arithmetic  10.7 us (5%)
  local copies, waits for them, and re-layouts  5.91 us (3%)
    ppermute x24, starting transfers between devices, sent(): lax.ppermute(value, 'row', [(n, move(n)) for n in range(ROWS) if COUNT[b]...  71.6 us
    ppermute x24, waiting for transfers between devices, sent(): lax.ppermute(value, 'row', [(n, move(n)) for n in range(ROWS) if COUNT[b]...  47.2 us
    pallas_call x2, Pallas kernels, terms(): pl.pallas_call(functools.partial(terms_kernel, b), in_specs=[smem] * 3 +...  20.8 us
    ppermute x1, waiting for transfers between devices, body(): lax.ppermute(strip_high, 'sec', down(2))  11.6 us
    ppermute x2, waiting for transfers between devices, reduced(): above = lax.ppermute(jnp.stack(raised), ('sec', 'row'), pairs)  9.45 us
    ppermute x1, starting transfers between devices, body(): rim1 = lax.ppermute(rim0, 'row', [(n, n ^ 1) for n in range(ROWS)])  5.98 us
    ppermute x1, starting transfers between devices, body(): lax.ppermute(strip, 'sec', down(1))  4.54 us
  transfers between devices with their start and end apart: 31, of which 15 were waited for; matrix products, arithmetic and copies ran while one was open for 6% of the time, Pallas kernels for 5%

profile of v7, /device:TPU:12, one launch (start us, length us, event | category | flops | bytes accessed | tf_op | source)
XLA Modules:
  0.0 207.0 jit_solution(6702273664100494643)
XLA Ops:
  0.6 2.6 %shard_map.73 = (bf16[272,512]{1,0:T(8,128)(2,1)}, bf16[272,512]{1,0:T(8,128)(2,1)}, bf16[272,512]{1,0:T(8,128)(2,1)}, bf16[272,512]{1,0:T(8,128)(2,1)}) custom-call(s32[2]{0:T(128)} %pad_add_fusion.place, s32[2,16]{1,0:T(2,128)} %bitcast.57, s32[2,16]{1,0:T(2,128)} %bitcast.59, s32[3,2,8]{2,1,0:T(2,128)} %bitcast.61, f32[2,8]{1,0:T(2,128)} %coeffs.1, ...), custom_call_target="tpu_custom_call" | custom-call | tf_op jit(solution)/shard_map/pallas_call | solution.py:233
  3.2 5.2 %collective-permute-start = (bf16[272,512]{1,0:T(8,128)(2,1)}, bf16[272,512]{1,0:T(8,128)(2,1)S(1)}, u32[]{:S(2)}, u32[]{:S(2)}) collective-permute-start(bf16[272,512]{1,0:T(8,128)(2,1)} %get-tuple-element.50.refs_0_), channel_id=1, source_target_pairs={{1,5},{2,6},{3,7},{4,8},{6,10},{7,11},{8,12},{10,14},{11,15},{12,0... | collective-permute-start | bytes 835592 | tf_op jit(solution)/shard_map/ppermute | solution.py:246
  8.4 4.3 %collective-permute-start.2 = (bf16[272,512]{1,0:T(8,128)(2,1)}, bf16[272,512]{1,0:T(8,128)(2,1)S(1)}, u32[]{:S(2)}, u32[]{:S(2)}) collective-permute-start(bf16[272,512]{1,0:T(8,128)(2,1)} %get-tuple-element.50.refs_0_), channel_id=1, source_target_pairs={{1,13},{2,14},{3,15},{4,0},{6,2},{7,3},{8,4},{10,6},{11,7},{12,8},... | collective-permute-start | bytes 835592 | tf_op jit(solution)/shard_map/ppermute | solution.py:246
  12.7 4.0 %collective-permute-start.1 = (bf16[272,512]{1,0:T(8,128)(2,1)}, bf16[272,512]{1,0:T(8,128)(2,1)S(1)}, u32[]{:S(2)}, u32[]{:S(2)}) collective-permute-start(bf16[272,512]{1,0:T(8,128)(2,1)} %get-tuple-element.36.refs_1_), channel_id=1, source_target_pairs={{2,6},{3,7},{6,10},{7,11},{8,12},{11,15},{12,0},{15,3},{18,22},{19... | collective-permute-start | bytes 835592 | tf_op jit(solution)/shard_map/ppermute | solution.py:246
  16.7 2.5 %shard_map.74 = (bf16[6,256,256]{2,1,0:T(8,128)(2,1)}, bf16[6,64,256]{2,1,0:T(8,128)(2,1)}, bf16[3,64,256]{2,1,0:T(8,128)(2,1)}, bf16[3,64,256]{2,1,0:T(8,128)(2,1)}) custom-call(s32[2]{0:T(128)} %pad_add_fusion.place, bf16[4,2,256,256]{3,2,1,0:T(8,128)(2,1)} %bitcast.56), custom_call_target="tpu_custom_call" | custom-call | tf_op jit(solution)/shard_map/pallas_call | solution.py:261
  21.1 4.5 %collective-permute-start.7 = (bf16[6,64,256]{2,1,0:T(8,128)(2,1)}, bf16[6,64,256]{2,1,0:T(8,128)(2,1)S(1)}, u32[]{:S(2)}, u32[]{:S(2)}) collective-permute-start(bf16[6,64,256]{2,1,0:T(8,128)(2,1)} %get-tuple-element.40), channel_id=1, source_target_pairs={{16,0},{32,16},{48,32},{64,48},{80,64},{96,80},{112,96},{128,112},... | collective-permute-start | bytes 589832 | tf_op jit(solution)/shard_map/ppermute | solution.py:277
  33.0 11.6 %collective-permute-done.8 = bf16[3,64,256]{2,1,0:T(8,128)(2,1)S(1)} collective-permute-done((bf16[3,64,256]{2,1,0:T(8,128)(2,1)}, bf16[3,64,256]{2,1,0:T(8,128)(2,1)S(1)}, u32[]{:S(2)}, u32[]{:S(2)}) %collective-permute-start.8) | collective-permute-done | bytes 98336 | tf_op jit(solution)/shard_map/ppermute | solution.py:278
  44.6 6.0 %collective-permute-start.9 = (bf16[12,64,256]{2,1,0:T(8,128)(2,1)S(1)}, bf16[12,64,256]{2,1,0:T(8,128)(2,1)S(1)}, u32[]{:S(2)}, u32[]{:S(2)}) collective-permute-start(bf16[12,64,256]{2,1,0:T(8,128)(2,1)S(1)} %constant_dynamic-update-slice_fusion.refs_10_.refs_18_), channel_id=1, source_target_pairs={{0,1},{1,0},{2,3},{3,2},{4,5},{5,4},{6,7},{7,6},{8,9},{9,8},{10,11... | collective-permute-start | bytes 1179656 | tf_op jit(solution)/shard_map/ppermute | solution.py:280
  50.6 4.9 %collective-permute-start.17 = (bf16[272,512]{1,0:T(8,128)(2,1)}, bf16[272,512]{1,0:T(8,128)(2,1)}, u32[]{:S(2)}, u32[]{:S(2)}) collective-permute-start(bf16[272,512]{1,0:T(8,128)(2,1)} %get-tuple-element.55.refs_8_), channel_id=1, source_target_pairs={{0,4},{1,5},{2,6},{4,8},{5,9},{6,10},{7,11},{9,13},{10,14},{11,15}... | collective-permute-start | bytes 835592 | tf_op jit(solution)/shard_map/ppermute | solution.py:246
  55.5 3.1 %collective-permute-start.20 = (bf16[272,512]{1,0:T(8,128)(2,1)}, bf16[272,512]{1,0:T(8,128)(2,1)}, u32[]{:S(2)}, u32[]{:S(2)}) collective-permute-start(bf16[272,512]{1,0:T(8,128)(2,1)} %get-tuple-element.56.refs_9_), channel_id=1, source_target_pairs={{0,12},{1,13},{2,14},{5,1},{6,2},{9,5},{10,6},{11,7},{14,10},{15,1... | collective-permute-start | bytes 835592 | tf_op jit(solution)/shard_map/ppermute | solution.py:246
  60.0 6.7 %collective-permute-start.5 = (bf16[272,512]{1,0:T(8,128)(2,1)S(1)}, bf16[272,512]{1,0:T(8,128)(2,1)S(1)}, u32[]{:S(2)}, u32[]{:S(2)}) collective-permute-start(bf16[272,512]{1,0:T(8,128)(2,1)S(1)} %collective-permute-done.3.refs_5_), channel_id=1, source_target_pairs={{2,14},{3,15},{4,0},{7,3},{8,4},{11,7},{14,10},{15,11},{18,30},{19... | collective-permute-start | bytes 835592 | tf_op jit(solution)/shard_map/ppermute | solution.py:246
  67.7 6.0 %collective-permute-done.4.refs_6_ = bf16[272,512]{1,0:T(8,128)(2,1)S(1)} collective-permute-done((bf16[272,512]{1,0:T(8,128)(2,1)S(1)}, bf16[272,512]{1,0:T(8,128)(2,1)S(1)}, u32[]{:S(2)}, u32[]{:S(2)}) %collective-permute-start.4) | collective-permute-done | bytes 278560 | tf_op jit(solution)/shard_map/ppermute | solution.py:246
  73.8 5.5 %collective-permute-done.5.refs_7_ = bf16[272,512]{1,0:T(8,128)(2,1)S(1)} collective-permute-done((bf16[272,512]{1,0:T(8,128)(2,1)S(1)}, bf16[272,512]{1,0:T(8,128)(2,1)S(1)}, u32[]{:S(2)}, u32[]{:S(2)}) %collective-permute-start.5) | collective-permute-done | bytes 278560 | tf_op jit(solution)/shard_map/ppermute | solution.py:246
  83.9 7.8 %shard_map.75 = (bf16[2,256,512]{2,1,0:T(8,128)(2,1)}, bf16[2,256,512]{2,1,0:T(8,128)(2,1)}, bf16[2,256,512]{2,1,0:T(8,128)(2,1)}, bf16[2,256,512]{2,1,0:T(8,128...) custom-call(s32[2]{0:T(128)} %pad_add_fusion.place, ...), custom_call_target="tpu_custom_call" | custom-call | tf_op jit(solution)/shard_map/pallas_call | solution.py:287
  95.0 9.4 %collective-permute-start.22 = (bf16[272,512]{1,0:T(8,128)(2,1)}, bf16[272,512]{1,0:T(8,128)(2,1)S(1)}, u32[]{:S(2)}, u32[]{:S(2)}) collective-permute-start(bf16[272,512]{1,0:T(8,128)(2,1)} %collective-permute-done.20.refs_13_), channel_id=1, source_target_pairs={{1,13},{2,14},{5,1},{6,2},{7,3},{10,6},{11,7},{12,8},{13,9},{14,10... | collective-permute-start | bytes 835592 | tf_op jit(solution)/shard_map/ppermute | solution.py:246
  106.3 3.9 %collective-permute-start.14 = (bf16[2,256,512]{2,1,0:T(8,128)(2,1)}, bf16[2,256,512]{2,1,0:T(8,128)(2,1)S(1)}, u32[]{:S(2)}, u32[]{:S(2)}) collective-permute-start(bf16[2,256,512]{2,1,0:T(8,128)(2,1)} %get-tuple-element.47), channel_id=1, source_target_pairs={{1,2},{2,3},{5,6},{6,7},{10,11},{11,8},{14,15},{15,12},{17,18},{18... | collective-permute-start | bytes 1572872 | tf_op jit(solution)/shard_map/ppermute | solution.py:246
  110.2 2.8 %collective-permute-start.18 = (bf16[272,512]{1,0:T(8,128)(2,1)S(1)}, bf16[272,512]{1,0:T(8,128)(2,1)S(1)}, u32[]{:S(2)}, u32[]{:S(2)}) collective-permute-start(bf16[272,512]{1,0:T(8,128)(2,1)S(1)} %copy-done.17), channel_id=1, source_target_pairs={{0,4},{1,5},{2,6},{5,9},{6,10},{9,13},{10,14},{11,15},{14,2},{15,3... | collective-permute-start | bytes 835592 | tf_op jit(solution)/shard_map/ppermute | solution.py:246
  114.2 5.2 %collective-permute-start.19 = (bf16[272,512]{1,0:T(8,128)(2,1)S(1)}, bf16[272,512]{1,0:T(8,128)(2,1)S(1)}, u32[]{:S(2)}, u32[]{:S(2)}) collective-permute-start(bf16[272,512]{1,0:T(8,128)(2,1)S(1)} %copy-done.16), channel_id=1, source_target_pairs={{0,12},{1,13},{2,14},{4,0},{5,1},{6,2},{7,3},{9,5},{10,6},{11,7},{... | collective-permute-start | bytes 835592 | tf_op jit(solution)/shard_map/ppermute | solution.py:246
  120.6 1.9 collective-permute-start.12
  124.4 4.3 %collective-permute-done.19.refs_12_ = bf16[272,512]{1,0:T(8,128)(2,1)S(1)} collective-permute-done((bf16[272,512]{1,0:T(8,128)(2,1)S(1)}, bf16[272,512]{1,0:T(8,128)(2,1)S(1)}, u32[]{:S(2)}, u32[]{:S(2)}) %collective-permute-start.19) | collective-permute-done | bytes 278560 | tf_op jit(solution)/shard_map/ppermute | solution.py:246
  128.7 4.8 %collective-permute-done.12 = bf16[2,256,512]{2,1,0:T(8,128)(2,1)S(1)} collective-permute-done((bf16[2,256,512]{2,1,0:T(8,128)(2,1)S(1)}, bf16[2,256,512]{2,1,0:T(8,128)(2,1)S(1)}, u32[]{:S(2)}, u32[]{:S(2)}) %collective-permute-start.12) | collective-permute-done | bytes 524320 | tf_op jit(solution)/shard_map/ppermute | solution.py:246
  133.5 4.4 %collective-permute-done.16 = bf16[2,256,512]{2,1,0:T(8,128)(2,1)S(1)} collective-permute-done((bf16[2,256,512]{2,1,0:T(8,128)(2,1)S(1)}, bf16[2,256,512]{2,1,0:T(8,128)(2,1)S(1)}, u32[]{:S(2)}, u32[]{:S(2)}) %collective-permute-start.16) | collective-permute-done | bytes 524320 | tf_op jit(solution)/shard_map/ppermute | solution.py:246
  139.3 13.0 %shard_map.76 = (bf16[2,256,512]{2,1,0:T(8,128)(2,1)}, bf16[2,256,512]{2,1,0:T(8,128)(2,1)}, bf16[2,256,512]{2,1,0:T(8,128)(2,1)}, bf16[2,256,512]{2,1,0:T(8,128...) custom-call(s32[2]{0:T(128)} %pad_add_fusion.place, ...), custom_call_target="tpu_custom_call" | custom-call | tf_op jit(solution)/shard_map/pallas_call | solution.py:287
  160.3 3.7 %collective-permute-done.23 = bf16[2,256,512]{2,1,0:T(8,128)(2,1)S(1)} collective-permute-done((bf16[2,256,512]{2,1,0:T(8,128)(2,1)}, bf16[2,256,512]{2,1,0:T(8,128)(2,1)S(1)}, u32[]{:S(2)}, u32[]{:S(2)}) %collective-permute-start.23) | collective-permute-done | bytes 524320 | tf_op jit(solution)/shard_map/ppermute | solution.py:246
  166.5 4.6 %collective-permute-done.27 = bf16[2,256,512]{2,1,0:T(8,128)(2,1)S(1)} collective-permute-done((bf16[2,256,512]{2,1,0:T(8,128)(2,1)}, bf16[2,256,512]{2,1,0:T(8,128)(2,1)S(1)}, u32[]{:S(2)}, u32[]{:S(2)}) %collective-permute-start.27) | collective-permute-done | bytes 524320 | tf_op jit(solution)/shard_map/ppermute | solution.py:246
  171.2 1.9 collective-permute-start.28
  174.2 1.9 collective-permute-start.29
  176.1 6.2 %collective-permute-done.25 = bf16[2,256,512]{2,1,0:T(8,128)(2,1)S(1)} collective-permute-done((bf16[2,256,512]{2,1,0:T(8,128)(2,1)}, bf16[2,256,512]{2,1,0:T(8,128)(2,1)S(1)}, u32[]{:S(2)}, u32[]{:S(2)}) %collective-permute-start.25) | collective-permute-done | bytes 524320 | tf_op jit(solution)/shard_map/ppermute | solution.py:246
  184.7 5.8 %collective-permute-done.28 = bf16[2,256,512]{2,1,0:T(8,128)(2,1)S(1)} collective-permute-done((bf16[2,256,512]{2,1,0:T(8,128)(2,1)S(1)}, bf16[2,256,512]{2,1,0:T(8,128)(2,1)S(1)}, u32[]{:S(2)}, u32[]{:S(2)}) %collective-permute-start.28) | collective-permute-done | bytes 524320 | tf_op jit(solution)/shard_map/ppermute | solution.py:246
  191.5 1.9 collective-permute-start.30
  193.5 9.4 %collective-permute-done.30.refs_5_ = bf16[2,256,512]{2,1,0:T(8,128)(2,1)S(1)} collective-permute-done((bf16[2,256,512]{2,1,0:T(8,128)(2,1)S(1)}, bf16[2,256,512]{2,1,0:T(8,128)(2,1)S(1)}, u32[]{:S(2)}, u32[]{:S(2)}) %collective-permute-start.30) | collective-permute-done | bytes 524320 | tf_op jit(solution)/shard_map/ppermute | solution.py:322
  203.7 3.2 %shard_map.77 = bf16[4,256,512]{2,1,0:T(8,128)(2,1)} custom-call(s32[2]{0:T(128)} %pad_add_fusion.place, s32[2,16]{1,0:T(2,128)} %bitcast.58, s32[2,16]{1,0:T(2,128)} %bitcast.60, f32[256,512]{1,0:T(8,128)} %get-tuple-element.70.refs_0_, f32[256,512]{1,0:T(8,128)} %get-tuple-element.72.refs_1_, f32[256,512]{1,0:T(8,128)} %get-tuple-element.66.refs_2_, ...), custom_call_target="tpu_custom_call" | custom-call | tf_op jit(solution)/shard_map/pallas_call | solution.py:333
  (114 shorter events, 43.3 us)
Async XLA Ops:
  3.2 55.4 %collective-permute-start = (bf16[272,512]{1,0:T(8,128)(2,1)}, bf16[272,512]{1,0:T(8,128)(2,1)S(1)}, u32[]{:S(2)}, u32[]{:S(2)}) collective-permute-start(bf16[272,512]{1,0:T(8,128)(2,1)} %get-tuple-element.50.refs_0_), channel_id=1, source_target_pairs={{1,5},{2,6},{3,7},{4,8},{6,10},{7,11},{8,12},{10,14},{11,15},{12,0... | collective-permute-start | bytes 835592 | tf_op jit(solution)/shard_map/ppermute | solution.py:246
  8.4 42.3 %collective-permute-start.2 = (bf16[272,512]{1,0:T(8,128)(2,1)}, bf16[272,512]{1,0:T(8,128)(2,1)S(1)}, u32[]{:S(2)}, u32[]{:S(2)}) collective-permute-start(bf16[272,512]{1,0:T(8,128)(2,1)} %get-tuple-element.50.refs_0_), channel_id=1, source_target_pairs={{1,13},{2,14},{3,15},{4,0},{6,2},{7,3},{8,4},{10,6},{11,7},{12,8},... | collective-permute-start | bytes 835592 | tf_op jit(solution)/shard_map/ppermute | solution.py:246
  12.7 37.9 %collective-permute-start.1 = (bf16[272,512]{1,0:T(8,128)(2,1)}, bf16[272,512]{1,0:T(8,128)(2,1)S(1)}, u32[]{:S(2)}, u32[]{:S(2)}) collective-permute-start(bf16[272,512]{1,0:T(8,128)(2,1)} %get-tuple-element.36.refs_1_), channel_id=1, source_target_pairs={{2,6},{3,7},{6,10},{7,11},{8,12},{11,15},{12,0},{15,3},{18,22},{19... | collective-permute-start | bytes 835592 | tf_op jit(solution)/shard_map/ppermute | solution.py:246
  19.2 9.9 %collective-permute-start.6 = (bf16[3,64,256]{2,1,0:T(8,128)(2,1)}, bf16[3,64,256]{2,1,0:T(8,128)(2,1)S(1)}, u32[]{:S(2)}, u32[]{:S(2)}) collective-permute-start(bf16[3,64,256]{2,1,0:T(8,128)(2,1)} %get-tuple-element.39), channel_id=1, source_target_pairs={{0,16},{16,32},{32,48},{48,64},{64,80},{80,96},{96,112},{112,128},... | collective-permute-start | bytes 294920 | tf_op jit(solution)/shard_map/ppermute | solution.py:276
  21.1 9.9 %collective-permute-start.7 = (bf16[6,64,256]{2,1,0:T(8,128)(2,1)}, bf16[6,64,256]{2,1,0:T(8,128)(2,1)S(1)}, u32[]{:S(2)}, u32[]{:S(2)}) collective-permute-start(bf16[6,64,256]{2,1,0:T(8,128)(2,1)} %get-tuple-element.40), channel_id=1, source_target_pairs={{16,0},{32,16},{48,32},{64,48},{80,64},{96,80},{112,96},{128,112},... | collective-permute-start | bytes 589832 | tf_op jit(solution)/shard_map/ppermute | solution.py:277
  29.1 30.9 %collective-permute-start.3 = (bf16[272,512]{1,0:T(8,128)(2,1)}, bf16[272,512]{1,0:T(8,128)(2,1)S(1)}, u32[]{:S(2)}, u32[]{:S(2)}) collective-permute-start(bf16[272,512]{1,0:T(8,128)(2,1)} %get-tuple-element.36.refs_1_), channel_id=1, source_target_pairs={{2,14},{3,15},{6,2},{7,3},{8,4},{11,7},{12,8},{15,11},{18,30},{19,... | collective-permute-start | bytes 835592 | tf_op jit(solution)/shard_map/ppermute | solution.py:246
  31.0 13.6 %collective-permute-start.8 = (bf16[3,64,256]{2,1,0:T(8,128)(2,1)}, bf16[3,64,256]{2,1,0:T(8,128)(2,1)S(1)}, u32[]{:S(2)}, u32[]{:S(2)}) collective-permute-start(bf16[3,64,256]{2,1,0:T(8,128)(2,1)} %get-tuple-element.41), channel_id=1, source_target_pairs={{32,0},{48,16},{64,32},{80,48},{96,64},{112,80},{128,96},{144,112}... | collective-permute-start | bytes 294920 | tf_op jit(solution)/shard_map/ppermute | solution.py:278
  44.6 38.3 %copy-start.2 = (bf16[12,64,256]{2,1,0:T(8,128)(2,1)}, bf16[12,64,256]{2,1,0:T(8,128)(2,1)S(1)}, u32[]{:S(2)}) copy-start(bf16[12,64,256]{2,1,0:T(8,128)(2,1)S(1)} %constant_dynamic-update-slice_fusion.refs_10_.refs_18_) | copy-start | bytes 1179652
  44.6 22.0 %collective-permute-start.9 = (bf16[12,64,256]{2,1,0:T(8,128)(2,1)S(1)}, bf16[12,64,256]{2,1,0:T(8,128)(2,1)S(1)}, u32[]{:S(2)}, u32[]{:S(2)}) collective-permute-start(bf16[12,64,256]{2,1,0:T(8,128)(2,1)S(1)} %constant_dynamic-update-slice_fusion.refs_10_.refs_18_), channel_id=1, source_target_pairs={{0,1},{1,0},{2,3},{3,2},{4,5},{5,4},{6,7},{7,6},{8,9},{9,8},{10,11... | collective-permute-start | bytes 1179656 | tf_op jit(solution)/shard_map/ppermute | solution.py:280
  50.6 29.3 %collective-permute-start.17 = (bf16[272,512]{1,0:T(8,128)(2,1)}, bf16[272,512]{1,0:T(8,128)(2,1)}, u32[]{:S(2)}, u32[]{:S(2)}) collective-permute-start(bf16[272,512]{1,0:T(8,128)(2,1)} %get-tuple-element.55.refs_8_), channel_id=1, source_target_pairs={{0,4},{1,5},{2,6},{4,8},{5,9},{6,10},{7,11},{9,13},{10,14},{11,15}... | collective-permute-start | bytes 835592 | tf_op jit(solution)/shard_map/ppermute | solution.py:246
  55.5 38.8 %collective-permute-start.20 = (bf16[272,512]{1,0:T(8,128)(2,1)}, bf16[272,512]{1,0:T(8,128)(2,1)}, u32[]{:S(2)}, u32[]{:S(2)}) collective-permute-start(bf16[272,512]{1,0:T(8,128)(2,1)} %get-tuple-element.56.refs_9_), channel_id=1, source_target_pairs={{0,12},{1,13},{2,14},{5,1},{6,2},{9,5},{10,6},{11,7},{14,10},{15,1... | collective-permute-start | bytes 835592 | tf_op jit(solution)/shard_map/ppermute | solution.py:246
  58.6 15.1 %collective-permute-start.4 = (bf16[272,512]{1,0:T(8,128)(2,1)S(1)}, bf16[272,512]{1,0:T(8,128)(2,1)S(1)}, u32[]{:S(2)}, u32[]{:S(2)}) collective-permute-start(bf16[272,512]{1,0:T(8,128)(2,1)S(1)} %collective-permute-done.refs_2_), channel_id=1, source_target_pairs={{0,4},{1,5},{3,7},{5,9},{6,10},{7,11},{8,12},{10,14},{11,15},{12,0... | collective-permute-start | bytes 835592 | tf_op jit(solution)/shard_map/ppermute | solution.py:246
  60.0 19.3 %collective-permute-start.5 = (bf16[272,512]{1,0:T(8,128)(2,1)S(1)}, bf16[272,512]{1,0:T(8,128)(2,1)S(1)}, u32[]{:S(2)}, u32[]{:S(2)}) collective-permute-start(bf16[272,512]{1,0:T(8,128)(2,1)S(1)} %collective-permute-done.3.refs_5_), channel_id=1, source_target_pairs={{2,14},{3,15},{4,0},{7,3},{8,4},{11,7},{14,10},{15,11},{18,30},{19... | collective-permute-start | bytes 835592 | tf_op jit(solution)/shard_map/ppermute | solution.py:246
  67.7 15.3 %collective-permute-start.10 = (bf16[24,64,256]{2,1,0:T(8,128)(2,1)}, bf16[24,64,256]{2,1,0:T(8,128)(2,1)S(1)}, u32[]{:S(2)}, u32[]{:S(2)}) collective-permute-start(bf16[24,64,256]{2,1,0:T(8,128)(2,1)} %pad_maximum_fusion), channel_id=1, source_target_pairs={{0,3},{1,2},{2,1},{3,0},{4,7},{5,6},{6,5},{7,4},{8,11},{9,10},{10,... | collective-permute-start | bytes 2359304 | tf_op jit(solution)/shard_map/ppermute | solution.py:281
  79.9 24.4 %collective-permute-start.21 = (bf16[272,512]{1,0:T(8,128)(2,1)}, bf16[272,512]{1,0:T(8,128)(2,1)S(1)}, u32[]{:S(2)}, u32[]{:S(2)}) collective-permute-start(bf16[272,512]{1,0:T(8,128)(2,1)} %collective-permute-done.17.refs_10_), channel_id=1, source_target_pairs={{1,5},{2,6},{3,7},{4,8},{5,9},{6,10},{8,12},{9,13},{10,14},{11,15}... | collective-permute-start | bytes 835592 | tf_op jit(solution)/shard_map/ppermute | solution.py:246
  91.8 18.5 %collective-permute-start.11 = (bf16[2,256,512]{2,1,0:T(8,128)(2,1)}, bf16[2,256,512]{2,1,0:T(8,128)(2,1)S(1)}, u32[]{:S(2)}, u32[]{:S(2)}) collective-permute-start(bf16[2,256,512]{2,1,0:T(8,128)(2,1)} %get-tuple-element.44), channel_id=1, source_target_pairs={{0,1},{1,2},{3,0},{4,5},{5,6},{6,7},{8,9},{9,10},{10,11},{13,14},{... | collective-permute-start | bytes 1572872 | tf_op jit(solution)/shard_map/ppermute | solution.py:246
  93.7 20.6 %collective-permute-start.15 = (bf16[2,256,512]{2,1,0:T(8,128)(2,1)}, bf16[2,256,512]{2,1,0:T(8,128)(2,1)S(1)}, u32[]{:S(2)}, u32[]{:S(2)}) collective-permute-start(bf16[2,256,512]{2,1,0:T(8,128)(2,1)} %get-tuple-element.49), channel_id=1, source_target_pairs={{0,3},{1,0},{4,7},{5,4},{9,8},{10,9},{13,12},{14,13},{16,19},{17,1... | collective-permute-start | bytes 1572872 | tf_op jit(solution)/shard_map/ppermute | solution.py:246
  95.0 25.6 %collective-permute-start.22 = (bf16[272,512]{1,0:T(8,128)(2,1)}, bf16[272,512]{1,0:T(8,128)(2,1)S(1)}, u32[]{:S(2)}, u32[]{:S(2)}) collective-permute-start(bf16[272,512]{1,0:T(8,128)(2,1)} %collective-permute-done.20.refs_13_), channel_id=1, source_target_pairs={{1,13},{2,14},{5,1},{6,2},{7,3},{10,6},{11,7},{12,8},{13,9},{14,10... | collective-permute-start | bytes 835592 | tf_op jit(solution)/shard_map/ppermute | solution.py:246
  104.4 24.3 %collective-permute-start.13 = (bf16[2,256,512]{2,1,0:T(8,128)(2,1)}, bf16[2,256,512]{2,1,0:T(8,128)(2,1)S(1)}, u32[]{:S(2)}, u32[]{:S(2)}) collective-permute-start(bf16[2,256,512]{2,1,0:T(8,128)(2,1)} %get-tuple-element.45), channel_id=1, source_target_pairs={{0,3},{2,1},{3,2},{4,7},{5,4},{7,6},{8,11},{9,8},{11,10},{12,15},{... | collective-permute-start | bytes 1572872 | tf_op jit(solution)/shard_map/ppermute | solution.py:246
  106.3 22.4 %collective-permute-start.14 = (bf16[2,256,512]{2,1,0:T(8,128)(2,1)}, bf16[2,256,512]{2,1,0:T(8,128)(2,1)S(1)}, u32[]{:S(2)}, u32[]{:S(2)}) collective-permute-start(bf16[2,256,512]{2,1,0:T(8,128)(2,1)} %get-tuple-element.47), channel_id=1, source_target_pairs={{1,2},{2,3},{5,6},{6,7},{10,11},{11,8},{14,15},{15,12},{17,18},{18... | collective-permute-start | bytes 1572872 | tf_op jit(solution)/shard_map/ppermute | solution.py:246
  110.2 12.8 %collective-permute-start.18 = (bf16[272,512]{1,0:T(8,128)(2,1)S(1)}, bf16[272,512]{1,0:T(8,128)(2,1)S(1)}, u32[]{:S(2)}, u32[]{:S(2)}) collective-permute-start(bf16[272,512]{1,0:T(8,128)(2,1)S(1)} %copy-done.17), channel_id=1, source_target_pairs={{0,4},{1,5},{2,6},{5,9},{6,10},{9,13},{10,14},{11,15},{14,2},{15,3... | collective-permute-start | bytes 835592 | tf_op jit(solution)/shard_map/ppermute | solution.py:246
  114.2 14.5 %collective-permute-start.19 = (bf16[272,512]{1,0:T(8,128)(2,1)S(1)}, bf16[272,512]{1,0:T(8,128)(2,1)S(1)}, u32[]{:S(2)}, u32[]{:S(2)}) collective-permute-start(bf16[272,512]{1,0:T(8,128)(2,1)S(1)} %copy-done.16), channel_id=1, source_target_pairs={{0,12},{1,13},{2,14},{4,0},{5,1},{6,2},{7,3},{9,5},{10,6},{11,7},{... | collective-permute-start | bytes 835592 | tf_op jit(solution)/shard_map/ppermute | solution.py:246
  120.6 12.9 %collective-permute-start.12 = (bf16[2,256,512]{2,1,0:T(8,128)(2,1)S(1)}, bf16[2,256,512]{2,1,0:T(8,128)(2,1)S(1)}, u32[]{:S(2)}, u32[]{:S(2)}) collective-permute-start(bf16[2,256,512]{2,1,0:T(8,128)(2,1)S(1)} %add_convert_fusion.3), channel_id=1, source_target_pairs={{0,1},{1,2},{2,3},{5,6},{6,7},{7,4},{9,10},{10,11},{11,8},{12,13},... | collective-permute-start | bytes 1572872 | tf_op jit(solution)/shard_map/ppermute | solution.py:246
  123.1 14.9 %collective-permute-start.16 = (bf16[2,256,512]{2,1,0:T(8,128)(2,1)S(1)}, bf16[2,256,512]{2,1,0:T(8,128)(2,1)S(1)}, u32[]{:S(2)}, u32[]{:S(2)}) collective-permute-start(bf16[2,256,512]{2,1,0:T(8,128)(2,1)S(1)} %add_convert_fusion.2), channel_id=1, source_target_pairs={{0,3},{3,2},{4,7},{7,6},{8,11},{9,8},{12,15},{13,12},{16,19},{19,1... | collective-permute-start | bytes 1572872 | tf_op jit(solution)/shard_map/ppermute | solution.py:246
  152.4 11.6 %collective-permute-start.23 = (bf16[2,256,512]{2,1,0:T(8,128)(2,1)}, bf16[2,256,512]{2,1,0:T(8,128)(2,1)S(1)}, u32[]{:S(2)}, u32[]{:S(2)}) collective-permute-start(bf16[2,256,512]{2,1,0:T(8,128)(2,1)} %get-tuple-element.59), channel_id=1, source_target_pairs={{0,1},{2,3},{3,0},{4,5},{5,6},{6,7},{7,4},{8,9},{9,10},{11,8},{12,... | collective-permute-start | bytes 1572872 | tf_op jit(solution)/shard_map/ppermute | solution.py:246
  154.1 17.0 %collective-permute-start.27 = (bf16[2,256,512]{2,1,0:T(8,128)(2,1)}, bf16[2,256,512]{2,1,0:T(8,128)(2,1)S(1)}, u32[]{:S(2)}, u32[]{:S(2)}) collective-permute-start(bf16[2,256,512]{2,1,0:T(8,128)(2,1)} %get-tuple-element.64), channel_id=1, source_target_pairs={{0,3},{2,1},{3,2},{4,7},{7,6},{8,11},{9,8},{11,10},{12,15},{13,12}... | collective-permute-start | bytes 1572872 | tf_op jit(solution)/shard_map/ppermute | solution.py:246
  156.0 26.3 %collective-permute-start.25 = (bf16[2,256,512]{2,1,0:T(8,128)(2,1)}, bf16[2,256,512]{2,1,0:T(8,128)(2,1)S(1)}, u32[]{:S(2)}, u32[]{:S(2)}) collective-permute-start(bf16[2,256,512]{2,1,0:T(8,128)(2,1)} %get-tuple-element.60), channel_id=1, source_target_pairs={{1,0},{2,1},{3,2},{4,7},{5,4},{6,5},{7,6},{8,11},{10,9},{11,10},{1... | collective-permute-start | bytes 1572872 | tf_op jit(solution)/shard_map/ppermute | solution.py:246
  158.0 26.8 %collective-permute-start.26 = (bf16[2,256,512]{2,1,0:T(8,128)(2,1)}, bf16[2,256,512]{2,1,0:T(8,128)(2,1)S(1)}, u32[]{:S(2)}, u32[]{:S(2)}) collective-permute-start(bf16[2,256,512]{2,1,0:T(8,128)(2,1)} %get-tuple-element.62), channel_id=1, source_target_pairs={{0,1},{1,2},{3,0},{4,5},{5,6},{8,9},{9,10},{10,11},{13,14},{14,15}... | collective-permute-start | bytes 1572872 | tf_op jit(solution)/shard_map/ppermute | solution.py:246
  165.2 18.5 %collective-permute-start.24 = (bf16[2,256,512]{2,1,0:T(8,128)(2,1)S(1)}, bf16[2,256,512]{2,1,0:T(8,128)(2,1)S(1)}, u32[]{:S(2)}, u32[]{:S(2)}) collective-permute-start(bf16[2,256,512]{2,1,0:T(8,128)(2,1)S(1)} %add_convert_fusion.1), channel_id=1, source_target_pairs={{0,1},{1,2},{3,0},{4,5},{5,6},{6,7},{7,4},{8,9},{9,10},{10,11},{12... | collective-permute-start | bytes 1572872 | tf_op jit(solution)/shard_map/ppermute | solution.py:246
  171.2 19.3 %collective-permute-start.28 = (bf16[2,256,512]{2,1,0:T(8,128)(2,1)S(1)}, bf16[2,256,512]{2,1,0:T(8,128)(2,1)S(1)}, u32[]{:S(2)}, u32[]{:S(2)}) collective-permute-start(bf16[2,256,512]{2,1,0:T(8,128)(2,1)S(1)} %add_convert_fusion), channel_id=1, source_target_pairs={{1,0},{2,1},{3,2},{6,5},{7,6},{8,11},{10,9},{11,10},{12,15},{15,14... | collective-permute-start | bytes 1572872 | tf_op jit(solution)/shard_map/ppermute | solution.py:246
  174.2 19.3 %collective-permute-start.29 = (bf16[2,256,512]{2,1,0:T(8,128)(2,1)S(1)}, bf16[2,256,512]{2,1,0:T(8,128)(2,1)S(1)}, u32[]{:S(2)}, u32[]{:S(2)}) collective-permute-start(bf16[2,256,512]{2,1,0:T(8,128)(2,1)S(1)} %pad_maximum_fusion.1), channel_id=1, source_target_pairs={{1,17},{2,18},{3,19},{4,20},{6,22},{7,23},{8,24},{10,26},{11,27},{... | collective-permute-start | bytes 1572872 | tf_op jit(solution)/shard_map/ppermute | solution.py:322
  191.5 11.4 %collective-permute-start.30 = (bf16[2,256,512]{2,1,0:T(8,128)(2,1)S(1)}, bf16[2,256,512]{2,1,0:T(8,128)(2,1)S(1)}, u32[]{:S(2)}, u32[]{:S(2)}) collective-permute-start(bf16[2,256,512]{2,1,0:T(8,128)(2,1)S(1)} %pad_maximum_fusion.2), channel_id=1, source_target_pairs={{0,16},{1,17},{2,18},{4,20},{5,21},{6,22},{7,23},{9,25},{10,26},{1... | collective-permute-start | bytes 1572872 | tf_op jit(solution)/shard_map/ppermute | solution.py:322
  (21 other events, 399.0 us)

commit v8 on v6

--- a/solution.py
+++ b/solution.py
@@ -72,13 +72,13 @@
     return (row_at < rows) & (col_at < cols)
 
 
-def prepare_kernel(place, ket_sizes, bra_sizes, entries, coeffs, env, first_out, second_out, third_out, moving):
+def prepare_kernel(place, ket_sizes, bra_sizes, entries, coeffs, env, pair_out, third_out, moving):
     r, a = place[0], place[1]
     lane = lax.broadcasted_iota(jnp.int32, (HEAD, KB), 1)
     slot, field = lane // 8, lane % 8
     places, count = packed_cells(r, a, ket_sizes, bra_sizes)
     for i, (cell, rows, cols) in enumerate(places):
-        target = (first_out, second_out, third_out, moving)[i]
+        target = (pair_out.at[0], pair_out.at[1], third_out, moving)[i]
         j, b = cell // 2, cell % 2
         head = jnp.zeros((HEAD, KB), F32)
         for n in range(EPW):
@@ -121,23 +121,27 @@
 
 
 def terms_kernel(place, ints, values, *refs):
-    envs, across2b, ket_in, bra_own, rim0, rim1, rim2 = refs[:12], *refs[12:18]
-    outs = refs[18:34]
-    env_all, ket, bra_all, total, rounded, todo, scale, size, env_sem, ket_sem, bra_sem, out_sem = refs[34:]
-    x = place[0] % NX
+    two, three, lone = (refs[0], refs[2], refs[4]), (refs[1], refs[3], refs[5]), refs[6:9]
+    across2b, ket_in, bra_own, rim = refs[9:13]
+    outs = refs[13:29]
+    env_all, ket, bra_all, total, rounded, todo, scale, size, env_sem, ket_sem, bra_sem, out_sem = refs[29:]
     copies = []
-    for n in range(12):
-        rows = BB if n < 11 else BB // 2
-        copies.append(pltpu.make_async_copy(envs[n].at[pl.ds(HEAD, rows)], env_all.at[n, pl.ds(0, rows)], env_sem.at[n]))
+    body_rows = pl.ds(HEAD, BB)
+    views = []
+    for first, third in zip(two, three):
+        views += [first.at[0, body_rows], first.at[1, body_rows], third.at[body_rows]]
+    views += [lone[0].at[body_rows], lone[1].at[body_rows]]
+    copies += [pltpu.make_async_copy(view, env_all.at[n], env_sem.at[n]) for n, view in enumerate(views)]
+    half_rows = pl.ds(0, BB // 2)
+    copies.append(pltpu.make_async_copy(lone[2].at[pl.ds(HEAD, BB // 2)], env_all.at[11, half_rows], env_sem.at[11]))
     copies.append(pltpu.make_async_copy(across2b, env_all.at[11, pl.ds(BB // 2, BB // 2)], env_sem.at[12]))
     copies += [pltpu.make_async_copy(ket_in.at[s], ket.at[pl.ds(2 * s, 2)], ket_sem.at[s]) for s in range(4)]
     copies.append(pltpu.make_async_copy(bra_own, bra_all.at[pl.ds(6, 6)], bra_sem.at[0]))
-    y = NX - 1 - x
-    for n, (ref, at, owner) in enumerate(((rim0, 0, x), (rim1, 0, x + 1 - 2 * (x % 2)), (rim2, 0, y), (rim2, 12, y + 1 - 2 * (y % 2)))):
-        lines = pl.ds(pl.multiple_of(QUARTER * owner, QUARTER), QUARTER)
+    for n in range(NX):
+        lines = pl.ds(QUARTER * n, QUARTER)
         for m, (first, count, to) in enumerate(((0, 3, 0), (3, 6, 12), (9, 3, 21))):
             copies.append(pltpu.make_async_copy(
-                ref.at[pl.ds(at + first, count)], bra_all.at[pl.ds(to, count), lines], bra_sem.at[1 + 3 * n + m]
+                rim.at[n, pl.ds(first, count)], bra_all.at[pl.ds(to, count), lines], bra_sem.at[1 + 3 * n + m]
             ))
     for copy in copies:
         copy.start()
@@ -236,11 +240,11 @@
     pair = shape((2, BB, KB), BF)
     params = pltpu.CompilerParams(vmem_limit_bytes=VMEM_BYTES)
     payload = shape((HEAD + BB, KB), BF)
-    own0, own1, own2, moving = pl.pallas_call(
+    own01, own2, moving = pl.pallas_call(
         prepare_kernel,
         in_specs=[smem] * 5 + [vmem],
-        out_specs=[vmem] * 4,
-        out_shape=[payload] * 4,
+        out_specs=[vmem] * 3,
+        out_shape=[shape((2, HEAD + BB, KB), BF), payload, payload],
         compiler_params=params,
     )(place, ket_flat, bra_flat, entries.transpose(2, 0, 1), coeffs, env_in.reshape(4, BB, KB))
 
@@ -259,20 +263,9 @@
         takers.add(taker)
         lent.append((n, taker))
     three = {n for n in range(ROWS) if COUNT[n] > 2} | takers
-    behind0 = sent(own0, z_up, same, everyone)
-    ahead1 = sent(own1, z_down, same, everyone)
-    borrowed = lax.ppermute(moving, "row", lent)
-    own2 = own2 + borrowed
-    behind1 = sent(after(own1, behind0, ahead1), z_up, same, everyone)
-    ahead0 = sent(after(own0, behind0, ahead1), z_down, same, everyone)
-    behind2 = sent(own2, z_up, same, three)
-    ahead2 = sent(own2, z_down, same, three)
-    across0 = sent(behind0, z_up, z_down, everyone)
-    across1 = sent(ahead1, z_down, z_up, everyone)
-    across2a = sent(behind2[: HEAD + BB // 2], z_up, z_down, three)
-    across2b = sent(ahead2[HEAD + BB // 2 :], z_down, z_up, three)
-
-    bra_in = after(bra_mps, borrowed)
+    behind01 = sent(own01, z_up, same, everyone)
+    ahead01 = sent(own01, z_down, same, everyone)
+
     bra_own, strip, strip_low, strip_high = pl.pallas_call(
         bra_kernel,
         in_specs=[smem, vmem],
@@ -284,24 +277,33 @@
             shape((3, QUARTER, BB), BF),
         ],
         compiler_params=params,
-    )(place, bra_in[:, 0])
+    )(place, after(bra_mps, own01)[:, 0])
     up = lambda n: [(i, i + n) for i in range(SECS - n)]
     down = lambda n: [(i + n, i) for i in range(SECS - n)]
-    rim0 = jnp.concatenate([
-        lax.ppermute(strip_low, "sec", up(1)),
+    rim_low = lax.ppermute(strip_low, "sec", up(1))
+    borrowed = lax.ppermute(after(moving, rim_low), "row", lent)
+    own2 = own2 + borrowed
+    behind2 = sent(own2, z_up, same, three)
+    ahead2 = sent(own2, z_down, same, three)
+    across0 = sent(behind01[0], z_up, z_down, everyone)
+    across1 = sent(ahead01[1], z_down, z_up, everyone)
+    across2a = sent(behind2[: HEAD + BB // 2], z_up, z_down, three)
+    across2b = sent(ahead2[HEAD + BB // 2 :], z_down, z_up, three)
+    rim = jnp.concatenate([
+        rim_low,
         lax.ppermute(strip, "sec", down(1)),
         lax.ppermute(strip_high, "sec", down(2)),
     ])
-    rim1 = lax.ppermute(rim0, "row", [(n, n ^ 1) for n in range(ROWS)])
-    rim2 = lax.ppermute(jnp.concatenate([rim0, rim1]), "row", [(n, n ^ 3) for n in range(ROWS)])
-
-    envs = [own0, own1, own2, behind0, behind1, behind2, ahead0, ahead1, ahead2, across0, across1, across2a]
-    values = jnp.concatenate([part[0, :64] for part in envs]).astype(F32)
+    bra_rim = lax.all_gather(rim, "row", axis_index_groups=[[NX * z + x for x in range(NX)] for z in range(NZ)])
+
+    heads = [own01[0], own01[1], own2, behind01[0], behind01[1], behind2, ahead01[0], ahead01[1], ahead2,
+             across0, across1, across2a]
+    values = jnp.concatenate([head[0, :64] for head in heads]).astype(F32)
 
     hbm = pl.BlockSpec(memory_space=pl.ANY)
     sums = pl.pallas_call(
         terms_kernel,
-        in_specs=[smem] * 3 + [hbm] * 18,
+        in_specs=[smem] * 3 + [hbm] * 13,
         out_specs=[hbm] * 16,
         out_shape=[pair] * 16,
         scratch_shapes=[
@@ -319,7 +321,8 @@
             pltpu.SemaphoreType.DMA((16,)),
         ],
         compiler_params=params,
-    )(place, values.astype(jnp.int32), values, *envs, across2b, ket_mps[:, 0], bra_own, rim0, rim1, rim2)
+    )(place, values.astype(jnp.int32), values, own01, own2, behind01, behind2, ahead01, ahead2,
+      across0, across1, across2a, across2b, ket_mps[:, 0], bra_own, bra_rim)
     mine, left, right, far = sums[:4], sums[4:8], sums[8:12], sums[12:]
 
     def added(*parts):
@@ -328,21 +331,21 @@
     def moved(value, move, owner, i):
         return sent(value, move, owner, {n for n in range(ROWS) if COUNT[n] > i})
 
-    far_up, far_down, from_left, from_right = {}, {}, {}, {}
-    gate = ()
+    far_up = {i: moved(far[i], x_up, x_far, i) for i in (0, 2)}
+    far_down = {i: moved(far[i], x_down, x_far, i) for i in (1, 3)}
+    from_left = {i: moved(right[i], x_up, x_up, i) for i in (1, 3)}
+    from_right = {i: moved(left[i], x_down, x_down, i) for i in (0, 2)}
+    for i in (0, 2):
+        from_left[i] = moved(added(right[i], far_up[i]).astype(BF), x_up, x_up, i)
+    for i in (1, 3):
+        from_right[i] = moved(added(left[i], far_down[i]).astype(BF), x_down, x_down, i)
+
+    here = [added(mine[i][0], from_left[i][0], from_right[i][0]) for i in range(4)]
+    raised = [added(mine[i][1], from_left[i][1], from_right[i][1]).astype(BF) for i in range(4)]
     above = []
     for i in (0, 2):
-        far_up[i] = moved(after(far[i], *gate), x_up, x_far, i)
-        far_down[i + 1] = moved(after(far[i + 1], *gate), x_down, x_far, i + 1)
-        from_left[i + 1] = moved(after(right[i + 1], *gate), x_up, x_up, i + 1)
-        from_right[i] = moved(after(left[i], *gate), x_down, x_down, i)
-        from_left[i] = moved(added(right[i], far_up[i]).astype(BF), x_up, x_up, i)
-        from_right[i + 1] = moved(added(left[i + 1], far_down[i + 1]).astype(BF), x_down, x_down, i + 1)
-        gate = (far_up[i], far_down[i + 1])
-        raised = [added(mine[n][1], from_left[n][1], from_right[n][1]).astype(BF) for n in (i, i + 1)]
         pairs = [(a * ROWS + n, (a + 1) * ROWS + n) for a in range(SECS - 1) for n in range(ROWS) if COUNT[n] > i]
-        above.append(lax.ppermute(jnp.stack(raised), ("sec", "row"), pairs))
-    here = [added(mine[n][0], from_left[n][0], from_right[n][0]) for n in range(4)]
+        above.append(lax.ppermute(jnp.stack(raised[i : i + 2]), ("sec", "row"), pairs))
 
     out = pl.pallas_call(
         unpack_kernel,

time: 203 us -> 200 us (0.985)
  the two profiles are of different devices: /device:TPU:36 before, /device:TPU:12 now
where the time goes in v8:
time: 200 us
  starting transfers between devices  75.2 us (38%)
  waiting for transfers between devices  74.2 us (37%)
  Pallas kernels  22.8 us (11%)
  between operations  13.9 us (7%)
  other arithmetic  11.1 us (6%)
  local copies, waits for them, and re-layouts  2.73 us (1%)
    ppermute x20, starting transfers between devices, sent(): lax.ppermute(value, 'row', [(n, move(n)) for n in range(ROWS) if owner(n)...  59.9 us
    ppermute x20, waiting for transfers between devices, sent(): lax.ppermute(value, 'row', [(n, move(n)) for n in range(ROWS) if owner(n)...  47.5 us
    pallas_call x1, Pallas kernels, body(): pl.pallas_call(terms_kernel, in_specs=[smem] * 3 + [hbm] * 13, out_specs=...  14.5 us
    ppermute x1, waiting for transfers between devices, body(): rim_low = lax.ppermute(strip_low, 'sec', up(1))  13.7 us
    ppermute x2, waiting for transfers between devices, body(): lax.ppermute(jnp.stack(raised[i:i + 2]), ('sec', 'row'), pairs)  9.45 us
    convert_element_type x4, other arithmetic, body(): added(mine[i][1], from_left[i][1], from_right[i][1]).astype(BF)  4.01 us
  transfers between devices with their start and end apart: 27, of which 12 were waited for; matrix products, arithmetic and copies ran while one was open for 6% of the time, Pallas kernels for 1%

profile of v8, /device:TPU:12, one launch (start us, length us, event | category | flops | bytes accessed | tf_op | source)
XLA Modules:
  0.0 199.9 jit_solution(10218269918672928888)
XLA Ops:
  7.2 2.6 %shard_map.73 = (bf16[2,272,512]{2,1,0:T(8,128)(2,1)}, bf16[272,512]{1,0:T(8,128)(2,1)}, bf16[272,512]{1,0:T(8,128)(2,1)}) custom-call(s32[2]{0:T(128)} %pad_add_fusion.place, s32[2,16]{1,0:T(2,128)} %bitcast.60, s32[2,16]{1,0:T(2,128)} %bitcast.62, s32[3,2,8]{2,1,0:T(2,128)} %bitcast.64, f32[2,8]{1,0:T(2,128)} %coeffs.1, bf16[4,256,512]{2,1,0:T(8,128)(2,1)} %bitcast.58), custom_call_target="tpu_custom_call" | custom-call | tf_op jit(solution)/shard_map/pallas_call | solution.py:243
  9.8 6.3 %collective-permute-start.4 = (bf16[2,272,512]{2,1,0:T(8,128)(2,1)}, bf16[2,272,512]{2,1,0:T(8,128)(2,1)S(1)}, u32[]{:S(2)}, u32[]{:S(2)}) collective-permute-start(bf16[2,272,512]{2,1,0:T(8,128)(2,1)} %get-tuple-element.30.refs_0_), channel_id=1, source_target_pairs={{0,12},{1,13},{2,14},{3,15},{4,0},{5,1},{6,2},{7,3},{8,4},{9,5},{1... | collective-permute-start | bytes 1671176 | tf_op jit(solution)/shard_map/ppermute | solution.py:256
  16.1 2.5 %shard_map.74 = (bf16[6,256,256]{2,1,0:T(8,128)(2,1)}, bf16[6,64,256]{2,1,0:T(8,128)(2,1)}, bf16[3,64,256]{2,1,0:T(8,128)(2,1)}, bf16[3,64,256]{2,1,0:T(8,128)(2,1)}) custom-call(s32[2]{0:T(128)} %pad_add_fusion.place, bf16[4,2,256,256]{3,2,1,0:T(8,128)(2,1)} %bitcast.59), custom_call_target="tpu_custom_call" | custom-call | tf_op jit(solution)/shard_map/pallas_call | solution.py:269
  18.6 1.9 collective-permute-start
  20.5 2.8 %collective-permute-start.11 = (bf16[3,64,256]{2,1,0:T(8,128)(2,1)}, bf16[3,64,256]{2,1,0:T(8,128)(2,1)S(1)}, u32[]{:S(2)}, u32[]{:S(2)}) collective-permute-start(bf16[3,64,256]{2,1,0:T(8,128)(2,1)} %get-tuple-element.38), channel_id=1, source_target_pairs={{32,0},{48,16},{64,32},{80,48},{96,64},{112,80},{128,96},{144,112}... | collective-permute-start | bytes 294920 | tf_op jit(solution)/shard_map/ppermute | solution.py:295
  23.3 3.6 %collective-permute-start.10 = (bf16[6,64,256]{2,1,0:T(8,128)(2,1)}, bf16[6,64,256]{2,1,0:T(8,128)(2,1)S(1)}, u32[]{:S(2)}, u32[]{:S(2)}) collective-permute-start(bf16[6,64,256]{2,1,0:T(8,128)(2,1)} %get-tuple-element.37), channel_id=1, source_target_pairs={{16,0},{32,16},{48,32},{64,48},{80,64},{96,80},{112,96},{128,112},... | collective-permute-start | bytes 589832 | tf_op jit(solution)/shard_map/ppermute | solution.py:294
  28.0 13.7 %collective-permute-done = bf16[3,64,256]{2,1,0:T(8,128)(2,1)S(1)} collective-permute-done((bf16[3,64,256]{2,1,0:T(8,128)(2,1)}, bf16[3,64,256]{2,1,0:T(8,128)(2,1)S(1)}, u32[]{:S(2)}, u32[]{:S(2)}) %collective-permute-start) | collective-permute-done | bytes 98336 | tf_op jit(solution)/shard_map/ppermute | solution.py:283
  41.7 3.1 %collective-permute-start.1 = (bf16[272,512]{1,0:T(8,128)(2,1)}, bf16[272,512]{1,0:T(8,128)(2,1)S(1)}, u32[]{:S(2)}, u32[]{:S(2)}) collective-permute-start(bf16[272,512]{1,0:T(8,128)(2,1)} %get-tuple-element.35), channel_id=1, source_target_pairs={{2,3},{6,5},{11,8},{15,12},{18,19},{22,21},{27,24},{31,28},{34,35}... | collective-permute-start | bytes 835592 | tf_op jit(solution)/shard_map/ppermute | solution.py:284
  46.4 2.8 %collective-permute-done.1 = bf16[272,512]{1,0:T(8,128)(2,1)S(1)} collective-permute-done((bf16[272,512]{1,0:T(8,128)(2,1)}, bf16[272,512]{1,0:T(8,128)(2,1)S(1)}, u32[]{:S(2)}, u32[]{:S(2)}) %collective-permute-start.1) | collective-permute-done | bytes 278560 | tf_op jit(solution)/shard_map/ppermute | solution.py:284
  50.3 2.3 %collective-permute-start.5 = (bf16[272,512]{1,0:T(8,128)(2,1)S(1)}, bf16[272,512]{1,0:T(8,128)(2,1)S(1)}, u32[]{:S(2)}, u32[]{:S(2)}) collective-permute-start(bf16[272,512]{1,0:T(8,128)(2,1)S(1)} %add.83.refs_1_), channel_id=1, source_target_pairs={{1,13},{2,14},{3,15},{5,1},{6,2},{7,3},{8,4},{10,6},{11,7},{12,8},... | collective-permute-start | bytes 835592 | tf_op jit(solution)/shard_map/ppermute | solution.py:256
  52.6 4.4 %collective-permute-start.3 = (bf16[272,512]{1,0:T(8,128)(2,1)S(1)}, bf16[272,512]{1,0:T(8,128)(2,1)S(1)}, u32[]{:S(2)}, u32[]{:S(2)}) collective-permute-start(bf16[272,512]{1,0:T(8,128)(2,1)S(1)} %add.83.refs_1_), channel_id=1, source_target_pairs={{1,5},{2,6},{3,7},{5,9},{6,10},{7,11},{8,12},{10,14},{11,15},{12,0... | collective-permute-start | bytes 835592 | tf_op jit(solution)/shard_map/ppermute | solution.py:256
  57.3 3.0 %collective-permute-start.6 = (bf16[272,512]{1,0:T(8,128)(2,1)S(1)}, bf16[272,512]{1,0:T(8,128)(2,1)S(1)}, u32[]{:S(2)}, u32[]{:S(2)}) collective-permute-start(bf16[272,512]{1,0:T(8,128)(2,1)S(1)} %get-tuple-element.66), channel_id=1, source_target_pairs={{0,4},{1,5},{2,6},{3,7},{4,8},{5,9},{6,10},{7,11},{8,12},{9,13},{1... | collective-permute-start | bytes 835592 | tf_op jit(solution)/shard_map/ppermute | solution.py:256
  60.2 6.8 %collective-permute-done.5.refs_5_ = bf16[272,512]{1,0:T(8,128)(2,1)S(1)} collective-permute-done((bf16[272,512]{1,0:T(8,128)(2,1)S(1)}, bf16[272,512]{1,0:T(8,128)(2,1)S(1)}, u32[]{:S(2)}, u32[]{:S(2)}) %collective-permute-start.5) | collective-permute-done | bytes 278560 | tf_op jit(solution)/shard_map/ppermute | solution.py:256
  67.1 5.5 %collective-permute-start.9 = (bf16[128,512]{1,0:T(8,128)(2,1)S(1)}, bf16[128,512]{1,0:T(8,128)(2,1)S(1)}, u32[]{:S(2)}, u32[]{:S(2)}) collective-permute-start(bf16[128,512]{1,0:T(8,128)(2,1)S(1)} %slice.195), channel_id=1, source_target_pairs={{1,13},{2,14},{3,15},{4,0},{6,2},{7,3},{8,4},{11,7},{13,9},{14,10}... | collective-permute-start | bytes 393224 | tf_op jit(solution)/shard_map/ppermute | solution.py:256
  72.6 1.3 collective-permute-start.8
  73.9 14.7 %collective-permute-done.8.refs_8_ = bf16[144,512]{1,0:T(8,128)(2,1)S(1)} collective-permute-done((bf16[144,512]{1,0:T(8,128)(2,1)S(1)}, bf16[144,512]{1,0:T(8,128)(2,1)S(1)}, u32[]{:S(2)}, u32[]{:S(2)}) %collective-permute-start.8) | collective-permute-done | bytes 147488 | tf_op jit(solution)/shard_map/ppermute | solution.py:256
  90.2 14.5 %shard_map.75 = (bf16[2,256,512]{2,1,0:T(8,128)(2,1)}, bf16[2,256,512]{2,1,0:T(8,128)(2,1)}, bf16[2,256,512]{2,1,0:T(8,128)(2,1)}, bf16[2,256,512]{2,1,0:T(8,128...) custom-call(s32[2]{0:T(128)} %pad_add_fusion.place, ...), custom_call_target="tpu_custom_call" | custom-call | tf_op jit(solution)/shard_map/pallas_call | solution.py:304
  104.7 5.8 %collective-permute-start.12 = (bf16[2,256,512]{2,1,0:T(8,128)(2,1)}, bf16[2,256,512]{2,1,0:T(8,128)(2,1)S(1)}, u32[]{:S(2)}, u32[]{:S(2)}) collective-permute-start(bf16[2,256,512]{2,1,0:T(8,128)(2,1)} %get-tuple-element.41), channel_id=1, source_target_pairs={{0,1},{1,2},{2,3},{3,0},{4,5},{5,6},{6,7},{7,4},{8,9},{9,10},{10,1... | collective-permute-start | bytes 1572872 | tf_op jit(solution)/shard_map/ppermute | solution.py:256
  110.5 2.1 %collective-permute-start.15 = (bf16[2,256,512]{2,1,0:T(8,128)(2,1)}, bf16[2,256,512]{2,1,0:T(8,128)(2,1)S(1)}, u32[]{:S(2)}, u32[]{:S(2)}) collective-permute-start(bf16[2,256,512]{2,1,0:T(8,128)(2,1)} %get-tuple-element.44), channel_id=1, source_target_pairs={{0,1},{1,2},{2,3},{3,0},{4,5},{5,6},{6,7},{7,4},{8,9},{9,10},{10,1... | collective-permute-start | bytes 1572872 | tf_op jit(solution)/shard_map/ppermute | solution.py:256
  113.3 9.9 %collective-permute-done.12 = bf16[2,256,512]{2,1,0:T(8,128)(2,1)S(1)} collective-permute-done((bf16[2,256,512]{2,1,0:T(8,128)(2,1)}, bf16[2,256,512]{2,1,0:T(8,128)(2,1)S(1)}, u32[]{:S(2)}, u32[]{:S(2)}) %collective-permute-start.12) | collective-permute-done | bytes 524320 | tf_op jit(solution)/shard_map/ppermute | solution.py:256
  125.6 2.8 %collective-permute-start.13 = (bf16[2,256,512]{2,1,0:T(8,128)(2,1)S(1)}, bf16[2,256,512]{2,1,0:T(8,128)(2,1)S(1)}, u32[]{:S(2)}, u32[]{:S(2)}) collective-permute-start(bf16[2,256,512]{2,1,0:T(8,128)(2,1)S(1)} %add_convert_fusion.3), channel_id=1, source_target_pairs={{0,1},{1,2},{2,3},{3,0},{4,5},{5,6},{6,7},{7,4},{8,9},{9,10},{10,1... | collective-permute-start | bytes 1572872 | tf_op jit(solution)/shard_map/ppermute | solution.py:256
  129.6 10.0 %collective-permute-start.17 = (bf16[2,256,512]{2,1,0:T(8,128)(2,1)S(1)}, bf16[2,256,512]{2,1,0:T(8,128)(2,1)S(1)}, u32[]{:S(2)}, u32[]{:S(2)}) collective-permute-start(bf16[2,256,512]{2,1,0:T(8,128)(2,1)S(1)} %add_convert_fusion.2), channel_id=1, source_target_pairs={{0,3},{1,0},{2,1},{3,2},{4,7},{5,4},{6,5},{7,6},{8,11},{9,8},{10,9... | collective-permute-start | bytes 1572872 | tf_op jit(solution)/shard_map/ppermute | solution.py:256
  140.8 11.0 %collective-permute-start.20 = (bf16[2,256,512]{2,1,0:T(8,128)(2,1)S(1)}, bf16[2,256,512]{2,1,0:T(8,128)(2,1)S(1)}, u32[]{:S(2)}, u32[]{:S(2)}) collective-permute-start(bf16[2,256,512]{2,1,0:T(8,128)(2,1)S(1)} %copy-done.17), channel_id=1, source_target_pairs={{2,1},{3,2},{4,7},{7,6},{8,11},{11,10},{12,15},{18,17},{19,18},{20... | collective-permute-start | bytes 1572872 | tf_op jit(solution)/shard_map/ppermute | solution.py:256
  152.0 1.4 collective-permute-start.21
  153.5 1.3 collective-permute-start.19
  157.1 1.4 collective-permute-done.17
  159.6 1.9 collective-permute-start.24
  161.5 8.3 %collective-permute-done.20 = bf16[2,256,512]{2,1,0:T(8,128)(2,1)S(1)} collective-permute-done((bf16[2,256,512]{2,1,0:T(8,128)(2,1)S(1)}, bf16[2,256,512]{2,1,0:T(8,128)(2,1)S(1)}, u32[]{:S(2)}, u32[]{:S(2)}) %collective-permute-start.20) | collective-permute-done | bytes 524320 | tf_op jit(solution)/shard_map/ppermute | solution.py:256
  169.8 5.1 %collective-permute-done.19 = bf16[2,256,512]{2,1,0:T(8,128)(2,1)S(1)} collective-permute-done((bf16[2,256,512]{2,1,0:T(8,128)(2,1)S(1)}, bf16[2,256,512]{2,1,0:T(8,128)(2,1)S(1)}, u32[]{:S(2)}, u32[]{:S(2)}) %collective-permute-start.19) | collective-permute-done | bytes 524320 | tf_op jit(solution)/shard_map/ppermute | solution.py:256
  177.6 1.9 collective-permute-start.25
  179.6 9.4 %collective-permute-done.25.refs_5_ = bf16[2,256,512]{2,1,0:T(8,128)(2,1)S(1)} collective-permute-done((bf16[2,256,512]{2,1,0:T(8,128)(2,1)S(1)}, bf16[2,256,512]{2,1,0:T(8,128)(2,1)S(1)}, u32[]{:S(2)}, u32[]{:S(2)}) %collective-permute-start.25) | collective-permute-done | bytes 524320 | tf_op jit(solution)/shard_map/ppermute | solution.py:348
  189.8 3.2 %shard_map.76 = bf16[4,256,512]{2,1,0:T(8,128)(2,1)} custom-call(s32[2]{0:T(128)} %pad_add_fusion.place, s32[2,16]{1,0:T(2,128)} %bitcast.61, s32[2,16]{1,0:T(2,128)} %bitcast.63, f32[256,512]{1,0:T(8,128)} %get-tuple-element.60.refs_0_, f32[256,512]{1,0:T(8,128)} %get-tuple-element.62.refs_1_, f32[256,512]{1,0:T(8,128)} %get-tuple-element.56.refs_2_, ...), custom_call_target="tpu_custom_call" | custom-call | tf_op jit(solution)/shard_map/pallas_call | solution.py:350
  (92 shorter events, 18.4 us)
Async XLA Ops:
  6.5 83.0 %all-gather.3.cloned.1.call-start = ((), (), s32[]{:S(2)}) async-start(), calls=%async_computation | async-start | bytes 1966080 | tf_op jit(solution)/shard_map/all_gather | solution.py:297
  9.8 47.2 %collective-permute-start.4 = (bf16[2,272,512]{2,1,0:T(8,128)(2,1)}, bf16[2,272,512]{2,1,0:T(8,128)(2,1)S(1)}, u32[]{:S(2)}, u32[]{:S(2)}) collective-permute-start(bf16[2,272,512]{2,1,0:T(8,128)(2,1)} %get-tuple-element.30.refs_0_), channel_id=1, source_target_pairs={{0,12},{1,13},{2,14},{3,15},{4,0},{5,1},{6,2},{7,3},{8,4},{9,5},{1... | collective-permute-start | bytes 1671176 | tf_op jit(solution)/shard_map/ppermute | solution.py:256
  16.1 41.1 %collective-permute-start.2 = (bf16[2,272,512]{2,1,0:T(8,128)(2,1)}, bf16[2,272,512]{2,1,0:T(8,128)(2,1)S(1)}, u32[]{:S(2)}, u32[]{:S(2)}) collective-permute-start(bf16[2,272,512]{2,1,0:T(8,128)(2,1)} %get-tuple-element.30.refs_0_), channel_id=1, source_target_pairs={{0,4},{1,5},{2,6},{3,7},{4,8},{5,9},{6,10},{7,11},{8,12},{9,13},{1... | collective-permute-start | bytes 1671176 | tf_op jit(solution)/shard_map/ppermute | solution.py:256
  18.6 23.2 %collective-permute-start = (bf16[3,64,256]{2,1,0:T(8,128)(2,1)}, bf16[3,64,256]{2,1,0:T(8,128)(2,1)S(1)}, u32[]{:S(2)}, u32[]{:S(2)}) collective-permute-start(bf16[3,64,256]{2,1,0:T(8,128)(2,1)} %get-tuple-element.34), channel_id=1, source_target_pairs={{0,16},{16,32},{32,48},{48,64},{64,80},{80,96},{96,112},{112,128},... | collective-permute-start | bytes 294920 | tf_op jit(solution)/shard_map/ppermute | solution.py:283
  20.5 24.4 %collective-permute-start.11 = (bf16[3,64,256]{2,1,0:T(8,128)(2,1)}, bf16[3,64,256]{2,1,0:T(8,128)(2,1)S(1)}, u32[]{:S(2)}, u32[]{:S(2)}) collective-permute-start(bf16[3,64,256]{2,1,0:T(8,128)(2,1)} %get-tuple-element.38), channel_id=1, source_target_pairs={{32,0},{48,16},{64,32},{80,48},{96,64},{112,80},{128,96},{144,112}... | collective-permute-start | bytes 294920 | tf_op jit(solution)/shard_map/ppermute | solution.py:295
  23.3 22.3 %collective-permute-start.10 = (bf16[6,64,256]{2,1,0:T(8,128)(2,1)}, bf16[6,64,256]{2,1,0:T(8,128)(2,1)S(1)}, u32[]{:S(2)}, u32[]{:S(2)}) collective-permute-start(bf16[6,64,256]{2,1,0:T(8,128)(2,1)} %get-tuple-element.37), channel_id=1, source_target_pairs={{16,0},{32,16},{48,32},{64,48},{80,64},{96,80},{112,96},{128,112},... | collective-permute-start | bytes 589832 | tf_op jit(solution)/shard_map/ppermute | solution.py:294
  41.7 7.5 %collective-permute-start.1 = (bf16[272,512]{1,0:T(8,128)(2,1)}, bf16[272,512]{1,0:T(8,128)(2,1)S(1)}, u32[]{:S(2)}, u32[]{:S(2)}) collective-permute-start(bf16[272,512]{1,0:T(8,128)(2,1)} %get-tuple-element.35), channel_id=1, source_target_pairs={{2,3},{6,5},{11,8},{15,12},{18,19},{22,21},{27,24},{31,28},{34,35}... | collective-permute-start | bytes 835592 | tf_op jit(solution)/shard_map/ppermute | solution.py:284
  50.2 39.3 %copy-start.2 = (bf16[272,512]{1,0:T(8,128)(2,1)}, bf16[272,512]{1,0:T(8,128)(2,1)S(1)}, u32[]{:S(2)}) copy-start(bf16[272,512]{1,0:T(8,128)(2,1)S(1)} %add.83.refs_1_) | copy-start | bytes 835588
  50.3 16.8 %collective-permute-start.5 = (bf16[272,512]{1,0:T(8,128)(2,1)S(1)}, bf16[272,512]{1,0:T(8,128)(2,1)S(1)}, u32[]{:S(2)}, u32[]{:S(2)}) collective-permute-start(bf16[272,512]{1,0:T(8,128)(2,1)S(1)} %add.83.refs_1_), channel_id=1, source_target_pairs={{1,13},{2,14},{3,15},{5,1},{6,2},{7,3},{8,4},{10,6},{11,7},{12,8},... | collective-permute-start | bytes 835592 | tf_op jit(solution)/shard_map/ppermute | solution.py:256
  52.6 20.0 %collective-permute-start.3 = (bf16[272,512]{1,0:T(8,128)(2,1)S(1)}, bf16[272,512]{1,0:T(8,128)(2,1)S(1)}, u32[]{:S(2)}, u32[]{:S(2)}) collective-permute-start(bf16[272,512]{1,0:T(8,128)(2,1)S(1)} %add.83.refs_1_), channel_id=1, source_target_pairs={{1,5},{2,6},{3,7},{5,9},{6,10},{7,11},{8,12},{10,14},{11,15},{12,0... | collective-permute-start | bytes 835592 | tf_op jit(solution)/shard_map/ppermute | solution.py:256
  57.1 31.6 %collective-permute-start.7 = (bf16[272,512]{1,0:T(8,128)(2,1)S(1)}, bf16[272,512]{1,0:T(8,128)(2,1)S(1)}, u32[]{:S(2)}, u32[]{:S(2)}) collective-permute-start(bf16[272,512]{1,0:T(8,128)(2,1)S(1)} %get-tuple-element.63), channel_id=1, source_target_pairs={{0,12},{1,13},{2,14},{3,15},{4,0},{5,1},{6,2},{7,3},{8,4},{9,5},{1... | collective-permute-start | bytes 835592 | tf_op jit(solution)/shard_map/ppermute | solution.py:256
  57.3 31.4 %collective-permute-start.6 = (bf16[272,512]{1,0:T(8,128)(2,1)S(1)}, bf16[272,512]{1,0:T(8,128)(2,1)S(1)}, u32[]{:S(2)}, u32[]{:S(2)}) collective-permute-start(bf16[272,512]{1,0:T(8,128)(2,1)S(1)} %get-tuple-element.66), channel_id=1, source_target_pairs={{0,4},{1,5},{2,6},{3,7},{4,8},{5,9},{6,10},{7,11},{8,12},{9,13},{1... | collective-permute-start | bytes 835592 | tf_op jit(solution)/shard_map/ppermute | solution.py:256
  67.1 22.5 %collective-permute-start.9 = (bf16[128,512]{1,0:T(8,128)(2,1)S(1)}, bf16[128,512]{1,0:T(8,128)(2,1)S(1)}, u32[]{:S(2)}, u32[]{:S(2)}) collective-permute-start(bf16[128,512]{1,0:T(8,128)(2,1)S(1)} %slice.195), channel_id=1, source_target_pairs={{1,13},{2,14},{3,15},{4,0},{6,2},{7,3},{8,4},{11,7},{13,9},{14,10}... | collective-permute-start | bytes 393224 | tf_op jit(solution)/shard_map/ppermute | solution.py:256
  72.6 16.1 %collective-permute-start.8 = (bf16[144,512]{1,0:T(8,128)(2,1)S(1)}, bf16[144,512]{1,0:T(8,128)(2,1)S(1)}, u32[]{:S(2)}, u32[]{:S(2)}) collective-permute-start(bf16[144,512]{1,0:T(8,128)(2,1)S(1)} %slice.193), channel_id=1, source_target_pairs={{0,4},{3,7},{5,9},{6,10},{7,11},{9,13},{10,14},{11,15},{12,0},{14,... | collective-permute-start | bytes 442376 | tf_op jit(solution)/shard_map/ppermute | solution.py:256
  104.7 36.1 %copy-start.17 = (bf16[2,256,512]{2,1,0:T(8,128)(2,1)S(1)}, bf16[2,256,512]{2,1,0:T(8,128)(2,1)}, u32[]{:S(2)}) copy-start(bf16[2,256,512]{2,1,0:T(8,128)(2,1)} %get-tuple-element.50) | copy-start | bytes 1572868
  104.7 47.2 %copy-start.5 = (bf16[2,256,512]{2,1,0:T(8,128)(2,1)S(1)}, bf16[2,256,512]{2,1,0:T(8,128)(2,1)}, u32[]{:S(2)}) copy-start(bf16[2,256,512]{2,1,0:T(8,128)(2,1)} %get-tuple-element.53) | copy-start | bytes 1572868
  104.7 47.3 %copy-start.16 = (bf16[2,256,512]{2,1,0:T(8,128)(2,1)S(1)}, bf16[2,256,512]{2,1,0:T(8,128)(2,1)}, u32[]{:S(2)}) copy-start(bf16[2,256,512]{2,1,0:T(8,128)(2,1)} %get-tuple-element.52) | copy-start | bytes 1572868
  104.7 50.1 %copy-start.9 = (bf16[2,256,512]{2,1,0:T(8,128)(2,1)S(1)}, bf16[2,256,512]{2,1,0:T(8,128)(2,1)}, u32[]{:S(2)}) copy-start(bf16[2,256,512]{2,1,0:T(8,128)(2,1)} %get-tuple-element.39) | copy-start | bytes 1572868
  104.7 18.5 %collective-permute-start.12 = (bf16[2,256,512]{2,1,0:T(8,128)(2,1)}, bf16[2,256,512]{2,1,0:T(8,128)(2,1)S(1)}, u32[]{:S(2)}, u32[]{:S(2)}) collective-permute-start(bf16[2,256,512]{2,1,0:T(8,128)(2,1)} %get-tuple-element.41), channel_id=1, source_target_pairs={{0,1},{1,2},{2,3},{3,0},{4,5},{5,6},{6,7},{7,4},{8,9},{9,10},{10,1... | collective-permute-start | bytes 1572872 | tf_op jit(solution)/shard_map/ppermute | solution.py:256
  110.5 15.1 %collective-permute-start.16 = (bf16[2,256,512]{2,1,0:T(8,128)(2,1)}, bf16[2,256,512]{2,1,0:T(8,128)(2,1)S(1)}, u32[]{:S(2)}, u32[]{:S(2)}) collective-permute-start(bf16[2,256,512]{2,1,0:T(8,128)(2,1)} %get-tuple-element.46), channel_id=1, source_target_pairs={{0,3},{1,0},{2,1},{3,2},{4,7},{5,4},{6,5},{7,6},{8,11},{9,8},{10,9... | collective-permute-start | bytes 1572872 | tf_op jit(solution)/shard_map/ppermute | solution.py:256
  110.5 41.5 %collective-permute-start.14 = (bf16[2,256,512]{2,1,0:T(8,128)(2,1)}, bf16[2,256,512]{2,1,0:T(8,128)(2,1)S(1)}, u32[]{:S(2)}, u32[]{:S(2)}) collective-permute-start(bf16[2,256,512]{2,1,0:T(8,128)(2,1)} %get-tuple-element.42), channel_id=1, source_target_pairs={{0,3},{1,0},{2,1},{3,2},{4,7},{5,4},{6,5},{7,6},{8,11},{9,8},{10,9... | collective-permute-start | bytes 1572872 | tf_op jit(solution)/shard_map/ppermute | solution.py:256
  110.5 45.3 %collective-permute-start.15 = (bf16[2,256,512]{2,1,0:T(8,128)(2,1)}, bf16[2,256,512]{2,1,0:T(8,128)(2,1)S(1)}, u32[]{:S(2)}, u32[]{:S(2)}) collective-permute-start(bf16[2,256,512]{2,1,0:T(8,128)(2,1)} %get-tuple-element.44), channel_id=1, source_target_pairs={{0,1},{1,2},{2,3},{3,0},{4,5},{5,6},{6,7},{7,4},{8,9},{9,10},{10,1... | collective-permute-start | bytes 1572872 | tf_op jit(solution)/shard_map/ppermute | solution.py:256
  112.6 17.0 %collective-permute-start.18 = (bf16[2,256,512]{2,1,0:T(8,128)(2,1)}, bf16[2,256,512]{2,1,0:T(8,128)(2,1)S(1)}, u32[]{:S(2)}, u32[]{:S(2)}) collective-permute-start(bf16[2,256,512]{2,1,0:T(8,128)(2,1)} %get-tuple-element.49), channel_id=1, source_target_pairs={{0,1},{3,0},{4,5},{5,6},{8,9},{9,10},{13,14},{16,17},{19,16},{20,2... | collective-permute-start | bytes 1572872 | tf_op jit(solution)/shard_map/ppermute | solution.py:256
  123.2 17.6 %collective-permute-start.22 = (bf16[2,256,512]{2,1,0:T(8,128)(2,1)}, bf16[2,256,512]{2,1,0:T(8,128)(2,1)S(1)}, u32[]{:S(2)}, u32[]{:S(2)}) collective-permute-start(bf16[2,256,512]{2,1,0:T(8,128)(2,1)} %get-tuple-element.54), channel_id=1, source_target_pairs={{0,3},{4,7},{9,8},{13,12},{16,19},{20,23},{25,24},{29,28},{32,35},... | collective-permute-start | bytes 1572872 | tf_op jit(solution)/shard_map/ppermute | solution.py:256
  125.6 27.9 %collective-permute-start.13 = (bf16[2,256,512]{2,1,0:T(8,128)(2,1)S(1)}, bf16[2,256,512]{2,1,0:T(8,128)(2,1)S(1)}, u32[]{:S(2)}, u32[]{:S(2)}) collective-permute-start(bf16[2,256,512]{2,1,0:T(8,128)(2,1)S(1)} %add_convert_fusion.3), channel_id=1, source_target_pairs={{0,1},{1,2},{2,3},{3,0},{4,5},{5,6},{6,7},{7,4},{8,9},{9,10},{10,1... | collective-permute-start | bytes 1572872 | tf_op jit(solution)/shard_map/ppermute | solution.py:256
  129.6 28.9 %collective-permute-start.17 = (bf16[2,256,512]{2,1,0:T(8,128)(2,1)S(1)}, bf16[2,256,512]{2,1,0:T(8,128)(2,1)S(1)}, u32[]{:S(2)}, u32[]{:S(2)}) collective-permute-start(bf16[2,256,512]{2,1,0:T(8,128)(2,1)S(1)} %add_convert_fusion.2), channel_id=1, source_target_pairs={{0,3},{1,0},{2,1},{3,2},{4,7},{5,4},{6,5},{7,6},{8,11},{9,8},{10,9... | collective-permute-start | bytes 1572872 | tf_op jit(solution)/shard_map/ppermute | solution.py:256
  140.8 29.0 %collective-permute-start.20 = (bf16[2,256,512]{2,1,0:T(8,128)(2,1)S(1)}, bf16[2,256,512]{2,1,0:T(8,128)(2,1)S(1)}, u32[]{:S(2)}, u32[]{:S(2)}) collective-permute-start(bf16[2,256,512]{2,1,0:T(8,128)(2,1)S(1)} %copy-done.17), channel_id=1, source_target_pairs={{2,1},{3,2},{4,7},{7,6},{8,11},{11,10},{12,15},{18,17},{19,18},{20... | collective-permute-start | bytes 1572872 | tf_op jit(solution)/shard_map/ppermute | solution.py:256
  152.0 23.8 %collective-permute-start.21 = (bf16[2,256,512]{2,1,0:T(8,128)(2,1)S(1)}, bf16[2,256,512]{2,1,0:T(8,128)(2,1)S(1)}, u32[]{:S(2)}, u32[]{:S(2)}) collective-permute-start(bf16[2,256,512]{2,1,0:T(8,128)(2,1)S(1)} %copy-done.16), channel_id=1, source_target_pairs={{1,2},{5,6},{10,11},{14,15},{17,18},{21,22},{26,27},{30,31},{33,34... | collective-permute-start | bytes 1572872 | tf_op jit(solution)/shard_map/ppermute | solution.py:256
  153.5 21.4 %collective-permute-start.19 = (bf16[2,256,512]{2,1,0:T(8,128)(2,1)S(1)}, bf16[2,256,512]{2,1,0:T(8,128)(2,1)S(1)}, u32[]{:S(2)}, u32[]{:S(2)}) collective-permute-start(bf16[2,256,512]{2,1,0:T(8,128)(2,1)S(1)} %add_convert_fusion.1), channel_id=1, source_target_pairs={{0,1},{1,2},{5,6},{6,7},{9,10},{10,11},{14,15},{16,17},{17,18},{21... | collective-permute-start | bytes 1572872 | tf_op jit(solution)/shard_map/ppermute | solution.py:256
  155.8 20.8 %collective-permute-start.23 = (bf16[2,256,512]{2,1,0:T(8,128)(2,1)S(1)}, bf16[2,256,512]{2,1,0:T(8,128)(2,1)S(1)}, u32[]{:S(2)}, u32[]{:S(2)}) collective-permute-start(bf16[2,256,512]{2,1,0:T(8,128)(2,1)S(1)} %add_convert_fusion), channel_id=1, source_target_pairs={{3,2},{7,6},{8,11},{12,15},{19,18},{23,22},{24,27},{28,31},{35,34}... | collective-permute-start | bytes 1572872 | tf_op jit(solution)/shard_map/ppermute | solution.py:256
  159.6 20.0 %collective-permute-start.24 = (bf16[2,256,512]{2,1,0:T(8,128)(2,1)S(1)}, bf16[2,256,512]{2,1,0:T(8,128)(2,1)S(1)}, u32[]{:S(2)}, u32[]{:S(2)}) collective-permute-start(bf16[2,256,512]{2,1,0:T(8,128)(2,1)S(1)} %pad_maximum_fusion), channel_id=1, source_target_pairs={{0,16},{1,17},{2,18},{3,19},{4,20},{5,21},{6,22},{7,23},{8,24},{9,... | collective-permute-start | bytes 1572872 | tf_op jit(solution)/shard_map/ppermute | solution.py:348
  177.6 11.4 %collective-permute-start.25 = (bf16[2,256,512]{2,1,0:T(8,128)(2,1)S(1)}, bf16[2,256,512]{2,1,0:T(8,128)(2,1)S(1)}, u32[]{:S(2)}, u32[]{:S(2)}) collective-permute-start(bf16[2,256,512]{2,1,0:T(8,128)(2,1)S(1)} %pad_maximum_fusion.1), channel_id=1, source_target_pairs={{1,17},{2,18},{6,22},{7,23},{10,26},{11,27},{15,31},{17,33},{18,34... | collective-permute-start | bytes 1572872 | tf_op jit(solution)/shard_map/ppermute | solution.py:348
  (13 other events, 212.6 us)
Sparse Core Ops, SparseCore 0:
  46.5 28.1 all-gather.2

commit v9 on v8

--- a/solution.py
+++ b/solution.py
@@ -122,9 +122,9 @@
 
 def terms_kernel(place, ints, values, *refs):
     two, three, lone = (refs[0], refs[2], refs[4]), (refs[1], refs[3], refs[5]), refs[6:9]
-    across2b, ket_in, bra_own, rim = refs[9:13]
-    outs = refs[13:29]
-    env_all, ket, bra_all, total, rounded, todo, scale, size, env_sem, ket_sem, bra_sem, out_sem = refs[29:]
+    across2b, ket_in, bra_own, rim, swapped, crossed = refs[9:15]
+    outs = refs[15:31]
+    env_all, ket, bra_all, total, rounded, todo, scale, size, env_sem, ket_sem, bra_sem, out_sem = refs[31:]
     copies = []
     body_rows = pl.ds(HEAD, BB)
     views = []
@@ -137,11 +137,14 @@
     copies.append(pltpu.make_async_copy(across2b, env_all.at[11, pl.ds(BB // 2, BB // 2)], env_sem.at[12]))
     copies += [pltpu.make_async_copy(ket_in.at[s], ket.at[pl.ds(2 * s, 2)], ket_sem.at[s]) for s in range(4)]
     copies.append(pltpu.make_async_copy(bra_own, bra_all.at[pl.ds(6, 6)], bra_sem.at[0]))
-    for n in range(NX):
-        lines = pl.ds(QUARTER * n, QUARTER)
+    x = place[0] % NX
+    y = NX - 1 - x
+    quarters = ((rim, 0, x), (swapped, 0, x + 1 - 2 * (x % 2)), (crossed, 0, y), (crossed, 12, y + 1 - 2 * (y % 2)))
+    for n, (ref, at, owner) in enumerate(quarters):
+        lines = pl.ds(pl.multiple_of(QUARTER * owner, QUARTER), QUARTER)
         for m, (first, count, to) in enumerate(((0, 3, 0), (3, 6, 12), (9, 3, 21))):
             copies.append(pltpu.make_async_copy(
-                rim.at[n, pl.ds(first, count)], bra_all.at[pl.ds(to, count), lines], bra_sem.at[1 + 3 * n + m]
+                ref.at[pl.ds(at + first, count)], bra_all.at[pl.ds(to, count), lines], bra_sem.at[1 + 3 * n + m]
             ))
     for copy in copies:
         copy.start()
@@ -294,7 +297,8 @@
         lax.ppermute(strip, "sec", down(1)),
         lax.ppermute(strip_high, "sec", down(2)),
     ])
-    bra_rim = lax.all_gather(rim, "row", axis_index_groups=[[NX * z + x for x in range(NX)] for z in range(NZ)])
+    swapped = lax.ppermute(rim, "row", [(n, n ^ 1) for n in range(ROWS)])
+    crossed = lax.ppermute(jnp.concatenate([rim, swapped]), "row", [(n, n ^ 3) for n in range(ROWS)])
 
     heads = [own01[0], own01[1], own2, behind01[0], behind01[1], behind2, ahead01[0], ahead01[1], ahead2,
              across0, across1, across2a]
@@ -303,7 +307,7 @@
     hbm = pl.BlockSpec(memory_space=pl.ANY)
     sums = pl.pallas_call(
         terms_kernel,
-        in_specs=[smem] * 3 + [hbm] * 13,
+        in_specs=[smem] * 3 + [hbm] * 15,
         out_specs=[hbm] * 16,
         out_shape=[pair] * 16,
         scratch_shapes=[
@@ -322,7 +326,7 @@
         ],
         compiler_params=params,
     )(place, values.astype(jnp.int32), values, own01, own2, behind01, behind2, ahead01, ahead2,
-      across0, across1, across2a, across2b, ket_mps[:, 0], bra_own, bra_rim)
+      across0, across1, across2a, across2b, ket_mps[:, 0], bra_own, rim, swapped, crossed)
     mine, left, right, far = sums[:4], sums[4:8], sums[8:12], sums[12:]
 
     def added(*parts):

time: 200 us -> 189 us (0.945)
  between operations: 13.9 us -> 0.59 us
  local copies, waits for them, and re-layouts: 2.73 us -> 5.85 us
    ppermute x20, waiting for transfers between devices: 47.5 us -> 45.4 us  [sent(): lax.ppermute(value, 'row', [(n, move(n)) for n in range(ROWS) if owner(n)...]
  transfers between devices with their start and end apart: 27 -> 28, of which waited for: 12 -> 12; matrix products, arithmetic and copies ran while one was open for 6% -> 7% of each run, Pallas kernels for 1% -> 1%
where the time goes in v9:
time: 189 us; the launch traced here: 190 us
  starting transfers between devices  74.7 us (40%)
  waiting for transfers between devices  73.9 us (39%)
  Pallas kernels  24.4 us (13%)
  other arithmetic  10.2 us (5%)
  local copies, waits for them, and re-layouts  5.85 us (3%)
    ppermute x20, starting transfers between devices, sent(): lax.ppermute(value, 'row', [(n, move(n)) for n in range(ROWS) if owner(n)...  58 us
    ppermute x20, waiting for transfers between devices, sent(): lax.ppermute(value, 'row', [(n, move(n)) for n in range(ROWS) if owner(n)...  45.4 us
    pallas_call x1, Pallas kernels, body(): pl.pallas_call(terms_kernel, in_specs=[smem] * 3 + [hbm] * 15, out_specs=...  16.1 us
    ppermute x1, waiting for transfers between devices, body(): rim_low = lax.ppermute(strip_low, 'sec', up(1))  13.7 us
    ppermute x2, waiting for transfers between devices, body(): lax.ppermute(jnp.stack(raised[i:i + 2]), ('sec', 'row'), pairs)  9.45 us
    ppermute x1, waiting for transfers between devices, body(): borrowed = lax.ppermute(after(moving, rim_low), 'row', lent)  4.73 us
    convert_element_type x4, other arithmetic, body(): added(mine[i][1], from_left[i][1], from_right[i][1]).astype(BF)  4.03 us
    ppermute x2, starting transfers between devices, body(): lax.ppermute(jnp.stack(raised[i:i + 2]), ('sec', 'row'), pairs)  3.84 us
  transfers between devices with their start and end apart: 28, of which 12 were waited for; matrix products, arithmetic and copies ran while one was open for 7% of the time, Pallas kernels for 1%

profile of v9, /device:TPU:12, one launch (start us, length us, event | category | flops | bytes accessed | tf_op | source)
XLA Modules:
  0.0 189.7 jit_solution(7097422578059071425)
XLA Ops:
  0.6 2.6 %shard_map.73 = (bf16[2,272,512]{2,1,0:T(8,128)(2,1)}, bf16[272,512]{1,0:T(8,128)(2,1)}, bf16[272,512]{1,0:T(8,128)(2,1)}) custom-call(s32[2]{0:T(128)} %pad_add_fusion.place, s32[2,16]{1,0:T(2,128)} %bitcast.58, s32[2,16]{1,0:T(2,128)} %bitcast.60, s32[3,2,8]{2,1,0:T(2,128)} %bitcast.62, f32[2,8]{1,0:T(2,128)} %coeffs.1, bf16[4,256,512]{2,1,0:T(8,128)(2,1)} %bitcast.56), custom_call_target="tpu_custom_call" | custom-call | tf_op jit(solution)/shard_map/pallas_call | solution.py:246
  3.2 6.3 %collective-permute-start.4 = (bf16[2,272,512]{2,1,0:T(8,128)(2,1)}, bf16[2,272,512]{2,1,0:T(8,128)(2,1)S(1)}, u32[]{:S(2)}, u32[]{:S(2)}) collective-permute-start(bf16[2,272,512]{2,1,0:T(8,128)(2,1)} %get-tuple-element.30.refs_0_), channel_id=1, source_target_pairs={{0,12},{1,13},{2,14},{3,15},{4,0},{5,1},{6,2},{7,3},{8,4},{9,5},{1... | collective-permute-start | bytes 1671176 | tf_op jit(solution)/shard_map/ppermute | solution.py:259
  9.5 2.5 %shard_map.74 = (bf16[6,256,256]{2,1,0:T(8,128)(2,1)}, bf16[6,64,256]{2,1,0:T(8,128)(2,1)}, bf16[3,64,256]{2,1,0:T(8,128)(2,1)}, bf16[3,64,256]{2,1,0:T(8,128)(2,1)}) custom-call(s32[2]{0:T(128)} %pad_add_fusion.place, bf16[4,2,256,256]{3,2,1,0:T(8,128)(2,1)} %bitcast.57), custom_call_target="tpu_custom_call" | custom-call | tf_op jit(solution)/shard_map/pallas_call | solution.py:272
  12.0 1.9 %collective-permute-start = (bf16[3,64,256]{2,1,0:T(8,128)(2,1)}, bf16[3,64,256]{2,1,0:T(8,128)(2,1)S(1)}, u32[]{:S(2)}, u32[]{:S(2)}) collective-permute-start(bf16[3,64,256]{2,1,0:T(8,128)(2,1)} %get-tuple-element.34), channel_id=1, source_target_pairs={{0,16},{16,32},{32,48},{48,64},{64,80},{80,96},{96,112},{112,128},... | collective-permute-start | bytes 294920 | tf_op jit(solution)/shard_map/ppermute | solution.py:286
  13.9 2.8 %collective-permute-start.11 = (bf16[3,64,256]{2,1,0:T(8,128)(2,1)}, bf16[3,64,256]{2,1,0:T(8,128)(2,1)S(1)}, u32[]{:S(2)}, u32[]{:S(2)}) collective-permute-start(bf16[3,64,256]{2,1,0:T(8,128)(2,1)} %get-tuple-element.38), channel_id=1, source_target_pairs={{32,0},{48,16},{64,32},{80,48},{96,64},{112,80},{128,96},{144,112}... | collective-permute-start | bytes 294920 | tf_op jit(solution)/shard_map/ppermute | solution.py:298
  16.7 3.6 %collective-permute-start.10 = (bf16[6,64,256]{2,1,0:T(8,128)(2,1)}, bf16[6,64,256]{2,1,0:T(8,128)(2,1)S(1)}, u32[]{:S(2)}, u32[]{:S(2)}) collective-permute-start(bf16[6,64,256]{2,1,0:T(8,128)(2,1)} %get-tuple-element.37), channel_id=1, source_target_pairs={{16,0},{32,16},{48,32},{64,48},{80,64},{96,80},{112,96},{128,112},... | collective-permute-start | bytes 589832 | tf_op jit(solution)/shard_map/ppermute | solution.py:297
  21.5 13.7 %collective-permute-done = bf16[3,64,256]{2,1,0:T(8,128)(2,1)S(1)} collective-permute-done((bf16[3,64,256]{2,1,0:T(8,128)(2,1)}, bf16[3,64,256]{2,1,0:T(8,128)(2,1)S(1)}, u32[]{:S(2)}, u32[]{:S(2)}) %collective-permute-start) | collective-permute-done | bytes 98336 | tf_op jit(solution)/shard_map/ppermute | solution.py:286
  35.2 3.1 %collective-permute-start.1 = (bf16[272,512]{1,0:T(8,128)(2,1)}, bf16[272,512]{1,0:T(8,128)(2,1)S(1)}, u32[]{:S(2)}, u32[]{:S(2)}) collective-permute-start(bf16[272,512]{1,0:T(8,128)(2,1)} %get-tuple-element.35), channel_id=1, source_target_pairs={{2,3},{6,5},{11,8},{15,12},{18,19},{22,21},{27,24},{31,28},{34,35}... | collective-permute-start | bytes 835592 | tf_op jit(solution)/shard_map/ppermute | solution.py:287
  40.3 4.7 %collective-permute-done.1 = bf16[272,512]{1,0:T(8,128)(2,1)S(1)} collective-permute-done((bf16[272,512]{1,0:T(8,128)(2,1)}, bf16[272,512]{1,0:T(8,128)(2,1)S(1)}, u32[]{:S(2)}, u32[]{:S(2)}) %collective-permute-start.1) | collective-permute-done | bytes 278560 | tf_op jit(solution)/shard_map/ppermute | solution.py:287
  46.1 1.9 %collective-permute-start.5 = (bf16[272,512]{1,0:T(8,128)(2,1)S(1)}, bf16[272,512]{1,0:T(8,128)(2,1)S(1)}, u32[]{:S(2)}, u32[]{:S(2)}) collective-permute-start(bf16[272,512]{1,0:T(8,128)(2,1)S(1)} %add.83.refs_1_), channel_id=1, source_target_pairs={{1,13},{2,14},{3,15},{5,1},{6,2},{7,3},{8,4},{10,6},{11,7},{12,8},... | collective-permute-start | bytes 835592 | tf_op jit(solution)/shard_map/ppermute | solution.py:259
  48.0 4.8 %collective-permute-start.3 = (bf16[272,512]{1,0:T(8,128)(2,1)S(1)}, bf16[272,512]{1,0:T(8,128)(2,1)S(1)}, u32[]{:S(2)}, u32[]{:S(2)}) collective-permute-start(bf16[272,512]{1,0:T(8,128)(2,1)S(1)} %add.83.refs_1_), channel_id=1, source_target_pairs={{1,5},{2,6},{3,7},{5,9},{6,10},{7,11},{8,12},{10,14},{11,15},{12,0... | collective-permute-start | bytes 835592 | tf_op jit(solution)/shard_map/ppermute | solution.py:259
  53.1 3.0 %collective-permute-start.6 = (bf16[272,512]{1,0:T(8,128)(2,1)S(1)}, bf16[272,512]{1,0:T(8,128)(2,1)S(1)}, u32[]{:S(2)}, u32[]{:S(2)}) collective-permute-start(bf16[272,512]{1,0:T(8,128)(2,1)S(1)} %get-tuple-element.66), channel_id=1, source_target_pairs={{0,4},{1,5},{2,6},{3,7},{4,8},{5,9},{6,10},{7,11},{8,12},{9,13},{1... | collective-permute-start | bytes 835592 | tf_op jit(solution)/shard_map/ppermute | solution.py:259
  56.3 9.8 %collective-permute-done.5.refs_5_ = bf16[272,512]{1,0:T(8,128)(2,1)S(1)} collective-permute-done((bf16[272,512]{1,0:T(8,128)(2,1)S(1)}, bf16[272,512]{1,0:T(8,128)(2,1)S(1)}, u32[]{:S(2)}, u32[]{:S(2)}) %collective-permute-start.5) | collective-permute-done | bytes 278560 | tf_op jit(solution)/shard_map/ppermute | solution.py:259
  66.8 5.4 %collective-permute-start.9 = (bf16[128,512]{1,0:T(8,128)(2,1)}, bf16[128,512]{1,0:T(8,128)(2,1)}, u32[]{:S(2)}, u32[]{:S(2)}) collective-permute-start(bf16[128,512]{1,0:T(8,128)(2,1)} %slice.195), channel_id=1, source_target_pairs={{1,13},{2,14},{3,15},{4,0},{6,2},{7,3},{8,4},{11,7},{13,9},{14,10}... | collective-permute-start | bytes 393224 | tf_op jit(solution)/shard_map/ppermute | solution.py:259
  72.3 1.3 collective-permute-start.8
  73.6 9.8 %collective-permute-done.8.refs_8_ = bf16[144,512]{1,0:T(8,128)(2,1)S(1)} collective-permute-done((bf16[144,512]{1,0:T(8,128)(2,1)S(1)}, bf16[144,512]{1,0:T(8,128)(2,1)S(1)}, u32[]{:S(2)}, u32[]{:S(2)}) %collective-permute-start.8) | collective-permute-done | bytes 147488 | tf_op jit(solution)/shard_map/ppermute | solution.py:259
  87.2 16.1 %shard_map.75 = (bf16[2,256,512]{2,1,0:T(8,128)(2,1)}, bf16[2,256,512]{2,1,0:T(8,128)(2,1)}, bf16[2,256,512]{2,1,0:T(8,128)(2,1)}, bf16[2,256,512]{2,1,0:T(8,128...) custom-call(s32[2]{0:T(128)} %pad_add_fusion.place, ...), custom_call_target="tpu_custom_call" | custom-call | tf_op jit(solution)/shard_map/pallas_call | solution.py:308
  103.3 4.0 %collective-permute-start.14 = (bf16[2,256,512]{2,1,0:T(8,128)(2,1)}, bf16[2,256,512]{2,1,0:T(8,128)(2,1)S(1)}, u32[]{:S(2)}, u32[]{:S(2)}) collective-permute-start(bf16[2,256,512]{2,1,0:T(8,128)(2,1)} %get-tuple-element.41), channel_id=1, source_target_pairs={{0,1},{1,2},{2,3},{3,0},{4,5},{5,6},{6,7},{7,4},{8,9},{9,10},{10,1... | collective-permute-start | bytes 1572872 | tf_op jit(solution)/shard_map/ppermute | solution.py:259
  107.3 2.1 %collective-permute-start.17 = (bf16[2,256,512]{2,1,0:T(8,128)(2,1)}, bf16[2,256,512]{2,1,0:T(8,128)(2,1)S(1)}, u32[]{:S(2)}, u32[]{:S(2)}) collective-permute-start(bf16[2,256,512]{2,1,0:T(8,128)(2,1)} %get-tuple-element.44), channel_id=1, source_target_pairs={{0,1},{1,2},{2,3},{3,0},{4,5},{5,6},{6,7},{7,4},{8,9},{9,10},{10,1... | collective-permute-start | bytes 1572872 | tf_op jit(solution)/shard_map/ppermute | solution.py:259
  110.0 9.9 %collective-permute-done.14 = bf16[2,256,512]{2,1,0:T(8,128)(2,1)S(1)} collective-permute-done((bf16[2,256,512]{2,1,0:T(8,128)(2,1)}, bf16[2,256,512]{2,1,0:T(8,128)(2,1)S(1)}, u32[]{:S(2)}, u32[]{:S(2)}) %collective-permute-start.14) | collective-permute-done | bytes 524320 | tf_op jit(solution)/shard_map/ppermute | solution.py:259
  122.3 2.6 %collective-permute-start.15 = (bf16[2,256,512]{2,1,0:T(8,128)(2,1)S(1)}, bf16[2,256,512]{2,1,0:T(8,128)(2,1)S(1)}, u32[]{:S(2)}, u32[]{:S(2)}) collective-permute-start(bf16[2,256,512]{2,1,0:T(8,128)(2,1)S(1)} %add_convert_fusion.3), channel_id=1, source_target_pairs={{0,1},{1,2},{2,3},{3,0},{4,5},{5,6},{6,7},{7,4},{8,9},{9,10},{10,1... | collective-permute-start | bytes 1572872 | tf_op jit(solution)/shard_map/ppermute | solution.py:259
  126.1 10.2 %collective-permute-start.19 = (bf16[2,256,512]{2,1,0:T(8,128)(2,1)S(1)}, bf16[2,256,512]{2,1,0:T(8,128)(2,1)S(1)}, u32[]{:S(2)}, u32[]{:S(2)}) collective-permute-start(bf16[2,256,512]{2,1,0:T(8,128)(2,1)S(1)} %add_convert_fusion.2), channel_id=1, source_target_pairs={{0,3},{1,0},{2,1},{3,2},{4,7},{5,4},{6,5},{7,6},{8,11},{9,8},{10,9... | collective-permute-start | bytes 1572872 | tf_op jit(solution)/shard_map/ppermute | solution.py:259
  137.6 11.0 %collective-permute-start.22 = (bf16[2,256,512]{2,1,0:T(8,128)(2,1)S(1)}, bf16[2,256,512]{2,1,0:T(8,128)(2,1)S(1)}, u32[]{:S(2)}, u32[]{:S(2)}) collective-permute-start(bf16[2,256,512]{2,1,0:T(8,128)(2,1)S(1)} %copy-done.19), channel_id=1, source_target_pairs={{2,1},{3,2},{4,7},{7,6},{8,11},{11,10},{12,15},{18,17},{19,18},{20... | collective-permute-start | bytes 1572872 | tf_op jit(solution)/shard_map/ppermute | solution.py:259
  148.8 1.4 collective-permute-start.23
  150.2 1.3 collective-permute-start.21
  153.8 1.4 collective-permute-done.19
  156.3 1.9 %collective-permute-start.26 = (bf16[2,256,512]{2,1,0:T(8,128)(2,1)S(1)}, bf16[2,256,512]{2,1,0:T(8,128)(2,1)S(1)}, u32[]{:S(2)}, u32[]{:S(2)}) collective-permute-start(bf16[2,256,512]{2,1,0:T(8,128)(2,1)S(1)} %pad_maximum_fusion.1), channel_id=1, source_target_pairs={{0,16},{1,17},{2,18},{3,19},{4,20},{5,21},{6,22},{7,23},{8,24},{9,... | collective-permute-start | bytes 1572872 | tf_op jit(solution)/shard_map/ppermute | solution.py:352
  158.3 8.2 %collective-permute-done.22 = bf16[2,256,512]{2,1,0:T(8,128)(2,1)S(1)} collective-permute-done((bf16[2,256,512]{2,1,0:T(8,128)(2,1)S(1)}, bf16[2,256,512]{2,1,0:T(8,128)(2,1)S(1)}, u32[]{:S(2)}, u32[]{:S(2)}) %collective-permute-start.22) | collective-permute-done | bytes 524320 | tf_op jit(solution)/shard_map/ppermute | solution.py:259
  166.5 5.0 %collective-permute-done.21 = bf16[2,256,512]{2,1,0:T(8,128)(2,1)S(1)} collective-permute-done((bf16[2,256,512]{2,1,0:T(8,128)(2,1)S(1)}, bf16[2,256,512]{2,1,0:T(8,128)(2,1)S(1)}, u32[]{:S(2)}, u32[]{:S(2)}) %collective-permute-start.21) | collective-permute-done | bytes 524320 | tf_op jit(solution)/shard_map/ppermute | solution.py:259
  174.2 1.9 %collective-permute-start.27 = (bf16[2,256,512]{2,1,0:T(8,128)(2,1)S(1)}, bf16[2,256,512]{2,1,0:T(8,128)(2,1)S(1)}, u32[]{:S(2)}, u32[]{:S(2)}) collective-permute-start(bf16[2,256,512]{2,1,0:T(8,128)(2,1)S(1)} %pad_maximum_fusion.2), channel_id=1, source_target_pairs={{1,17},{2,18},{6,22},{7,23},{10,26},{11,27},{15,31},{17,33},{18,34... | collective-permute-start | bytes 1572872 | tf_op jit(solution)/shard_map/ppermute | solution.py:352
  176.2 9.4 %collective-permute-done.27.refs_5_ = bf16[2,256,512]{2,1,0:T(8,128)(2,1)S(1)} collective-permute-done((bf16[2,256,512]{2,1,0:T(8,128)(2,1)S(1)}, bf16[2,256,512]{2,1,0:T(8,128)(2,1)S(1)}, u32[]{:S(2)}, u32[]{:S(2)}) %collective-permute-start.27) | collective-permute-done | bytes 524320 | tf_op jit(solution)/shard_map/ppermute | solution.py:352
  186.4 3.2 %shard_map.76 = bf16[4,256,512]{2,1,0:T(8,128)(2,1)} custom-call(s32[2]{0:T(128)} %pad_add_fusion.place, s32[2,16]{1,0:T(2,128)} %bitcast.59, s32[2,16]{1,0:T(2,128)} %bitcast.61, f32[256,512]{1,0:T(8,128)} %get-tuple-element.60.refs_0_, f32[256,512]{1,0:T(8,128)} %get-tuple-element.62.refs_1_, f32[256,512]{1,0:T(8,128)} %get-tuple-element.56.refs_2_, ...), custom_call_target="tpu_custom_call" | custom-call | tf_op jit(solution)/shard_map/pallas_call | solution.py:354
  (100 shorter events, 22.0 us)
Async XLA Ops:
  3.2 49.7 %collective-permute-start.4 = (bf16[2,272,512]{2,1,0:T(8,128)(2,1)}, bf16[2,272,512]{2,1,0:T(8,128)(2,1)S(1)}, u32[]{:S(2)}, u32[]{:S(2)}) collective-permute-start(bf16[2,272,512]{2,1,0:T(8,128)(2,1)} %get-tuple-element.30.refs_0_), channel_id=1, source_target_pairs={{0,12},{1,13},{2,14},{3,15},{4,0},{5,1},{6,2},{7,3},{8,4},{9,5},{1... | collective-permute-start | bytes 1671176 | tf_op jit(solution)/shard_map/ppermute | solution.py:259
  9.5 43.5 %collective-permute-start.2 = (bf16[2,272,512]{2,1,0:T(8,128)(2,1)}, bf16[2,272,512]{2,1,0:T(8,128)(2,1)S(1)}, u32[]{:S(2)}, u32[]{:S(2)}) collective-permute-start(bf16[2,272,512]{2,1,0:T(8,128)(2,1)} %get-tuple-element.30.refs_0_), channel_id=1, source_target_pairs={{0,4},{1,5},{2,6},{3,7},{4,8},{5,9},{6,10},{7,11},{8,12},{9,13},{1... | collective-permute-start | bytes 1671176 | tf_op jit(solution)/shard_map/ppermute | solution.py:259
  12.0 23.2 %collective-permute-start = (bf16[3,64,256]{2,1,0:T(8,128)(2,1)}, bf16[3,64,256]{2,1,0:T(8,128)(2,1)S(1)}, u32[]{:S(2)}, u32[]{:S(2)}) collective-permute-start(bf16[3,64,256]{2,1,0:T(8,128)(2,1)} %get-tuple-element.34), channel_id=1, source_target_pairs={{0,16},{16,32},{32,48},{48,64},{64,80},{80,96},{96,112},{112,128},... | collective-permute-start | bytes 294920 | tf_op jit(solution)/shard_map/ppermute | solution.py:286
  13.9 25.1 %collective-permute-start.11 = (bf16[3,64,256]{2,1,0:T(8,128)(2,1)}, bf16[3,64,256]{2,1,0:T(8,128)(2,1)S(1)}, u32[]{:S(2)}, u32[]{:S(2)}) collective-permute-start(bf16[3,64,256]{2,1,0:T(8,128)(2,1)} %get-tuple-element.38), channel_id=1, source_target_pairs={{32,0},{48,16},{64,32},{80,48},{96,64},{112,80},{128,96},{144,112}... | collective-permute-start | bytes 294920 | tf_op jit(solution)/shard_map/ppermute | solution.py:298
  16.7 22.3 %collective-permute-start.10 = (bf16[6,64,256]{2,1,0:T(8,128)(2,1)}, bf16[6,64,256]{2,1,0:T(8,128)(2,1)S(1)}, u32[]{:S(2)}, u32[]{:S(2)}) collective-permute-start(bf16[6,64,256]{2,1,0:T(8,128)(2,1)} %get-tuple-element.37), channel_id=1, source_target_pairs={{16,0},{32,16},{48,32},{64,48},{80,64},{96,80},{112,96},{128,112},... | collective-permute-start | bytes 589832 | tf_op jit(solution)/shard_map/ppermute | solution.py:297
  35.2 9.9 %collective-permute-start.1 = (bf16[272,512]{1,0:T(8,128)(2,1)}, bf16[272,512]{1,0:T(8,128)(2,1)S(1)}, u32[]{:S(2)}, u32[]{:S(2)}) collective-permute-start(bf16[272,512]{1,0:T(8,128)(2,1)} %get-tuple-element.35), channel_id=1, source_target_pairs={{2,3},{6,5},{11,8},{15,12},{18,19},{22,21},{27,24},{31,28},{34,35}... | collective-permute-start | bytes 835592 | tf_op jit(solution)/shard_map/ppermute | solution.py:287
  39.0 17.0 %collective-permute-start.12 = (bf16[12,64,256]{2,1,0:T(8,128)(2,1)S(1)}, bf16[12,64,256]{2,1,0:T(8,128)(2,1)S(1)}, u32[]{:S(2)}, u32[]{:S(2)}) collective-permute-start(bf16[12,64,256]{2,1,0:T(8,128)(2,1)S(1)} %constant_dynamic-update-slice_fusion.refs_12_), channel_id=1, source_target_pairs={{0,1},{1,0},{2,3},{3,2},{4,5},{5,4},{6,7},{7,6},{8,9},{9,8},{10,11... | collective-permute-start | bytes 1179656 | tf_op jit(solution)/shard_map/ppermute | solution.py:300
  46.1 40.2 %copy-start.3 = (bf16[272,512]{1,0:T(8,128)(2,1)}, bf16[272,512]{1,0:T(8,128)(2,1)S(1)}, u32[]{:S(2)}) copy-start(bf16[272,512]{1,0:T(8,128)(2,1)S(1)} %add.83.refs_1_) | copy-start | bytes 835588
  46.1 20.0 %collective-permute-start.5 = (bf16[272,512]{1,0:T(8,128)(2,1)S(1)}, bf16[272,512]{1,0:T(8,128)(2,1)S(1)}, u32[]{:S(2)}, u32[]{:S(2)}) collective-permute-start(bf16[272,512]{1,0:T(8,128)(2,1)S(1)} %add.83.refs_1_), channel_id=1, source_target_pairs={{1,13},{2,14},{3,15},{5,1},{6,2},{7,3},{8,4},{10,6},{11,7},{12,8},... | collective-permute-start | bytes 835592 | tf_op jit(solution)/shard_map/ppermute | solution.py:259
  48.0 24.2 %collective-permute-start.3 = (bf16[272,512]{1,0:T(8,128)(2,1)S(1)}, bf16[272,512]{1,0:T(8,128)(2,1)S(1)}, u32[]{:S(2)}, u32[]{:S(2)}) collective-permute-start(bf16[272,512]{1,0:T(8,128)(2,1)S(1)} %add.83.refs_1_), channel_id=1, source_target_pairs={{1,5},{2,6},{3,7},{5,9},{6,10},{7,11},{8,12},{10,14},{11,15},{12,0... | collective-permute-start | bytes 835592 | tf_op jit(solution)/shard_map/ppermute | solution.py:259
  52.9 30.5 %collective-permute-start.7 = (bf16[272,512]{1,0:T(8,128)(2,1)S(1)}, bf16[272,512]{1,0:T(8,128)(2,1)S(1)}, u32[]{:S(2)}, u32[]{:S(2)}) collective-permute-start(bf16[272,512]{1,0:T(8,128)(2,1)S(1)} %get-tuple-element.63), channel_id=1, source_target_pairs={{0,12},{1,13},{2,14},{3,15},{4,0},{5,1},{6,2},{7,3},{8,4},{9,5},{1... | collective-permute-start | bytes 835592 | tf_op jit(solution)/shard_map/ppermute | solution.py:259
  53.1 30.3 %collective-permute-start.6 = (bf16[272,512]{1,0:T(8,128)(2,1)S(1)}, bf16[272,512]{1,0:T(8,128)(2,1)S(1)}, u32[]{:S(2)}, u32[]{:S(2)}) collective-permute-start(bf16[272,512]{1,0:T(8,128)(2,1)S(1)} %get-tuple-element.66), channel_id=1, source_target_pairs={{0,4},{1,5},{2,6},{3,7},{4,8},{5,9},{6,10},{7,11},{8,12},{9,13},{1... | collective-permute-start | bytes 835592 | tf_op jit(solution)/shard_map/ppermute | solution.py:259
  56.2 30.1 %collective-permute-start.13 = (bf16[24,64,256]{2,1,0:T(8,128)(2,1)S(1)}, bf16[24,64,256]{2,1,0:T(8,128)(2,1)S(1)}, u32[]{:S(2)}, u32[]{:S(2)}) collective-permute-start(bf16[24,64,256]{2,1,0:T(8,128)(2,1)S(1)} %pad_maximum_fusion), channel_id=1, source_target_pairs={{0,3},{1,2},{2,1},{3,0},{4,7},{5,6},{6,5},{7,4},{8,11},{9,10},{10,... | collective-permute-start | bytes 2359304 | tf_op jit(solution)/shard_map/ppermute | solution.py:301
  66.8 19.5 %collective-permute-start.9 = (bf16[128,512]{1,0:T(8,128)(2,1)}, bf16[128,512]{1,0:T(8,128)(2,1)}, u32[]{:S(2)}, u32[]{:S(2)}) collective-permute-start(bf16[128,512]{1,0:T(8,128)(2,1)} %slice.195), channel_id=1, source_target_pairs={{1,13},{2,14},{3,15},{4,0},{6,2},{7,3},{8,4},{11,7},{13,9},{14,10}... | collective-permute-start | bytes 393224 | tf_op jit(solution)/shard_map/ppermute | solution.py:259
  72.3 11.2 %collective-permute-start.8 = (bf16[144,512]{1,0:T(8,128)(2,1)S(1)}, bf16[144,512]{1,0:T(8,128)(2,1)S(1)}, u32[]{:S(2)}, u32[]{:S(2)}) collective-permute-start(bf16[144,512]{1,0:T(8,128)(2,1)S(1)} %slice.193), channel_id=1, source_target_pairs={{0,4},{3,7},{5,9},{6,10},{7,11},{9,13},{10,14},{11,15},{12,0},{14,... | collective-permute-start | bytes 442376 | tf_op jit(solution)/shard_map/ppermute | solution.py:259
  103.3 45.3 %copy-start.8 = (bf16[2,256,512]{2,1,0:T(8,128)(2,1)S(1)}, bf16[2,256,512]{2,1,0:T(8,128)(2,1)}, u32[]{:S(2)}) copy-start(bf16[2,256,512]{2,1,0:T(8,128)(2,1)} %get-tuple-element.53) | copy-start | bytes 1572868
  103.3 45.5 %copy-start.18 = (bf16[2,256,512]{2,1,0:T(8,128)(2,1)S(1)}, bf16[2,256,512]{2,1,0:T(8,128)(2,1)}, u32[]{:S(2)}) copy-start(bf16[2,256,512]{2,1,0:T(8,128)(2,1)} %get-tuple-element.52) | copy-start | bytes 1572868
  103.3 48.2 %copy-start.12 = (bf16[2,256,512]{2,1,0:T(8,128)(2,1)S(1)}, bf16[2,256,512]{2,1,0:T(8,128)(2,1)}, u32[]{:S(2)}) copy-start(bf16[2,256,512]{2,1,0:T(8,128)(2,1)} %get-tuple-element.39) | copy-start | bytes 1572868
  103.3 16.6 %collective-permute-start.14 = (bf16[2,256,512]{2,1,0:T(8,128)(2,1)}, bf16[2,256,512]{2,1,0:T(8,128)(2,1)S(1)}, u32[]{:S(2)}, u32[]{:S(2)}) collective-permute-start(bf16[2,256,512]{2,1,0:T(8,128)(2,1)} %get-tuple-element.41), channel_id=1, source_target_pairs={{0,1},{1,2},{2,3},{3,0},{4,5},{5,6},{6,7},{7,4},{8,9},{9,10},{10,1... | collective-permute-start | bytes 1572872 | tf_op jit(solution)/shard_map/ppermute | solution.py:259
  107.3 15.1 %collective-permute-start.18 = (bf16[2,256,512]{2,1,0:T(8,128)(2,1)}, bf16[2,256,512]{2,1,0:T(8,128)(2,1)S(1)}, u32[]{:S(2)}, u32[]{:S(2)}) collective-permute-start(bf16[2,256,512]{2,1,0:T(8,128)(2,1)} %get-tuple-element.46), channel_id=1, source_target_pairs={{0,3},{1,0},{2,1},{3,2},{4,7},{5,4},{6,5},{7,6},{8,11},{9,8},{10,9... | collective-permute-start | bytes 1572872 | tf_op jit(solution)/shard_map/ppermute | solution.py:259
  107.3 41.5 %collective-permute-start.16 = (bf16[2,256,512]{2,1,0:T(8,128)(2,1)}, bf16[2,256,512]{2,1,0:T(8,128)(2,1)S(1)}, u32[]{:S(2)}, u32[]{:S(2)}) collective-permute-start(bf16[2,256,512]{2,1,0:T(8,128)(2,1)} %get-tuple-element.42), channel_id=1, source_target_pairs={{0,3},{1,0},{2,1},{3,2},{4,7},{5,4},{6,5},{7,6},{8,11},{9,8},{10,9... | collective-permute-start | bytes 1572872 | tf_op jit(solution)/shard_map/ppermute | solution.py:259
  107.3 45.3 %collective-permute-start.17 = (bf16[2,256,512]{2,1,0:T(8,128)(2,1)}, bf16[2,256,512]{2,1,0:T(8,128)(2,1)S(1)}, u32[]{:S(2)}, u32[]{:S(2)}) collective-permute-start(bf16[2,256,512]{2,1,0:T(8,128)(2,1)} %get-tuple-element.44), channel_id=1, source_target_pairs={{0,1},{1,2},{2,3},{3,0},{4,5},{5,6},{6,7},{7,4},{8,9},{9,10},{10,1... | collective-permute-start | bytes 1572872 | tf_op jit(solution)/shard_map/ppermute | solution.py:259
  109.3 16.8 %collective-permute-start.20 = (bf16[2,256,512]{2,1,0:T(8,128)(2,1)}, bf16[2,256,512]{2,1,0:T(8,128)(2,1)S(1)}, u32[]{:S(2)}, u32[]{:S(2)}) collective-permute-start(bf16[2,256,512]{2,1,0:T(8,128)(2,1)} %get-tuple-element.49), channel_id=1, source_target_pairs={{0,1},{3,0},{4,5},{5,6},{8,9},{9,10},{13,14},{16,17},{19,16},{20,2... | collective-permute-start | bytes 1572872 | tf_op jit(solution)/shard_map/ppermute | solution.py:259
  120.0 17.6 %collective-permute-start.24 = (bf16[2,256,512]{2,1,0:T(8,128)(2,1)}, bf16[2,256,512]{2,1,0:T(8,128)(2,1)S(1)}, u32[]{:S(2)}, u32[]{:S(2)}) collective-permute-start(bf16[2,256,512]{2,1,0:T(8,128)(2,1)} %get-tuple-element.54), channel_id=1, source_target_pairs={{0,3},{4,7},{9,8},{13,12},{16,19},{20,23},{25,24},{29,28},{32,35},... | collective-permute-start | bytes 1572872 | tf_op jit(solution)/shard_map/ppermute | solution.py:259
  122.3 27.9 %collective-permute-start.15 = (bf16[2,256,512]{2,1,0:T(8,128)(2,1)S(1)}, bf16[2,256,512]{2,1,0:T(8,128)(2,1)S(1)}, u32[]{:S(2)}, u32[]{:S(2)}) collective-permute-start(bf16[2,256,512]{2,1,0:T(8,128)(2,1)S(1)} %add_convert_fusion.3), channel_id=1, source_target_pairs={{0,1},{1,2},{2,3},{3,0},{4,5},{5,6},{6,7},{7,4},{8,9},{9,10},{10,1... | collective-permute-start | bytes 1572872 | tf_op jit(solution)/shard_map/ppermute | solution.py:259
  126.1 29.1 %collective-permute-start.19 = (bf16[2,256,512]{2,1,0:T(8,128)(2,1)S(1)}, bf16[2,256,512]{2,1,0:T(8,128)(2,1)S(1)}, u32[]{:S(2)}, u32[]{:S(2)}) collective-permute-start(bf16[2,256,512]{2,1,0:T(8,128)(2,1)S(1)} %add_convert_fusion.2), channel_id=1, source_target_pairs={{0,3},{1,0},{2,1},{3,2},{4,7},{5,4},{6,5},{7,6},{8,11},{9,8},{10,9... | collective-permute-start | bytes 1572872 | tf_op jit(solution)/shard_map/ppermute | solution.py:259
  137.6 29.0 %collective-permute-start.22 = (bf16[2,256,512]{2,1,0:T(8,128)(2,1)S(1)}, bf16[2,256,512]{2,1,0:T(8,128)(2,1)S(1)}, u32[]{:S(2)}, u32[]{:S(2)}) collective-permute-start(bf16[2,256,512]{2,1,0:T(8,128)(2,1)S(1)} %copy-done.19), channel_id=1, source_target_pairs={{2,1},{3,2},{4,7},{7,6},{8,11},{11,10},{12,15},{18,17},{19,18},{20... | collective-permute-start | bytes 1572872 | tf_op jit(solution)/shard_map/ppermute | solution.py:259
  148.8 23.7 %collective-permute-start.23 = (bf16[2,256,512]{2,1,0:T(8,128)(2,1)S(1)}, bf16[2,256,512]{2,1,0:T(8,128)(2,1)S(1)}, u32[]{:S(2)}, u32[]{:S(2)}) collective-permute-start(bf16[2,256,512]{2,1,0:T(8,128)(2,1)S(1)} %copy-done.18), channel_id=1, source_target_pairs={{1,2},{5,6},{10,11},{14,15},{17,18},{21,22},{26,27},{30,31},{33,34... | collective-permute-start | bytes 1572872 | tf_op jit(solution)/shard_map/ppermute | solution.py:259
  150.2 21.3 %collective-permute-start.21 = (bf16[2,256,512]{2,1,0:T(8,128)(2,1)S(1)}, bf16[2,256,512]{2,1,0:T(8,128)(2,1)S(1)}, u32[]{:S(2)}, u32[]{:S(2)}) collective-permute-start(bf16[2,256,512]{2,1,0:T(8,128)(2,1)S(1)} %add_convert_fusion.1), channel_id=1, source_target_pairs={{0,1},{1,2},{5,6},{6,7},{9,10},{10,11},{14,15},{16,17},{17,18},{21... | collective-permute-start | bytes 1572872 | tf_op jit(solution)/shard_map/ppermute | solution.py:259
  152.5 20.6 %collective-permute-start.25 = (bf16[2,256,512]{2,1,0:T(8,128)(2,1)S(1)}, bf16[2,256,512]{2,1,0:T(8,128)(2,1)S(1)}, u32[]{:S(2)}, u32[]{:S(2)}) collective-permute-start(bf16[2,256,512]{2,1,0:T(8,128)(2,1)S(1)} %add_convert_fusion), channel_id=1, source_target_pairs={{3,2},{7,6},{8,11},{12,15},{19,18},{23,22},{24,27},{28,31},{35,34}... | collective-permute-start | bytes 1572872 | tf_op jit(solution)/shard_map/ppermute | solution.py:259
  156.3 19.8 %collective-permute-start.26 = (bf16[2,256,512]{2,1,0:T(8,128)(2,1)S(1)}, bf16[2,256,512]{2,1,0:T(8,128)(2,1)S(1)}, u32[]{:S(2)}, u32[]{:S(2)}) collective-permute-start(bf16[2,256,512]{2,1,0:T(8,128)(2,1)S(1)} %pad_maximum_fusion.1), channel_id=1, source_target_pairs={{0,16},{1,17},{2,18},{3,19},{4,20},{5,21},{6,22},{7,23},{8,24},{9,... | collective-permute-start | bytes 1572872 | tf_op jit(solution)/shard_map/ppermute | solution.py:352
  174.2 11.4 %collective-permute-start.27 = (bf16[2,256,512]{2,1,0:T(8,128)(2,1)S(1)}, bf16[2,256,512]{2,1,0:T(8,128)(2,1)S(1)}, u32[]{:S(2)}, u32[]{:S(2)}) collective-permute-start(bf16[2,256,512]{2,1,0:T(8,128)(2,1)S(1)} %pad_maximum_fusion.2), channel_id=1, source_target_pairs={{1,17},{2,18},{6,22},{7,23},{10,26},{11,27},{15,31},{17,33},{18,34... | collective-permute-start | bytes 1572872 | tf_op jit(solution)/shard_map/ppermute | solution.py:352
  (16 other events, 266.8 us)

commit v10 on v9

--- a/solution.py
+++ b/solution.py
@@ -120,11 +120,12 @@
             out[cell] = jnp.where(keep(rows, cols), value, 0.0).astype(BF)
 
 
-def terms_kernel(place, ints, values, *refs):
+def terms_kernel(slots, place, ints, values, *refs):
+    width = 4 * len(slots)
     two, three, lone = (refs[0], refs[2], refs[4]), (refs[1], refs[3], refs[5]), refs[6:9]
     across2b, ket_in, bra_own, rim, swapped, crossed = refs[9:15]
-    outs = refs[15:31]
-    env_all, ket, bra_all, total, rounded, todo, scale, size, env_sem, ket_sem, bra_sem, out_sem = refs[31:]
+    outs = refs[15 : 15 + width]
+    env_all, ket, bra_all, total, rounded, todo, scale, size, env_sem, ket_sem, bra_sem, out_sem = refs[15 + width :]
     copies = []
     body_rows = pl.ds(HEAD, BB)
     views = []
@@ -151,10 +152,10 @@
 
     r, a = place[0], place[1]
     my_z, my_x = r // NX, r % NX
-    for d in range(4):
+    for d, slot in enumerate(slots):
         for i in range(4):
 
-            @pl.when(i < live_count(row_x(r, STEPS[d])))
+            @pl.when(i < live_count(row_x(r, STEPS[slot])))
             def _(at=8 * d + 2 * i):
                 total[at] = jnp.zeros((BB, KB), F32)
                 total[at + 1] = jnp.zeros((BB, KB), F32)
@@ -172,11 +173,13 @@
         def _():
             out_r, out_j = out_w // CH, out_w % CH
 
-            @pl.when(live_at(out_r, p_b, out_j) == 1)
+            forward = (out_r % NX - my_x + NX) % NX
+            slot = jnp.where(forward == 1, 2, jnp.where(forward == 3, 1, jnp.where(forward == 2, 3, 0)))
+            inside = (slot >= slots[0]) & (slot <= slots[-1])
+
+            @pl.when(inside & (live_at(out_r, p_b, out_j) == 1))
             def _():
                 sp, at = ints[base + 1], size[0]
-                forward = (out_r % NX - my_x + NX) % NX
-                slot = jnp.where(forward == 1, 2, jnp.where(forward == 3, 1, jnp.where(forward == 2, 3, 0)))
                 out_a, out_b = charge(out_w)
                 low = live_at(out_r, 0, 0)
                 inside = low + live_at(out_r, 0, 1) + out_j * live_at(out_r, 1, 0)
@@ -184,7 +187,7 @@
                 todo[4 * at] = item // EPW
                 todo[4 * at + 1] = 2 * s + q_b
                 todo[4 * at + 2] = 6 * (s_a + out_a + 1) + 3 * (sp % 2) + p_b + out_b + sp // 2
-                todo[4 * at + 3] = 8 * slot + 2 * position + s_a
+                todo[4 * at + 3] = 8 * (slot - slots[0]) + 2 * position + s_a
                 scale[at] = values[base + 3] + values[base + 4] + values[base + 5]
                 size[0] = at + 1
 
@@ -192,7 +195,7 @@
     for n in range(TOGETHER - 1):
         for field in range(3):
             todo[4 * (count + n) + field] = 0
-        todo[4 * (count + n) + 3] = 32
+        todo[4 * (count + n) + 3] = 2 * width
         scale[count + n] = 0.0
 
     for copy in copies:
@@ -214,19 +217,19 @@
     def stored(d, i):
         return pltpu.make_async_copy(rounded.at[4 * d + i], outs[4 * d + i], out_sem.at[4 * d + i])
 
-    for d in (3, 2, 1, 0):
+    for d in range(len(slots)):
         for i in range(4):
 
-            @pl.when(i < live_count(row_x(r, STEPS[d])))
+            @pl.when(i < live_count(row_x(r, STEPS[slots[d]])))
             def _(d=d, i=i):
                 for up in range(2):
                     rounded[4 * d + i, up] = total[8 * d + 2 * i + up].astype(BF)
                 stored(d, i).start()
 
-    for d in (3, 2, 1, 0):
+    for d in range(len(slots)):
         for i in range(4):
 
-            @pl.when(i < live_count(row_x(r, STEPS[d])))
+            @pl.when(i < live_count(row_x(r, STEPS[slots[d]])))
             def _(d=d, i=i):
                 stored(d, i).wait()
 
@@ -305,29 +308,34 @@
     values = jnp.concatenate([head[0, :64] for head in heads]).astype(F32)
 
     hbm = pl.BlockSpec(memory_space=pl.ANY)
-    sums = pl.pallas_call(
-        terms_kernel,
-        in_specs=[smem] * 3 + [hbm] * 15,
-        out_specs=[hbm] * 16,
-        out_shape=[pair] * 16,
-        scratch_shapes=[
-            pltpu.VMEM((12, BB, KB), BF),
-            pltpu.VMEM((8, KB, KB), BF),
-            pltpu.VMEM((24, BB, BB), BF),
-            pltpu.VMEM((33, BB, KB), F32),
-            pltpu.VMEM((16, 2, BB, KB), BF),
-            pltpu.SMEM((4 * (12 * EPW + TOGETHER),), jnp.int32),
-            pltpu.SMEM((12 * EPW + TOGETHER,), F32),
-            pltpu.SMEM((1,), jnp.int32),
-            pltpu.SemaphoreType.DMA((13,)),
-            pltpu.SemaphoreType.DMA((4,)),
-            pltpu.SemaphoreType.DMA((13,)),
-            pltpu.SemaphoreType.DMA((16,)),
-        ],
-        compiler_params=params,
-    )(place, values.astype(jnp.int32), values, own01, own2, behind01, behind2, ahead01, ahead2,
-      across0, across1, across2a, across2b, ket_mps[:, 0], bra_own, rim, swapped, crossed)
-    mine, left, right, far = sums[:4], sums[4:8], sums[8:12], sums[12:]
+    def terms(slots, own):
+        width = 4 * len(slots)
+        return pl.pallas_call(
+            functools.partial(terms_kernel, slots),
+            in_specs=[smem] * 3 + [hbm] * 15,
+            out_specs=[hbm] * width,
+            out_shape=[pair] * width,
+            scratch_shapes=[
+                pltpu.VMEM((12, BB, KB), BF),
+                pltpu.VMEM((8, KB, KB), BF),
+                pltpu.VMEM((24, BB, BB), BF),
+                pltpu.VMEM((2 * width + 1, BB, KB), F32),
+                pltpu.VMEM((width, 2, BB, KB), BF),
+                pltpu.SMEM((4 * (12 * EPW + TOGETHER),), jnp.int32),
+                pltpu.SMEM((12 * EPW + TOGETHER,), F32),
+                pltpu.SMEM((1,), jnp.int32),
+                pltpu.SemaphoreType.DMA((13,)),
+                pltpu.SemaphoreType.DMA((4,)),
+                pltpu.SemaphoreType.DMA((13,)),
+                pltpu.SemaphoreType.DMA((width,)),
+            ],
+            compiler_params=params,
+        )(place, values.astype(jnp.int32), values, own, own2, behind01, behind2, ahead01, ahead2,
+          across0, across1, across2a, across2b, ket_mps[:, 0], bra_own, rim, swapped, crossed)
+
+    far = terms((3,), own01)
+    sums = terms((0, 1, 2), after(own01, *far))
+    mine, left, right = sums[:4], sums[4:8], sums[8:]
 
     def added(*parts):
         return functools.reduce(jnp.add, [part.astype(F32) for part in parts])

time: 189 us -> 185 us (0.979)
  starting transfers between devices: 74.7 us -> 59.2 us
  Pallas kernels: 24.4 us -> 30.2 us
  local copies, waits for them, and re-layouts: 5.85 us -> 11.3 us
    ppermute x20, starting transfers between devices: 58 us -> 42.6 us  [sent(): lax.ppermute(value, 'row', [(n, move(n)) for n in range(ROWS) if owner(n)...]
    pallas_call x1 -> x2, Pallas kernels: 16.1 us -> 21.9 us  [terms(): pl.pallas_call(functools.partial(terms_kernel, slots), in_specs=[smem] *...]
    concatenate x1, local copies, waits for them, and re-layouts: 0.77 us -> 3.38 us  [body(): values = jnp.concatenate([head[0, :64] for head in heads]).astype(F32)]
    squeeze x9, local copies, waits for them, and re-layouts: 0.63 us -> 2.83 us  [body(): values = jnp.concatenate([head[0, :64] for head in heads]).astype(F32)]
  transfers between devices with their start and end apart: 28 -> 28, of which waited for: 12 -> 10; matrix products, arithmetic and copies ran while one was open for 7% -> 10% of each run, Pallas kernels for 1% -> 9%
where the time goes in v10:
time: 185 us
  waiting for transfers between devices  72.2 us (39%)
  starting transfers between devices  59.2 us (32%)
  Pallas kernels  30.2 us (16%)
  local copies, waits for them, and re-layouts  11.3 us (6%)
  other arithmetic  11.2 us (6%)
    ppermute x20, waiting for transfers between devices, sent(): lax.ppermute(value, 'row', [(n, move(n)) for n in range(ROWS) if owner(n)...  43.6 us
    ppermute x20, starting transfers between devices, sent(): lax.ppermute(value, 'row', [(n, move(n)) for n in range(ROWS) if owner(n)...  42.6 us
    pallas_call x2, Pallas kernels, terms(): pl.pallas_call(functools.partial(terms_kernel, slots), in_specs=[smem] *...  21.9 us
    ppermute x1, waiting for transfers between devices, body(): rim_low = lax.ppermute(strip_low, 'sec', up(1))  13.7 us
    ppermute x2, waiting for transfers between devices, body(): lax.ppermute(jnp.stack(raised[i:i + 2]), ('sec', 'row'), pairs)  9.45 us
    ppermute x1, waiting for transfers between devices, body(): borrowed = lax.ppermute(after(moving, rim_low), 'row', lent)  4.73 us
    convert_element_type x4, other arithmetic, body(): added(mine[i][1], from_left[i][1], from_right[i][1]).astype(BF)  4.01 us
    ppermute x2, starting transfers between devices, body(): lax.ppermute(jnp.stack(raised[i:i + 2]), ('sec', 'row'), pairs)  3.84 us
  transfers between devices with their start and end apart: 28, of which 10 were waited for; matrix products, arithmetic and copies ran while one was open for 10% of the time, Pallas kernels for 9%

profile of v10, /device:TPU:12, one launch (start us, length us, event | category | flops | bytes accessed | tf_op | source)
XLA Modules:
  0.0 184.6 jit_solution(327534125692043425)
XLA Ops:
  0.6 2.6 %shard_map.73 = (bf16[2,272,512]{2,1,0:T(8,128)(2,1)}, bf16[272,512]{1,0:T(8,128)(2,1)}, bf16[272,512]{1,0:T(8,128)(2,1)}) custom-call(s32[2]{0:T(128)} %pad_add_fusion.place, s32[2,16]{1,0:T(2,128)} %bitcast.59, s32[2,16]{1,0:T(2,128)} %bitcast.61, s32[3,2,8]{2,1,0:T(2,128)} %bitcast.63, f32[2,8]{1,0:T(2,128)} %coeffs.1, bf16[4,256,512]{2,1,0:T(8,128)(2,1)} %bitcast.57), custom_call_target="tpu_custom_call" | custom-call | tf_op jit(solution)/shard_map/pallas_call | solution.py:249
  3.2 6.3 %collective-permute-start.4 = (bf16[2,272,512]{2,1,0:T(8,128)(2,1)}, bf16[2,272,512]{2,1,0:T(8,128)(2,1)S(1)}, u32[]{:S(2)}, u32[]{:S(2)}) collective-permute-start(bf16[2,272,512]{2,1,0:T(8,128)(2,1)} %get-tuple-element.44.refs_0_), channel_id=1, source_target_pairs={{0,12},{1,13},{2,14},{3,15},{4,0},{5,1},{6,2},{7,3},{8,4},{9,5},{1... | collective-permute-start | bytes 1671176 | tf_op jit(solution)/shard_map/ppermute | solution.py:262
  9.5 2.5 %shard_map.74 = (bf16[6,256,256]{2,1,0:T(8,128)(2,1)}, bf16[6,64,256]{2,1,0:T(8,128)(2,1)}, bf16[3,64,256]{2,1,0:T(8,128)(2,1)}, bf16[3,64,256]{2,1,0:T(8,128)(2,1)}) custom-call(s32[2]{0:T(128)} %pad_add_fusion.place, bf16[4,2,256,256]{3,2,1,0:T(8,128)(2,1)} %bitcast.58), custom_call_target="tpu_custom_call" | custom-call | tf_op jit(solution)/shard_map/pallas_call | solution.py:275
  12.0 1.9 %collective-permute-start = (bf16[3,64,256]{2,1,0:T(8,128)(2,1)}, bf16[3,64,256]{2,1,0:T(8,128)(2,1)S(1)}, u32[]{:S(2)}, u32[]{:S(2)}) collective-permute-start(bf16[3,64,256]{2,1,0:T(8,128)(2,1)} %get-tuple-element.35), channel_id=1, source_target_pairs={{0,16},{16,32},{32,48},{48,64},{64,80},{80,96},{96,112},{112,128},... | collective-permute-start | bytes 294920 | tf_op jit(solution)/shard_map/ppermute | solution.py:289
  13.9 2.8 %collective-permute-start.11 = (bf16[3,64,256]{2,1,0:T(8,128)(2,1)}, bf16[3,64,256]{2,1,0:T(8,128)(2,1)S(1)}, u32[]{:S(2)}, u32[]{:S(2)}) collective-permute-start(bf16[3,64,256]{2,1,0:T(8,128)(2,1)} %get-tuple-element.39), channel_id=1, source_target_pairs={{32,0},{48,16},{64,32},{80,48},{96,64},{112,80},{128,96},{144,112}... | collective-permute-start | bytes 294920 | tf_op jit(solution)/shard_map/ppermute | solution.py:301
  16.8 3.6 %collective-permute-start.10 = (bf16[6,64,256]{2,1,0:T(8,128)(2,1)}, bf16[6,64,256]{2,1,0:T(8,128)(2,1)S(1)}, u32[]{:S(2)}, u32[]{:S(2)}) collective-permute-start(bf16[6,64,256]{2,1,0:T(8,128)(2,1)} %get-tuple-element.38), channel_id=1, source_target_pairs={{16,0},{32,16},{48,32},{64,48},{80,64},{96,80},{112,96},{128,112},... | collective-permute-start | bytes 589832 | tf_op jit(solution)/shard_map/ppermute | solution.py:300
  21.5 13.7 %collective-permute-done = bf16[3,64,256]{2,1,0:T(8,128)(2,1)S(1)} collective-permute-done((bf16[3,64,256]{2,1,0:T(8,128)(2,1)}, bf16[3,64,256]{2,1,0:T(8,128)(2,1)S(1)}, u32[]{:S(2)}, u32[]{:S(2)}) %collective-permute-start) | collective-permute-done | bytes 98336 | tf_op jit(solution)/shard_map/ppermute | solution.py:289
  35.2 3.1 %collective-permute-start.1 = (bf16[272,512]{1,0:T(8,128)(2,1)}, bf16[272,512]{1,0:T(8,128)(2,1)S(1)}, u32[]{:S(2)}, u32[]{:S(2)}) collective-permute-start(bf16[272,512]{1,0:T(8,128)(2,1)} %get-tuple-element.36), channel_id=1, source_target_pairs={{2,3},{6,5},{11,8},{15,12},{18,19},{22,21},{27,24},{31,28},{34,35}... | collective-permute-start | bytes 835592 | tf_op jit(solution)/shard_map/ppermute | solution.py:290
  39.1 1.3 collective-permute-start.12
  40.3 4.7 %collective-permute-done.1 = bf16[272,512]{1,0:T(8,128)(2,1)S(1)} collective-permute-done((bf16[272,512]{1,0:T(8,128)(2,1)}, bf16[272,512]{1,0:T(8,128)(2,1)S(1)}, u32[]{:S(2)}, u32[]{:S(2)}) %collective-permute-start.1) | collective-permute-done | bytes 278560 | tf_op jit(solution)/shard_map/ppermute | solution.py:290
  46.1 1.9 %collective-permute-start.5 = (bf16[272,512]{1,0:T(8,128)(2,1)S(1)}, bf16[272,512]{1,0:T(8,128)(2,1)S(1)}, u32[]{:S(2)}, u32[]{:S(2)}) collective-permute-start(bf16[272,512]{1,0:T(8,128)(2,1)S(1)} %add.83.refs_1_), channel_id=1, source_target_pairs={{1,13},{2,14},{3,15},{5,1},{6,2},{7,3},{8,4},{10,6},{11,7},{12,8},... | collective-permute-start | bytes 835592 | tf_op jit(solution)/shard_map/ppermute | solution.py:262
  48.0 4.8 %collective-permute-start.3 = (bf16[272,512]{1,0:T(8,128)(2,1)S(1)}, bf16[272,512]{1,0:T(8,128)(2,1)S(1)}, u32[]{:S(2)}, u32[]{:S(2)}) collective-permute-start(bf16[272,512]{1,0:T(8,128)(2,1)S(1)} %add.83.refs_1_), channel_id=1, source_target_pairs={{1,5},{2,6},{3,7},{5,9},{6,10},{7,11},{8,12},{10,14},{11,15},{12,0... | collective-permute-start | bytes 835592 | tf_op jit(solution)/shard_map/ppermute | solution.py:262
  53.1 3.0 %collective-permute-start.6 = (bf16[272,512]{1,0:T(8,128)(2,1)S(1)}, bf16[272,512]{1,0:T(8,128)(2,1)S(1)}, u32[]{:S(2)}, u32[]{:S(2)}) collective-permute-start(bf16[272,512]{1,0:T(8,128)(2,1)S(1)} %get-tuple-element.68), channel_id=1, source_target_pairs={{0,4},{1,5},{2,6},{3,7},{4,8},{5,9},{6,10},{7,11},{8,12},{9,13},{1... | collective-permute-start | bytes 835592 | tf_op jit(solution)/shard_map/ppermute | solution.py:262
  57.2 8.9 %collective-permute-done.5.refs_5_ = bf16[272,512]{1,0:T(8,128)(2,1)S(1)} collective-permute-done((bf16[272,512]{1,0:T(8,128)(2,1)S(1)}, bf16[272,512]{1,0:T(8,128)(2,1)S(1)}, u32[]{:S(2)}, u32[]{:S(2)}) %collective-permute-start.5) | collective-permute-done | bytes 278560 | tf_op jit(solution)/shard_map/ppermute | solution.py:262
  66.8 5.4 %collective-permute-start.9 = (bf16[128,512]{1,0:T(8,128)(2,1)}, bf16[128,512]{1,0:T(8,128)(2,1)}, u32[]{:S(2)}, u32[]{:S(2)}) collective-permute-start(bf16[128,512]{1,0:T(8,128)(2,1)} %slice.195), channel_id=1, source_target_pairs={{1,13},{2,14},{3,15},{4,0},{6,2},{7,3},{8,4},{11,7},{13,9},{14,10}... | collective-permute-start | bytes 393224 | tf_op jit(solution)/shard_map/ppermute | solution.py:262
  72.3 1.3 collective-permute-start.8
  74.7 8.7 %collective-permute-done.8.refs_8_ = bf16[144,512]{1,0:T(8,128)(2,1)S(1)} collective-permute-done((bf16[144,512]{1,0:T(8,128)(2,1)S(1)}, bf16[144,512]{1,0:T(8,128)(2,1)S(1)}, u32[]{:S(2)}, u32[]{:S(2)}) %collective-permute-start.8) | collective-permute-done | bytes 147488 | tf_op jit(solution)/shard_map/ppermute | solution.py:262
  86.6 3.4 %concatenate.10 = bf16[768]{0:T(1024)(128)(2,1)S(1)} concatenate(bf16[64]{0:T(256)(128)(2,1)S(1)} %get-tuple-element.74, bf16[64]{0:T(256)(128)(2,1)S(1)} %get-tuple-element.73, bf16[64]{0:T(256)(128)(2,1)S(1)} %slice_bitcast_fusion.15, bf16[64]{0:T(256)(128)(2,1)S(1)} %get-tuple-element.76, bf16[64]{0:T(256)(128)(2,1)S(1)} %get-tuple-element.75, ...), dimensions={0} | concatenate | bytes 3072 | tf_op jit(solution)/shard_map/concatenate | solution.py:308
  91.5 7.8 %shard_map.75 = (bf16[2,256,512]{2,1,0:T(8,128)(2,1)}, bf16[2,256,512]{2,1,0:T(8,128)(2,1)}, bf16[2,256,512]{2,1,0:T(8,128)(2,1)}, bf16[2,256,512]{2,1,0:T(8,128)(2,1)}) custom-call(s32[2]{0:T(128)} %pad_add_fusion.place, s32[768]{0:T(1024)} %get-tuple-element.72.ints, f32[768]{0:T(1024)} %get-tuple-element.71.values, ...), custom_call_target="tpu_custom_call" | custom-call | tf_op jit(solution)/shard_map/pallas_call | solution.py:313
  99.4 3.9 %collective-permute-start.14 = (bf16[2,256,512]{2,1,0:T(8,128)(2,1)}, bf16[2,256,512]{2,1,0:T(8,128)(2,1)S(1)}, u32[]{:S(2)}, u32[]{:S(2)}) collective-permute-start(bf16[2,256,512]{2,1,0:T(8,128)(2,1)} %get-tuple-element.40), channel_id=1, source_target_pairs={{0,1},{1,2},{2,3},{3,0},{4,5},{5,6},{6,7},{7,4},{8,9},{9,10},{10,1... | collective-permute-start | bytes 1572872 | tf_op jit(solution)/shard_map/ppermute | solution.py:262
  104.7 14.1 %shard_map.76 = (bf16[2,256,512]{2,1,0:T(8,128)(2,1)}, bf16[2,256,512]{2,1,0:T(8,128)(2,1)}, bf16[2,256,512]{2,1,0:T(8,128)(2,1)}, bf16[2,256,512]{2,1,0:T(8,128...) custom-call(s32[2]{0:T(128)} %pad_add_fusion.place, ...), custom_call_target="tpu_custom_call" | custom-call | tf_op jit(solution)/shard_map/pallas_call | solution.py:313
  119.1 4.5 %collective-permute-start.17 = (bf16[2,256,512]{2,1,0:T(8,128)(2,1)}, bf16[2,256,512]{2,1,0:T(8,128)(2,1)S(1)}, u32[]{:S(2)}, u32[]{:S(2)}) collective-permute-start(bf16[2,256,512]{2,1,0:T(8,128)(2,1)} %get-tuple-element.49), channel_id=1, source_target_pairs={{0,1},{1,2},{2,3},{3,0},{4,5},{5,6},{6,7},{7,4},{8,9},{9,10},{10,1... | collective-permute-start | bytes 1572872 | tf_op jit(solution)/shard_map/ppermute | solution.py:262
  124.8 3.2 %collective-permute-start.15 = (bf16[2,256,512]{2,1,0:T(8,128)(2,1)S(1)}, bf16[2,256,512]{2,1,0:T(8,128)(2,1)S(1)}, u32[]{:S(2)}, u32[]{:S(2)}) collective-permute-start(bf16[2,256,512]{2,1,0:T(8,128)(2,1)S(1)} %add_convert_fusion.3), channel_id=1, source_target_pairs={{0,1},{1,2},{2,3},{3,0},{4,5},{5,6},{6,7},{7,4},{8,9},{9,10},{10,1... | collective-permute-start | bytes 1572872 | tf_op jit(solution)/shard_map/ppermute | solution.py:262
  130.6 2.5 %collective-permute-start.22 = (bf16[2,256,512]{2,1,0:T(8,128)(2,1)S(1)}, bf16[2,256,512]{2,1,0:T(8,128)(2,1)S(1)}, u32[]{:S(2)}, u32[]{:S(2)}) collective-permute-start(bf16[2,256,512]{2,1,0:T(8,128)(2,1)S(1)} %copy-done.19), channel_id=1, source_target_pairs={{2,1},{3,2},{4,7},{7,6},{8,11},{11,10},{12,15},{18,17},{19,18},{20... | collective-permute-start | bytes 1572872 | tf_op jit(solution)/shard_map/ppermute | solution.py:262
  133.3 3.3 %collective-permute-done.16 = bf16[2,256,512]{2,1,0:T(8,128)(2,1)S(1)} collective-permute-done((bf16[2,256,512]{2,1,0:T(8,128)(2,1)}, bf16[2,256,512]{2,1,0:T(8,128)(2,1)S(1)}, u32[]{:S(2)}, u32[]{:S(2)}) %collective-permute-start.16) | collective-permute-done | bytes 524320 | tf_op jit(solution)/shard_map/ppermute | solution.py:262
  137.8 9.6 %collective-permute-done.15 = bf16[2,256,512]{2,1,0:T(8,128)(2,1)S(1)} collective-permute-done((bf16[2,256,512]{2,1,0:T(8,128)(2,1)S(1)}, bf16[2,256,512]{2,1,0:T(8,128)(2,1)S(1)}, u32[]{:S(2)}, u32[]{:S(2)}) %collective-permute-start.15) | collective-permute-done | bytes 524320 | tf_op jit(solution)/shard_map/ppermute | solution.py:262
  152.1 1.9 %collective-permute-start.26 = (bf16[2,256,512]{2,1,0:T(8,128)(2,1)S(1)}, bf16[2,256,512]{2,1,0:T(8,128)(2,1)S(1)}, u32[]{:S(2)}, u32[]{:S(2)}) collective-permute-start(bf16[2,256,512]{2,1,0:T(8,128)(2,1)S(1)} %pad_maximum_fusion.1), channel_id=1, source_target_pairs={{0,16},{1,17},{2,18},{3,19},{4,20},{5,21},{6,22},{7,23},{8,24},{9,... | collective-permute-start | bytes 1572872 | tf_op jit(solution)/shard_map/ppermute | solution.py:360
  154.1 5.0 %collective-permute-done.22 = bf16[2,256,512]{2,1,0:T(8,128)(2,1)S(1)} collective-permute-done((bf16[2,256,512]{2,1,0:T(8,128)(2,1)S(1)}, bf16[2,256,512]{2,1,0:T(8,128)(2,1)S(1)}, u32[]{:S(2)}, u32[]{:S(2)}) %collective-permute-start.22) | collective-permute-done | bytes 524320 | tf_op jit(solution)/shard_map/ppermute | solution.py:262
  159.0 8.0 %collective-permute-done.21 = bf16[2,256,512]{2,1,0:T(8,128)(2,1)S(1)} collective-permute-done((bf16[2,256,512]{2,1,0:T(8,128)(2,1)S(1)}, bf16[2,256,512]{2,1,0:T(8,128)(2,1)S(1)}, u32[]{:S(2)}, u32[]{:S(2)}) %collective-permute-start.21) | collective-permute-done | bytes 524320 | tf_op jit(solution)/shard_map/ppermute | solution.py:262
  169.1 1.9 %collective-permute-start.27 = (bf16[2,256,512]{2,1,0:T(8,128)(2,1)S(1)}, bf16[2,256,512]{2,1,0:T(8,128)(2,1)S(1)}, u32[]{:S(2)}, u32[]{:S(2)}) collective-permute-start(bf16[2,256,512]{2,1,0:T(8,128)(2,1)S(1)} %pad_maximum_fusion.2), channel_id=1, source_target_pairs={{1,17},{2,18},{6,22},{7,23},{10,26},{11,27},{15,31},{17,33},{18,34... | collective-permute-start | bytes 1572872 | tf_op jit(solution)/shard_map/ppermute | solution.py:360
  171.1 9.4 %collective-permute-done.27.refs_5_ = bf16[2,256,512]{2,1,0:T(8,128)(2,1)S(1)} collective-permute-done((bf16[2,256,512]{2,1,0:T(8,128)(2,1)S(1)}, bf16[2,256,512]{2,1,0:T(8,128)(2,1)S(1)}, u32[]{:S(2)}, u32[]{:S(2)}) %collective-permute-start.27) | collective-permute-done | bytes 524320 | tf_op jit(solution)/shard_map/ppermute | solution.py:360
  181.3 3.2 %shard_map.77 = bf16[4,256,512]{2,1,0:T(8,128)(2,1)} custom-call(s32[2]{0:T(128)} %pad_add_fusion.place, s32[2,16]{1,0:T(2,128)} %bitcast.60, s32[2,16]{1,0:T(2,128)} %bitcast.62, f32[256,512]{1,0:T(8,128)} %get-tuple-element.62.refs_0_, f32[256,512]{1,0:T(8,128)} %get-tuple-element.64.refs_1_, f32[256,512]{1,0:T(8,128)} %get-tuple-element.58.refs_2_, ...), custom_call_target="tpu_custom_call" | custom-call | tf_op jit(solution)/shard_map/pallas_call | solution.py:362
  (101 shorter events, 25.4 us)
Async XLA Ops:
  3.2 49.7 %collective-permute-start.4 = (bf16[2,272,512]{2,1,0:T(8,128)(2,1)}, bf16[2,272,512]{2,1,0:T(8,128)(2,1)S(1)}, u32[]{:S(2)}, u32[]{:S(2)}) collective-permute-start(bf16[2,272,512]{2,1,0:T(8,128)(2,1)} %get-tuple-element.44.refs_0_), channel_id=1, source_target_pairs={{0,12},{1,13},{2,14},{3,15},{4,0},{5,1},{6,2},{7,3},{8,4},{9,5},{1... | collective-permute-start | bytes 1671176 | tf_op jit(solution)/shard_map/ppermute | solution.py:262
  9.5 43.5 %collective-permute-start.2 = (bf16[2,272,512]{2,1,0:T(8,128)(2,1)}, bf16[2,272,512]{2,1,0:T(8,128)(2,1)S(1)}, u32[]{:S(2)}, u32[]{:S(2)}) collective-permute-start(bf16[2,272,512]{2,1,0:T(8,128)(2,1)} %get-tuple-element.44.refs_0_), channel_id=1, source_target_pairs={{0,4},{1,5},{2,6},{3,7},{4,8},{5,9},{6,10},{7,11},{8,12},{9,13},{1... | collective-permute-start | bytes 1671176 | tf_op jit(solution)/shard_map/ppermute | solution.py:262
  12.0 23.2 %collective-permute-start = (bf16[3,64,256]{2,1,0:T(8,128)(2,1)}, bf16[3,64,256]{2,1,0:T(8,128)(2,1)S(1)}, u32[]{:S(2)}, u32[]{:S(2)}) collective-permute-start(bf16[3,64,256]{2,1,0:T(8,128)(2,1)} %get-tuple-element.35), channel_id=1, source_target_pairs={{0,16},{16,32},{32,48},{48,64},{64,80},{80,96},{96,112},{112,128},... | collective-permute-start | bytes 294920 | tf_op jit(solution)/shard_map/ppermute | solution.py:289
  13.9 25.1 %collective-permute-start.11 = (bf16[3,64,256]{2,1,0:T(8,128)(2,1)}, bf16[3,64,256]{2,1,0:T(8,128)(2,1)S(1)}, u32[]{:S(2)}, u32[]{:S(2)}) collective-permute-start(bf16[3,64,256]{2,1,0:T(8,128)(2,1)} %get-tuple-element.39), channel_id=1, source_target_pairs={{32,0},{48,16},{64,32},{80,48},{96,64},{112,80},{128,96},{144,112}... | collective-permute-start | bytes 294920 | tf_op jit(solution)/shard_map/ppermute | solution.py:301
  16.8 22.3 %collective-permute-start.10 = (bf16[6,64,256]{2,1,0:T(8,128)(2,1)}, bf16[6,64,256]{2,1,0:T(8,128)(2,1)S(1)}, u32[]{:S(2)}, u32[]{:S(2)}) collective-permute-start(bf16[6,64,256]{2,1,0:T(8,128)(2,1)} %get-tuple-element.38), channel_id=1, source_target_pairs={{16,0},{32,16},{48,32},{64,48},{80,64},{96,80},{112,96},{128,112},... | collective-permute-start | bytes 589832 | tf_op jit(solution)/shard_map/ppermute | solution.py:300
  35.2 9.9 %collective-permute-start.1 = (bf16[272,512]{1,0:T(8,128)(2,1)}, bf16[272,512]{1,0:T(8,128)(2,1)S(1)}, u32[]{:S(2)}, u32[]{:S(2)}) collective-permute-start(bf16[272,512]{1,0:T(8,128)(2,1)} %get-tuple-element.36), channel_id=1, source_target_pairs={{2,3},{6,5},{11,8},{15,12},{18,19},{22,21},{27,24},{31,28},{34,35}... | collective-permute-start | bytes 835592 | tf_op jit(solution)/shard_map/ppermute | solution.py:290
  39.1 51.5 %copy-start.5 = (bf16[12,64,256]{2,1,0:T(8,128)(2,1)}, bf16[12,64,256]{2,1,0:T(8,128)(2,1)S(1)}, u32[]{:S(2)}) copy-start(bf16[12,64,256]{2,1,0:T(8,128)(2,1)S(1)} %constant_dynamic-update-slice_fusion.refs_12_) | copy-start | bytes 1179652
  39.1 17.0 %collective-permute-start.12 = (bf16[12,64,256]{2,1,0:T(8,128)(2,1)S(1)}, bf16[12,64,256]{2,1,0:T(8,128)(2,1)S(1)}, u32[]{:S(2)}, u32[]{:S(2)}) collective-permute-start(bf16[12,64,256]{2,1,0:T(8,128)(2,1)S(1)} %constant_dynamic-update-slice_fusion.refs_12_), channel_id=1, source_target_pairs={{0,1},{1,0},{2,3},{3,2},{4,5},{5,4},{6,7},{7,6},{8,9},{9,8},{10,11... | collective-permute-start | bytes 1179656 | tf_op jit(solution)/shard_map/ppermute | solution.py:303
  46.1 44.5 %copy-start.4 = (bf16[272,512]{1,0:T(8,128)(2,1)}, bf16[272,512]{1,0:T(8,128)(2,1)S(1)}, u32[]{:S(2)}) copy-start(bf16[272,512]{1,0:T(8,128)(2,1)S(1)} %add.83.refs_1_) | copy-start | bytes 835588
  46.1 20.0 %collective-permute-start.5 = (bf16[272,512]{1,0:T(8,128)(2,1)S(1)}, bf16[272,512]{1,0:T(8,128)(2,1)S(1)}, u32[]{:S(2)}, u32[]{:S(2)}) collective-permute-start(bf16[272,512]{1,0:T(8,128)(2,1)S(1)} %add.83.refs_1_), channel_id=1, source_target_pairs={{1,13},{2,14},{3,15},{5,1},{6,2},{7,3},{8,4},{10,6},{11,7},{12,8},... | collective-permute-start | bytes 835592 | tf_op jit(solution)/shard_map/ppermute | solution.py:262
  48.0 24.2 %collective-permute-start.3 = (bf16[272,512]{1,0:T(8,128)(2,1)S(1)}, bf16[272,512]{1,0:T(8,128)(2,1)S(1)}, u32[]{:S(2)}, u32[]{:S(2)}) collective-permute-start(bf16[272,512]{1,0:T(8,128)(2,1)S(1)} %add.83.refs_1_), channel_id=1, source_target_pairs={{1,5},{2,6},{3,7},{5,9},{6,10},{7,11},{8,12},{10,14},{11,15},{12,0... | collective-permute-start | bytes 835592 | tf_op jit(solution)/shard_map/ppermute | solution.py:262
  52.9 37.7 %copy-start = (bf16[2,272,512]{2,1,0:T(8,128)(2,1)}, bf16[2,272,512]{2,1,0:T(8,128)(2,1)S(1)}, u32[]{:S(2)}) copy-start(bf16[2,272,512]{2,1,0:T(8,128)(2,1)S(1)} %collective-permute-done.4.refs_4_) | copy-start | bytes 1671172
  53.0 31.1 %collective-permute-start.7 = (bf16[272,512]{1,0:T(8,128)(2,1)S(1)}, bf16[272,512]{1,0:T(8,128)(2,1)S(1)}, u32[]{:S(2)}, u32[]{:S(2)}) collective-permute-start(bf16[272,512]{1,0:T(8,128)(2,1)S(1)} %get-tuple-element.65), channel_id=1, source_target_pairs={{0,12},{1,13},{2,14},{3,15},{4,0},{5,1},{6,2},{7,3},{8,4},{9,5},{1... | collective-permute-start | bytes 835592 | tf_op jit(solution)/shard_map/ppermute | solution.py:262
  53.1 32.2 %collective-permute-start.6 = (bf16[272,512]{1,0:T(8,128)(2,1)S(1)}, bf16[272,512]{1,0:T(8,128)(2,1)S(1)}, u32[]{:S(2)}, u32[]{:S(2)}) collective-permute-start(bf16[272,512]{1,0:T(8,128)(2,1)S(1)} %get-tuple-element.68), channel_id=1, source_target_pairs={{0,4},{1,5},{2,6},{3,7},{4,8},{5,9},{6,10},{7,11},{8,12},{9,13},{1... | collective-permute-start | bytes 835592 | tf_op jit(solution)/shard_map/ppermute | solution.py:262
  57.2 33.4 %collective-permute-start.13 = (bf16[24,64,256]{2,1,0:T(8,128)(2,1)}, bf16[24,64,256]{2,1,0:T(8,128)(2,1)S(1)}, u32[]{:S(2)}, u32[]{:S(2)}) collective-permute-start(bf16[24,64,256]{2,1,0:T(8,128)(2,1)} %pad_maximum_fusion), channel_id=1, source_target_pairs={{0,3},{1,2},{2,1},{3,0},{4,7},{5,6},{6,5},{7,4},{8,11},{9,10},{10,... | collective-permute-start | bytes 2359304 | tf_op jit(solution)/shard_map/ppermute | solution.py:304
  66.8 23.8 %collective-permute-start.9 = (bf16[128,512]{1,0:T(8,128)(2,1)}, bf16[128,512]{1,0:T(8,128)(2,1)}, u32[]{:S(2)}, u32[]{:S(2)}) collective-permute-start(bf16[128,512]{1,0:T(8,128)(2,1)} %slice.195), channel_id=1, source_target_pairs={{1,13},{2,14},{3,15},{4,0},{6,2},{7,3},{8,4},{11,7},{13,9},{14,10}... | collective-permute-start | bytes 393224 | tf_op jit(solution)/shard_map/ppermute | solution.py:262
  72.3 11.1 %collective-permute-start.8 = (bf16[144,512]{1,0:T(8,128)(2,1)S(1)}, bf16[144,512]{1,0:T(8,128)(2,1)S(1)}, u32[]{:S(2)}, u32[]{:S(2)}) collective-permute-start(bf16[144,512]{1,0:T(8,128)(2,1)S(1)} %slice.193), channel_id=1, source_target_pairs={{0,4},{3,7},{5,9},{6,10},{7,11},{9,13},{10,14},{11,15},{12,0},{14,... | collective-permute-start | bytes 442376 | tf_op jit(solution)/shard_map/ppermute | solution.py:262
  99.4 19.7 %collective-permute-start.14 = (bf16[2,256,512]{2,1,0:T(8,128)(2,1)}, bf16[2,256,512]{2,1,0:T(8,128)(2,1)S(1)}, u32[]{:S(2)}, u32[]{:S(2)}) collective-permute-start(bf16[2,256,512]{2,1,0:T(8,128)(2,1)} %get-tuple-element.40), channel_id=1, source_target_pairs={{0,1},{1,2},{2,3},{3,0},{4,5},{5,6},{6,7},{7,4},{8,9},{9,10},{10,1... | collective-permute-start | bytes 1572872 | tf_op jit(solution)/shard_map/ppermute | solution.py:262
  103.3 21.6 %collective-permute-start.18 = (bf16[2,256,512]{2,1,0:T(8,128)(2,1)}, bf16[2,256,512]{2,1,0:T(8,128)(2,1)S(1)}, u32[]{:S(2)}, u32[]{:S(2)}) collective-permute-start(bf16[2,256,512]{2,1,0:T(8,128)(2,1)} %get-tuple-element.41), channel_id=1, source_target_pairs={{0,3},{1,0},{2,1},{3,2},{4,7},{5,4},{6,5},{7,6},{8,11},{9,8},{10,9... | collective-permute-start | bytes 1572872 | tf_op jit(solution)/shard_map/ppermute | solution.py:262
  103.3 27.3 %collective-permute-start.20 = (bf16[2,256,512]{2,1,0:T(8,128)(2,1)}, bf16[2,256,512]{2,1,0:T(8,128)(2,1)S(1)}, u32[]{:S(2)}, u32[]{:S(2)}) collective-permute-start(bf16[2,256,512]{2,1,0:T(8,128)(2,1)} %get-tuple-element.42), channel_id=1, source_target_pairs={{0,1},{3,0},{4,5},{5,6},{8,9},{9,10},{13,14},{16,17},{19,16},{20,2... | collective-permute-start | bytes 1572872 | tf_op jit(solution)/shard_map/ppermute | solution.py:262
  104.0 25.3 %collective-permute-start.24 = (bf16[2,256,512]{2,1,0:T(8,128)(2,1)}, bf16[2,256,512]{2,1,0:T(8,128)(2,1)S(1)}, u32[]{:S(2)}, u32[]{:S(2)}) collective-permute-start(bf16[2,256,512]{2,1,0:T(8,128)(2,1)} %get-tuple-element.43), channel_id=1, source_target_pairs={{0,3},{4,7},{9,8},{13,12},{16,19},{20,23},{25,24},{29,28},{32,35},... | collective-permute-start | bytes 1572872 | tf_op jit(solution)/shard_map/ppermute | solution.py:262
  118.8 17.7 %collective-permute-start.16 = (bf16[2,256,512]{2,1,0:T(8,128)(2,1)}, bf16[2,256,512]{2,1,0:T(8,128)(2,1)S(1)}, u32[]{:S(2)}, u32[]{:S(2)}) collective-permute-start(bf16[2,256,512]{2,1,0:T(8,128)(2,1)} %get-tuple-element.47), channel_id=1, source_target_pairs={{0,3},{1,0},{2,1},{3,2},{4,7},{5,4},{6,5},{7,6},{8,11},{9,8},{10,9... | collective-permute-start | bytes 1572872 | tf_op jit(solution)/shard_map/ppermute | solution.py:262
  119.1 30.7 %collective-permute-start.17 = (bf16[2,256,512]{2,1,0:T(8,128)(2,1)}, bf16[2,256,512]{2,1,0:T(8,128)(2,1)S(1)}, u32[]{:S(2)}, u32[]{:S(2)}) collective-permute-start(bf16[2,256,512]{2,1,0:T(8,128)(2,1)} %get-tuple-element.49), channel_id=1, source_target_pairs={{0,1},{1,2},{2,3},{3,0},{4,5},{5,6},{6,7},{7,4},{8,9},{9,10},{10,1... | collective-permute-start | bytes 1572872 | tf_op jit(solution)/shard_map/ppermute | solution.py:262
  124.8 22.6 %collective-permute-start.15 = (bf16[2,256,512]{2,1,0:T(8,128)(2,1)S(1)}, bf16[2,256,512]{2,1,0:T(8,128)(2,1)S(1)}, u32[]{:S(2)}, u32[]{:S(2)}) collective-permute-start(bf16[2,256,512]{2,1,0:T(8,128)(2,1)S(1)} %add_convert_fusion.3), channel_id=1, source_target_pairs={{0,1},{1,2},{2,3},{3,0},{4,5},{5,6},{6,7},{7,4},{8,9},{9,10},{10,1... | collective-permute-start | bytes 1572872 | tf_op jit(solution)/shard_map/ppermute | solution.py:262
  129.2 21.8 %collective-permute-start.19 = (bf16[2,256,512]{2,1,0:T(8,128)(2,1)S(1)}, bf16[2,256,512]{2,1,0:T(8,128)(2,1)S(1)}, u32[]{:S(2)}, u32[]{:S(2)}) collective-permute-start(bf16[2,256,512]{2,1,0:T(8,128)(2,1)S(1)} %add_convert_fusion.2), channel_id=1, source_target_pairs={{0,3},{1,0},{2,1},{3,2},{4,7},{5,4},{6,5},{7,6},{8,11},{9,8},{10,9... | collective-permute-start | bytes 1572872 | tf_op jit(solution)/shard_map/ppermute | solution.py:262
  129.3 37.7 %copy-start.13 = (bf16[2,256,512]{2,1,0:T(8,128)(2,1)S(1)}, bf16[2,256,512]{2,1,0:T(8,128)(2,1)}, u32[]{:S(2)}) copy-start(bf16[2,256,512]{2,1,0:T(8,128)(2,1)} %get-tuple-element.51) | copy-start | bytes 1572868
  130.6 28.4 %collective-permute-start.22 = (bf16[2,256,512]{2,1,0:T(8,128)(2,1)S(1)}, bf16[2,256,512]{2,1,0:T(8,128)(2,1)S(1)}, u32[]{:S(2)}, u32[]{:S(2)}) collective-permute-start(bf16[2,256,512]{2,1,0:T(8,128)(2,1)S(1)} %copy-done.19), channel_id=1, source_target_pairs={{2,1},{3,2},{4,7},{7,6},{8,11},{11,10},{12,15},{18,17},{19,18},{20... | collective-permute-start | bytes 1572872 | tf_op jit(solution)/shard_map/ppermute | solution.py:262
  136.5 31.5 %collective-permute-start.23 = (bf16[2,256,512]{2,1,0:T(8,128)(2,1)S(1)}, bf16[2,256,512]{2,1,0:T(8,128)(2,1)S(1)}, u32[]{:S(2)}, u32[]{:S(2)}) collective-permute-start(bf16[2,256,512]{2,1,0:T(8,128)(2,1)S(1)} %copy-done.18), channel_id=1, source_target_pairs={{1,2},{5,6},{10,11},{14,15},{17,18},{21,22},{26,27},{30,31},{33,34... | collective-permute-start | bytes 1572872 | tf_op jit(solution)/shard_map/ppermute | solution.py:262
  147.5 19.6 %collective-permute-start.21 = (bf16[2,256,512]{2,1,0:T(8,128)(2,1)S(1)}, bf16[2,256,512]{2,1,0:T(8,128)(2,1)S(1)}, u32[]{:S(2)}, u32[]{:S(2)}) collective-permute-start(bf16[2,256,512]{2,1,0:T(8,128)(2,1)S(1)} %add_convert_fusion.1), channel_id=1, source_target_pairs={{0,1},{1,2},{5,6},{6,7},{9,10},{10,11},{14,15},{16,17},{17,18},{21... | collective-permute-start | bytes 1572872 | tf_op jit(solution)/shard_map/ppermute | solution.py:262
  149.8 18.3 %collective-permute-start.25 = (bf16[2,256,512]{2,1,0:T(8,128)(2,1)S(1)}, bf16[2,256,512]{2,1,0:T(8,128)(2,1)S(1)}, u32[]{:S(2)}, u32[]{:S(2)}) collective-permute-start(bf16[2,256,512]{2,1,0:T(8,128)(2,1)S(1)} %add_convert_fusion), channel_id=1, source_target_pairs={{3,2},{7,6},{8,11},{12,15},{19,18},{23,22},{24,27},{28,31},{35,34}... | collective-permute-start | bytes 1572872 | tf_op jit(solution)/shard_map/ppermute | solution.py:262
  152.1 18.9 %collective-permute-start.26 = (bf16[2,256,512]{2,1,0:T(8,128)(2,1)S(1)}, bf16[2,256,512]{2,1,0:T(8,128)(2,1)S(1)}, u32[]{:S(2)}, u32[]{:S(2)}) collective-permute-start(bf16[2,256,512]{2,1,0:T(8,128)(2,1)S(1)} %pad_maximum_fusion.1), channel_id=1, source_target_pairs={{0,16},{1,17},{2,18},{3,19},{4,20},{5,21},{6,22},{7,23},{8,24},{9,... | collective-permute-start | bytes 1572872 | tf_op jit(solution)/shard_map/ppermute | solution.py:360
  169.1 11.4 %collective-permute-start.27 = (bf16[2,256,512]{2,1,0:T(8,128)(2,1)S(1)}, bf16[2,256,512]{2,1,0:T(8,128)(2,1)S(1)}, u32[]{:S(2)}, u32[]{:S(2)}) collective-permute-start(bf16[2,256,512]{2,1,0:T(8,128)(2,1)S(1)} %pad_maximum_fusion.2), channel_id=1, source_target_pairs={{1,17},{2,18},{6,22},{7,23},{10,26},{11,27},{15,31},{17,33},{18,34... | collective-permute-start | bytes 1572872 | tf_op jit(solution)/shard_map/ppermute | solution.py:360
  (16 other events, 267.0 us)

commit v11 on v10

--- a/solution.py
+++ b/solution.py
@@ -17,6 +17,7 @@
 STEPS = (0, -1, 1, 2)
 VMEM_BYTES = 56 * 1024 * 1024
 HEAD = 16
+LANES = 128
 BRA_CELLS = ((0, 0), (0, 1), (2, 1), (1, 0), (1, 1), (3, 1))
 CELLS = [(b, j) for b in range(2) for j in range(CH)]
 
@@ -109,15 +110,35 @@
             strip_high[n - 3] = value
 
 
-def unpack_kernel(place, ket_sizes, bra_sizes, *refs):
-    here, above, out = refs[:4], refs[4:6], refs[6]
+def unpack_kernel(place, ket_sizes, bra_sizes, here0, here1, above, out):
     out[...] = jnp.zeros_like(out)
-    for i, (cell, rows, cols) in enumerate(packed_cells(place[0], place[1], ket_sizes, bra_sizes)[0]):
+    places = packed_cells(place[0], place[1], ket_sizes, bra_sizes)[0]
+    for i, here in enumerate((here0, here1)):
+        cell, rows, cols = places[i]
 
         @pl.when(rows > 0)
-        def _(i=i, cell=cell, rows=rows, cols=cols):
-            value = here[i][...] + above[i // 2][i % 2].astype(F32)
+        def _(i=i, here=here, cell=cell, rows=rows, cols=cols):
+            value = here[...] + above[i].astype(F32)
             out[cell] = jnp.where(keep(rows, cols), value, 0.0).astype(BF)
+
+
+def finish_kernel(place, ket_sizes, bra_sizes, here2, here3, above, _, out, done, sem):
+    places = packed_cells(place[0], place[1], ket_sizes, bra_sizes)[0]
+    for i, here in enumerate((here2, here3)):
+        cell, rows, cols = places[2 + i]
+
+        @pl.when(rows > 0)
+        def _(i=i, here=here, cell=cell, rows=rows, cols=cols):
+            value = here[...] + above[i].astype(F32)
+            done[i] = jnp.where(keep(rows, cols), value, 0.0).astype(BF)
+            pltpu.make_async_copy(done.at[i], out.at[cell], sem.at[i]).start()
+
+    for i in range(2):
+        cell, rows, _ = places[2 + i]
+
+        @pl.when(rows > 0)
+        def _(i=i, cell=cell):
+            pltpu.make_async_copy(done.at[i], out.at[cell], sem.at[i]).wait()
 
 
 def terms_kernel(slots, place, ints, values, *refs):
@@ -164,7 +185,7 @@
 
     @pl.loop(0, 12 * EPW)
     def _(item):
-        base = 64 * (item // EPW) + 8 * (item % EPW)
+        base = LANES * (item // EPW) + 8 * (item % EPW)
         out_w, s, code = ints[base], ints[base + 2], ints[base + 7]
         q_b = code - 1
         p_b, s_a = q_b + s // 2, s % 2
@@ -305,7 +326,7 @@
 
     heads = [own01[0], own01[1], own2, behind01[0], behind01[1], behind2, ahead01[0], ahead01[1], ahead2,
              across0, across1, across2a]
-    values = jnp.concatenate([head[0, :64] for head in heads]).astype(F32)
+    values = jnp.concatenate([lax.optimization_barrier(head[0, :LANES].astype(F32)) for head in heads])
 
     hbm = pl.BlockSpec(memory_space=pl.ANY)
     def terms(slots, own):
@@ -359,13 +380,23 @@
         pairs = [(a * ROWS + n, (a + 1) * ROWS + n) for a in range(SECS - 1) for n in range(ROWS) if COUNT[n] > i]
         above.append(lax.ppermute(jnp.stack(raised[i : i + 2]), ("sec", "row"), pairs))
 
+    whole = shape((4, BB, KB), BF)
     out = pl.pallas_call(
         unpack_kernel,
-        in_specs=[smem] * 3 + [vmem] * 6,
+        in_specs=[smem] * 3 + [vmem] * 3,
         out_specs=vmem,
-        out_shape=shape((4, BB, KB), BF),
+        out_shape=whole,
         compiler_params=params,
-    )(place, ket_flat, bra_flat, *here, *above)
+    )(place, ket_flat, bra_flat, here[0], here[1], above[0])
+    out = pl.pallas_call(
+        finish_kernel,
+        in_specs=[smem] * 3 + [vmem] * 3 + [hbm],
+        out_specs=hbm,
+        out_shape=whole,
+        scratch_shapes=[pltpu.VMEM((2, BB, KB), BF), pltpu.SemaphoreType.DMA((2,))],
+        input_output_aliases={6: 0},
+        compiler_params=params,
+    )(place, ket_flat, bra_flat, here[2], here[3], above[1], out)
     return out.reshape(CH, 1, 2, BB, KB)
 
 

time: 185 us -> 179 us (0.968)
  local copies, waits for them, and re-layouts: 11.3 us -> 3.8 us
    ppermute x2, waiting for transfers between devices: 9.45 us -> 6.06 us  [body(): lax.ppermute(jnp.stack(raised[i:i + 2]), ('sec', 'row'), pairs)]
    concatenate x1, local copies, waits for them, and re-layouts: 3.38 us -> 0.01 us  [body(): jnp.concatenate([lax.optimization_barrier(head[0, :LANES].astype(F32)) fo...]
    squeeze x9 -> x0, local copies, waits for them, and re-layouts: 2.83 us -> none  [body(): values = jnp.concatenate([head[0, :64] for head in heads]).astype(F32)]
    ppermute x20, waiting for transfers between devices: 43.6 us -> 46 us  [sent(): lax.ppermute(value, 'row', [(n, move(n)) for n in range(ROWS) if owner(n)...]
    pallas_call x1 -> x2, Pallas kernels: 3.24 us -> 4.91 us  [the longest x1 2.58 us: body(): pl.pallas_call(unpack_kernel, in_specs=[smem] * 3 + [vmem] * 3, out_specs...]
  transfers between devices with their start and end apart: 28 -> 28, of which waited for: 10 -> 10; matrix products, arithmetic and copies ran while one was open for 10% -> 6% of each run, Pallas kernels for 9% -> 10%
where the time goes in v11:
time: 179 us; the launch traced here: 177 us
  waiting for transfers between devices  71.2 us (40%)
  starting transfers between devices  59.7 us (33%)
  Pallas kernels  31.3 us (17%)
  other arithmetic  10.4 us (6%)
  local copies, waits for them, and re-layouts  3.8 us (2%)
    ppermute x20, waiting for transfers between devices, sent(): lax.ppermute(value, 'row', [(n, move(n)) for n in range(ROWS) if owner(n)...  46 us
    ppermute x20, starting transfers between devices, sent(): lax.ppermute(value, 'row', [(n, move(n)) for n in range(ROWS) if owner(n)...  43 us
    pallas_call x2, Pallas kernels, terms(): pl.pallas_call(functools.partial(terms_kernel, slots), in_specs=[smem] *...  21.2 us
    ppermute x1, waiting for transfers between devices, body(): rim_low = lax.ppermute(strip_low, 'sec', up(1))  13.7 us
    ppermute x2, waiting for transfers between devices, body(): lax.ppermute(jnp.stack(raised[i:i + 2]), ('sec', 'row'), pairs)  6.06 us
    ppermute x1, waiting for transfers between devices, body(): borrowed = lax.ppermute(after(moving, rim_low), 'row', lent)  4.73 us
    convert_element_type x4, other arithmetic, body(): added(mine[i][1], from_left[i][1], from_right[i][1]).astype(BF)  4.01 us
    ppermute x2, starting transfers between devices, body(): lax.ppermute(jnp.stack(raised[i:i + 2]), ('sec', 'row'), pairs)  3.84 us
  transfers between devices with their start and end apart: 28, of which 10 were waited for; matrix products, arithmetic and copies ran while one was open for 6% of the time, Pallas kernels for 10%

profile of v11, /device:TPU:12, one launch (start us, length us, event | category | flops | bytes accessed | tf_op | source)
XLA Modules:
  0.0 177.2 jit_solution(17569412824726366559)
XLA Ops:
  0.6 2.6 %shard_map.73 = (bf16[2,272,512]{2,1,0:T(8,128)(2,1)}, bf16[272,512]{1,0:T(8,128)(2,1)}, bf16[272,512]{1,0:T(8,128)(2,1)}) custom-call(s32[2]{0:T(128)} %pad_add_fusion.place, s32[2,16]{1,0:T(2,128)} %bitcast.95, s32[2,16]{1,0:T(2,128)} %bitcast.98, s32[3,2,8]{2,1,0:T(2,128)} %bitcast.101, f32[2,8]{1,0:T(2,128)} %coeffs.1, bf16[4,256,512]{2,1,0:T(8,128)(2,1)} %bitcast.93), custom_call_target="tpu_custom_call" | custom-call | tf_op jit(solution)/shard_map/pallas_call | solution.py:270
  3.2 6.3 %collective-permute-start.4 = (bf16[2,272,512]{2,1,0:T(8,128)(2,1)}, bf16[2,272,512]{2,1,0:T(8,128)(2,1)S(1)}, u32[]{:S(2)}, u32[]{:S(2)}) collective-permute-start(bf16[2,272,512]{2,1,0:T(8,128)(2,1)} %get-tuple-element.44.refs_0_), channel_id=1, source_target_pairs={{0,12},{1,13},{2,14},{3,15},{4,0},{5,1},{6,2},{7,3},{8,4},{9,5},{1... | collective-permute-start | bytes 1671176 | tf_op jit(solution)/shard_map/ppermute | solution.py:283
  9.5 2.5 %shard_map.74 = (bf16[6,256,256]{2,1,0:T(8,128)(2,1)}, bf16[6,64,256]{2,1,0:T(8,128)(2,1)}, bf16[3,64,256]{2,1,0:T(8,128)(2,1)}, bf16[3,64,256]{2,1,0:T(8,128)(2,1)}) custom-call(s32[2]{0:T(128)} %pad_add_fusion.place, bf16[4,2,256,256]{3,2,1,0:T(8,128)(2,1)} %bitcast.94), custom_call_target="tpu_custom_call" | custom-call | tf_op jit(solution)/shard_map/pallas_call | solution.py:296
  12.0 1.9 %collective-permute-start = (bf16[3,64,256]{2,1,0:T(8,128)(2,1)}, bf16[3,64,256]{2,1,0:T(8,128)(2,1)S(1)}, u32[]{:S(2)}, u32[]{:S(2)}) collective-permute-start(bf16[3,64,256]{2,1,0:T(8,128)(2,1)} %get-tuple-element.35), channel_id=1, source_target_pairs={{0,16},{16,32},{32,48},{48,64},{64,80},{80,96},{96,112},{112,128},... | collective-permute-start | bytes 294920 | tf_op jit(solution)/shard_map/ppermute | solution.py:310
  13.9 2.8 %collective-permute-start.11 = (bf16[3,64,256]{2,1,0:T(8,128)(2,1)}, bf16[3,64,256]{2,1,0:T(8,128)(2,1)S(1)}, u32[]{:S(2)}, u32[]{:S(2)}) collective-permute-start(bf16[3,64,256]{2,1,0:T(8,128)(2,1)} %get-tuple-element.39), channel_id=1, source_target_pairs={{32,0},{48,16},{64,32},{80,48},{96,64},{112,80},{128,96},{144,112}... | collective-permute-start | bytes 294920 | tf_op jit(solution)/shard_map/ppermute | solution.py:322
  16.8 3.6 %collective-permute-start.10 = (bf16[6,64,256]{2,1,0:T(8,128)(2,1)}, bf16[6,64,256]{2,1,0:T(8,128)(2,1)S(1)}, u32[]{:S(2)}, u32[]{:S(2)}) collective-permute-start(bf16[6,64,256]{2,1,0:T(8,128)(2,1)} %get-tuple-element.38), channel_id=1, source_target_pairs={{16,0},{32,16},{48,32},{64,48},{80,64},{96,80},{112,96},{128,112},... | collective-permute-start | bytes 589832 | tf_op jit(solution)/shard_map/ppermute | solution.py:321
  21.5 13.7 %collective-permute-done = bf16[3,64,256]{2,1,0:T(8,128)(2,1)S(1)} collective-permute-done((bf16[3,64,256]{2,1,0:T(8,128)(2,1)}, bf16[3,64,256]{2,1,0:T(8,128)(2,1)S(1)}, u32[]{:S(2)}, u32[]{:S(2)}) %collective-permute-start) | collective-permute-done | bytes 98336 | tf_op jit(solution)/shard_map/ppermute | solution.py:310
  35.2 3.1 %collective-permute-start.1 = (bf16[272,512]{1,0:T(8,128)(2,1)}, bf16[272,512]{1,0:T(8,128)(2,1)S(1)}, u32[]{:S(2)}, u32[]{:S(2)}) collective-permute-start(bf16[272,512]{1,0:T(8,128)(2,1)} %get-tuple-element.36), channel_id=1, source_target_pairs={{2,3},{6,5},{11,8},{15,12},{18,19},{22,21},{27,24},{31,28},{34,35}... | collective-permute-start | bytes 835592 | tf_op jit(solution)/shard_map/ppermute | solution.py:311
  39.1 1.3 collective-permute-start.12
  40.3 4.7 %collective-permute-done.1 = bf16[272,512]{1,0:T(8,128)(2,1)S(1)} collective-permute-done((bf16[272,512]{1,0:T(8,128)(2,1)}, bf16[272,512]{1,0:T(8,128)(2,1)S(1)}, u32[]{:S(2)}, u32[]{:S(2)}) %collective-permute-start.1) | collective-permute-done | bytes 278560 | tf_op jit(solution)/shard_map/ppermute | solution.py:311
  46.1 1.9 %collective-permute-start.5 = (bf16[272,512]{1,0:T(8,128)(2,1)S(1)}, bf16[272,512]{1,0:T(8,128)(2,1)S(1)}, u32[]{:S(2)}, u32[]{:S(2)}) collective-permute-start(bf16[272,512]{1,0:T(8,128)(2,1)S(1)} %add.83.refs_1_), channel_id=1, source_target_pairs={{1,13},{2,14},{3,15},{5,1},{6,2},{7,3},{8,4},{10,6},{11,7},{12,8},... | collective-permute-start | bytes 835592 | tf_op jit(solution)/shard_map/ppermute | solution.py:283
  48.0 4.8 %collective-permute-start.3 = (bf16[272,512]{1,0:T(8,128)(2,1)S(1)}, bf16[272,512]{1,0:T(8,128)(2,1)S(1)}, u32[]{:S(2)}, u32[]{:S(2)}) collective-permute-start(bf16[272,512]{1,0:T(8,128)(2,1)S(1)} %add.83.refs_1_), channel_id=1, source_target_pairs={{1,5},{2,6},{3,7},{5,9},{6,10},{7,11},{8,12},{10,14},{11,15},{12,0... | collective-permute-start | bytes 835592 | tf_op jit(solution)/shard_map/ppermute | solution.py:283
  53.1 3.0 %collective-permute-start.6 = (bf16[272,512]{1,0:T(8,128)(2,1)S(1)}, bf16[272,512]{1,0:T(8,128)(2,1)S(1)}, u32[]{:S(2)}, u32[]{:S(2)}) collective-permute-start(bf16[272,512]{1,0:T(8,128)(2,1)S(1)} %get-tuple-element.68), channel_id=1, source_target_pairs={{0,4},{1,5},{2,6},{3,7},{4,8},{5,9},{6,10},{7,11},{8,12},{9,13},{1... | collective-permute-start | bytes 835592 | tf_op jit(solution)/shard_map/ppermute | solution.py:283
  56.4 9.8 %collective-permute-done.5.refs_5_ = bf16[272,512]{1,0:T(8,128)(2,1)S(1)} collective-permute-done((bf16[272,512]{1,0:T(8,128)(2,1)S(1)}, bf16[272,512]{1,0:T(8,128)(2,1)S(1)}, u32[]{:S(2)}, u32[]{:S(2)}) %collective-permute-start.5) | collective-permute-done | bytes 278560 | tf_op jit(solution)/shard_map/ppermute | solution.py:283
  66.1 5.4 %collective-permute-start.9 = (bf16[128,512]{1,0:T(8,128)(2,1)S(1)}, bf16[128,512]{1,0:T(8,128)(2,1)S(1)}, u32[]{:S(2)}, u32[]{:S(2)}) collective-permute-start(bf16[128,512]{1,0:T(8,128)(2,1)S(1)} %slice.195), channel_id=1, source_target_pairs={{1,13},{2,14},{3,15},{4,0},{6,2},{7,3},{8,4},{11,7},{13,9},{14,10}... | collective-permute-start | bytes 393224 | tf_op jit(solution)/shard_map/ppermute | solution.py:283
  71.6 1.3 collective-permute-start.8
  73.0 10.4 %collective-permute-done.8.refs_8_ = bf16[144,512]{1,0:T(8,128)(2,1)S(1)} collective-permute-done((bf16[144,512]{1,0:T(8,128)(2,1)S(1)}, bf16[144,512]{1,0:T(8,128)(2,1)S(1)}, u32[]{:S(2)}, u32[]{:S(2)}) %collective-permute-start.8) | collective-permute-done | bytes 147488 | tf_op jit(solution)/shard_map/ppermute | solution.py:283
  85.2 7.9 %shard_map.75 = (bf16[2,256,512]{2,1,0:T(8,128)(2,1)}, bf16[2,256,512]{2,1,0:T(8,128)(2,1)}, bf16[2,256,512]{2,1,0:T(8,128)(2,1)}, bf16[2,256,512]{2,1,0:T(8,128)(2,1)}) custom-call(s32[2]{0:T(128)} %pad_add_fusion.place, s32[1536]{0:T(1024)} %convert_element_type.248.ints, f32[1536]{0:T(1024)} %copy-done.19, ...), custom_call_target="tpu_custom_call" | custom-call | tf_op jit(solution)/shard_map/pallas_call | solution.py:334
  93.1 3.7 %collective-permute-start.21 = (bf16[2,256,512]{2,1,0:T(8,128)(2,1)}, bf16[2,256,512]{2,1,0:T(8,128)(2,1)S(1)}, u32[]{:S(2)}, u32[]{:S(2)}) collective-permute-start(bf16[2,256,512]{2,1,0:T(8,128)(2,1)} %get-tuple-element.40), channel_id=1, source_target_pairs={{0,1},{1,2},{2,3},{3,0},{4,5},{5,6},{6,7},{7,4},{8,9},{9,10},{10,1... | collective-permute-start | bytes 1572872 | tf_op jit(solution)/shard_map/ppermute | solution.py:283
  98.2 13.4 %shard_map.76 = (bf16[2,256,512]{2,1,0:T(8,128)(2,1)}, bf16[2,256,512]{2,1,0:T(8,128)(2,1)}, bf16[2,256,512]{2,1,0:T(8,128)(2,1)}, bf16[2,256,512]{2,1,0:T(8,128...) custom-call(s32[2]{0:T(128)} %pad_add_fusion.place, ...), custom_call_target="tpu_custom_call" | custom-call | tf_op jit(solution)/shard_map/pallas_call | solution.py:334
  111.9 5.2 %collective-permute-start.24 = (bf16[2,256,512]{2,1,0:T(8,128)(2,1)}, bf16[2,256,512]{2,1,0:T(8,128)(2,1)S(1)}, u32[]{:S(2)}, u32[]{:S(2)}) collective-permute-start(bf16[2,256,512]{2,1,0:T(8,128)(2,1)} %get-tuple-element.55), channel_id=1, source_target_pairs={{0,1},{1,2},{2,3},{3,0},{4,5},{5,6},{6,7},{7,4},{8,9},{9,10},{10,1... | collective-permute-start | bytes 1572872 | tf_op jit(solution)/shard_map/ppermute | solution.py:283
  118.3 3.2 %collective-permute-start.22 = (bf16[2,256,512]{2,1,0:T(8,128)(2,1)S(1)}, bf16[2,256,512]{2,1,0:T(8,128)(2,1)S(1)}, u32[]{:S(2)}, u32[]{:S(2)}) collective-permute-start(bf16[2,256,512]{2,1,0:T(8,128)(2,1)S(1)} %add_convert_fusion.1), channel_id=1, source_target_pairs={{0,1},{1,2},{2,3},{3,0},{4,5},{5,6},{6,7},{7,4},{8,9},{9,10},{10,1... | collective-permute-start | bytes 1572872 | tf_op jit(solution)/shard_map/ppermute | solution.py:283
  124.1 2.5 %collective-permute-start.16 = (bf16[2,256,512]{2,1,0:T(8,128)(2,1)S(1)}, bf16[2,256,512]{2,1,0:T(8,128)(2,1)S(1)}, u32[]{:S(2)}, u32[]{:S(2)}) collective-permute-start(bf16[2,256,512]{2,1,0:T(8,128)(2,1)S(1)} %copy-done.21), channel_id=1, source_target_pairs={{2,1},{3,2},{4,7},{7,6},{8,11},{11,10},{12,15},{18,17},{19,18},{20... | collective-permute-start | bytes 1572872 | tf_op jit(solution)/shard_map/ppermute | solution.py:283
  126.8 3.3 %collective-permute-done.23 = bf16[2,256,512]{2,1,0:T(8,128)(2,1)S(1)} collective-permute-done((bf16[2,256,512]{2,1,0:T(8,128)(2,1)}, bf16[2,256,512]{2,1,0:T(8,128)(2,1)S(1)}, u32[]{:S(2)}, u32[]{:S(2)}) %collective-permute-start.23) | collective-permute-done | bytes 524320 | tf_op jit(solution)/shard_map/ppermute | solution.py:283
  131.3 9.7 %collective-permute-done.22 = bf16[2,256,512]{2,1,0:T(8,128)(2,1)S(1)} collective-permute-done((bf16[2,256,512]{2,1,0:T(8,128)(2,1)S(1)}, bf16[2,256,512]{2,1,0:T(8,128)(2,1)S(1)}, u32[]{:S(2)}, u32[]{:S(2)}) %collective-permute-start.22) | collective-permute-done | bytes 524320 | tf_op jit(solution)/shard_map/ppermute | solution.py:283
  145.7 1.9 %collective-permute-start.27 = (bf16[2,256,512]{2,1,0:T(8,128)(2,1)S(1)}, bf16[2,256,512]{2,1,0:T(8,128)(2,1)S(1)}, u32[]{:S(2)}, u32[]{:S(2)}) collective-permute-start(bf16[2,256,512]{2,1,0:T(8,128)(2,1)S(1)} %pad_maximum_fusion.2), channel_id=1, source_target_pairs={{0,16},{1,17},{2,18},{3,19},{4,20},{5,21},{6,22},{7,23},{8,24},{9,... | collective-permute-start | bytes 1572872 | tf_op jit(solution)/shard_map/ppermute | solution.py:381
  147.6 4.9 %collective-permute-done.16 = bf16[2,256,512]{2,1,0:T(8,128)(2,1)S(1)} collective-permute-done((bf16[2,256,512]{2,1,0:T(8,128)(2,1)S(1)}, bf16[2,256,512]{2,1,0:T(8,128)(2,1)S(1)}, u32[]{:S(2)}, u32[]{:S(2)}) %collective-permute-start.16) | collective-permute-done | bytes 524320 | tf_op jit(solution)/shard_map/ppermute | solution.py:283
  152.5 7.9 %collective-permute-done.15 = bf16[2,256,512]{2,1,0:T(8,128)(2,1)S(1)} collective-permute-done((bf16[2,256,512]{2,1,0:T(8,128)(2,1)S(1)}, bf16[2,256,512]{2,1,0:T(8,128)(2,1)S(1)}, u32[]{:S(2)}, u32[]{:S(2)}) %collective-permute-start.15) | collective-permute-done | bytes 524320 | tf_op jit(solution)/shard_map/ppermute | solution.py:283
  162.5 1.9 %collective-permute-start.20 = (bf16[2,256,512]{2,1,0:T(8,128)(2,1)S(1)}, bf16[2,256,512]{2,1,0:T(8,128)(2,1)S(1)}, u32[]{:S(2)}, u32[]{:S(2)}) collective-permute-start(bf16[2,256,512]{2,1,0:T(8,128)(2,1)S(1)} %pad_maximum_fusion.1), channel_id=1, source_target_pairs={{1,17},{2,18},{6,22},{7,23},{10,26},{11,27},{15,31},{17,33},{18,34... | collective-permute-start | bytes 1572872 | tf_op jit(solution)/shard_map/ppermute | solution.py:381
  165.3 2.6 %shard_map.77._ = bf16[4,256,512]{2,1,0:T(8,128)(2,1)} custom-call(s32[2]{0:T(128)} %pad_add_fusion.place, s32[2,16]{1,0:T(2,128)} %bitcast.96, s32[2,16]{1,0:T(2,128)} %bitcast.99, f32[256,512]{1,0:T(8,128)} %get-tuple-element.58.here0, f32[256,512]{1,0:T(8,128)} %get-tuple-element.60.here1, bf16[2,256,512]{2,1,0:T(8,128)(2,1)} %copy-done.13), custom_call_target="tpu_custom_call" | custom-call | tf_op jit(solution)/shard_map/pallas_call | solution.py:384
  167.8 6.1 %collective-permute-done.20.above = bf16[2,256,512]{2,1,0:T(8,128)(2,1)S(1)} collective-permute-done((bf16[2,256,512]{2,1,0:T(8,128)(2,1)S(1)}, bf16[2,256,512]{2,1,0:T(8,128)(2,1)S(1)}, u32[]{:S(2)}, u32[]{:S(2)}) %collective-permute-start.20) | collective-permute-done | bytes 524320 | tf_op jit(solution)/shard_map/ppermute | solution.py:381
  174.7 2.3 %shard_map.78 = bf16[4,256,512]{2,1,0:T(8,128)(2,1)} custom-call(s32[2]{0:T(128)} %pad_add_fusion.place, s32[2,16]{1,0:T(2,128)} %bitcast.97, s32[2,16]{1,0:T(2,128)} %bitcast.100, f32[256,512]{1,0:T(8,128)} %get-tuple-element.62.here2, f32[256,512]{1,0:T(8,128)} %get-tuple-element.64.here3, ...), custom_call_target="tpu_custom_call", output_to_operand_aliasing={{}: (6, {})} | custom-call | tf_op jit(solution)/shard_map/pallas_call | solution.py:391
  (119 shorter events, 20.6 us)
Async XLA Ops:
  3.2 49.7 %collective-permute-start.4 = (bf16[2,272,512]{2,1,0:T(8,128)(2,1)}, bf16[2,272,512]{2,1,0:T(8,128)(2,1)S(1)}, u32[]{:S(2)}, u32[]{:S(2)}) collective-permute-start(bf16[2,272,512]{2,1,0:T(8,128)(2,1)} %get-tuple-element.44.refs_0_), channel_id=1, source_target_pairs={{0,12},{1,13},{2,14},{3,15},{4,0},{5,1},{6,2},{7,3},{8,4},{9,5},{1... | collective-permute-start | bytes 1671176 | tf_op jit(solution)/shard_map/ppermute | solution.py:283
  9.5 43.6 %collective-permute-start.2 = (bf16[2,272,512]{2,1,0:T(8,128)(2,1)}, bf16[2,272,512]{2,1,0:T(8,128)(2,1)S(1)}, u32[]{:S(2)}, u32[]{:S(2)}) collective-permute-start(bf16[2,272,512]{2,1,0:T(8,128)(2,1)} %get-tuple-element.44.refs_0_), channel_id=1, source_target_pairs={{0,4},{1,5},{2,6},{3,7},{4,8},{5,9},{6,10},{7,11},{8,12},{9,13},{1... | collective-permute-start | bytes 1671176 | tf_op jit(solution)/shard_map/ppermute | solution.py:283
  12.0 23.2 %collective-permute-start = (bf16[3,64,256]{2,1,0:T(8,128)(2,1)}, bf16[3,64,256]{2,1,0:T(8,128)(2,1)S(1)}, u32[]{:S(2)}, u32[]{:S(2)}) collective-permute-start(bf16[3,64,256]{2,1,0:T(8,128)(2,1)} %get-tuple-element.35), channel_id=1, source_target_pairs={{0,16},{16,32},{32,48},{48,64},{64,80},{80,96},{96,112},{112,128},... | collective-permute-start | bytes 294920 | tf_op jit(solution)/shard_map/ppermute | solution.py:310
  13.9 25.1 %collective-permute-start.11 = (bf16[3,64,256]{2,1,0:T(8,128)(2,1)}, bf16[3,64,256]{2,1,0:T(8,128)(2,1)S(1)}, u32[]{:S(2)}, u32[]{:S(2)}) collective-permute-start(bf16[3,64,256]{2,1,0:T(8,128)(2,1)} %get-tuple-element.39), channel_id=1, source_target_pairs={{32,0},{48,16},{64,32},{80,48},{96,64},{112,80},{128,96},{144,112}... | collective-permute-start | bytes 294920 | tf_op jit(solution)/shard_map/ppermute | solution.py:322
  16.8 22.3 %collective-permute-start.10 = (bf16[6,64,256]{2,1,0:T(8,128)(2,1)}, bf16[6,64,256]{2,1,0:T(8,128)(2,1)S(1)}, u32[]{:S(2)}, u32[]{:S(2)}) collective-permute-start(bf16[6,64,256]{2,1,0:T(8,128)(2,1)} %get-tuple-element.38), channel_id=1, source_target_pairs={{16,0},{32,16},{48,32},{64,48},{80,64},{96,80},{112,96},{128,112},... | collective-permute-start | bytes 589832 | tf_op jit(solution)/shard_map/ppermute | solution.py:321
  35.2 9.9 %collective-permute-start.1 = (bf16[272,512]{1,0:T(8,128)(2,1)}, bf16[272,512]{1,0:T(8,128)(2,1)S(1)}, u32[]{:S(2)}, u32[]{:S(2)}) collective-permute-start(bf16[272,512]{1,0:T(8,128)(2,1)} %get-tuple-element.36), channel_id=1, source_target_pairs={{2,3},{6,5},{11,8},{15,12},{18,19},{22,21},{27,24},{31,28},{34,35}... | collective-permute-start | bytes 835592 | tf_op jit(solution)/shard_map/ppermute | solution.py:311
  39.1 45.2 %copy-start.5 = (bf16[12,64,256]{2,1,0:T(8,128)(2,1)}, bf16[12,64,256]{2,1,0:T(8,128)(2,1)S(1)}, u32[]{:S(2)}) copy-start(bf16[12,64,256]{2,1,0:T(8,128)(2,1)S(1)} %constant_dynamic-update-slice_fusion.1.refs_12_) | copy-start | bytes 1179652
  39.1 17.1 %collective-permute-start.12 = (bf16[12,64,256]{2,1,0:T(8,128)(2,1)S(1)}, bf16[12,64,256]{2,1,0:T(8,128)(2,1)S(1)}, u32[]{:S(2)}, u32[]{:S(2)}) collective-permute-start(bf16[12,64,256]{2,1,0:T(8,128)(2,1)S(1)} %constant_dynamic-update-slice_fusion.1.refs_12_), channel_id=1, source_target_pairs={{0,1},{1,0},{2,3},{3,2},{4,5},{5,4},{6,7},{7,6},{8,9},{9,8},{10,11... | collective-permute-start | bytes 1179656 | tf_op jit(solution)/shard_map/ppermute | solution.py:324
  46.1 38.2 %copy-start.4 = (bf16[272,512]{1,0:T(8,128)(2,1)}, bf16[272,512]{1,0:T(8,128)(2,1)S(1)}, u32[]{:S(2)}) copy-start(bf16[272,512]{1,0:T(8,128)(2,1)S(1)} %add.83.refs_1_) | copy-start | bytes 835588
  46.1 20.0 %collective-permute-start.5 = (bf16[272,512]{1,0:T(8,128)(2,1)S(1)}, bf16[272,512]{1,0:T(8,128)(2,1)S(1)}, u32[]{:S(2)}, u32[]{:S(2)}) collective-permute-start(bf16[272,512]{1,0:T(8,128)(2,1)S(1)} %add.83.refs_1_), channel_id=1, source_target_pairs={{1,13},{2,14},{3,15},{5,1},{6,2},{7,3},{8,4},{10,6},{11,7},{12,8},... | collective-permute-start | bytes 835592 | tf_op jit(solution)/shard_map/ppermute | solution.py:283
  48.0 23.6 %collective-permute-start.3 = (bf16[272,512]{1,0:T(8,128)(2,1)S(1)}, bf16[272,512]{1,0:T(8,128)(2,1)S(1)}, u32[]{:S(2)}, u32[]{:S(2)}) collective-permute-start(bf16[272,512]{1,0:T(8,128)(2,1)S(1)} %add.83.refs_1_), channel_id=1, source_target_pairs={{1,5},{2,6},{3,7},{5,9},{6,10},{7,11},{8,12},{10,14},{11,15},{12,0... | collective-permute-start | bytes 835592 | tf_op jit(solution)/shard_map/ppermute | solution.py:283
  53.0 30.5 %collective-permute-start.7 = (bf16[272,512]{1,0:T(8,128)(2,1)S(1)}, bf16[272,512]{1,0:T(8,128)(2,1)S(1)}, u32[]{:S(2)}, u32[]{:S(2)}) collective-permute-start(bf16[272,512]{1,0:T(8,128)(2,1)S(1)} %get-tuple-element.65), channel_id=1, source_target_pairs={{0,12},{1,13},{2,14},{3,15},{4,0},{5,1},{6,2},{7,3},{8,4},{9,5},{1... | collective-permute-start | bytes 835592 | tf_op jit(solution)/shard_map/ppermute | solution.py:283
  53.1 30.3 %collective-permute-start.6 = (bf16[272,512]{1,0:T(8,128)(2,1)S(1)}, bf16[272,512]{1,0:T(8,128)(2,1)S(1)}, u32[]{:S(2)}, u32[]{:S(2)}) collective-permute-start(bf16[272,512]{1,0:T(8,128)(2,1)S(1)} %get-tuple-element.68), channel_id=1, source_target_pairs={{0,4},{1,5},{2,6},{3,7},{4,8},{5,9},{6,10},{7,11},{8,12},{9,13},{1... | collective-permute-start | bytes 835592 | tf_op jit(solution)/shard_map/ppermute | solution.py:283
  56.3 28.0 %collective-permute-start.13 = (bf16[24,64,256]{2,1,0:T(8,128)(2,1)S(1)}, bf16[24,64,256]{2,1,0:T(8,128)(2,1)S(1)}, u32[]{:S(2)}, u32[]{:S(2)}) collective-permute-start(bf16[24,64,256]{2,1,0:T(8,128)(2,1)S(1)} %pad_maximum_fusion), channel_id=1, source_target_pairs={{0,3},{1,2},{2,1},{3,0},{4,7},{5,6},{6,5},{7,4},{8,11},{9,10},{10,... | collective-permute-start | bytes 2359304 | tf_op jit(solution)/shard_map/ppermute | solution.py:325
  66.1 18.1 %collective-permute-start.9 = (bf16[128,512]{1,0:T(8,128)(2,1)S(1)}, bf16[128,512]{1,0:T(8,128)(2,1)S(1)}, u32[]{:S(2)}, u32[]{:S(2)}) collective-permute-start(bf16[128,512]{1,0:T(8,128)(2,1)S(1)} %slice.195), channel_id=1, source_target_pairs={{1,13},{2,14},{3,15},{4,0},{6,2},{7,3},{8,4},{11,7},{13,9},{14,10}... | collective-permute-start | bytes 393224 | tf_op jit(solution)/shard_map/ppermute | solution.py:283
  71.6 11.8 %collective-permute-start.8 = (bf16[144,512]{1,0:T(8,128)(2,1)S(1)}, bf16[144,512]{1,0:T(8,128)(2,1)S(1)}, u32[]{:S(2)}, u32[]{:S(2)}) collective-permute-start(bf16[144,512]{1,0:T(8,128)(2,1)S(1)} %slice.193), channel_id=1, source_target_pairs={{0,4},{3,7},{5,9},{6,10},{7,11},{9,13},{10,14},{11,15},{12,0},{14,... | collective-permute-start | bytes 442376 | tf_op jit(solution)/shard_map/ppermute | solution.py:283
  93.1 18.8 %collective-permute-start.21 = (bf16[2,256,512]{2,1,0:T(8,128)(2,1)}, bf16[2,256,512]{2,1,0:T(8,128)(2,1)S(1)}, u32[]{:S(2)}, u32[]{:S(2)}) collective-permute-start(bf16[2,256,512]{2,1,0:T(8,128)(2,1)} %get-tuple-element.40), channel_id=1, source_target_pairs={{0,1},{1,2},{2,3},{3,0},{4,5},{5,6},{6,7},{7,4},{8,9},{9,10},{10,1... | collective-permute-start | bytes 1572872 | tf_op jit(solution)/shard_map/ppermute | solution.py:283
  96.8 21.6 %collective-permute-start.25 = (bf16[2,256,512]{2,1,0:T(8,128)(2,1)}, bf16[2,256,512]{2,1,0:T(8,128)(2,1)S(1)}, u32[]{:S(2)}, u32[]{:S(2)}) collective-permute-start(bf16[2,256,512]{2,1,0:T(8,128)(2,1)} %get-tuple-element.41), channel_id=1, source_target_pairs={{0,3},{1,0},{2,1},{3,2},{4,7},{5,4},{6,5},{7,6},{8,11},{9,8},{10,9... | collective-permute-start | bytes 1572872 | tf_op jit(solution)/shard_map/ppermute | solution.py:283
  96.8 27.3 %collective-permute-start.14 = (bf16[2,256,512]{2,1,0:T(8,128)(2,1)}, bf16[2,256,512]{2,1,0:T(8,128)(2,1)S(1)}, u32[]{:S(2)}, u32[]{:S(2)}) collective-permute-start(bf16[2,256,512]{2,1,0:T(8,128)(2,1)} %get-tuple-element.42), channel_id=1, source_target_pairs={{0,1},{3,0},{4,5},{5,6},{8,9},{9,10},{13,14},{16,17},{19,16},{20,2... | collective-permute-start | bytes 1572872 | tf_op jit(solution)/shard_map/ppermute | solution.py:283
  97.5 25.3 %collective-permute-start.18 = (bf16[2,256,512]{2,1,0:T(8,128)(2,1)}, bf16[2,256,512]{2,1,0:T(8,128)(2,1)S(1)}, u32[]{:S(2)}, u32[]{:S(2)}) collective-permute-start(bf16[2,256,512]{2,1,0:T(8,128)(2,1)} %get-tuple-element.43), channel_id=1, source_target_pairs={{0,3},{4,7},{9,8},{13,12},{16,19},{20,23},{25,24},{29,28},{32,35},... | collective-permute-start | bytes 1572872 | tf_op jit(solution)/shard_map/ppermute | solution.py:283
  111.6 18.4 %collective-permute-start.23 = (bf16[2,256,512]{2,1,0:T(8,128)(2,1)}, bf16[2,256,512]{2,1,0:T(8,128)(2,1)S(1)}, u32[]{:S(2)}, u32[]{:S(2)}) collective-permute-start(bf16[2,256,512]{2,1,0:T(8,128)(2,1)} %get-tuple-element.53), channel_id=1, source_target_pairs={{0,3},{1,0},{2,1},{3,2},{4,7},{5,4},{6,5},{7,6},{8,11},{9,8},{10,9... | collective-permute-start | bytes 1572872 | tf_op jit(solution)/shard_map/ppermute | solution.py:283
  111.9 31.4 %collective-permute-start.24 = (bf16[2,256,512]{2,1,0:T(8,128)(2,1)}, bf16[2,256,512]{2,1,0:T(8,128)(2,1)S(1)}, u32[]{:S(2)}, u32[]{:S(2)}) collective-permute-start(bf16[2,256,512]{2,1,0:T(8,128)(2,1)} %get-tuple-element.55), channel_id=1, source_target_pairs={{0,1},{1,2},{2,3},{3,0},{4,5},{5,6},{6,7},{7,4},{8,9},{9,10},{10,1... | collective-permute-start | bytes 1572872 | tf_op jit(solution)/shard_map/ppermute | solution.py:283
  118.3 22.7 %collective-permute-start.22 = (bf16[2,256,512]{2,1,0:T(8,128)(2,1)S(1)}, bf16[2,256,512]{2,1,0:T(8,128)(2,1)S(1)}, u32[]{:S(2)}, u32[]{:S(2)}) collective-permute-start(bf16[2,256,512]{2,1,0:T(8,128)(2,1)S(1)} %add_convert_fusion.1), channel_id=1, source_target_pairs={{0,1},{1,2},{2,3},{3,0},{4,5},{5,6},{6,7},{7,4},{8,9},{9,10},{10,1... | collective-permute-start | bytes 1572872 | tf_op jit(solution)/shard_map/ppermute | solution.py:283
  122.7 21.9 %collective-permute-start.26 = (bf16[2,256,512]{2,1,0:T(8,128)(2,1)S(1)}, bf16[2,256,512]{2,1,0:T(8,128)(2,1)S(1)}, u32[]{:S(2)}, u32[]{:S(2)}) collective-permute-start(bf16[2,256,512]{2,1,0:T(8,128)(2,1)S(1)} %add_convert_fusion), channel_id=1, source_target_pairs={{0,3},{1,0},{2,1},{3,2},{4,7},{5,4},{6,5},{7,6},{8,11},{9,8},{10,9... | collective-permute-start | bytes 1572872 | tf_op jit(solution)/shard_map/ppermute | solution.py:283
  122.8 37.6 %copy-start.16 = (bf16[2,256,512]{2,1,0:T(8,128)(2,1)S(1)}, bf16[2,256,512]{2,1,0:T(8,128)(2,1)}, u32[]{:S(2)}) copy-start(bf16[2,256,512]{2,1,0:T(8,128)(2,1)} %get-tuple-element.45) | copy-start | bytes 1572868
  124.1 28.4 %collective-permute-start.16 = (bf16[2,256,512]{2,1,0:T(8,128)(2,1)S(1)}, bf16[2,256,512]{2,1,0:T(8,128)(2,1)S(1)}, u32[]{:S(2)}, u32[]{:S(2)}) collective-permute-start(bf16[2,256,512]{2,1,0:T(8,128)(2,1)S(1)} %copy-done.21), channel_id=1, source_target_pairs={{2,1},{3,2},{4,7},{7,6},{8,11},{11,10},{12,15},{18,17},{19,18},{20... | collective-permute-start | bytes 1572872 | tf_op jit(solution)/shard_map/ppermute | solution.py:283
  126.7 34.7 %copy-start.15 = (bf16[2,256,512]{2,1,0:T(8,128)(2,1)S(1)}, bf16[2,256,512]{2,1,0:T(8,128)(2,1)}, u32[]{:S(2)}) copy-start(bf16[2,256,512]{2,1,0:T(8,128)(2,1)} %get-tuple-element.48) | copy-start | bytes 1572868
  130.0 31.4 %collective-permute-start.17 = (bf16[2,256,512]{2,1,0:T(8,128)(2,1)S(1)}, bf16[2,256,512]{2,1,0:T(8,128)(2,1)S(1)}, u32[]{:S(2)}, u32[]{:S(2)}) collective-permute-start(bf16[2,256,512]{2,1,0:T(8,128)(2,1)S(1)} %copy-done.20), channel_id=1, source_target_pairs={{1,2},{5,6},{10,11},{14,15},{17,18},{21,22},{26,27},{30,31},{33,34... | collective-permute-start | bytes 1572872 | tf_op jit(solution)/shard_map/ppermute | solution.py:283
  141.0 19.4 %collective-permute-start.15 = (bf16[2,256,512]{2,1,0:T(8,128)(2,1)S(1)}, bf16[2,256,512]{2,1,0:T(8,128)(2,1)S(1)}, u32[]{:S(2)}, u32[]{:S(2)}) collective-permute-start(bf16[2,256,512]{2,1,0:T(8,128)(2,1)S(1)} %add_convert_fusion.3), channel_id=1, source_target_pairs={{0,1},{1,2},{5,6},{6,7},{9,10},{10,11},{14,15},{16,17},{17,18},{21... | collective-permute-start | bytes 1572872 | tf_op jit(solution)/shard_map/ppermute | solution.py:283
  143.3 18.1 %collective-permute-start.19 = (bf16[2,256,512]{2,1,0:T(8,128)(2,1)S(1)}, bf16[2,256,512]{2,1,0:T(8,128)(2,1)S(1)}, u32[]{:S(2)}, u32[]{:S(2)}) collective-permute-start(bf16[2,256,512]{2,1,0:T(8,128)(2,1)S(1)} %add_convert_fusion.2), channel_id=1, source_target_pairs={{3,2},{7,6},{8,11},{12,15},{19,18},{23,22},{24,27},{28,31},{35,34}... | collective-permute-start | bytes 1572872 | tf_op jit(solution)/shard_map/ppermute | solution.py:283
  145.7 18.8 %collective-permute-start.27 = (bf16[2,256,512]{2,1,0:T(8,128)(2,1)S(1)}, bf16[2,256,512]{2,1,0:T(8,128)(2,1)S(1)}, u32[]{:S(2)}, u32[]{:S(2)}) collective-permute-start(bf16[2,256,512]{2,1,0:T(8,128)(2,1)S(1)} %pad_maximum_fusion.2), channel_id=1, source_target_pairs={{0,16},{1,17},{2,18},{3,19},{4,20},{5,21},{6,22},{7,23},{8,24},{9,... | collective-permute-start | bytes 1572872 | tf_op jit(solution)/shard_map/ppermute | solution.py:381
  162.5 11.4 %collective-permute-start.20 = (bf16[2,256,512]{2,1,0:T(8,128)(2,1)S(1)}, bf16[2,256,512]{2,1,0:T(8,128)(2,1)S(1)}, u32[]{:S(2)}, u32[]{:S(2)}) collective-permute-start(bf16[2,256,512]{2,1,0:T(8,128)(2,1)S(1)} %pad_maximum_fusion.1), channel_id=1, source_target_pairs={{1,17},{2,18},{6,22},{7,23},{10,26},{11,27},{15,31},{17,33},{18,34... | collective-permute-start | bytes 1572872 | tf_op jit(solution)/shard_map/ppermute | solution.py:381
  (18 other events, 232.8 us)

commit v12 on v11

--- a/solution.py
+++ b/solution.py
@@ -12,7 +12,7 @@
 SECS, ROWS = 16, 16
 BB, KB = 256, 512
 QUARTER = BB // NX
-TOGETHER = 2
+TOGETHER = 4
 BF, F32 = jnp.bfloat16, jnp.float32
 STEPS = (0, -1, 1, 2)
 VMEM_BYTES = 56 * 1024 * 1024
@@ -355,8 +355,8 @@
           across0, across1, across2a, across2b, ket_mps[:, 0], bra_own, rim, swapped, crossed)
 
     far = terms((3,), own01)
-    sums = terms((0, 1, 2), after(own01, *far))
-    mine, left, right = sums[:4], sums[4:8], sums[8:]
+    sides = terms((1, 2), after(own01, *far))
+    left, right = sides[:4], sides[4:]
 
     def added(*parts):
         return functools.reduce(jnp.add, [part.astype(F32) for part in parts])
@@ -366,12 +366,13 @@
 
     far_up = {i: moved(far[i], x_up, x_far, i) for i in (0, 2)}
     far_down = {i: moved(far[i], x_down, x_far, i) for i in (1, 3)}
+    mine = terms((0,), after(own01, *sides, far_up[0], far_down[1]))
     from_left = {i: moved(right[i], x_up, x_up, i) for i in (1, 3)}
     from_right = {i: moved(left[i], x_down, x_down, i) for i in (0, 2)}
     for i in (0, 2):
-        from_left[i] = moved(added(right[i], far_up[i]).astype(BF), x_up, x_up, i)
+        from_left[i] = moved(added(after(right[i], *mine), far_up[i]).astype(BF), x_up, x_up, i)
     for i in (1, 3):
-        from_right[i] = moved(added(left[i], far_down[i]).astype(BF), x_down, x_down, i)
+        from_right[i] = moved(added(after(left[i], *mine), far_down[i]).astype(BF), x_down, x_down, i)
 
     here = [added(mine[i][0], from_left[i][0], from_right[i][0]) for i in range(4)]
     raised = [added(mine[i][1], from_left[i][1], from_right[i][1]).astype(BF) for i in range(4)]

time: 179 us -> 176 us (0.983); the launches traced: 177 us -> 176 us
  waiting for transfers between devices: 71.2 us -> 67.7 us
  other arithmetic: 10.4 us -> 7.14 us
  Pallas kernels: 31.3 us -> 34.4 us
  starting transfers between devices: 59.7 us -> 62.2 us
    ppermute x20, waiting for transfers between devices: 46 us -> 42.6 us  [sent(): lax.ppermute(value, 'row', [(n, move(n)) for n in range(ROWS) if owner(n)...]
    convert_element_type x4, other arithmetic: 3.78 us -> 0.54 us  [the longest x2 0.27 us: body(): added(after(left[i], *mine), far_down[i]).astype(BF)]
    pallas_call x2 -> x3, Pallas kernels: 21.2 us -> 24.4 us  [terms(): pl.pallas_call(functools.partial(terms_kernel, slots), in_specs=[smem] *...]
    ppermute x20, starting transfers between devices: 43 us -> 45.5 us  [sent(): lax.ppermute(value, 'row', [(n, move(n)) for n in range(ROWS) if owner(n)...]
  transfers between devices with their start and end apart: 28 -> 28, of which waited for: 10 -> 10; matrix products, arithmetic and copies ran while one was open for 6% -> 4% of each run, Pallas kernels for 10% -> 12%
where the time goes in v12:
time: 176 us
  waiting for transfers between devices  67.7 us (38%)
  starting transfers between devices  62.2 us (35%)
  Pallas kernels  34.4 us (20%)
  other arithmetic  7.14 us (4%)
  local copies, waits for them, and re-layouts  3.78 us (2%)
    ppermute x20, starting transfers between devices, sent(): lax.ppermute(value, 'row', [(n, move(n)) for n in range(ROWS) if owner(n)...  45.5 us
    ppermute x20, waiting for transfers between devices, sent(): lax.ppermute(value, 'row', [(n, move(n)) for n in range(ROWS) if owner(n)...  42.6 us
    pallas_call x3, Pallas kernels, terms(): pl.pallas_call(functools.partial(terms_kernel, slots), in_specs=[smem] *...  24.4 us
    ppermute x1, waiting for transfers between devices, body(): rim_low = lax.ppermute(strip_low, 'sec', up(1))  13.6 us
    ppermute x2, waiting for transfers between devices, body(): lax.ppermute(jnp.stack(raised[i:i + 2]), ('sec', 'row'), pairs)  6.07 us
    ppermute x1, waiting for transfers between devices, body(): borrowed = lax.ppermute(after(moving, rim_low), 'row', lent)  4.73 us
    convert_element_type x4, other arithmetic, body(): added(mine[i][1], from_left[i][1], from_right[i][1]).astype(BF)  4 us
    ppermute x2, starting transfers between devices, body(): lax.ppermute(jnp.stack(raised[i:i + 2]), ('sec', 'row'), pairs)  3.84 us
  transfers between devices with their start and end apart: 28, of which 10 were waited for; matrix products, arithmetic and copies ran while one was open for 4% of the time, Pallas kernels for 12%

profile of v12, /device:TPU:12, one launch (start us, length us, event | category | flops | bytes accessed | tf_op | source)
XLA Modules:
  0.0 176.2 jit_solution(6451938393096583899)
XLA Ops:
  0.6 2.6 %shard_map.73 = (bf16[2,272,512]{2,1,0:T(8,128)(2,1)}, bf16[272,512]{1,0:T(8,128)(2,1)}, bf16[272,512]{1,0:T(8,128)(2,1)}) custom-call(s32[2]{0:T(128)} %pad_add_fusion.place, s32[2,16]{1,0:T(2,128)} %bitcast.96, s32[2,16]{1,0:T(2,128)} %bitcast.99, s32[3,2,8]{2,1,0:T(2,128)} %bitcast.102, f32[2,8]{1,0:T(2,128)} %coeffs.1, bf16[4,256,512]{2,1,0:T(8,128)(2,1)} %bitcast.94), custom_call_target="tpu_custom_call" | custom-call | tf_op jit(solution)/shard_map/pallas_call | solution.py:270
  3.2 6.3 %collective-permute-start.4 = (bf16[2,272,512]{2,1,0:T(8,128)(2,1)}, bf16[2,272,512]{2,1,0:T(8,128)(2,1)S(1)}, u32[]{:S(2)}, u32[]{:S(2)}) collective-permute-start(bf16[2,272,512]{2,1,0:T(8,128)(2,1)} %get-tuple-element.58.refs_0_), channel_id=1, source_target_pairs={{0,12},{1,13},{2,14},{3,15},{4,0},{5,1},{6,2},{7,3},{8,4},{9,5},{1... | collective-permute-start | bytes 1671176 | tf_op jit(solution)/shard_map/ppermute | solution.py:283
  9.5 2.5 %shard_map.74 = (bf16[6,256,256]{2,1,0:T(8,128)(2,1)}, bf16[6,64,256]{2,1,0:T(8,128)(2,1)}, bf16[3,64,256]{2,1,0:T(8,128)(2,1)}, bf16[3,64,256]{2,1,0:T(8,128)(2,1)}) custom-call(s32[2]{0:T(128)} %pad_add_fusion.place, bf16[4,2,256,256]{3,2,1,0:T(8,128)(2,1)} %bitcast.95), custom_call_target="tpu_custom_call" | custom-call | tf_op jit(solution)/shard_map/pallas_call | solution.py:296
  12.0 1.9 %collective-permute-start = (bf16[3,64,256]{2,1,0:T(8,128)(2,1)}, bf16[3,64,256]{2,1,0:T(8,128)(2,1)S(1)}, u32[]{:S(2)}, u32[]{:S(2)}) collective-permute-start(bf16[3,64,256]{2,1,0:T(8,128)(2,1)} %get-tuple-element.40), channel_id=1, source_target_pairs={{0,16},{16,32},{32,48},{48,64},{64,80},{80,96},{96,112},{112,128},... | collective-permute-start | bytes 294920 | tf_op jit(solution)/shard_map/ppermute | solution.py:310
  13.9 2.8 %collective-permute-start.11 = (bf16[3,64,256]{2,1,0:T(8,128)(2,1)}, bf16[3,64,256]{2,1,0:T(8,128)(2,1)S(1)}, u32[]{:S(2)}, u32[]{:S(2)}) collective-permute-start(bf16[3,64,256]{2,1,0:T(8,128)(2,1)} %get-tuple-element.44), channel_id=1, source_target_pairs={{32,0},{48,16},{64,32},{80,48},{96,64},{112,80},{128,96},{144,112}... | collective-permute-start | bytes 294920 | tf_op jit(solution)/shard_map/ppermute | solution.py:322
  16.7 3.6 %collective-permute-start.10 = (bf16[6,64,256]{2,1,0:T(8,128)(2,1)}, bf16[6,64,256]{2,1,0:T(8,128)(2,1)S(1)}, u32[]{:S(2)}, u32[]{:S(2)}) collective-permute-start(bf16[6,64,256]{2,1,0:T(8,128)(2,1)} %get-tuple-element.43), channel_id=1, source_target_pairs={{16,0},{32,16},{48,32},{64,48},{80,64},{96,80},{112,96},{128,112},... | collective-permute-start | bytes 589832 | tf_op jit(solution)/shard_map/ppermute | solution.py:321
  21.5 13.6 %collective-permute-done = bf16[3,64,256]{2,1,0:T(8,128)(2,1)S(1)} collective-permute-done((bf16[3,64,256]{2,1,0:T(8,128)(2,1)}, bf16[3,64,256]{2,1,0:T(8,128)(2,1)S(1)}, u32[]{:S(2)}, u32[]{:S(2)}) %collective-permute-start) | collective-permute-done | bytes 98336 | tf_op jit(solution)/shard_map/ppermute | solution.py:310
  35.1 3.1 %collective-permute-start.1 = (bf16[272,512]{1,0:T(8,128)(2,1)}, bf16[272,512]{1,0:T(8,128)(2,1)S(1)}, u32[]{:S(2)}, u32[]{:S(2)}) collective-permute-start(bf16[272,512]{1,0:T(8,128)(2,1)} %get-tuple-element.41), channel_id=1, source_target_pairs={{2,3},{6,5},{11,8},{15,12},{18,19},{22,21},{27,24},{31,28},{34,35}... | collective-permute-start | bytes 835592 | tf_op jit(solution)/shard_map/ppermute | solution.py:311
  40.3 4.7 %collective-permute-done.1 = bf16[272,512]{1,0:T(8,128)(2,1)S(1)} collective-permute-done((bf16[272,512]{1,0:T(8,128)(2,1)}, bf16[272,512]{1,0:T(8,128)(2,1)S(1)}, u32[]{:S(2)}, u32[]{:S(2)}) %collective-permute-start.1) | collective-permute-done | bytes 278560 | tf_op jit(solution)/shard_map/ppermute | solution.py:311
  46.1 1.9 %collective-permute-start.5 = (bf16[272,512]{1,0:T(8,128)(2,1)S(1)}, bf16[272,512]{1,0:T(8,128)(2,1)S(1)}, u32[]{:S(2)}, u32[]{:S(2)}) collective-permute-start(bf16[272,512]{1,0:T(8,128)(2,1)S(1)} %add.83.refs_1_), channel_id=1, source_target_pairs={{1,13},{2,14},{3,15},{5,1},{6,2},{7,3},{8,4},{10,6},{11,7},{12,8},... | collective-permute-start | bytes 835592 | tf_op jit(solution)/shard_map/ppermute | solution.py:283
  48.0 4.8 %collective-permute-start.3 = (bf16[272,512]{1,0:T(8,128)(2,1)S(1)}, bf16[272,512]{1,0:T(8,128)(2,1)S(1)}, u32[]{:S(2)}, u32[]{:S(2)}) collective-permute-start(bf16[272,512]{1,0:T(8,128)(2,1)S(1)} %add.83.refs_1_), channel_id=1, source_target_pairs={{1,5},{2,6},{3,7},{5,9},{6,10},{7,11},{8,12},{10,14},{11,15},{12,0... | collective-permute-start | bytes 835592 | tf_op jit(solution)/shard_map/ppermute | solution.py:283
  53.1 3.0 %collective-permute-start.6 = (bf16[272,512]{1,0:T(8,128)(2,1)S(1)}, bf16[272,512]{1,0:T(8,128)(2,1)S(1)}, u32[]{:S(2)}, u32[]{:S(2)}) collective-permute-start(bf16[272,512]{1,0:T(8,128)(2,1)S(1)} %get-tuple-element.78), channel_id=1, source_target_pairs={{0,4},{1,5},{2,6},{3,7},{4,8},{5,9},{6,10},{7,11},{8,12},{9,13},{1... | collective-permute-start | bytes 835592 | tf_op jit(solution)/shard_map/ppermute | solution.py:283
  56.3 9.8 %collective-permute-done.5.refs_5_ = bf16[272,512]{1,0:T(8,128)(2,1)S(1)} collective-permute-done((bf16[272,512]{1,0:T(8,128)(2,1)S(1)}, bf16[272,512]{1,0:T(8,128)(2,1)S(1)}, u32[]{:S(2)}, u32[]{:S(2)}) %collective-permute-start.5) | collective-permute-done | bytes 278560 | tf_op jit(solution)/shard_map/ppermute | solution.py:283
  66.1 5.4 %collective-permute-start.9 = (bf16[128,512]{1,0:T(8,128)(2,1)S(1)}, bf16[128,512]{1,0:T(8,128)(2,1)S(1)}, u32[]{:S(2)}, u32[]{:S(2)}) collective-permute-start(bf16[128,512]{1,0:T(8,128)(2,1)S(1)} %slice.195), channel_id=1, source_target_pairs={{1,13},{2,14},{3,15},{4,0},{6,2},{7,3},{8,4},{11,7},{13,9},{14,10}... | collective-permute-start | bytes 393224 | tf_op jit(solution)/shard_map/ppermute | solution.py:283
  71.6 1.3 collective-permute-start.8
  72.9 10.4 %collective-permute-done.8.refs_8_ = bf16[144,512]{1,0:T(8,128)(2,1)S(1)} collective-permute-done((bf16[144,512]{1,0:T(8,128)(2,1)S(1)}, bf16[144,512]{1,0:T(8,128)(2,1)S(1)}, u32[]{:S(2)}, u32[]{:S(2)}) %collective-permute-start.8) | collective-permute-done | bytes 147488 | tf_op jit(solution)/shard_map/ppermute | solution.py:283
  85.2 8.3 %shard_map.75 = (bf16[2,256,512]{2,1,0:T(8,128)(2,1)}, bf16[2,256,512]{2,1,0:T(8,128)(2,1)}, bf16[2,256,512]{2,1,0:T(8,128)(2,1)}, bf16[2,256,512]{2,1,0:T(8,128)(2,1)}) custom-call(s32[2]{0:T(128)} %pad_add_fusion.place, s32[1536]{0:T(1024)} %convert_element_type.249.ints, f32[1536]{0:T(1024)} %copy-done.22, ...), custom_call_target="tpu_custom_call" | custom-call | tf_op jit(solution)/shard_map/pallas_call | solution.py:334
  93.6 3.8 %collective-permute-start.14 = (bf16[2,256,512]{2,1,0:T(8,128)(2,1)}, bf16[2,256,512]{2,1,0:T(8,128)(2,1)S(1)}, u32[]{:S(2)}, u32[]{:S(2)}) collective-permute-start(bf16[2,256,512]{2,1,0:T(8,128)(2,1)} %get-tuple-element.45), channel_id=1, source_target_pairs={{0,1},{1,2},{2,3},{3,0},{4,5},{5,6},{6,7},{7,4},{8,9},{9,10},{10,1... | collective-permute-start | bytes 1572872 | tf_op jit(solution)/shard_map/ppermute | solution.py:283
  98.7 8.1 %shard_map.76 = (bf16[2,256,512]{2,1,0:T(8,128)(2,1)}, bf16[2,256,512]{2,1,0:T(8,128)(2,1)}, bf16[2,256,512]{2,1,0:T(8,128)(2,1)}, bf16[2,256,512]{2,1,0:T(8,128...) custom-call(s32[2]{0:T(128)} %pad_add_fusion.place, ...), custom_call_target="tpu_custom_call" | custom-call | tf_op jit(solution)/shard_map/pallas_call | solution.py:334
  107.8 6.2 %collective-permute-start.25 = (bf16[2,256,512]{2,1,0:T(8,128)(2,1)}, bf16[2,256,512]{2,1,0:T(8,128)(2,1)S(1)}, u32[]{:S(2)}, u32[]{:S(2)}) collective-permute-start(bf16[2,256,512]{2,1,0:T(8,128)(2,1)} %get-tuple-element.55), channel_id=1, source_target_pairs={{0,1},{1,2},{2,3},{3,0},{4,5},{5,6},{6,7},{7,4},{8,9},{9,10},{10,1... | collective-permute-start | bytes 1572872 | tf_op jit(solution)/shard_map/ppermute | solution.py:283
  114.0 7.9 %shard_map.77 = (bf16[2,256,512]{2,1,0:T(8,128)(2,1)}, bf16[2,256,512]{2,1,0:T(8,128)(2,1)}, bf16[2,256,512]{2,1,0:T(8,128)(2,1)}, bf16[2,256,512]{2,1,0:T(8,128)(2,1)}) custom-call(s32[2]{0:T(128)} %pad_add_fusion.place, s32[1536]{0:T(1024)} %convert_element_type.249.ints, f32[1536]{0:T(1024)} %copy-done.22, ...), custom_call_target="tpu_custom_call" | custom-call | tf_op jit(solution)/shard_map/pallas_call | solution.py:334
  122.1 2.8 %collective-permute-start.26 = (bf16[2,256,512]{2,1,0:T(8,128)(2,1)S(1)}, bf16[2,256,512]{2,1,0:T(8,128)(2,1)S(1)}, u32[]{:S(2)}, u32[]{:S(2)}) collective-permute-start(bf16[2,256,512]{2,1,0:T(8,128)(2,1)S(1)} %add_convert_fusion), channel_id=1, source_target_pairs={{0,3},{1,0},{2,1},{3,2},{4,7},{5,4},{6,5},{7,6},{8,11},{9,8},{10,9... | collective-permute-start | bytes 1572872 | tf_op jit(solution)/shard_map/ppermute | solution.py:283
  125.6 3.7 %collective-permute-start.18 = (bf16[2,256,512]{2,1,0:T(8,128)(2,1)S(1)}, bf16[2,256,512]{2,1,0:T(8,128)(2,1)S(1)}, u32[]{:S(2)}, u32[]{:S(2)}) collective-permute-start(bf16[2,256,512]{2,1,0:T(8,128)(2,1)S(1)} %copy-done.24), channel_id=1, source_target_pairs={{2,1},{3,2},{4,7},{7,6},{8,11},{11,10},{12,15},{18,17},{19,18},{20... | collective-permute-start | bytes 1572872 | tf_op jit(solution)/shard_map/ppermute | solution.py:283
  129.4 1.4 collective-permute-start.19
  130.9 9.1 %collective-permute-done.23 = bf16[2,256,512]{2,1,0:T(8,128)(2,1)S(1)} collective-permute-done((bf16[2,256,512]{2,1,0:T(8,128)(2,1)S(1)}, bf16[2,256,512]{2,1,0:T(8,128)(2,1)S(1)}, u32[]{:S(2)}, u32[]{:S(2)}) %collective-permute-start.23) | collective-permute-done | bytes 524320 | tf_op jit(solution)/shard_map/ppermute | solution.py:283
  144.7 1.9 %collective-permute-start.27 = (bf16[2,256,512]{2,1,0:T(8,128)(2,1)S(1)}, bf16[2,256,512]{2,1,0:T(8,128)(2,1)S(1)}, u32[]{:S(2)}, u32[]{:S(2)}) collective-permute-start(bf16[2,256,512]{2,1,0:T(8,128)(2,1)S(1)} %pad_maximum_fusion.2), channel_id=1, source_target_pairs={{0,16},{1,17},{2,18},{3,19},{4,20},{5,21},{6,22},{7,23},{8,24},{9,... | collective-permute-start | bytes 1572872 | tf_op jit(solution)/shard_map/ppermute | solution.py:382
  146.6 2.6 %collective-permute-done.18 = bf16[2,256,512]{2,1,0:T(8,128)(2,1)S(1)} collective-permute-done((bf16[2,256,512]{2,1,0:T(8,128)(2,1)S(1)}, bf16[2,256,512]{2,1,0:T(8,128)(2,1)S(1)}, u32[]{:S(2)}, u32[]{:S(2)}) %collective-permute-start.18) | collective-permute-done | bytes 524320 | tf_op jit(solution)/shard_map/ppermute | solution.py:283
  149.2 10.3 %collective-permute-done.17 = bf16[2,256,512]{2,1,0:T(8,128)(2,1)S(1)} collective-permute-done((bf16[2,256,512]{2,1,0:T(8,128)(2,1)S(1)}, bf16[2,256,512]{2,1,0:T(8,128)(2,1)S(1)}, u32[]{:S(2)}, u32[]{:S(2)}) %collective-permute-start.17) | collective-permute-done | bytes 524320 | tf_op jit(solution)/shard_map/ppermute | solution.py:283
  161.5 1.9 %collective-permute-start.22 = (bf16[2,256,512]{2,1,0:T(8,128)(2,1)S(1)}, bf16[2,256,512]{2,1,0:T(8,128)(2,1)S(1)}, u32[]{:S(2)}, u32[]{:S(2)}) collective-permute-start(bf16[2,256,512]{2,1,0:T(8,128)(2,1)S(1)} %pad_maximum_fusion.1), channel_id=1, source_target_pairs={{1,17},{2,18},{6,22},{7,23},{10,26},{11,27},{15,31},{17,33},{18,34... | collective-permute-start | bytes 1572872 | tf_op jit(solution)/shard_map/ppermute | solution.py:382
  164.3 2.6 %shard_map.78._ = bf16[4,256,512]{2,1,0:T(8,128)(2,1)} custom-call(s32[2]{0:T(128)} %pad_add_fusion.place, s32[2,16]{1,0:T(2,128)} %bitcast.97, s32[2,16]{1,0:T(2,128)} %bitcast.100, f32[256,512]{1,0:T(8,128)} %get-tuple-element.68.here0, f32[256,512]{1,0:T(8,128)} %get-tuple-element.70.here1, bf16[2,256,512]{2,1,0:T(8,128)(2,1)} %copy-done.16), custom_call_target="tpu_custom_call" | custom-call | tf_op jit(solution)/shard_map/pallas_call | solution.py:385
  166.9 6.1 %collective-permute-done.22.above = bf16[2,256,512]{2,1,0:T(8,128)(2,1)S(1)} collective-permute-done((bf16[2,256,512]{2,1,0:T(8,128)(2,1)S(1)}, bf16[2,256,512]{2,1,0:T(8,128)(2,1)S(1)}, u32[]{:S(2)}, u32[]{:S(2)}) %collective-permute-start.22) | collective-permute-done | bytes 524320 | tf_op jit(solution)/shard_map/ppermute | solution.py:382
  173.7 2.3 %shard_map.79 = bf16[4,256,512]{2,1,0:T(8,128)(2,1)} custom-call(s32[2]{0:T(128)} %pad_add_fusion.place, s32[2,16]{1,0:T(2,128)} %bitcast.98, s32[2,16]{1,0:T(2,128)} %bitcast.101, f32[256,512]{1,0:T(8,128)} %get-tuple-element.72.here2, f32[256,512]{1,0:T(8,128)} %get-tuple-element.74.here3, ...), custom_call_target="tpu_custom_call", output_to_operand_aliasing={{}: (6, {})} | custom-call | tf_op jit(solution)/shard_map/pallas_call | solution.py:392
  (126 shorter events, 18.3 us)
Async XLA Ops:
  3.2 49.7 %collective-permute-start.4 = (bf16[2,272,512]{2,1,0:T(8,128)(2,1)}, bf16[2,272,512]{2,1,0:T(8,128)(2,1)S(1)}, u32[]{:S(2)}, u32[]{:S(2)}) collective-permute-start(bf16[2,272,512]{2,1,0:T(8,128)(2,1)} %get-tuple-element.58.refs_0_), channel_id=1, source_target_pairs={{0,12},{1,13},{2,14},{3,15},{4,0},{5,1},{6,2},{7,3},{8,4},{9,5},{1... | collective-permute-start | bytes 1671176 | tf_op jit(solution)/shard_map/ppermute | solution.py:283
  9.5 43.6 %collective-permute-start.2 = (bf16[2,272,512]{2,1,0:T(8,128)(2,1)}, bf16[2,272,512]{2,1,0:T(8,128)(2,1)S(1)}, u32[]{:S(2)}, u32[]{:S(2)}) collective-permute-start(bf16[2,272,512]{2,1,0:T(8,128)(2,1)} %get-tuple-element.58.refs_0_), channel_id=1, source_target_pairs={{0,4},{1,5},{2,6},{3,7},{4,8},{5,9},{6,10},{7,11},{8,12},{9,13},{1... | collective-permute-start | bytes 1671176 | tf_op jit(solution)/shard_map/ppermute | solution.py:283
  12.0 23.2 %collective-permute-start = (bf16[3,64,256]{2,1,0:T(8,128)(2,1)}, bf16[3,64,256]{2,1,0:T(8,128)(2,1)S(1)}, u32[]{:S(2)}, u32[]{:S(2)}) collective-permute-start(bf16[3,64,256]{2,1,0:T(8,128)(2,1)} %get-tuple-element.40), channel_id=1, source_target_pairs={{0,16},{16,32},{32,48},{48,64},{64,80},{80,96},{96,112},{112,128},... | collective-permute-start | bytes 294920 | tf_op jit(solution)/shard_map/ppermute | solution.py:310
  13.9 25.1 %collective-permute-start.11 = (bf16[3,64,256]{2,1,0:T(8,128)(2,1)}, bf16[3,64,256]{2,1,0:T(8,128)(2,1)S(1)}, u32[]{:S(2)}, u32[]{:S(2)}) collective-permute-start(bf16[3,64,256]{2,1,0:T(8,128)(2,1)} %get-tuple-element.44), channel_id=1, source_target_pairs={{32,0},{48,16},{64,32},{80,48},{96,64},{112,80},{128,96},{144,112}... | collective-permute-start | bytes 294920 | tf_op jit(solution)/shard_map/ppermute | solution.py:322
  16.7 22.2 %collective-permute-start.10 = (bf16[6,64,256]{2,1,0:T(8,128)(2,1)}, bf16[6,64,256]{2,1,0:T(8,128)(2,1)S(1)}, u32[]{:S(2)}, u32[]{:S(2)}) collective-permute-start(bf16[6,64,256]{2,1,0:T(8,128)(2,1)} %get-tuple-element.43), channel_id=1, source_target_pairs={{16,0},{32,16},{48,32},{64,48},{80,64},{96,80},{112,96},{128,112},... | collective-permute-start | bytes 589832 | tf_op jit(solution)/shard_map/ppermute | solution.py:321
  35.1 9.9 %collective-permute-start.1 = (bf16[272,512]{1,0:T(8,128)(2,1)}, bf16[272,512]{1,0:T(8,128)(2,1)S(1)}, u32[]{:S(2)}, u32[]{:S(2)}) collective-permute-start(bf16[272,512]{1,0:T(8,128)(2,1)} %get-tuple-element.41), channel_id=1, source_target_pairs={{2,3},{6,5},{11,8},{15,12},{18,19},{22,21},{27,24},{31,28},{34,35}... | collective-permute-start | bytes 835592 | tf_op jit(solution)/shard_map/ppermute | solution.py:311
  39.0 45.3 %copy-start.5 = (bf16[12,64,256]{2,1,0:T(8,128)(2,1)}, bf16[12,64,256]{2,1,0:T(8,128)(2,1)S(1)}, u32[]{:S(2)}) copy-start(bf16[12,64,256]{2,1,0:T(8,128)(2,1)S(1)} %constant_dynamic-update-slice_fusion.1.refs_12_) | copy-start | bytes 1179652
  39.0 17.1 %collective-permute-start.12 = (bf16[12,64,256]{2,1,0:T(8,128)(2,1)S(1)}, bf16[12,64,256]{2,1,0:T(8,128)(2,1)S(1)}, u32[]{:S(2)}, u32[]{:S(2)}) collective-permute-start(bf16[12,64,256]{2,1,0:T(8,128)(2,1)S(1)} %constant_dynamic-update-slice_fusion.1.refs_12_), channel_id=1, source_target_pairs={{0,1},{1,0},{2,3},{3,2},{4,5},{5,4},{6,7},{7,6},{8,9},{9,8},{10,11... | collective-permute-start | bytes 1179656 | tf_op jit(solution)/shard_map/ppermute | solution.py:324
  46.1 38.2 %copy-start.4 = (bf16[272,512]{1,0:T(8,128)(2,1)}, bf16[272,512]{1,0:T(8,128)(2,1)S(1)}, u32[]{:S(2)}) copy-start(bf16[272,512]{1,0:T(8,128)(2,1)S(1)} %add.83.refs_1_) | copy-start | bytes 835588
  46.1 20.0 %collective-permute-start.5 = (bf16[272,512]{1,0:T(8,128)(2,1)S(1)}, bf16[272,512]{1,0:T(8,128)(2,1)S(1)}, u32[]{:S(2)}, u32[]{:S(2)}) collective-permute-start(bf16[272,512]{1,0:T(8,128)(2,1)S(1)} %add.83.refs_1_), channel_id=1, source_target_pairs={{1,13},{2,14},{3,15},{5,1},{6,2},{7,3},{8,4},{10,6},{11,7},{12,8},... | collective-permute-start | bytes 835592 | tf_op jit(solution)/shard_map/ppermute | solution.py:283
  48.0 23.6 %collective-permute-start.3 = (bf16[272,512]{1,0:T(8,128)(2,1)S(1)}, bf16[272,512]{1,0:T(8,128)(2,1)S(1)}, u32[]{:S(2)}, u32[]{:S(2)}) collective-permute-start(bf16[272,512]{1,0:T(8,128)(2,1)S(1)} %add.83.refs_1_), channel_id=1, source_target_pairs={{1,5},{2,6},{3,7},{5,9},{6,10},{7,11},{8,12},{10,14},{11,15},{12,0... | collective-permute-start | bytes 835592 | tf_op jit(solution)/shard_map/ppermute | solution.py:283
  52.9 31.4 %copy-start = (bf16[2,272,512]{2,1,0:T(8,128)(2,1)}, bf16[2,272,512]{2,1,0:T(8,128)(2,1)S(1)}, u32[]{:S(2)}) copy-start(bf16[2,272,512]{2,1,0:T(8,128)(2,1)S(1)} %collective-permute-done.4.refs_4_) | copy-start | bytes 1671172
  52.9 30.5 %collective-permute-start.7 = (bf16[272,512]{1,0:T(8,128)(2,1)S(1)}, bf16[272,512]{1,0:T(8,128)(2,1)S(1)}, u32[]{:S(2)}, u32[]{:S(2)}) collective-permute-start(bf16[272,512]{1,0:T(8,128)(2,1)S(1)} %get-tuple-element.75), channel_id=1, source_target_pairs={{0,12},{1,13},{2,14},{3,15},{4,0},{5,1},{6,2},{7,3},{8,4},{9,5},{1... | collective-permute-start | bytes 835592 | tf_op jit(solution)/shard_map/ppermute | solution.py:283
  53.1 30.3 %collective-permute-start.6 = (bf16[272,512]{1,0:T(8,128)(2,1)S(1)}, bf16[272,512]{1,0:T(8,128)(2,1)S(1)}, u32[]{:S(2)}, u32[]{:S(2)}) collective-permute-start(bf16[272,512]{1,0:T(8,128)(2,1)S(1)} %get-tuple-element.78), channel_id=1, source_target_pairs={{0,4},{1,5},{2,6},{3,7},{4,8},{5,9},{6,10},{7,11},{8,12},{9,13},{1... | collective-permute-start | bytes 835592 | tf_op jit(solution)/shard_map/ppermute | solution.py:283
  56.2 28.1 %collective-permute-start.13 = (bf16[24,64,256]{2,1,0:T(8,128)(2,1)S(1)}, bf16[24,64,256]{2,1,0:T(8,128)(2,1)S(1)}, u32[]{:S(2)}, u32[]{:S(2)}) collective-permute-start(bf16[24,64,256]{2,1,0:T(8,128)(2,1)S(1)} %pad_maximum_fusion), channel_id=1, source_target_pairs={{0,3},{1,2},{2,1},{3,0},{4,7},{5,6},{6,5},{7,4},{8,11},{9,10},{10,... | collective-permute-start | bytes 2359304 | tf_op jit(solution)/shard_map/ppermute | solution.py:325
  66.1 18.2 %collective-permute-start.9 = (bf16[128,512]{1,0:T(8,128)(2,1)S(1)}, bf16[128,512]{1,0:T(8,128)(2,1)S(1)}, u32[]{:S(2)}, u32[]{:S(2)}) collective-permute-start(bf16[128,512]{1,0:T(8,128)(2,1)S(1)} %slice.195), channel_id=1, source_target_pairs={{1,13},{2,14},{3,15},{4,0},{6,2},{7,3},{8,4},{11,7},{13,9},{14,10}... | collective-permute-start | bytes 393224 | tf_op jit(solution)/shard_map/ppermute | solution.py:283
  71.6 11.8 %collective-permute-start.8 = (bf16[144,512]{1,0:T(8,128)(2,1)S(1)}, bf16[144,512]{1,0:T(8,128)(2,1)S(1)}, u32[]{:S(2)}, u32[]{:S(2)}) collective-permute-start(bf16[144,512]{1,0:T(8,128)(2,1)S(1)} %slice.193), channel_id=1, source_target_pairs={{0,4},{3,7},{5,9},{6,10},{7,11},{9,13},{10,14},{11,15},{12,0},{14,... | collective-permute-start | bytes 442376 | tf_op jit(solution)/shard_map/ppermute | solution.py:283
  93.6 14.2 %collective-permute-start.14 = (bf16[2,256,512]{2,1,0:T(8,128)(2,1)}, bf16[2,256,512]{2,1,0:T(8,128)(2,1)S(1)}, u32[]{:S(2)}, u32[]{:S(2)}) collective-permute-start(bf16[2,256,512]{2,1,0:T(8,128)(2,1)} %get-tuple-element.45), channel_id=1, source_target_pairs={{0,1},{1,2},{2,3},{3,0},{4,5},{5,6},{6,7},{7,4},{8,9},{9,10},{10,1... | collective-permute-start | bytes 1572872 | tf_op jit(solution)/shard_map/ppermute | solution.py:283
  97.3 16.7 %collective-permute-start.15 = (bf16[2,256,512]{2,1,0:T(8,128)(2,1)}, bf16[2,256,512]{2,1,0:T(8,128)(2,1)S(1)}, u32[]{:S(2)}, u32[]{:S(2)}) collective-permute-start(bf16[2,256,512]{2,1,0:T(8,128)(2,1)} %get-tuple-element.46), channel_id=1, source_target_pairs={{0,3},{1,0},{2,1},{3,2},{4,7},{5,4},{6,5},{7,6},{8,11},{9,8},{10,9... | collective-permute-start | bytes 1572872 | tf_op jit(solution)/shard_map/ppermute | solution.py:283
  97.3 28.2 %collective-permute-start.16 = (bf16[2,256,512]{2,1,0:T(8,128)(2,1)}, bf16[2,256,512]{2,1,0:T(8,128)(2,1)S(1)}, u32[]{:S(2)}, u32[]{:S(2)}) collective-permute-start(bf16[2,256,512]{2,1,0:T(8,128)(2,1)} %get-tuple-element.47), channel_id=1, source_target_pairs={{0,1},{3,0},{4,5},{5,6},{8,9},{9,10},{13,14},{16,17},{19,16},{20,2... | collective-permute-start | bytes 1572872 | tf_op jit(solution)/shard_map/ppermute | solution.py:283
  98.0 27.0 %collective-permute-start.20 = (bf16[2,256,512]{2,1,0:T(8,128)(2,1)}, bf16[2,256,512]{2,1,0:T(8,128)(2,1)S(1)}, u32[]{:S(2)}, u32[]{:S(2)}) collective-permute-start(bf16[2,256,512]{2,1,0:T(8,128)(2,1)} %get-tuple-element.48), channel_id=1, source_target_pairs={{0,3},{4,7},{9,8},{13,12},{16,19},{20,23},{25,24},{29,28},{32,35},... | collective-permute-start | bytes 1572872 | tf_op jit(solution)/shard_map/ppermute | solution.py:283
  106.9 22.5 %collective-permute-start.24 = (bf16[2,256,512]{2,1,0:T(8,128)(2,1)}, bf16[2,256,512]{2,1,0:T(8,128)(2,1)S(1)}, u32[]{:S(2)}, u32[]{:S(2)}) collective-permute-start(bf16[2,256,512]{2,1,0:T(8,128)(2,1)} %get-tuple-element.50), channel_id=1, source_target_pairs={{0,3},{1,0},{2,1},{3,2},{4,7},{5,4},{6,5},{7,6},{8,11},{9,8},{10,9... | collective-permute-start | bytes 1572872 | tf_op jit(solution)/shard_map/ppermute | solution.py:283
  107.8 34.5 %collective-permute-start.25 = (bf16[2,256,512]{2,1,0:T(8,128)(2,1)}, bf16[2,256,512]{2,1,0:T(8,128)(2,1)S(1)}, u32[]{:S(2)}, u32[]{:S(2)}) collective-permute-start(bf16[2,256,512]{2,1,0:T(8,128)(2,1)} %get-tuple-element.55), channel_id=1, source_target_pairs={{0,1},{1,2},{2,3},{3,0},{4,5},{5,6},{6,7},{7,4},{8,9},{9,10},{10,1... | collective-permute-start | bytes 1572872 | tf_op jit(solution)/shard_map/ppermute | solution.py:283
  122.1 21.5 %collective-permute-start.26 = (bf16[2,256,512]{2,1,0:T(8,128)(2,1)S(1)}, bf16[2,256,512]{2,1,0:T(8,128)(2,1)S(1)}, u32[]{:S(2)}, u32[]{:S(2)}) collective-permute-start(bf16[2,256,512]{2,1,0:T(8,128)(2,1)S(1)} %add_convert_fusion), channel_id=1, source_target_pairs={{0,3},{1,0},{2,1},{3,2},{4,7},{5,4},{6,5},{7,6},{8,11},{9,8},{10,9... | collective-permute-start | bytes 1572872 | tf_op jit(solution)/shard_map/ppermute | solution.py:283
  125.1 34.4 %copy-start.19 = (bf16[2,256,512]{2,1,0:T(8,128)(2,1)S(1)}, bf16[2,256,512]{2,1,0:T(8,128)(2,1)}, u32[]{:S(2)}) copy-start(bf16[2,256,512]{2,1,0:T(8,128)(2,1)} %get-tuple-element.59) | copy-start | bytes 1572868
  125.1 14.9 %collective-permute-start.23 = (bf16[2,256,512]{2,1,0:T(8,128)(2,1)S(1)}, bf16[2,256,512]{2,1,0:T(8,128)(2,1)S(1)}, u32[]{:S(2)}, u32[]{:S(2)}) collective-permute-start(bf16[2,256,512]{2,1,0:T(8,128)(2,1)S(1)} %add_convert_fusion.1), channel_id=1, source_target_pairs={{0,1},{1,2},{2,3},{3,0},{4,5},{5,6},{6,7},{7,4},{8,9},{9,10},{10,1... | collective-permute-start | bytes 1572872 | tf_op jit(solution)/shard_map/ppermute | solution.py:283
  125.6 23.7 %collective-permute-start.18 = (bf16[2,256,512]{2,1,0:T(8,128)(2,1)S(1)}, bf16[2,256,512]{2,1,0:T(8,128)(2,1)S(1)}, u32[]{:S(2)}, u32[]{:S(2)}) collective-permute-start(bf16[2,256,512]{2,1,0:T(8,128)(2,1)S(1)} %copy-done.24), channel_id=1, source_target_pairs={{2,1},{3,2},{4,7},{7,6},{8,11},{11,10},{12,15},{18,17},{19,18},{20... | collective-permute-start | bytes 1572872 | tf_op jit(solution)/shard_map/ppermute | solution.py:283
  129.4 31.0 %collective-permute-start.19 = (bf16[2,256,512]{2,1,0:T(8,128)(2,1)S(1)}, bf16[2,256,512]{2,1,0:T(8,128)(2,1)S(1)}, u32[]{:S(2)}, u32[]{:S(2)}) collective-permute-start(bf16[2,256,512]{2,1,0:T(8,128)(2,1)S(1)} %copy-done.23), channel_id=1, source_target_pairs={{1,2},{5,6},{10,11},{14,15},{17,18},{21,22},{26,27},{30,31},{33,34... | collective-permute-start | bytes 1572872 | tf_op jit(solution)/shard_map/ppermute | solution.py:283
  140.0 19.4 %collective-permute-start.17 = (bf16[2,256,512]{2,1,0:T(8,128)(2,1)S(1)}, bf16[2,256,512]{2,1,0:T(8,128)(2,1)S(1)}, u32[]{:S(2)}, u32[]{:S(2)}) collective-permute-start(bf16[2,256,512]{2,1,0:T(8,128)(2,1)S(1)} %add_convert_fusion.3), channel_id=1, source_target_pairs={{0,1},{1,2},{5,6},{6,7},{9,10},{10,11},{14,15},{16,17},{17,18},{21... | collective-permute-start | bytes 1572872 | tf_op jit(solution)/shard_map/ppermute | solution.py:283
  142.3 18.2 %collective-permute-start.21 = (bf16[2,256,512]{2,1,0:T(8,128)(2,1)S(1)}, bf16[2,256,512]{2,1,0:T(8,128)(2,1)S(1)}, u32[]{:S(2)}, u32[]{:S(2)}) collective-permute-start(bf16[2,256,512]{2,1,0:T(8,128)(2,1)S(1)} %add_convert_fusion.2), channel_id=1, source_target_pairs={{3,2},{7,6},{8,11},{12,15},{19,18},{23,22},{24,27},{28,31},{35,34}... | collective-permute-start | bytes 1572872 | tf_op jit(solution)/shard_map/ppermute | solution.py:283
  144.7 18.8 %collective-permute-start.27 = (bf16[2,256,512]{2,1,0:T(8,128)(2,1)S(1)}, bf16[2,256,512]{2,1,0:T(8,128)(2,1)S(1)}, u32[]{:S(2)}, u32[]{:S(2)}) collective-permute-start(bf16[2,256,512]{2,1,0:T(8,128)(2,1)S(1)} %pad_maximum_fusion.2), channel_id=1, source_target_pairs={{0,16},{1,17},{2,18},{3,19},{4,20},{5,21},{6,22},{7,23},{8,24},{9,... | collective-permute-start | bytes 1572872 | tf_op jit(solution)/shard_map/ppermute | solution.py:382
  161.5 11.4 %collective-permute-start.22 = (bf16[2,256,512]{2,1,0:T(8,128)(2,1)S(1)}, bf16[2,256,512]{2,1,0:T(8,128)(2,1)S(1)}, u32[]{:S(2)}, u32[]{:S(2)}) collective-permute-start(bf16[2,256,512]{2,1,0:T(8,128)(2,1)S(1)} %pad_maximum_fusion.1), channel_id=1, source_target_pairs={{1,17},{2,18},{6,22},{7,23},{10,26},{11,27},{15,31},{17,33},{18,34... | collective-permute-start | bytes 1572872 | tf_op jit(solution)/shard_map/ppermute | solution.py:382
  (21 other events, 218.3 us)

commit v13 on v12

--- a/solution.py
+++ b/solution.py
@@ -308,7 +308,7 @@
     up = lambda n: [(i, i + n) for i in range(SECS - n)]
     down = lambda n: [(i + n, i) for i in range(SECS - n)]
     rim_low = lax.ppermute(strip_low, "sec", up(1))
-    borrowed = lax.ppermute(after(moving, rim_low), "row", lent)
+    borrowed = lax.ppermute(after(moving, strip), "row", lent)
     own2 = own2 + borrowed
     behind2 = sent(own2, z_up, same, three)
     ahead2 = sent(own2, z_down, same, three)
@@ -318,8 +318,8 @@
     across2b = sent(ahead2[HEAD + BB // 2 :], z_down, z_up, three)
     rim = jnp.concatenate([
         rim_low,
-        lax.ppermute(strip, "sec", down(1)),
-        lax.ppermute(strip_high, "sec", down(2)),
+        lax.ppermute(after(strip, borrowed), "sec", down(1)),
+        lax.ppermute(after(strip_high, borrowed), "sec", down(2)),
     ])
     swapped = lax.ppermute(rim, "row", [(n, n ^ 1) for n in range(ROWS)])
     crossed = lax.ppermute(jnp.concatenate([rim, swapped]), "row", [(n, n ^ 3) for n in range(ROWS)])

time: 176 us -> 188 us (1.068)
  the two profiles are of different devices: /device:TPU:12 before, /device:TPU:52 now
where the time goes in v13:
time: 188 us; the launch traced here: 187 us
  starting transfers between devices  76 us (40%)
  waiting for transfers between devices  61.8 us (33%)
  Pallas kernels  37.5 us (20%)
  other arithmetic  7.15 us (4%)
  local copies, waits for them, and re-layouts  3.77 us (2%)
    ppermute x20, starting transfers between devices, sent(): lax.ppermute(value, 'row', [(n, move(n)) for n in range(ROWS) if owner(n)...  56.3 us
    ppermute x20, waiting for transfers between devices, sent(): lax.ppermute(value, 'row', [(n, move(n)) for n in range(ROWS) if owner(n)...  30.4 us
    pallas_call x3, Pallas kernels, terms(): pl.pallas_call(functools.partial(terms_kernel, slots), in_specs=[smem] *...  27.5 us
    ppermute x1, waiting for transfers between devices, body(): rim_low = lax.ppermute(strip_low, 'sec', up(1))  9.15 us
    ppermute x1, waiting for transfers between devices, body(): lax.ppermute(after(strip_high, borrowed), 'sec', down(2))  8.82 us
    ppermute x1, waiting for transfers between devices, body(): lax.ppermute(jnp.concatenate([rim, swapped]), 'row', [(n, n ^ 3) for n in...  8.32 us
    ppermute x1, starting transfers between devices, body(): swapped = lax.ppermute(rim, 'row', [(n, n ^ 1) for n in range(ROWS)])  6.36 us
    ppermute x2, waiting for transfers between devices, body(): lax.ppermute(jnp.stack(raised[i:i + 2]), ('sec', 'row'), pairs)  5.17 us
  transfers between devices with their start and end apart: 28, of which 8 were waited for; matrix products, arithmetic and copies ran while one was open for 4% of the time, Pallas kernels for 13%

profile of v13, /device:TPU:52, one launch (start us, length us, event | category | flops | bytes accessed | tf_op | source)
XLA Modules:
  0.0 187.2 jit_solution(5354651190861653046)
XLA Ops:
  0.6 2.6 %shard_map.73 = (bf16[2,272,512]{2,1,0:T(8,128)(2,1)}, bf16[272,512]{1,0:T(8,128)(2,1)}, bf16[272,512]{1,0:T(8,128)(2,1)}) custom-call(s32[2]{0:T(128)} %pad_add_fusion.place, s32[2,16]{1,0:T(2,128)} %bitcast.96, s32[2,16]{1,0:T(2,128)} %bitcast.99, s32[3,2,8]{2,1,0:T(2,128)} %bitcast.102, f32[2,8]{1,0:T(2,128)} %coeffs.1, bf16[4,256,512]{2,1,0:T(8,128)(2,1)} %bitcast.94), custom_call_target="tpu_custom_call" | custom-call | tf_op jit(solution)/shard_map/pallas_call | solution.py:270
  3.2 5.4 %collective-permute-start.3 = (bf16[2,272,512]{2,1,0:T(8,128)(2,1)}, bf16[2,272,512]{2,1,0:T(8,128)(2,1)S(1)}, u32[]{:S(2)}, u32[]{:S(2)}) collective-permute-start(bf16[2,272,512]{2,1,0:T(8,128)(2,1)} %get-tuple-element.62.refs_0_), channel_id=1, source_target_pairs={{0,12},{1,13},{2,14},{3,15},{4,0},{5,1},{6,2},{7,3},{8,4},{9,5},{1... | collective-permute-start | bytes 1671176 | tf_op jit(solution)/shard_map/ppermute | solution.py:283
  8.6 2.5 %shard_map.74 = (bf16[6,256,256]{2,1,0:T(8,128)(2,1)}, bf16[6,64,256]{2,1,0:T(8,128)(2,1)}, bf16[3,64,256]{2,1,0:T(8,128)(2,1)}, bf16[3,64,256]{2,1,0:T(8,128)(2,1)}) custom-call(s32[2]{0:T(128)} %pad_add_fusion.place, bf16[4,2,256,256]{3,2,1,0:T(8,128)(2,1)} %bitcast.95), custom_call_target="tpu_custom_call" | custom-call | tf_op jit(solution)/shard_map/pallas_call | solution.py:296
  11.1 1.9 %collective-permute-start.9 = (bf16[3,64,256]{2,1,0:T(8,128)(2,1)}, bf16[3,64,256]{2,1,0:T(8,128)(2,1)S(1)}, u32[]{:S(2)}, u32[]{:S(2)}) collective-permute-start(bf16[3,64,256]{2,1,0:T(8,128)(2,1)} %get-tuple-element.45), channel_id=1, source_target_pairs={{0,16},{16,32},{32,48},{48,64},{64,80},{80,96},{96,112},{112,128},... | collective-permute-start | bytes 294920 | tf_op jit(solution)/shard_map/ppermute | solution.py:310
  13.0 3.1 %collective-permute-start = (bf16[272,512]{1,0:T(8,128)(2,1)}, bf16[272,512]{1,0:T(8,128)(2,1)S(1)}, u32[]{:S(2)}, u32[]{:S(2)}) collective-permute-start(bf16[272,512]{1,0:T(8,128)(2,1)} %get-tuple-element.43), channel_id=1, source_target_pairs={{2,3},{6,5},{11,8},{15,12},{18,19},{22,21},{27,24},{31,28},{34,35}... | collective-permute-start | bytes 835592 | tf_op jit(solution)/shard_map/ppermute | solution.py:311
  17.2 9.1 %collective-permute-done.9 = bf16[3,64,256]{2,1,0:T(8,128)(2,1)S(1)} collective-permute-done((bf16[3,64,256]{2,1,0:T(8,128)(2,1)}, bf16[3,64,256]{2,1,0:T(8,128)(2,1)S(1)}, u32[]{:S(2)}, u32[]{:S(2)}) %collective-permute-start.9) | collective-permute-done | bytes 98336 | tf_op jit(solution)/shard_map/ppermute | solution.py:310
  26.4 1.9 %collective-permute-start.10 = (bf16[6,64,256]{2,1,0:T(8,128)(2,1)}, bf16[6,64,256]{2,1,0:T(8,128)(2,1)S(1)}, u32[]{:S(2)}, u32[]{:S(2)}) collective-permute-start(bf16[6,64,256]{2,1,0:T(8,128)(2,1)} %get-tuple-element.46), channel_id=1, source_target_pairs={{16,0},{32,16},{48,32},{64,48},{80,64},{96,80},{112,96},{128,112},... | collective-permute-start | bytes 589832 | tf_op jit(solution)/shard_map/ppermute | solution.py:321
  29.4 13.7 %collective-permute-start.4 = (bf16[272,512]{1,0:T(8,128)(2,1)S(1)}, bf16[272,512]{1,0:T(8,128)(2,1)S(1)}, u32[]{:S(2)}, u32[]{:S(2)}) collective-permute-start(bf16[272,512]{1,0:T(8,128)(2,1)S(1)} %add.83.refs_1_), channel_id=1, source_target_pairs={{1,13},{2,14},{3,15},{5,1},{6,2},{7,3},{8,4},{10,6},{11,7},{12,8},... | collective-permute-start | bytes 835592 | tf_op jit(solution)/shard_map/ppermute | solution.py:283
  44.5 2.5 %collective-permute-start.11 = (bf16[3,64,256]{2,1,0:T(8,128)(2,1)}, bf16[3,64,256]{2,1,0:T(8,128)(2,1)S(1)}, u32[]{:S(2)}, u32[]{:S(2)}) collective-permute-start(bf16[3,64,256]{2,1,0:T(8,128)(2,1)} %get-tuple-element.48), channel_id=1, source_target_pairs={{32,0},{48,16},{64,32},{80,48},{96,64},{112,80},{128,96},{144,112}... | collective-permute-start | bytes 294920 | tf_op jit(solution)/shard_map/ppermute | solution.py:322
  47.0 8.8 %collective-permute-done.11 = bf16[3,64,256]{2,1,0:T(8,128)(2,1)S(1)} collective-permute-done((bf16[3,64,256]{2,1,0:T(8,128)(2,1)}, bf16[3,64,256]{2,1,0:T(8,128)(2,1)S(1)}, u32[]{:S(2)}, u32[]{:S(2)}) %collective-permute-start.11) | collective-permute-done | bytes 98336 | tf_op jit(solution)/shard_map/ppermute | solution.py:322
  55.8 6.4 %collective-permute-start.12 = (bf16[12,64,256]{2,1,0:T(8,128)(2,1)S(1)}, bf16[12,64,256]{2,1,0:T(8,128)(2,1)S(1)}, u32[]{:S(2)}, u32[]{:S(2)}) collective-permute-start(bf16[12,64,256]{2,1,0:T(8,128)(2,1)S(1)} %constant_dynamic-update-slice_fusion.1.refs_12_), channel_id=1, source_target_pairs={{0,1},{1,0},{2,3},{3,2},{4,5},{5,4},{6,7},{7,6},{8,9},{9,8},{10,11... | collective-permute-start | bytes 1179656 | tf_op jit(solution)/shard_map/ppermute | solution.py:324
  62.2 9.2 %collective-permute-start.6 = (bf16[272,512]{1,0:T(8,128)(2,1)S(1)}, bf16[272,512]{1,0:T(8,128)(2,1)S(1)}, u32[]{:S(2)}, u32[]{:S(2)}) collective-permute-start(bf16[272,512]{1,0:T(8,128)(2,1)S(1)} %get-tuple-element.79), channel_id=1, source_target_pairs={{0,12},{1,13},{2,14},{3,15},{4,0},{5,1},{6,2},{7,3},{8,4},{9,5},{1... | collective-permute-start | bytes 835592 | tf_op jit(solution)/shard_map/ppermute | solution.py:283
  71.6 6.0 %collective-permute-start.8 = (bf16[128,512]{1,0:T(8,128)(2,1)S(1)}, bf16[128,512]{1,0:T(8,128)(2,1)S(1)}, u32[]{:S(2)}, u32[]{:S(2)}) collective-permute-start(bf16[128,512]{1,0:T(8,128)(2,1)S(1)} %slice.195), channel_id=1, source_target_pairs={{1,13},{2,14},{3,15},{4,0},{6,2},{7,3},{8,4},{11,7},{13,9},{14,10}... | collective-permute-start | bytes 393224 | tf_op jit(solution)/shard_map/ppermute | solution.py:283
  79.3 9.0 %collective-permute-done.7.refs_8_ = bf16[144,512]{1,0:T(8,128)(2,1)S(1)} collective-permute-done((bf16[144,512]{1,0:T(8,128)(2,1)S(1)}, bf16[144,512]{1,0:T(8,128)(2,1)S(1)}, u32[]{:S(2)}, u32[]{:S(2)}) %collective-permute-start.7) | collective-permute-done | bytes 147488 | tf_op jit(solution)/shard_map/ppermute | solution.py:283
  89.2 8.3 %collective-permute-done.13.refs_14_ = bf16[24,64,256]{2,1,0:T(8,128)(2,1)S(1)} collective-permute-done((bf16[24,64,256]{2,1,0:T(8,128)(2,1)S(1)}, bf16[24,64,256]{2,1,0:T(8,128)(2,1)S(1)}, u32[]{:S(2)}, u32[]{:S(2)}) %collective-permute-start.13) | collective-permute-done | bytes 786464 | tf_op jit(solution)/shard_map/ppermute | solution.py:325
  98.4 7.5 %shard_map.75 = (bf16[2,256,512]{2,1,0:T(8,128)(2,1)}, bf16[2,256,512]{2,1,0:T(8,128)(2,1)}, bf16[2,256,512]{2,1,0:T(8,128)(2,1)}, bf16[2,256,512]{2,1,0:T(8,128)(2,1)}) custom-call(s32[2]{0:T(128)} %pad_add_fusion.place, s32[1536]{0:T(1024)} %convert_element_type.249.ints, f32[1536]{0:T(1024)} %copy-done.22, ...), custom_call_target="tpu_custom_call" | custom-call | tf_op jit(solution)/shard_map/pallas_call | solution.py:334
  105.9 2.5 %collective-permute-start.14 = (bf16[2,256,512]{2,1,0:T(8,128)(2,1)}, bf16[2,256,512]{2,1,0:T(8,128)(2,1)S(1)}, u32[]{:S(2)}, u32[]{:S(2)}) collective-permute-start(bf16[2,256,512]{2,1,0:T(8,128)(2,1)} %get-tuple-element.49), channel_id=1, source_target_pairs={{0,1},{1,2},{2,3},{3,0},{4,5},{5,6},{6,7},{7,4},{8,9},{9,10},{10,1... | collective-permute-start | bytes 1572872 | tf_op jit(solution)/shard_map/ppermute | solution.py:283
  109.9 10.6 %shard_map.76 = (bf16[2,256,512]{2,1,0:T(8,128)(2,1)}, bf16[2,256,512]{2,1,0:T(8,128)(2,1)}, bf16[2,256,512]{2,1,0:T(8,128)(2,1)}, bf16[2,256,512]{2,1,0:T(8,128...) custom-call(s32[2]{0:T(128)} %pad_add_fusion.place, ...), custom_call_target="tpu_custom_call" | custom-call | tf_op jit(solution)/shard_map/pallas_call | solution.py:334
  120.5 2.0 %collective-permute-start.24 = (bf16[2,256,512]{2,1,0:T(8,128)(2,1)}, bf16[2,256,512]{2,1,0:T(8,128)(2,1)S(1)}, u32[]{:S(2)}, u32[]{:S(2)}) collective-permute-start(bf16[2,256,512]{2,1,0:T(8,128)(2,1)} %get-tuple-element.54), channel_id=1, source_target_pairs={{0,3},{1,0},{2,1},{3,2},{4,7},{5,4},{6,5},{7,6},{8,11},{9,8},{10,9... | collective-permute-start | bytes 1572872 | tf_op jit(solution)/shard_map/ppermute | solution.py:283
  122.5 5.3 %collective-permute-start.25 = (bf16[2,256,512]{2,1,0:T(8,128)(2,1)}, bf16[2,256,512]{2,1,0:T(8,128)(2,1)S(1)}, u32[]{:S(2)}, u32[]{:S(2)}) collective-permute-start(bf16[2,256,512]{2,1,0:T(8,128)(2,1)} %get-tuple-element.59), channel_id=1, source_target_pairs={{0,1},{1,2},{2,3},{3,0},{4,5},{5,6},{6,7},{7,4},{8,9},{9,10},{10,1... | collective-permute-start | bytes 1572872 | tf_op jit(solution)/shard_map/ppermute | solution.py:283
  127.8 9.4 %shard_map.77 = (bf16[2,256,512]{2,1,0:T(8,128)(2,1)}, bf16[2,256,512]{2,1,0:T(8,128)(2,1)}, bf16[2,256,512]{2,1,0:T(8,128)(2,1)}, bf16[2,256,512]{2,1,0:T(8,128)(2,1)}) custom-call(s32[2]{0:T(128)} %pad_add_fusion.place, s32[1536]{0:T(1024)} %convert_element_type.249.ints, f32[1536]{0:T(1024)} %copy-done.22, ...), custom_call_target="tpu_custom_call" | custom-call | tf_op jit(solution)/shard_map/pallas_call | solution.py:334
  137.6 2.1 %collective-permute-start.23 = (bf16[2,256,512]{2,1,0:T(8,128)(2,1)S(1)}, bf16[2,256,512]{2,1,0:T(8,128)(2,1)S(1)}, u32[]{:S(2)}, u32[]{:S(2)}) collective-permute-start(bf16[2,256,512]{2,1,0:T(8,128)(2,1)S(1)} %add_convert_fusion.1), channel_id=1, source_target_pairs={{0,1},{1,2},{2,3},{3,0},{4,5},{5,6},{6,7},{7,4},{8,9},{9,10},{10,1... | collective-permute-start | bytes 1572872 | tf_op jit(solution)/shard_map/ppermute | solution.py:283
  139.9 1.9 %collective-permute-start.18 = (bf16[2,256,512]{2,1,0:T(8,128)(2,1)S(1)}, bf16[2,256,512]{2,1,0:T(8,128)(2,1)S(1)}, u32[]{:S(2)}, u32[]{:S(2)}) collective-permute-start(bf16[2,256,512]{2,1,0:T(8,128)(2,1)S(1)} %copy-done.24), channel_id=1, source_target_pairs={{2,1},{3,2},{4,7},{7,6},{8,11},{11,10},{12,15},{18,17},{19,18},{20... | collective-permute-start | bytes 1572872 | tf_op jit(solution)/shard_map/ppermute | solution.py:283
  142.0 1.4 collective-permute-start.19
  143.4 9.1 %collective-permute-done.23 = bf16[2,256,512]{2,1,0:T(8,128)(2,1)S(1)} collective-permute-done((bf16[2,256,512]{2,1,0:T(8,128)(2,1)S(1)}, bf16[2,256,512]{2,1,0:T(8,128)(2,1)S(1)}, u32[]{:S(2)}, u32[]{:S(2)}) %collective-permute-start.23) | collective-permute-done | bytes 524320 | tf_op jit(solution)/shard_map/ppermute | solution.py:283
  157.3 1.9 %collective-permute-start.27 = (bf16[2,256,512]{2,1,0:T(8,128)(2,1)S(1)}, bf16[2,256,512]{2,1,0:T(8,128)(2,1)S(1)}, u32[]{:S(2)}, u32[]{:S(2)}) collective-permute-start(bf16[2,256,512]{2,1,0:T(8,128)(2,1)S(1)} %pad_maximum_fusion.2), channel_id=1, source_target_pairs={{0,16},{1,17},{2,18},{3,19},{4,20},{5,21},{6,22},{7,23},{8,24},{9,... | collective-permute-start | bytes 1572872 | tf_op jit(solution)/shard_map/ppermute | solution.py:382
  159.2 4.4 %collective-permute-done.18 = bf16[2,256,512]{2,1,0:T(8,128)(2,1)S(1)} collective-permute-done((bf16[2,256,512]{2,1,0:T(8,128)(2,1)S(1)}, bf16[2,256,512]{2,1,0:T(8,128)(2,1)S(1)}, u32[]{:S(2)}, u32[]{:S(2)}) %collective-permute-start.18) | collective-permute-done | bytes 524320 | tf_op jit(solution)/shard_map/ppermute | solution.py:283
  163.6 7.8 %collective-permute-done.17 = bf16[2,256,512]{2,1,0:T(8,128)(2,1)S(1)} collective-permute-done((bf16[2,256,512]{2,1,0:T(8,128)(2,1)S(1)}, bf16[2,256,512]{2,1,0:T(8,128)(2,1)S(1)}, u32[]{:S(2)}, u32[]{:S(2)}) %collective-permute-start.17) | collective-permute-done | bytes 524320 | tf_op jit(solution)/shard_map/ppermute | solution.py:283
  173.4 1.9 %collective-permute-start.22 = (bf16[2,256,512]{2,1,0:T(8,128)(2,1)S(1)}, bf16[2,256,512]{2,1,0:T(8,128)(2,1)S(1)}, u32[]{:S(2)}, u32[]{:S(2)}) collective-permute-start(bf16[2,256,512]{2,1,0:T(8,128)(2,1)S(1)} %pad_maximum_fusion.1), channel_id=1, source_target_pairs={{1,17},{2,18},{6,22},{7,23},{10,26},{11,27},{15,31},{17,33},{18,34... | collective-permute-start | bytes 1572872 | tf_op jit(solution)/shard_map/ppermute | solution.py:382
  176.2 2.6 %shard_map.78._ = bf16[4,256,512]{2,1,0:T(8,128)(2,1)} custom-call(s32[2]{0:T(128)} %pad_add_fusion.place, s32[2,16]{1,0:T(2,128)} %bitcast.97, s32[2,16]{1,0:T(2,128)} %bitcast.100, f32[256,512]{1,0:T(8,128)} %get-tuple-element.72.here0, f32[256,512]{1,0:T(8,128)} %get-tuple-element.74.here1, bf16[2,256,512]{2,1,0:T(8,128)(2,1)} %copy-done.16), custom_call_target="tpu_custom_call" | custom-call | tf_op jit(solution)/shard_map/pallas_call | solution.py:385
  178.7 5.2 %collective-permute-done.22.above = bf16[2,256,512]{2,1,0:T(8,128)(2,1)S(1)} collective-permute-done((bf16[2,256,512]{2,1,0:T(8,128)(2,1)S(1)}, bf16[2,256,512]{2,1,0:T(8,128)(2,1)S(1)}, u32[]{:S(2)}, u32[]{:S(2)}) %collective-permute-start.22) | collective-permute-done | bytes 524320 | tf_op jit(solution)/shard_map/ppermute | solution.py:382
  184.7 2.3 %shard_map.79 = bf16[4,256,512]{2,1,0:T(8,128)(2,1)} custom-call(s32[2]{0:T(128)} %pad_add_fusion.place, s32[2,16]{1,0:T(2,128)} %bitcast.98, s32[2,16]{1,0:T(2,128)} %bitcast.101, f32[256,512]{1,0:T(8,128)} %get-tuple-element.76.here2, f32[256,512]{1,0:T(8,128)} %get-tuple-element.78.here3, ...), custom_call_target="tpu_custom_call", output_to_operand_aliasing={{}: (6, {})} | custom-call | tf_op jit(solution)/shard_map/pallas_call | solution.py:392
  (126 shorter events, 17.8 us)
Async XLA Ops:
  3.2 59.0 %collective-permute-start.3 = (bf16[2,272,512]{2,1,0:T(8,128)(2,1)}, bf16[2,272,512]{2,1,0:T(8,128)(2,1)S(1)}, u32[]{:S(2)}, u32[]{:S(2)}) collective-permute-start(bf16[2,272,512]{2,1,0:T(8,128)(2,1)} %get-tuple-element.62.refs_0_), channel_id=1, source_target_pairs={{0,12},{1,13},{2,14},{3,15},{4,0},{5,1},{6,2},{7,3},{8,4},{9,5},{1... | collective-permute-start | bytes 1671176 | tf_op jit(solution)/shard_map/ppermute | solution.py:283
  8.6 62.8 %collective-permute-start.1 = (bf16[2,272,512]{2,1,0:T(8,128)(2,1)}, bf16[2,272,512]{2,1,0:T(8,128)(2,1)S(1)}, u32[]{:S(2)}, u32[]{:S(2)}) collective-permute-start(bf16[2,272,512]{2,1,0:T(8,128)(2,1)} %get-tuple-element.62.refs_0_), channel_id=1, source_target_pairs={{0,4},{1,5},{2,6},{3,7},{4,8},{5,9},{6,10},{7,11},{8,12},{9,13},{1... | collective-permute-start | bytes 1671176 | tf_op jit(solution)/shard_map/ppermute | solution.py:283
  11.1 15.3 %collective-permute-start.9 = (bf16[3,64,256]{2,1,0:T(8,128)(2,1)}, bf16[3,64,256]{2,1,0:T(8,128)(2,1)S(1)}, u32[]{:S(2)}, u32[]{:S(2)}) collective-permute-start(bf16[3,64,256]{2,1,0:T(8,128)(2,1)} %get-tuple-element.45), channel_id=1, source_target_pairs={{0,16},{16,32},{32,48},{48,64},{64,80},{80,96},{96,112},{112,128},... | collective-permute-start | bytes 294920 | tf_op jit(solution)/shard_map/ppermute | solution.py:310
  13.0 13.4 %collective-permute-start = (bf16[272,512]{1,0:T(8,128)(2,1)}, bf16[272,512]{1,0:T(8,128)(2,1)S(1)}, u32[]{:S(2)}, u32[]{:S(2)}) collective-permute-start(bf16[272,512]{1,0:T(8,128)(2,1)} %get-tuple-element.43), channel_id=1, source_target_pairs={{2,3},{6,5},{11,8},{15,12},{18,19},{22,21},{27,24},{31,28},{34,35}... | collective-permute-start | bytes 835592 | tf_op jit(solution)/shard_map/ppermute | solution.py:311
  26.4 18.1 %collective-permute-start.10 = (bf16[6,64,256]{2,1,0:T(8,128)(2,1)}, bf16[6,64,256]{2,1,0:T(8,128)(2,1)S(1)}, u32[]{:S(2)}, u32[]{:S(2)}) collective-permute-start(bf16[6,64,256]{2,1,0:T(8,128)(2,1)} %get-tuple-element.46), channel_id=1, source_target_pairs={{16,0},{32,16},{48,32},{64,48},{80,64},{96,80},{112,96},{128,112},... | collective-permute-start | bytes 589832 | tf_op jit(solution)/shard_map/ppermute | solution.py:321
  29.4 68.2 %copy-start.4 = (bf16[272,512]{1,0:T(8,128)(2,1)}, bf16[272,512]{1,0:T(8,128)(2,1)S(1)}, u32[]{:S(2)}) copy-start(bf16[272,512]{1,0:T(8,128)(2,1)S(1)} %add.83.refs_1_) | copy-start | bytes 835588
  29.4 42.2 %collective-permute-start.4 = (bf16[272,512]{1,0:T(8,128)(2,1)S(1)}, bf16[272,512]{1,0:T(8,128)(2,1)S(1)}, u32[]{:S(2)}, u32[]{:S(2)}) collective-permute-start(bf16[272,512]{1,0:T(8,128)(2,1)S(1)} %add.83.refs_1_), channel_id=1, source_target_pairs={{1,13},{2,14},{3,15},{5,1},{6,2},{7,3},{8,4},{10,6},{11,7},{12,8},... | collective-permute-start | bytes 835592 | tf_op jit(solution)/shard_map/ppermute | solution.py:283
  43.1 34.5 %collective-permute-start.2 = (bf16[272,512]{1,0:T(8,128)(2,1)S(1)}, bf16[272,512]{1,0:T(8,128)(2,1)S(1)}, u32[]{:S(2)}, u32[]{:S(2)}) collective-permute-start(bf16[272,512]{1,0:T(8,128)(2,1)S(1)} %add.83.refs_1_), channel_id=1, source_target_pairs={{1,5},{2,6},{3,7},{5,9},{6,10},{7,11},{8,12},{10,14},{11,15},{12,0... | collective-permute-start | bytes 835592 | tf_op jit(solution)/shard_map/ppermute | solution.py:283
  44.5 11.3 %collective-permute-start.11 = (bf16[3,64,256]{2,1,0:T(8,128)(2,1)}, bf16[3,64,256]{2,1,0:T(8,128)(2,1)S(1)}, u32[]{:S(2)}, u32[]{:S(2)}) collective-permute-start(bf16[3,64,256]{2,1,0:T(8,128)(2,1)} %get-tuple-element.48), channel_id=1, source_target_pairs={{32,0},{48,16},{64,32},{80,48},{96,64},{112,80},{128,96},{144,112}... | collective-permute-start | bytes 294920 | tf_op jit(solution)/shard_map/ppermute | solution.py:322
  55.8 41.7 %copy-start.5 = (bf16[12,64,256]{2,1,0:T(8,128)(2,1)}, bf16[12,64,256]{2,1,0:T(8,128)(2,1)S(1)}, u32[]{:S(2)}) copy-start(bf16[12,64,256]{2,1,0:T(8,128)(2,1)S(1)} %constant_dynamic-update-slice_fusion.1.refs_12_) | copy-start | bytes 1179652
  55.8 23.2 %collective-permute-start.12 = (bf16[12,64,256]{2,1,0:T(8,128)(2,1)S(1)}, bf16[12,64,256]{2,1,0:T(8,128)(2,1)S(1)}, u32[]{:S(2)}, u32[]{:S(2)}) collective-permute-start(bf16[12,64,256]{2,1,0:T(8,128)(2,1)S(1)} %constant_dynamic-update-slice_fusion.1.refs_12_), channel_id=1, source_target_pairs={{0,1},{1,0},{2,3},{3,2},{4,5},{5,4},{6,7},{7,6},{8,9},{9,8},{10,11... | collective-permute-start | bytes 1179656 | tf_op jit(solution)/shard_map/ppermute | solution.py:324
  62.2 35.3 %copy-start = (bf16[2,272,512]{2,1,0:T(8,128)(2,1)}, bf16[2,272,512]{2,1,0:T(8,128)(2,1)S(1)}, u32[]{:S(2)}) copy-start(bf16[2,272,512]{2,1,0:T(8,128)(2,1)S(1)} %collective-permute-done.3.refs_4_) | copy-start | bytes 1671172
  62.2 26.1 %collective-permute-start.6 = (bf16[272,512]{1,0:T(8,128)(2,1)S(1)}, bf16[272,512]{1,0:T(8,128)(2,1)S(1)}, u32[]{:S(2)}, u32[]{:S(2)}) collective-permute-start(bf16[272,512]{1,0:T(8,128)(2,1)S(1)} %get-tuple-element.79), channel_id=1, source_target_pairs={{0,12},{1,13},{2,14},{3,15},{4,0},{5,1},{6,2},{7,3},{8,4},{9,5},{1... | collective-permute-start | bytes 835592 | tf_op jit(solution)/shard_map/ppermute | solution.py:283
  71.4 16.9 %collective-permute-start.5 = (bf16[272,512]{1,0:T(8,128)(2,1)S(1)}, bf16[272,512]{1,0:T(8,128)(2,1)S(1)}, u32[]{:S(2)}, u32[]{:S(2)}) collective-permute-start(bf16[272,512]{1,0:T(8,128)(2,1)S(1)} %get-tuple-element.82), channel_id=1, source_target_pairs={{0,4},{1,5},{2,6},{3,7},{4,8},{5,9},{6,10},{7,11},{8,12},{9,13},{1... | collective-permute-start | bytes 835592 | tf_op jit(solution)/shard_map/ppermute | solution.py:283
  71.6 17.6 %collective-permute-start.8 = (bf16[128,512]{1,0:T(8,128)(2,1)S(1)}, bf16[128,512]{1,0:T(8,128)(2,1)S(1)}, u32[]{:S(2)}, u32[]{:S(2)}) collective-permute-start(bf16[128,512]{1,0:T(8,128)(2,1)S(1)} %slice.195), channel_id=1, source_target_pairs={{1,13},{2,14},{3,15},{4,0},{6,2},{7,3},{8,4},{11,7},{13,9},{14,10}... | collective-permute-start | bytes 393224 | tf_op jit(solution)/shard_map/ppermute | solution.py:283
  77.7 10.6 %collective-permute-start.7 = (bf16[144,512]{1,0:T(8,128)(2,1)S(1)}, bf16[144,512]{1,0:T(8,128)(2,1)S(1)}, u32[]{:S(2)}, u32[]{:S(2)}) collective-permute-start(bf16[144,512]{1,0:T(8,128)(2,1)S(1)} %slice.193), channel_id=1, source_target_pairs={{0,4},{3,7},{5,9},{6,10},{7,11},{9,13},{10,14},{11,15},{12,0},{14,... | collective-permute-start | bytes 442376 | tf_op jit(solution)/shard_map/ppermute | solution.py:283
  79.2 18.3 %collective-permute-start.13 = (bf16[24,64,256]{2,1,0:T(8,128)(2,1)S(1)}, bf16[24,64,256]{2,1,0:T(8,128)(2,1)S(1)}, u32[]{:S(2)}, u32[]{:S(2)}) collective-permute-start(bf16[24,64,256]{2,1,0:T(8,128)(2,1)S(1)} %pad_maximum_fusion), channel_id=1, source_target_pairs={{0,3},{1,2},{2,1},{3,0},{4,7},{5,6},{6,5},{7,4},{8,11},{9,10},{10,... | collective-permute-start | bytes 2359304 | tf_op jit(solution)/shard_map/ppermute | solution.py:325
  105.9 16.5 %collective-permute-start.14 = (bf16[2,256,512]{2,1,0:T(8,128)(2,1)}, bf16[2,256,512]{2,1,0:T(8,128)(2,1)S(1)}, u32[]{:S(2)}, u32[]{:S(2)}) collective-permute-start(bf16[2,256,512]{2,1,0:T(8,128)(2,1)} %get-tuple-element.49), channel_id=1, source_target_pairs={{0,1},{1,2},{2,3},{3,0},{4,5},{5,6},{6,7},{7,4},{8,9},{9,10},{10,1... | collective-permute-start | bytes 1572872 | tf_op jit(solution)/shard_map/ppermute | solution.py:283
  108.5 19.3 %collective-permute-start.15 = (bf16[2,256,512]{2,1,0:T(8,128)(2,1)}, bf16[2,256,512]{2,1,0:T(8,128)(2,1)S(1)}, u32[]{:S(2)}, u32[]{:S(2)}) collective-permute-start(bf16[2,256,512]{2,1,0:T(8,128)(2,1)} %get-tuple-element.50), channel_id=1, source_target_pairs={{0,3},{1,0},{2,1},{3,2},{4,7},{5,4},{6,5},{7,6},{8,11},{9,8},{10,9... | collective-permute-start | bytes 1572872 | tf_op jit(solution)/shard_map/ppermute | solution.py:283
  108.5 31.4 %collective-permute-start.16 = (bf16[2,256,512]{2,1,0:T(8,128)(2,1)}, bf16[2,256,512]{2,1,0:T(8,128)(2,1)S(1)}, u32[]{:S(2)}, u32[]{:S(2)}) collective-permute-start(bf16[2,256,512]{2,1,0:T(8,128)(2,1)} %get-tuple-element.51), channel_id=1, source_target_pairs={{0,1},{3,0},{4,5},{5,6},{8,9},{9,10},{13,14},{16,17},{19,16},{20,2... | collective-permute-start | bytes 1572872 | tf_op jit(solution)/shard_map/ppermute | solution.py:283
  109.2 28.5 %collective-permute-start.20 = (bf16[2,256,512]{2,1,0:T(8,128)(2,1)}, bf16[2,256,512]{2,1,0:T(8,128)(2,1)S(1)}, u32[]{:S(2)}, u32[]{:S(2)}) collective-permute-start(bf16[2,256,512]{2,1,0:T(8,128)(2,1)} %get-tuple-element.52), channel_id=1, source_target_pairs={{0,3},{4,7},{9,8},{13,12},{16,19},{20,23},{25,24},{29,28},{32,35},... | collective-permute-start | bytes 1572872 | tf_op jit(solution)/shard_map/ppermute | solution.py:283
  120.5 21.5 %collective-permute-start.24 = (bf16[2,256,512]{2,1,0:T(8,128)(2,1)}, bf16[2,256,512]{2,1,0:T(8,128)(2,1)S(1)}, u32[]{:S(2)}, u32[]{:S(2)}) collective-permute-start(bf16[2,256,512]{2,1,0:T(8,128)(2,1)} %get-tuple-element.54), channel_id=1, source_target_pairs={{0,3},{1,0},{2,1},{3,2},{4,7},{5,4},{6,5},{7,6},{8,11},{9,8},{10,9... | collective-permute-start | bytes 1572872 | tf_op jit(solution)/shard_map/ppermute | solution.py:283
  122.5 32.4 %collective-permute-start.25 = (bf16[2,256,512]{2,1,0:T(8,128)(2,1)}, bf16[2,256,512]{2,1,0:T(8,128)(2,1)S(1)}, u32[]{:S(2)}, u32[]{:S(2)}) collective-permute-start(bf16[2,256,512]{2,1,0:T(8,128)(2,1)} %get-tuple-element.59), channel_id=1, source_target_pairs={{0,1},{1,2},{2,3},{3,0},{4,5},{5,6},{6,7},{7,4},{8,9},{9,10},{10,1... | collective-permute-start | bytes 1572872 | tf_op jit(solution)/shard_map/ppermute | solution.py:283
  137.4 18.8 %collective-permute-start.26 = (bf16[2,256,512]{2,1,0:T(8,128)(2,1)S(1)}, bf16[2,256,512]{2,1,0:T(8,128)(2,1)S(1)}, u32[]{:S(2)}, u32[]{:S(2)}) collective-permute-start(bf16[2,256,512]{2,1,0:T(8,128)(2,1)S(1)} %add_convert_fusion), channel_id=1, source_target_pairs={{0,3},{1,0},{2,1},{3,2},{4,7},{5,4},{6,5},{7,6},{8,11},{9,8},{10,9... | collective-permute-start | bytes 1572872 | tf_op jit(solution)/shard_map/ppermute | solution.py:283
  137.6 33.7 %copy-start.19 = (bf16[2,256,512]{2,1,0:T(8,128)(2,1)S(1)}, bf16[2,256,512]{2,1,0:T(8,128)(2,1)}, u32[]{:S(2)}) copy-start(bf16[2,256,512]{2,1,0:T(8,128)(2,1)} %get-tuple-element.63) | copy-start | bytes 1572868
  137.6 14.9 %collective-permute-start.23 = (bf16[2,256,512]{2,1,0:T(8,128)(2,1)S(1)}, bf16[2,256,512]{2,1,0:T(8,128)(2,1)S(1)}, u32[]{:S(2)}, u32[]{:S(2)}) collective-permute-start(bf16[2,256,512]{2,1,0:T(8,128)(2,1)S(1)} %add_convert_fusion.1), channel_id=1, source_target_pairs={{0,1},{1,2},{2,3},{3,0},{4,5},{5,6},{6,7},{7,4},{8,9},{9,10},{10,1... | collective-permute-start | bytes 1572872 | tf_op jit(solution)/shard_map/ppermute | solution.py:283
  139.9 23.7 %collective-permute-start.18 = (bf16[2,256,512]{2,1,0:T(8,128)(2,1)S(1)}, bf16[2,256,512]{2,1,0:T(8,128)(2,1)S(1)}, u32[]{:S(2)}, u32[]{:S(2)}) collective-permute-start(bf16[2,256,512]{2,1,0:T(8,128)(2,1)S(1)} %copy-done.24), channel_id=1, source_target_pairs={{2,1},{3,2},{4,7},{7,6},{8,11},{11,10},{12,15},{18,17},{19,18},{20... | collective-permute-start | bytes 1572872 | tf_op jit(solution)/shard_map/ppermute | solution.py:283
  142.0 30.3 %collective-permute-start.19 = (bf16[2,256,512]{2,1,0:T(8,128)(2,1)S(1)}, bf16[2,256,512]{2,1,0:T(8,128)(2,1)S(1)}, u32[]{:S(2)}, u32[]{:S(2)}) collective-permute-start(bf16[2,256,512]{2,1,0:T(8,128)(2,1)S(1)} %copy-done.23), channel_id=1, source_target_pairs={{1,2},{5,6},{10,11},{14,15},{17,18},{21,22},{26,27},{30,31},{33,34... | collective-permute-start | bytes 1572872 | tf_op jit(solution)/shard_map/ppermute | solution.py:283
  152.6 18.8 %collective-permute-start.17 = (bf16[2,256,512]{2,1,0:T(8,128)(2,1)S(1)}, bf16[2,256,512]{2,1,0:T(8,128)(2,1)S(1)}, u32[]{:S(2)}, u32[]{:S(2)}) collective-permute-start(bf16[2,256,512]{2,1,0:T(8,128)(2,1)S(1)} %add_convert_fusion.3), channel_id=1, source_target_pairs={{0,1},{1,2},{5,6},{6,7},{9,10},{10,11},{14,15},{16,17},{17,18},{21... | collective-permute-start | bytes 1572872 | tf_op jit(solution)/shard_map/ppermute | solution.py:283
  154.9 17.5 %collective-permute-start.21 = (bf16[2,256,512]{2,1,0:T(8,128)(2,1)S(1)}, bf16[2,256,512]{2,1,0:T(8,128)(2,1)S(1)}, u32[]{:S(2)}, u32[]{:S(2)}) collective-permute-start(bf16[2,256,512]{2,1,0:T(8,128)(2,1)S(1)} %add_convert_fusion.2), channel_id=1, source_target_pairs={{3,2},{7,6},{8,11},{12,15},{19,18},{23,22},{24,27},{28,31},{35,34}... | collective-permute-start | bytes 1572872 | tf_op jit(solution)/shard_map/ppermute | solution.py:283
  157.3 18.1 %collective-permute-start.27 = (bf16[2,256,512]{2,1,0:T(8,128)(2,1)S(1)}, bf16[2,256,512]{2,1,0:T(8,128)(2,1)S(1)}, u32[]{:S(2)}, u32[]{:S(2)}) collective-permute-start(bf16[2,256,512]{2,1,0:T(8,128)(2,1)S(1)} %pad_maximum_fusion.2), channel_id=1, source_target_pairs={{0,16},{1,17},{2,18},{3,19},{4,20},{5,21},{6,22},{7,23},{8,24},{9,... | collective-permute-start | bytes 1572872 | tf_op jit(solution)/shard_map/ppermute | solution.py:382
  173.4 10.5 %collective-permute-start.22 = (bf16[2,256,512]{2,1,0:T(8,128)(2,1)S(1)}, bf16[2,256,512]{2,1,0:T(8,128)(2,1)S(1)}, u32[]{:S(2)}, u32[]{:S(2)}) collective-permute-start(bf16[2,256,512]{2,1,0:T(8,128)(2,1)S(1)} %pad_maximum_fusion.1), channel_id=1, source_target_pairs={{1,17},{2,18},{6,22},{7,23},{10,26},{11,27},{15,31},{17,33},{18,34... | collective-permute-start | bytes 1572872 | tf_op jit(solution)/shard_map/ppermute | solution.py:382
  (21 other events, 247.7 us)
